TPU v7x, 128 devices: a whole 4x4x4 slice. The times are simulated.
128 devices in a mesh: section: 2 (over core), dp: 4 (over z), ctx: 16 (over y, x).
Axes of the slice: x: 4, y: 4, z: 4, core: 2. Of those that a mesh axis runs over, the one named last changes fastest.
Arguments:
- boundary: bfloat16 [2, 2, 8192, 1536], P('section', None, ('dp', 'ctx')), may hold values from -6 to 6
- lengths: int32 [4, 2, 2], replicated, may hold values from 0 to 2048, as said below
- norm_gain: bfloat16 [2, 1536], P('section', 'dp'), may hold values from 0.5 to 1.5
- w_z: bfloat16 [2, 1536, 3072], P('section', 'dp'), may hold values from -0.15625 to 0.15625
- w_xbc: bfloat16 [2, 1536, 3328], P('section', 'dp'), may hold values from -0.15625 to 0.15625
- w_dt: bfloat16 [2, 1536, 48], P('section', 'dp'), may hold values from -0.15625 to 0.15625
- conv_weight: bfloat16 [2, 4, 3328], P('section', None, 'dp'), may hold values from -3 to 3
- conv_bias: bfloat16 [2, 3328], P('section', 'dp'), may hold values from -3 to 3
- dt_bias: float32 [2, 48], P('section')
- a_log: float32 [2, 48], P('section'), may hold values from -1 to 1
- d_skip: float32 [2, 48], P('section'), may hold values from 0.5 to 1.5
- gate_gain: bfloat16 [2, 3072], P('section', 'dp'), may hold values from 0.5 to 1.5
- w_out: bfloat16 [2, 3072, 1536], P('section', 'dp'), may hold values from -0.109375 to 0.109375
Outputs:
- boundary_out: float32 [2, 2, 8192, 1536], P('section', None, ('dp', 'ctx'))
- grad_norm_gain: float32 [2, 1536], P('section', ('dp', 'ctx'))
- grad_w_z: float32 [2, 1536, 3072], P('section', ('dp', 'ctx'))
- grad_w_xbc: float32 [2, 1536, 3328], P('section', ('dp', 'ctx'))
- grad_w_dt: float32 [2, 1536, 48], P('section', ('dp', 'ctx'))
- grad_conv_weight: float32 [2, 4, 3328], P('section', None, ('dp', 'ctx'))
- grad_conv_bias: float32 [2, 3328], P('section', ('dp', 'ctx'))
- grad_dt_bias: float32 [2, 48], P('section')
- grad_a_log: float32 [2, 48], P('section')
- grad_d_skip: float32 [2, 48], P('section')
- grad_gate_gain: float32 [2, 3072], P('section', ('dp', 'ctx'))
- grad_w_out: float32 [2, 3072, 1536], P('section', ('dp', 'ctx'))
Inputs may be any that keep to these rules, and one draw needn't show every extreme that they name: `lengths`: of each group and micro-batch, sequence one padded to a multiple of 256 plus sequence two fit in 2048 positions; in one micro-batch of each group, drawn from the seed, sequence one has all 2048 positions and sequence two is empty; otherwise both are at least 1 long.
All inputs are finite; a program needn't handle non-finite values.
Results may differ from a plain program's by a relative error of at most 0.013.
Values may be sent and summed in bfloat16 or wider, within the bound.
No kernel may reach another device: no remote copies, remote signals or barrier semaphores. Data moves between devices by JAX's collectives and lax.ppermute only.
A program may use at most 320 MiB of HBM per device.

v0:
```python
import jax
import jax.numpy as jnp
from jax import lax
from jax.sharding import PartitionSpec as P

HEADS = 48
HEADDIM = 64
STATE = 128
KERNEL = 4
SPAN = 256
MICRO = 2


EPSILON = 1e-05
PRECISE = lax.Precision.HIGHEST


def passed_along(value, axis, steps):
    count = lax.axis_size(axis)
    initial, last = (max(0, -steps), min(count, count - steps))
    return lax.ppermute(value, axis, [(source, source + steps) for source in range(initial, last)])


def prefix(value, axis, join, neutral):
    count, mine = (lax.axis_size(axis), lax.axis_index(axis))
    pieces = jax.tree.map(lambda part: lax.all_gather(part, axis), value)
    so_far = jax.tree.map(
        lambda part, zero: jnp.full_like(part, 0) + jnp.asarray(zero, part.dtype), value, neutral
    )

    def hop(position, so_far):
        longer = join(so_far, jax.tree.map(lambda part: part[position], pieces))
        return jax.tree.map(lambda new, old: jnp.where(position < mine, new, old), longer, so_far)

    return lax.fori_loop(0, count - 1, hop, so_far)


def prefix_2(value, axis, join, neutral):
    count = lax.axis_size(axis)
    place = lax.axis_index(axis)
    ahead = count - 1 - place
    gathered = jax.tree.map(
        lambda a, kind: lax.all_gather(a.astype(kind), axis),
        value,
        jax.tree.map(lambda a: jnp.bfloat16 if a.dtype == jnp.float32 else a.dtype, value),
    )
    state = jax.tree.map(lambda a, e: jnp.zeros_like(a) + jnp.asarray(e, a.dtype), value, neutral)

    def one(hop, state):
        source = count - 1 - hop
        return join(
            state,
            jax.tree.map(
                lambda a, own: lax.dynamic_index_in_dim(a, source, 0, False).astype(own.dtype),
                gathered,
                value,
            ),
        )

    return lax.fori_loop(0, ahead, one, state)


def rms_scale(values, gain_vec):
    return (
        values * lax.rsqrt(jnp.mean(values * values, axis=-1, keepdims=True) + EPSILON) * gain_vec
    )


def token_info(length_pair, row_count, offset):
    position = offset + jnp.arange(row_count, dtype=jnp.int32)
    first_len = length_pair[0]
    second_len = length_pair[1]
    padded = (first_len + SPAN - 1) // SPAN * SPAN
    in_second = position >= padded
    within = jnp.where(in_second, position - padded, position)
    usable = jnp.where(in_second, within < second_len, within < first_len)
    return (within, usable.astype(jnp.float32), (within == 0).astype(jnp.int32))


def mixer_inputs(extended, rate_in, conv_w, conv_b, dt_b, a_rate, within, usable):
    row_count = rate_in.shape[0]
    reach_back = conv_w.shape[0] - 1
    conv_sum = conv_b[None, :]
    for tap_index in range(reach_back + 1):
        allowed = (within >= reach_back - tap_index).astype(extended.dtype)
        conv_sum = (
            conv_sum
            + conv_w[tap_index][None, :]
            * extended[tap_index : tap_index + row_count]
            * allowed[:, None]
        )
    activated = jax.nn.silu(conv_sum)
    inner_width = HEADS * HEADDIM
    head_in = activated[:, :inner_width].reshape(row_count, HEADS, HEADDIM)
    b_proj = activated[:, inner_width : inner_width + STATE]
    c_proj = activated[:, inner_width + STATE :]
    dt_step = usable[:, None] * jax.nn.softplus(rate_in + dt_b[None, :])
    log_decay = dt_step * (-jnp.exp(a_rate))[None, :]
    return (head_in, b_proj, c_proj, dt_step, log_decay)


def ssd_output(head_in, b_proj, c_proj, dt_step, log_decay, starts, state_in):
    row_count = head_in.shape[0]
    cum_decay = jnp.cumsum(log_decay, axis=0)
    segment = jnp.cumsum(starts)
    row_index = jnp.arange(row_count, dtype=jnp.int32)
    visible = (row_index[:, None] >= row_index[None, :]) & (segment[:, None] == segment[None, :])
    gaps = cum_decay[:, None, :] - cum_decay[None, :, :]
    decay_mat = jnp.exp(jnp.where(visible[:, :, None], gaps, -1e30))
    scores = jnp.dot(c_proj, b_proj.T, precision=PRECISE)
    weights = decay_mat * scores[:, :, None] * dt_step[None, :, :]
    inside = jnp.einsum("ijh,jhp->ihp", weights, head_in, precision=PRECISE)
    entering = jnp.exp(cum_decay) * (segment == 0).astype(cum_decay.dtype)[:, None]
    carried = jnp.einsum("hpn,in->ihp", state_in, c_proj, precision=PRECISE)
    return inside + entering[:, :, None] * carried


def ssd_state(head_in, b_proj, dt_step, log_decay, starts):
    cum_decay = jnp.cumsum(log_decay, axis=0)
    segment = jnp.cumsum(starts)
    final_seg = segment[-1]
    tail_decay = (
        jnp.exp(cum_decay[-1][None, :] - cum_decay)
        * (segment == final_seg).astype(cum_decay.dtype)[:, None]
    )
    fresh_part = jnp.einsum(
        "jh,jhp,jn->hpn", tail_decay * dt_step, head_in, b_proj, precision=PRECISE
    )
    damping = jnp.exp(cum_decay[-1]) * (final_seg == 0).astype(cum_decay.dtype)
    return (damping, fresh_part)


def gate_norm(y_heads, head_in, skip_vec, gate_in, gain_vec):
    row_count = y_heads.shape[0]
    joined = (y_heads + skip_vec[None, :, None] * head_in).reshape(row_count, HEADS * HEADDIM)
    return rms_scale(joined * jax.nn.silu(gate_in), gain_vec)


def chain_pair(earlier, later):
    return (earlier[0] * later[0], later[0][:, None, None] * earlier[1] + later[1])


def forward_layer(hidden, weight_set, info):
    (
        norm_g,
        weight_z,
        weight_xbc,
        weight_dt,
        conv_w,
        conv_b,
        dt_b,
        a_rate,
        skip_vec,
        gain_two,
        weight_out,
    ) = weight_set
    within, usable, starts = info
    normed = rms_scale(hidden, norm_g.astype(jnp.float32)).astype(jnp.bfloat16)
    gate_in = jnp.dot(normed, weight_z, preferred_element_type=jnp.float32)
    mixed_in = jnp.dot(normed, weight_xbc, preferred_element_type=jnp.float32).astype(jnp.bfloat16)
    rate_in = jnp.dot(normed, weight_dt, preferred_element_type=jnp.float32)
    reach_back = KERNEL - 1
    edge_rows = passed_along(mixed_in[mixed_in.shape[0] - reach_back :], "ctx", 1)
    extended = jnp.concatenate([edge_rows, mixed_in], 0).astype(jnp.float32)
    head_in, b_proj, c_proj, dt_step, log_decay = mixer_inputs(
        extended,
        rate_in,
        conv_w.astype(jnp.float32),
        conv_b.astype(jnp.float32),
        dt_b,
        a_rate,
        within,
        usable,
    )
    damping, fresh_part = ssd_state(head_in, b_proj, dt_step, log_decay, starts)
    unit_decay = jnp.ones_like(damping)
    zero_state = jnp.zeros_like(fresh_part)
    state_in = prefix((damping, fresh_part), "ctx", chain_pair, (unit_decay, zero_state))[1]
    y_heads = ssd_output(head_in, b_proj, c_proj, dt_step, log_decay, starts, state_in)
    normed_two = gate_norm(
        y_heads, head_in, skip_vec, gate_in, gain_two.astype(jnp.float32)
    ).astype(jnp.bfloat16)
    branch = jnp.dot(normed_two, weight_out, preferred_element_type=jnp.float32)
    result = hidden + usable[:, None] * branch
    return (result, (hidden, normed, gate_in, extended, rate_in, state_in, normed_two))


def backward_layer(cotangent, saved, info, weight_set):
    (
        norm_g,
        weight_z,
        weight_xbc,
        weight_dt,
        conv_w,
        conv_b,
        dt_b,
        a_rate,
        skip_vec,
        gain_two,
        weight_out,
    ) = weight_set
    hidden, normed, gate_in, extended, rate_in, state_in, normed_two = saved
    within, usable, starts = info
    row_count = hidden.shape[0]
    branch_grad = (usable[:, None] * cotangent).astype(jnp.bfloat16)
    d_out_weight = jnp.dot(normed_two.T, branch_grad, preferred_element_type=jnp.float32)
    d_normed_two = jnp.dot(branch_grad, weight_out.T, preferred_element_type=jnp.float32)
    small_weights = (
        conv_w.astype(jnp.float32),
        conv_b.astype(jnp.float32),
        dt_b,
        a_rate,
        skip_vec,
        gain_two.astype(jnp.float32),
    )

    def tail_part(ext_val, rate_val, gate_val, state_val, small_val):
        conv_wt, conv_bs, dt_bs, a_val, skip_val, gain_val = small_val
        head_in, b_proj, c_proj, dt_step, log_decay = mixer_inputs(
            ext_val, rate_val, conv_wt, conv_bs, dt_bs, a_val, within, usable
        )
        y_heads = ssd_output(head_in, b_proj, c_proj, dt_step, log_decay, starts, state_val)
        return gate_norm(y_heads, head_in, skip_val, gate_val, gain_val)

    _, pull_tail = jax.vjp(tail_part, extended, rate_in, gate_in, state_in, small_weights)
    d_ext, d_rate, d_gate, own_state, d_small = pull_tail(d_normed_two)

    def carry_part(ext_val, rate_val, small_val):
        conv_wt, conv_bs, dt_bs, a_val = small_val
        head_in, b_proj, c_proj, dt_step, log_decay = mixer_inputs(
            ext_val, rate_val, conv_wt, conv_bs, dt_bs, a_val, within, usable
        )
        return ssd_state(head_in, b_proj, dt_step, log_decay, starts)

    (damping, _), pull_carry = jax.vjp(carry_part, extended, rate_in, small_weights[:4])
    unit_decay = jnp.ones_like(damping)
    zero_state = jnp.zeros_like(own_state)
    later_grad = prefix_2((damping, own_state), "ctx", chain_pair, (unit_decay, zero_state))[1]
    d_damping = jnp.sum(later_grad * state_in, axis=(1, 2))
    more_ext, more_rate, more_small = pull_carry((d_damping, later_grad))
    d_ext = d_ext + more_ext
    d_rate = d_rate + more_rate
    reach_back = KERNEL - 1
    back_edge = passed_along(d_ext[:reach_back].astype(jnp.bfloat16), "ctx", -1).astype(jnp.float32)
    d_mixed = d_ext[reach_back:] + jnp.pad(back_edge, ((row_count - reach_back, 0), (0, 0)))
    d_mixed_low = d_mixed.astype(jnp.bfloat16)
    d_gate_low = d_gate.astype(jnp.bfloat16)
    d_rate_low = d_rate.astype(jnp.bfloat16)
    d_normed = (
        jnp.dot(d_gate_low, weight_z.T, preferred_element_type=jnp.float32)
        + jnp.dot(d_mixed_low, weight_xbc.T, preferred_element_type=jnp.float32)
        + jnp.dot(d_rate_low, weight_dt.T, preferred_element_type=jnp.float32)
    )
    d_weight_z = jnp.dot(normed.T, d_gate_low, preferred_element_type=jnp.float32)
    d_weight_xbc = jnp.dot(normed.T, d_mixed_low, preferred_element_type=jnp.float32)
    d_weight_dt = jnp.dot(normed.T, d_rate_low, preferred_element_type=jnp.float32)
    _, pull_norm = jax.vjp(rms_scale, hidden, norm_g.astype(jnp.float32))
    d_hidden, d_norm_g = pull_norm(d_normed)
    d_hidden = cotangent + d_hidden
    grads = (
        d_norm_g,
        d_weight_z,
        d_weight_xbc,
        d_weight_dt,
        d_small[0] + more_small[0],
        d_small[1] + more_small[1],
        d_small[2] + more_small[2],
        d_small[3] + more_small[3],
        d_small[4],
        d_small[5],
        d_out_weight,
    )
    return (d_hidden, grads)


def assemble(pieces, dt_bias, a_log, d_skip):
    return (
        pieces[0][0],
        pieces[1][0],
        pieces[2][0],
        pieces[3][0],
        pieces[4][0],
        pieces[5][0],
        dt_bias[0],
        a_log[0],
        d_skip[0],
        pieces[6][0],
        pieces[7][0],
    )


def on_device(
    boundary,
    lengths,
    norm_gain,
    w_z,
    w_xbc,
    w_dt,
    conv_weight,
    conv_bias,
    dt_bias,
    a_log,
    d_skip,
    gate_gain,
    w_out,
):
    section_index = lax.axis_index("section")
    row_count = boundary.shape[2]
    width = boundary.shape[3]
    offset = lax.axis_index("ctx") * row_count
    group = lax.axis_index("dp")
    gathered = (
        lax.all_gather(norm_gain, "dp", axis=1, tiled=True),
        lax.all_gather(w_z, "dp", axis=1, tiled=True),
        lax.all_gather(w_xbc, "dp", axis=1, tiled=True),
        lax.all_gather(w_dt, "dp", axis=1, tiled=True),
        lax.all_gather(conv_weight, "dp", axis=2, tiled=True),
        lax.all_gather(conv_bias, "dp", axis=1, tiled=True),
        lax.all_gather(gate_gain, "dp", axis=1, tiled=True),
        lax.all_gather(w_out, "dp", axis=1, tiled=True),
    )
    fwd_weights = assemble(gathered, dt_bias, a_log, d_skip)
    received = jnp.zeros((row_count, width), jnp.bfloat16)
    fwd_out = []
    stored = []
    for tick_index in range(MICRO + 1):
        first_micro = min(tick_index, MICRO - 1)
        second_micro = max(tick_index - 1, 0)
        micro_index = jnp.where(section_index == 0, first_micro, second_micro)
        info = token_info(lengths[group, micro_index], row_count, offset)
        hidden = jnp.where(
            section_index == 0,
            boundary[0, first_micro].astype(jnp.float32),
            received.astype(jnp.float32),
        )
        result, saved = forward_layer(hidden, fwd_weights, info)
        fwd_out.append(result)
        stored.append((saved, info))
        if tick_index < MICRO:
            received = passed_along(result.astype(jnp.bfloat16), "section", 1)
    returned = jnp.zeros((row_count, width), jnp.bfloat16)
    bwd_dx = []
    big_sums = None
    head_sums = None
    for back_tick in range(MICRO + 1):
        upper_entry = stored[min(back_tick + 1, MICRO)]
        lower_entry = stored[max(back_tick - 1, 0)]
        saved, info = jax.tree.map(
            lambda first_val, second_val: jnp.where(section_index == 1, first_val, second_val),
            upper_entry,
            lower_entry,
        )
        live_last = 1.0 if back_tick < MICRO else 0.0
        live_first = 1.0 if back_tick >= 1 else 0.0
        cotangent = jnp.where(
            section_index == 1,
            boundary[0, min(back_tick, MICRO - 1)].astype(jnp.float32) * live_last,
            returned.astype(jnp.float32) * live_first,
        )
        d_hidden, grads = backward_layer(cotangent, saved, info, fwd_weights)
        bwd_dx.append(d_hidden)
        if back_tick < MICRO:
            returned = passed_along(d_hidden.astype(jnp.bfloat16), "section", -1)
        heads_now = (grads[6], grads[7], grads[8])
        head_sums = (
            heads_now if head_sums is None else tuple((a + b for a, b in zip(head_sums, heads_now)))
        )
        full_now = (grads[0], grads[1], grads[2], grads[3], grads[4], grads[5], grads[9], grads[10])
        big_sums = (
            full_now if big_sums is None else tuple((a + b for a, b in zip(big_sums, full_now)))
        )
    shards = (
        lax.psum_scatter(big_sums[0][None], ("dp", "ctx"), scatter_dimension=1, tiled=True),
        lax.psum_scatter(big_sums[1][None], ("dp", "ctx"), scatter_dimension=1, tiled=True),
        lax.psum_scatter(big_sums[2][None], ("dp", "ctx"), scatter_dimension=1, tiled=True),
        lax.psum_scatter(big_sums[3][None], ("dp", "ctx"), scatter_dimension=1, tiled=True),
        lax.psum_scatter(big_sums[4][None], ("dp", "ctx"), scatter_dimension=2, tiled=True),
        lax.psum_scatter(big_sums[5][None], ("dp", "ctx"), scatter_dimension=1, tiled=True),
        lax.psum_scatter(big_sums[6][None], ("dp", "ctx"), scatter_dimension=1, tiled=True),
        lax.psum_scatter(big_sums[7][None], ("dp", "ctx"), scatter_dimension=1, tiled=True),
    )
    head_total = lax.psum((head_sums[0], head_sums[1], head_sums[2]), ("dp", "ctx"))
    top = jnp.stack(
        [
            jnp.where(section_index == 0, bwd_dx[micro_index + 1], fwd_out[micro_index + 1])
            for micro_index in range(MICRO)
        ]
    )[None]
    return (
        top,
        shards[0],
        shards[1],
        shards[2],
        shards[3],
        shards[4],
        shards[5],
        head_total[0][None],
        head_total[1][None],
        head_total[2][None],
        shards[6],
        shards[7],
    )


def solution(mesh):
    in_specs = (
        P("section", None, ("dp", "ctx"), None),
        P(),
        P("section", "dp"),
        P("section", "dp", None),
        P("section", "dp", None),
        P("section", "dp", None),
        P("section", None, "dp"),
        P("section", "dp"),
        P("section", None),
        P("section", None),
        P("section", None),
        P("section", "dp"),
        P("section", "dp", None),
    )
    out_specs = (
        P("section", None, ("dp", "ctx"), None),
        P("section", ("dp", "ctx")),
        P("section", ("dp", "ctx"), None),
        P("section", ("dp", "ctx"), None),
        P("section", ("dp", "ctx"), None),
        P("section", None, ("dp", "ctx")),
        P("section", ("dp", "ctx")),
        P("section", None),
        P("section", None),
        P("section", None),
        P("section", ("dp", "ctx")),
        P("section", ("dp", "ctx"), None),
    )
    return jax.shard_map(
        on_device, mesh=mesh, in_specs=in_specs, out_specs=out_specs, check_vma=False
    )
```

profile of v0, /device:TPU:12, one launch (start us, length us, event | category | flops | bytes accessed | tf_op | source)
XLA Modules:
  0.0 2905.3 jit_solution(2310785886831841989)
XLA Ops:
  13.2 11.8 all_gather.86
  25.1 12.7 all_gather.88
  43.2 30.8 %all_gather.85 = bf16[1,4,3328]{1,0,2:T(2,128)(2,1)S(1)} all-gather(bf16[1,4,832]{1,0,2:T(2,128)(2,1)S(1)} %copy.384), channel_id=1, replica_groups=mesh['section'=2,'dp'=4,'ctx'=16] {'dp'}, dimensions={2}, use_global_device_ids=true | all-gather | bytes 33280 | tf_op jit(solution)/shard_map/all_gather | solution.py:317
  77.9 69.1 %slice_reduce_fusion.3 = (f32[3328]{0:T(1024)S(1)}, f32[3328]{0:T(1024)S(1)}, f32[3328]{0:T(1024)S(1)}, f32[3328]{0:T(1024)S(1)}) fusion(f32[1,4,3328]{1,0,2:T(1,128)S(1)} %convert_element_type.640), kind=kLoop, calls=%fused_computation.184 | loop fusion | bytes 106496 | tf_op jit(solution)/shard_map/jvp()/slice | solution.py:88
  158.3 9.8 all-reduce.72
  180.4 11.8 all_gather.93
  193.1 19.5 all-gather.6
  213.8 115.8 %all-gather.28.cloned.1.call-done = f32[768,64,128]{2,1,0:T(8,128)} async-done(((f32[48,64,128]{2,1,0:T(8,128)}), f32[768,64,128]{2,1,0:T(8,128)}) %all-gather.28.cloned.1.call-update) | async-done | bytes 25165840 | tf_op jit(solution)/shard_map/all_gather | solution.py:26
  329.6 28.1 while.87
  369.5 54.9 %all-gather.24.cloned.1.call-done = bf16[1,1536,3072]{2,1,0:T(8,128)(2,1)} async-done(((bf16[1,384,3072]{2,1,0:T(8,128)(2,1)}), bf16[1,1536,3072]{2,1,0:T(8,128)(2,1)}) %all-gather.24.cloned.1.call-update) | async-done | bytes 9437200 | tf_op jit(solution)/shard_map/all_gather | solution.py:314
  431.1 87.8 %all-gather.26.cloned.1.call-done = bf16[1,3072,1536]{2,1,0:T(8,128)(2,1)} async-done(((bf16[1,768,1536]{2,1,0:T(8,128)(2,1)}), bf16[1,3072,1536]{2,1,0:T(8,128)(2,1)}) %all-gather.26.cloned.1.call-update) | async-done | bytes 9437200 | tf_op jit(solution)/shard_map/all_gather | solution.py:320
  556.5 21.1 all-gather.7
  589.8 116.0 %all-gather.30.cloned.1.call-done = f32[768,64,128]{2,1,0:T(8,128)} async-done(((f32[48,64,128]{2,1,0:T(8,128)}), f32[768,64,128]{2,1,0:T(8,128)}) %all-gather.30.cloned.1.call-update) | async-done | bytes 25165840 | tf_op jit(solution)/shard_map/all_gather | solution.py:26
  705.8 49.3 %while.88 = (s32[]{:T(128)}, f32[48,64,128]{2,1,0:T(8,128)}, s32[]{:T(128)}, f32[16,48]{1,0:T(8,128)S(1)}, f32[16,48,64,128]{3,2,1,0:T(8,128)}, /*index=5*/s32[]{:T(128)}, s32[]{:T(128)}) while((s32[]{:T(128)}, f32[48,64,128]{2,1,0:T(8,128)}, s32[]{:T(128)}, f32[16,48]{1,0:T(8,128)S(1)}, f32[16,48,64,128]{3,2,1,0:T(8,128)}, ...), condition=%wide.region_12.14_spmd.clone, body=%wide.region_11.13_spmd.clone.sunk | while | flops 1572868 | bytes 4719281 | solution.py:35
  810.0 20.2 all-gather.8
  842.5 10.4 fusion.119
  874.4 8.0 fusion.33
  882.5 13.7 all-gather.32.cloned.1.call-done
  897.6 33.3 %while.84 = (s32[]{:T(128)}, f32[48,64,128]{2,1,0:T(8,128)}, s32[]{:T(128)}, bf16[16,48]{1,0:T(8,128)(2,1)}, bf16[16,48,64,128]{3,2,1,0:T(8,128)(2,1)}, /*index=5*/s32[]{:T(128)}, s32[]{:T(128)}, s32[]{:T(128)}, s32[]{:T(128)}) while((s32[]{:T(128)}, f32[48,64,128]{2,1,0:T(8,128)}, s32[]{:T(128)}, bf16[16,48]{1,0:T(8,128)(2,1)}, ...), condition=%wide.region_17.19_spmd, body=%wide.region_16.18_spmd.sunk | while | flops 1179702 | bytes 3932795 | solution.py:60
  1022.6 32.4 %all-gather.9 = f32[16,1,48]{2,1,0:T(1,128)S(1)} all-gather(f32[1,1,48]{2,1,0:T(1,128)S(1)} %copy-done.310), channel_id=1, replica_groups=mesh['section'=2,'dp'=4,'ctx'=16] {'ctx'}, dimensions={0}, use_global_device_ids=true | all-gather | bytes 3264 | tf_op jit(solution)/shard_map/all_gather | solution.py:26
  1077.7 97.0 %all-gather.34.cloned.1.call-done = f32[768,64,128]{2,1,0:T(8,128)} async-done(((f32[48,64,128]{2,1,0:T(8,128)}), f32[768,64,128]{2,1,0:T(8,128)}) %all-gather.34.cloned.1.call-update) | async-done | bytes 25165840 | tf_op jit(solution)/shard_map/all_gather | solution.py:26
  1174.7 49.0 %while.89 = (s32[]{:T(128)}, f32[48,64,128]{2,1,0:T(8,128)}, s32[]{:T(128)}, f32[16,48]{1,0:T(8,128)S(1)}, f32[16,48,64,128]{3,2,1,0:T(8,128)}, /*index=5*/s32[]{:T(128)}, s32[]{:T(128)}) while((s32[]{:T(128)}, f32[48,64,128]{2,1,0:T(8,128)}, s32[]{:T(128)}, f32[16,48]{1,0:T(8,128)S(1)}, f32[16,48,64,128]{3,2,1,0:T(8,128)}, ...), condition=%wide.region_35.37_spmd.clone, body=%wide.region_34.36_spmd.clone.sunk | while | flops 1572868 | bytes 4719281 | solution.py:35
  1285.5 20.4 all-gather.10
  1311.9 9.6 fusion.121
  1349.2 7.9 fusion.29
  1357.1 16.6 all-gather.36.cloned.1.call-done
  1375.1 32.8 %while.85 = (s32[]{:T(128)}, f32[48,64,128]{2,1,0:T(8,128)}, s32[]{:T(128)}, bf16[16,48]{1,0:T(8,128)(2,1)}, bf16[16,48,64,128]{3,2,1,0:T(8,128)(2,1)}, /*index=5*/s32[]{:T(128)}, s32[]{:T(128)}, s32[]{:T(128)}, s32[]{:T(128)}) while((s32[]{:T(128)}, f32[48,64,128]{2,1,0:T(8,128)}, s32[]{:T(128)}, bf16[16,48]{1,0:T(8,128)(2,1)}, ...), condition=%wide.region_40.42_spmd, body=%wide.region_39.41_spmd.sunk | while | flops 1179702 | bytes 3932795 | solution.py:60
  1422.7 8.5 multiply_reduce_fusion.14
  1470.5 8.3 multiply_reduce_fusion.30
  1491.3 10.5 fusion.538
  1507.7 39.1 %all-gather.11 = bf16[16,1,48]{2,1,0:T(2,128)(2,1)S(1)} all-gather(bf16[1,1,48]{2,1,0:T(2,128)(2,1)S(1)} %bitcast.688), channel_id=1, replica_groups=mesh['section'=2,'dp'=4,'ctx'=16] {'ctx'}, dimensions={0}, use_global_device_ids=true | all-gather | bytes 1632 | tf_op jit(solution)/shard_map/all_gather | solution.py:43
  1548.7 10.6 fusion.539
  1569.9 9.6 fusion.123
  1599.1 8.1 fusion.27
  1608.5 33.6 %while.86 = (s32[]{:T(128)}, f32[48,64,128]{2,1,0:T(8,128)}, s32[]{:T(128)}, bf16[16,48]{1,0:T(8,128)(2,1)}, bf16[16,48,64,128]{3,2,1,0:T(8,128)(2,1)}, /*index=5*/s32[]{:T(128)}, s32[]{:T(128)}, s32[]{:T(128)}, s32[]{:T(128)}) while((s32[]{:T(128)}, f32[48,64,128]{2,1,0:T(8,128)}, s32[]{:T(128)}, bf16[16,48]{1,0:T(8,128)(2,1)}, ...), condition=%wide.region_57.59_spmd, body=%wide.region_56.58_spmd.sunk | while | flops 1179702 | bytes 3932795 | solution.py:60
  1700.1 20.4 add_bitcast_fusion.2
  1721.8 7.9 fusion.321
  1730.9 9.0 fusion.319
  1739.9 21.1 add_bitcast_fusion.1
  1762.5 8.5 fusion.363
  1771.0 8.4 fusion.366
  1779.4 21.7 add_bitcast_fusion
  1803.7 15.5 reduce-scatter.19.cloned.1.call-done
  1827.4 120.5 %all-reduce.80.cloned.1.call-done = (f32[1,1536]{1,0:T(1,128)}, f32[1,4,3328]{2,1,0:T(4,128)}, f32[1,3328]{1,0:T(1,128)}, f32[1,48]{1,0:T(1,128)}, f32[1,48]{1,0:T(1,128)}, /*index=5*/f32[1,48]{1,0:T(1,128)}) async-done(((f32[1,1536]{1,0:T(1,128)}, f32[1,4,3328]{2,1,0:T(4,128)}, f32[1,3328]{1,0:T(1,128)}, f32[1,48]{1,0:T(1,128)}, f32[1,48]{1,0:T(1,128)}, /*index=5*/f32[1,48]{1,0:T(1,128)}), ...) | async-done | bytes 73296
  1951.8 217.1 %reduce-scatter.21.cloned.1.call-done = f32[1,24,48]{2,0,1:T(1,128)} async-done(((f32[1,1536,48]{2,0,1:T(1,128)}), f32[1,24,48]{2,0,1:T(1,128)}) %reduce-scatter.21.cloned.1.call-update) | async-done | bytes 4624
  2168.9 241.5 %reduce-scatter.13.cloned.1.call-done = f32[1,24,3072]{2,1,0:T(8,128)} async-done(((f32[1,1536,3072]{2,1,0:T(8,128)}), f32[1,24,3072]{2,1,0:T(8,128)}) %reduce-scatter.13.cloned.1.call-update) | async-done | bytes 294928 | tf_op jit(solution)/shard_map/reduce_scatter | solution.py:374
  2410.4 240.7 %reduce-scatter.17.cloned.1.call-done = f32[1,48,1536]{2,1,0:T(8,128)} async-done(((f32[1,3072,1536]{2,1,0:T(8,128)}), f32[1,48,1536]{2,1,0:T(8,128)}) %reduce-scatter.17.cloned.1.call-update) | async-done | bytes 294928 | tf_op jit(solution)/shard_map/reduce_scatter | solution.py:380
  2651.1 243.8 %reduce-scatter.15.cloned.1.call-done = f32[1,24,3328]{2,1,0:T(8,128)} async-done(((f32[1,1536,3328]{2,1,0:T(8,128)}), f32[1,24,3328]{2,1,0:T(8,128)}) %reduce-scatter.15.cloned.1.call-update) | async-done | bytes 319504 | tf_op jit(solution)/shard_map/reduce_scatter | solution.py:375
  (1259 shorter events, 808.6 us)
Async XLA Ops:
  7.2 33.7 %copy-start.7 = (bf16[1,2,128,1536]{3,2,1,0:T(8,128)(2,1)S(1)}, bf16[1,2,128,1536]{3,2,1,0:T(8,128)(2,1)}, u32[]{:S(2)}) copy-start(bf16[1,2,128,1536]{3,2,1,0:T(8,128)(2,1)} %param.26) | copy-start | bytes 2359300
  7.2 33.9 %copy-start.317 = (f32[1,48]{1,0:T(1,128)S(1)}, f32[1,48]{1,0:T(1,128)}, u32[]{:S(2)}) copy-start(f32[1,48]{1,0:T(1,128)} %param.35) | copy-start | bytes 580
  7.2 33.9 %copy-start.294 = (f32[1,48]{1,0:T(1,128)S(1)}, f32[1,48]{1,0:T(1,128)}, u32[]{:S(2)}) copy-start(f32[1,48]{1,0:T(1,128)} %param.34) | copy-start | bytes 580
  7.2 139.9 %all-gather.22.cloned.1.call-start = ((), (), s32[]{:S(2)}) async-start(), calls=%async_computation.5 | async-start | bytes 12779520 | tf_op jit(solution)/shard_map/all_gather | solution.py:315
  8.0 34.5 %copy-start.280 = (bf16[1,4,832]{2,1,0:T(4,128)(2,1)S(1)}, bf16[1,4,832]{2,1,0:T(4,128)(2,1)}, u32[]{:S(2)}) copy-start(bf16[1,4,832]{2,1,0:T(4,128)(2,1)} %param.32) | copy-start | bytes 19972
  8.0 321.6 %all-gather.28.cloned.1.call-start = ((), (), s32[]{:S(2)}) async-start(), calls=%async_computation.11 | async-start | bytes 26738688 | tf_op jit(solution)/shard_map/all_gather | solution.py:26
  40.9 35.6 %copy-start.286 = (f32[128]{0:T(128)}, f32[128]{0:T(128)S(1)}, u32[]{:S(2)}) copy-start(f32[128]{0:T(128)S(1)} %get-tuple-element.871) | copy-start | bytes 1540
  41.2 383.2 %copy-start.239 = (f32[128]{0:T(128)}, f32[128]{0:T(128)S(1)}, u32[]{:S(2)}) copy-start(f32[128]{0:T(128)S(1)} %add_rsqrt_fusion.5) | copy-start | bytes 1540
  77.8 448.2 %copy-start.236 = (f32[128]{0:T(128)}, f32[128]{0:T(128)S(1)}, u32[]{:S(2)}) copy-start(f32[128]{0:T(128)S(1)} %get-tuple-element.883) | copy-start | bytes 1540
  152.7 15.5 collective-permute-start
  168.1 373.9 %copy-start.97 = (f32[3328]{0:T(1024)}, f32[3328]{0:T(1024)S(1)}, u32[]{:S(2)}) copy-start(f32[3328]{0:T(1024)S(1)} %add.1235) | copy-start | bytes 39940
  177.6 246.8 %all-gather.24.cloned.1.call-start = ((), (), s32[]{:S(2)}) async-start(), calls=%async_computation.6 | async-start | bytes 11796480 | tf_op jit(solution)/shard_map/all_gather | solution.py:314
  178.3 340.6 %all-gather.26.cloned.1.call-start = ((), (), s32[]{:S(2)}) async-start(), calls=%async_computation.7 | async-start | bytes 11796480 | tf_op jit(solution)/shard_map/all_gather | solution.py:320
  178.9 527.0 %all-gather.30.cloned.1.call-start = ((), (), s32[]{:S(2)}) async-start(), calls=%async_computation.12 | async-start | bytes 26738688 | tf_op jit(solution)/shard_map/all_gather | solution.py:26
  180.4 345.6 %copy-start.276 = (s32[128]{0:T(128)}, s32[128]{0:T(128)S(1)}, u32[]{:S(2)}) copy-start(s32[128]{0:T(128)S(1)} %reduce.17) | copy-start | bytes 1540
  431.1 92.9 %copy-start.16 = (bf16[128,3072]{1,0:T(8,128)(2,1)}, bf16[128,3072]{1,0:T(8,128)(2,1)S(1)}, u32[]{:S(2)}) copy-start(bf16[128,3072]{1,0:T(8,128)(2,1)S(1)} %multiply_convert_fusion.2) | copy-start | bytes 2359300
  431.1 97.0 %copy-start.240 = (f32[128]{0:T(128)S(1)}, f32[128]{0:T(128)}, u32[]{:S(2)}) copy-start(f32[128]{0:T(128)} %copy-done.239) | copy-start | bytes 1540
  524.1 3.2 collective-permute-start.1
  529.1 255.4 %copy-start.45 = (bf16[128,1536]{1,0:T(8,128)(2,1)}, bf16[128,1536]{1,0:T(8,128)(2,1)S(1)}, u32[]{:S(2)}) copy-start(bf16[128,1536]{1,0:T(8,128)(2,1)S(1)} %get-tuple-element.830) | copy-start | bytes 1179652
  535.9 5.9 collective-permute-start.2
  551.9 344.3 %all-gather.32.cloned.1.call-start = ((), (), s32[]{:S(2)}) async-start(), calls=%async_computation.13 | async-start | bytes 13369344 | tf_op jit(solution)/shard_map/all_gather | solution.py:43
  555.6 217.9 %copy-start.94 = (f32[128,48]{0,1:T(8,128)}, f32[128,48]{0,1:T(8,128)S(1)}, u32[]{:S(2)}) copy-start(f32[128,48]{0,1:T(8,128)S(1)} %copy.394) | copy-start | bytes 73732
  555.7 217.8 %copy-start.122 = (f32[128,48]{0,1:T(8,128)}, f32[128,48]{0,1:T(8,128)S(1)}, u32[]{:S(2)}) copy-start(f32[128,48]{0,1:T(8,128)S(1)} %copy.396) | copy-start | bytes 73732
  589.8 183.7 %copy-start.158 = (f32[128,128]{1,0:T(8,128)}, f32[128,128]{1,0:T(8,128)S(1)}, u32[]{:S(2)}) copy-start(f32[128,128]{1,0:T(8,128)S(1)} %fusion.432) | copy-start | bytes 196612
  802.6 28.2 copy-start.313
  806.4 26.6 copy-start.9
  806.4 26.6 copy-start.76
  806.4 26.6 copy-start.238
  806.4 368.2 %all-gather.34.cloned.1.call-start = ((), (), s32[]{:S(2)}) async-start(), calls=%async_computation.14 | async-start | bytes 26738688 | tf_op jit(solution)/shard_map/all_gather | solution.py:26
  839.6 136.9 %collective-permute-start.5 = (bf16[128,1536]{1,0:T(8,128)(2,1)}, bf16[128,1536]{1,0:T(8,128)(2,1)}, u32[]{:S(2)}, u32[]{:S(2)}) collective-permute-start(bf16[128,1536]{1,0:T(8,128)(2,1)} %get-tuple-element.1049), channel_id=1, source_target_pairs={{0,64},{1,65},{2,66},{3,67},{4,68},{5,69},{6,70},{7,71},{8,72},{9,... | collective-permute-start | bytes 1179656 | tf_op jit(solution)/shard_map/ppermute | solution.py:21
  964.2 7.6 collective-permute-start.3
  989.6 9.2 collective-permute-start.6
  1008.4 365.4 %all-gather.36.cloned.1.call-start = ((), (), s32[]{:S(2)}) async-start(), calls=%async_computation.15 | async-start | bytes 13369344 | tf_op jit(solution)/shard_map/all_gather | solution.py:43
  1021.3 227.5 %collective-permute-start.4 = (bf16[128,1536]{1,0:T(8,128)(2,1)}, bf16[128,1536]{1,0:T(8,128)(2,1)}, u32[]{:S(2)}, u32[]{:S(2)}) collective-permute-start(bf16[128,1536]{1,0:T(8,128)(2,1)} %fusion.310), channel_id=1, source_target_pairs={{64,0},{65,1},{66,2},{67,3},{68,4},{69,5},{70,6},{71,7},{72,8},{73... | collective-permute-start | bytes 1179656 | tf_op jit(solution)/shard_map/ppermute | solution.py:21
  1276.8 72.3 %copy-start.59 = (bf16[128,3072]{1,0:T(8,128)(2,1)}, bf16[128,3072]{1,0:T(8,128)(2,1)S(1)}, u32[]{:S(2)}) copy-start(bf16[128,3072]{1,0:T(8,128)(2,1)S(1)} %get-tuple-element.911) | copy-start | bytes 2359300
  1280.2 27.0 copy-start.328
  1283.9 323.2 %all-gather.38.cloned.1.call-start = ((), (), s32[]{:S(2)}) async-start(), calls=%async_computation.16 | async-start | bytes 13369344 | tf_op jit(solution)/shard_map/all_gather | solution.py:43
  1441.1 7.6 collective-permute-start.7
  1458.6 11.8 collective-permute-start.8
  1489.6 329.6 %reduce-scatter.19.cloned.1.call-start = ((), (), s32[]{:S(2)}) async-start(), calls=%async_computation.17 | async-start | bytes 1597440
  1491.3 56.1 %copy-start.241 = (f32[128]{0:T(128)S(1)}, f32[128]{0:T(128)}, u32[]{:S(2)}) copy-start(f32[128]{0:T(128)} %copy-done.239) | copy-start | bytes 1540
  1501.8 46.6 %copy-start.207 = (f32[3072]{0:T(1024)S(1)}, f32[3072]{0:T(1024)}, u32[]{:S(2)}) copy-start(f32[3072]{0:T(1024)} %get-tuple-element.831) | copy-start | bytes 36868
  1598.4 349.5 %all-reduce.80.cloned.1.call-start = ((), (), s32[]{:S(2)}) async-start(), calls=%async_computation.19 | async-start | bytes 148480
  1679.7 11.7 collective-permute-start.9
  1698.0 470.9 %reduce-scatter.21.cloned.1.call-start = ((), (), s32[]{:S(2)}) async-start(), calls=%async_computation.18 | async-start | bytes 798720
  1700.0 710.4 %reduce-scatter.13.cloned.1.call-start = ((), (), s32[]{:S(2)}) async-start(), calls=%async_computation.8 | async-start | bytes 19169280 | tf_op jit(solution)/shard_map/reduce_scatter | solution.py:374
  1720.5 930.6 %reduce-scatter.17.cloned.1.call-start = ((), (), s32[]{:S(2)}) async-start(), calls=%async_computation.10 | async-start | bytes 19169280 | tf_op jit(solution)/shard_map/reduce_scatter | solution.py:380
  1761.0 1133.8 %reduce-scatter.15.cloned.1.call-start = ((), (), s32[]{:S(2)}) async-start(), calls=%async_computation.9 | async-start | bytes 20766720 | tf_op jit(solution)/shard_map/reduce_scatter | solution.py:375
  (325 other events, 2590.4 us)
Sparse Core Ops, SparseCore 0:
  9.7 115.8 all-gather.21
  177.7 151.8 all-gather.27
  331.3 93.0 all-gather.23
  425.9 93.0 all-gather.25
  552.0 153.7 all-gather.29
  806.6 89.5 all-gather.31
  1008.5 166.1 all-gather.33
  1284.0 89.6 all-gather.35
  1489.7 107.9 all-gather.37
  1601.8 217.2 reduce-scatter.18
  1825.4 122.4 all-reduce.79
  1953.3 215.5 reduce-scatter.20
  2174.9 235.4 reduce-scatter.12
  2415.6 235.4 reduce-scatter.16
  2657.0 237.7 reduce-scatter.14
where the time goes:
time: 2920 us; the launch traced here: 2910 us
  waiting for transfers between devices  1590 us (54%)
  matrix products  425 us (15%)
  other arithmetic  384 us (13%)
  blocking collectives  230 us (8%)
  local copies, waits for them, and re-layouts  210 us (7%)
  starting transfers between devices  34.8 us (1%)
    unnamed x18, waiting for transfers between devices  355 us
    all_gather x3, waiting for transfers between devices, prefix(): pieces = jax.tree.map(lambda part: lax.all_gather(part, axis), value)  329 us
    reduce_scatter x1, waiting for transfers between devices, on_device(): lax.psum_scatter(big_sums[2][None], ('dp', 'ctx'), scatter_dimension=1, t...  244 us
    reduce_scatter x1, waiting for transfers between devices, on_device(): lax.psum_scatter(big_sums[1][None], ('dp', 'ctx'), scatter_dimension=1, t...  242 us
    reduce_scatter x1, waiting for transfers between devices, on_device(): lax.psum_scatter(big_sums[7][None], ('dp', 'ctx'), scatter_dimension=1, t...  241 us
    select_n x45, other arithmetic, hop(): jnp.where(position < mine, new, old)  125 us
    dot_general x12, matrix products, ssd_output(): inside = jnp.einsum('ijh,jhp->ihp', weights, head_in, precision=PRECISE)  94.2 us
    all_gather x1, waiting for transfers between devices, on_device(): lax.all_gather(w_out, 'dp', axis=1, tiled=True)  87.8 us
  transfers between devices with their start and end apart: 25, of which 17 were waited for; matrix products, arithmetic and copies ran while one was open for 25% of the time, Pallas kernels for 0%

commit v1 on v0

v1 whole, which is shorter than its diff:
```python
import functools

import jax
import jax.numpy as jnp
from jax import lax
from jax.experimental import pallas as pl
from jax.experimental.pallas import tpu as pltpu
from jax.sharding import PartitionSpec as P

HEADS = 48
HEADDIM = 64
STATE = 128
KERNEL = 4
SPAN = 256
MICRO = 2
WIDTH = 1536
INNER = 3072
CONV_CH = 3328
LANES = 128
GROUPS = 8
OWN = HEADS // GROUPS
BLOCK = OWN * HEADDIM
ROWS = 256
HALF = 128
PACKED = CONV_CH + LANES
EPSILON = 1e-05
PRECISE = lax.Precision.HIGHEST
F32 = jnp.float32
BF16 = jnp.bfloat16
VMEM_LIMIT = 56 * 1024 * 1024


def params(**more):
    return pltpu.CompilerParams(vmem_limit_bytes=VMEM_LIMIT, **more)


def whole(shape):
    return pl.BlockSpec(shape, lambda *_: (0,) * len(shape))


def columns(rows, width):
    return pl.BlockSpec((rows, width), lambda g: (0, g))


def grouped(rows):
    return pl.BlockSpec((1, rows, BLOCK), lambda g: (g, 0, 0))


SMEM = pl.BlockSpec(memory_space=pltpu.SMEM)
ANYWHERE = pl.BlockSpec(memory_space=pl.ANY)


def shape(dims, kind=F32):
    return jax.ShapeDtypeStruct(dims, kind)


def dot(a, b):
    return jnp.dot(a, b, preferred_element_type=F32)


def dot_nt(a, b):
    return lax.dot_general(a, b, (((1,), (1,)), ((), ())), preferred_element_type=F32)


def exact_dot(a, b):
    return jnp.dot(a, b, precision=PRECISE, preferred_element_type=F32)


def lane_of(dims):
    return lax.broadcasted_iota(jnp.int32, dims, len(dims) - 1)


def row_of(dims):
    return lax.broadcasted_iota(jnp.int32, dims, len(dims) - 2)


def sigmoid(v):
    return 1.0 / (1.0 + jnp.exp(-v))


def softplus(v):
    return jnp.maximum(v, 0.0) + jnp.log1p(jnp.exp(-jnp.abs(v)))


def rolled(values, g):
    return pltpu.roll(values, lax.rem(LANES - 8 * g, LANES), axis=1)


def pair_lanes(values, p):
    low = lane_of((values.shape[0], LANES)) < HEADDIM
    return jnp.where(low, values[:, 2 * p : 2 * p + 1], values[:, 2 * p + 1 : 2 * p + 2])


def spread(values):
    return jnp.concatenate([pair_lanes(values, p) for p in range(OWN // 2)], axis=1)


def head_sum_matrix(g):
    head = row_of((BLOCK, LANES)) // HEADDIM
    return (lane_of((BLOCK, LANES)) == head + 8 * g).astype(BF16)


def lower_triangle(strict=False):
    i, j = row_of((HALF, HALF)), lane_of((HALF, HALF))
    return ((i > j) if strict else (i >= j)).astype(F32)


def usable_rows(info):
    return (row_of((ROWS, 1)) < info[0]).astype(F32)


def half(values, q):
    return values[q * HALF : (q + 1) * HALF]


def copies_of(plan, refs, buffer, sems, info, part, sizes, by_rows):
    out = []
    for n, (which, index, row, count, place) in enumerate(plan(info)):
        source = refs[which] if index is None else refs[which].at[index]
        if by_rows:
            src = source.at[pl.ds(row, count)]
            dst = buffer.at[pl.ds(place, count)]
        else:
            cols = pl.ds(pl.multiple_of(part * sizes, LANES), sizes)
            src = source.at[pl.ds(row, count), cols]
            dst = buffer.at[pl.ds(place, count), cols]
        out.append(pltpu.make_async_copy(src, dst, sems.at[n, part]))
    return out


def whole_plan(rows):
    def plan(info):
        return [(0, None, 0, rows, 0)]

    return plan


def in_proj_body(plan, refs, info, h_ref, gain_ref, *rest):
    w_refs, (normed_ref, mixed_ref, rate_ref, buffer, sems) = rest[:refs], rest[refs:]
    parts = PACKED // 384

    def start(part, _):
        for c in copies_of(plan, w_refs, buffer, sems, info, part, 384, False):
            c.start()
        return 0

    lax.fori_loop(0, parts, start, 0)
    h = h_ref[...].astype(F32)
    scale = lax.rsqrt(jnp.mean(h * h, axis=1, keepdims=True) + EPSILON)
    normed_ref[...] = (h * scale * gain_ref[...]).astype(BF16)

    def one(part, _):
        for c in copies_of(plan, w_refs, buffer, sems, info, part, 384, False):
            c.wait()
        cols = pl.ds(pl.multiple_of(part * 384, LANES), 384)
        value = dot(normed_ref[...], buffer[:, cols])

        @pl.when(part < parts - 1)
        def _():
            mixed_ref[:, cols] = value.astype(BF16)

        @pl.when(part == parts - 1)
        def _():
            mixed_ref[:, CONV_CH - 256 :] = value[:, :256].astype(BF16)
            rate_ref[...] = value[:, 256:]

        return 0

    lax.fori_loop(0, parts, one, 0)


def in_proj(info, h, gain, weights, plan, count):
    return pl.pallas_call(
        functools.partial(in_proj_body, plan, len(weights)),
        out_shape=(shape((ROWS, WIDTH), BF16), shape((ROWS, CONV_CH), BF16), shape((ROWS, LANES))),
        in_specs=[SMEM, whole((ROWS, WIDTH)), whole((1, WIDTH))] + [ANYWHERE] * len(weights),
        out_specs=(whole((ROWS, WIDTH)), whole((ROWS, CONV_CH)), whole((ROWS, LANES))),
        scratch_shapes=[
            pltpu.VMEM((WIDTH, PACKED), BF16),
            pltpu.SemaphoreType.DMA((count, PACKED // 384)),
        ],
        compiler_params=params(),
        cost_estimate=pl.CostEstimate(
            flops=2 * ROWS * WIDTH * PACKED, bytes_accessed=14_000_000, transcendentals=0
        ),
        name="in_proj",
    )(info, h, gain, *weights)


def gate_proj_body(plan, refs, info, normed_ref, *rest):
    w_refs, (gate_ref, buffer, sems) = rest[:refs], rest[refs:]
    parts = INNER // 512

    def start(part, _):
        for c in copies_of(plan, w_refs, buffer, sems, info, part, 512, False):
            c.start()
        return 0

    lax.fori_loop(0, parts, start, 0)

    def one(part, _):
        for c in copies_of(plan, w_refs, buffer, sems, info, part, 512, False):
            c.wait()
        cols = pl.ds(pl.multiple_of(part * 512, LANES), 512)
        gate_ref[:, cols] = dot(normed_ref[...], buffer[:, cols])
        return 0

    lax.fori_loop(0, parts, one, 0)


def gate_proj(info, normed, weights, plan, count):
    return pl.pallas_call(
        functools.partial(gate_proj_body, plan, len(weights)),
        out_shape=shape((ROWS, INNER)),
        in_specs=[SMEM, whole((ROWS, WIDTH))] + [ANYWHERE] * len(weights),
        out_specs=whole((ROWS, INNER)),
        scratch_shapes=[
            pltpu.VMEM((WIDTH, INNER), BF16),
            pltpu.SemaphoreType.DMA((count, INNER // 512)),
        ],
        compiler_params=params(),
        cost_estimate=pl.CostEstimate(
            flops=2 * ROWS * WIDTH * INNER, bytes_accessed=14_000_000, transcendentals=0
        ),
        name="gate_proj",
    )(info, normed, *weights)


def conv_sum_of(values, halo, cpar, keep, ext):
    width = values.shape[1]
    ext[0:16, :width] = halo.astype(F32) * keep
    ext[16 : 16 + ROWS, :width] = values.astype(F32)
    total = cpar[4:5, :]
    for k in range(KERNEL):
        total = total + cpar[k : k + 1, :] * ext[13 + k : 13 + k + ROWS, :width]
    return total


def state_body(
    info, mixed, halo, cpar, bc, halo_bc, cpar_bc, rate, hpar,
    xa_ref, bca_ref, cum_ref, dt_ref, s0_ref, msg_ref, ext, bt, tail,
):
    g = pl.program_id(0)
    keep = info[1].astype(F32)

    @pl.when(g == 0)
    def _():
        total = conv_sum_of(bc[...], halo_bc[...], cpar_bc[...], keep, ext)
        active = total * sigmoid(total)
        bca_ref[...] = active
        bt[...] = active[:, :STATE].T.astype(BF16)
        dt = usable_rows(info) * softplus(rate[...] + hpar[0:1, :])
        log_decay = dt * -jnp.exp(hpar[1:2, :])
        dt_ref[...] = dt
        tri = lower_triangle()
        for q in range(2):
            rows = pl.ds(q * HALF, HALF)
            cum = exact_dot(tri, half(log_decay, q))
            cum_ref[rows, :] = cum
            tail[rows, :] = jnp.exp(cum[HALF - 1 :, :] - cum) * half(dt, q)

    total = conv_sum_of(mixed[...], halo[...], cpar[...], keep, ext)
    xa = total * sigmoid(total)
    xa_ref[...] = xa
    weighted = (xa * spread(rolled(tail[...], g))).astype(BF16)
    ends = rolled(cum_ref[...], g)
    end0, end1 = ends[HALF - 1 : HALF], ends[ROWS - 1 : ROWS]
    s0 = dot(bt[:, :HALF], half(weighted, 0))
    s1 = dot(bt[:, HALF:], half(weighted, 1))
    s0_ref[0] = s0
    msg_ref[0, :STATE, :] = (spread(jnp.exp(end1)) * s0 + s1).astype(BF16)
    damp = spread(jnp.exp(end0 + end1))
    high = damp.astype(BF16)
    low = (damp - high.astype(F32)).astype(BF16)
    row = row_of((16, BLOCK))
    msg_ref[0, STATE:, :] = jnp.where(row == 0, high.astype(F32), low.astype(F32)).astype(BF16)


def state_call(info, mixed, halo, cpar, rate, hpar):
    bc_at = INNER // 256
    return pl.pallas_call(
        state_body,
        grid=(GROUPS,),
        out_shape=(
            shape((ROWS, INNER)),
            shape((ROWS, 256)),
            shape((ROWS, LANES)),
            shape((ROWS, LANES)),
            shape((GROUPS, STATE, BLOCK)),
            shape((GROUPS, STATE + 16, BLOCK), BF16),
        ),
        in_specs=[
            SMEM,
            columns(ROWS, BLOCK),
            columns(16, BLOCK),
            columns(8, BLOCK),
            pl.BlockSpec((ROWS, 256), lambda g: (0, bc_at)),
            pl.BlockSpec((16, 256), lambda g: (0, bc_at)),
            pl.BlockSpec((8, 256), lambda g: (0, bc_at)),
            whole((ROWS, LANES)),
            whole((8, LANES)),
        ],
        out_specs=(
            columns(ROWS, BLOCK),
            whole((ROWS, 256)),
            whole((ROWS, LANES)),
            whole((ROWS, LANES)),
            grouped(STATE),
            grouped(STATE + 16),
        ),
        scratch_shapes=[
            pltpu.VMEM((ROWS + 32, BLOCK), F32),
            pltpu.VMEM((STATE, ROWS), BF16),
            pltpu.VMEM((ROWS, LANES), F32),
        ],
        compiler_params=params(),
        cost_estimate=pl.CostEstimate(
            flops=2 * ROWS * STATE * INNER, bytes_accessed=9_000_000, transcendentals=800_000
        ),
        name="conv_state",
    )(info, mixed, halo, cpar, mixed, halo, cpar, rate, hpar)


def inside_body(xa, bca, cum, dt, hpar, y_ref, cum_t, scores):
    g = pl.program_id(0)

    @pl.when(g == 0)
    def _():
        tri = lower_triangle()
        for q in range(2):
            b, c = half(bca[:, :STATE], q).astype(BF16), half(bca[:, STATE:], q).astype(BF16)
            scores[q] = dot_nt(c, b) * tri
            cum_t[:, q * HALF : (q + 1) * HALF] = half(cum[...], q).T

    cols = rolled(cum[...], g)
    rows = cum_t[pl.ds(pl.multiple_of(8 * g, 8), 8), :]
    steps = rolled(dt[...], g)
    skips = rolled(hpar[...], g)[2:3, :]
    low = lane_of((HALF, LANES)) < HEADDIM
    for q in range(2):
        for p in range(OWN // 2):
            lanes = slice(p * LANES, (p + 1) * LANES)
            x = xa[q * HALF : (q + 1) * HALF, lanes]
            xdt = x * pair_lanes(half(steps, q), p)
            both = jnp.concatenate([jnp.where(low, xdt, 0.0), jnp.where(low, 0.0, xdt)], axis=0)
            mats = []
            for i in (2 * p, 2 * p + 1):
                gap = half(cols, q)[:, i : i + 1] - rows[i : i + 1, q * HALF : (q + 1) * HALF]
                mats.append((jnp.exp(jnp.minimum(gap, 0.0)) * scores[q]).astype(BF16))
            y = dot(jnp.concatenate(mats, axis=1), both.astype(BF16))
            y_ref[q * HALF : (q + 1) * HALF, lanes] = y + x * pair_lanes(skips, p)


def inside_call(xa, bca, cum, dt, hpar):
    return pl.pallas_call(
        inside_body,
        grid=(GROUPS,),
        out_shape=shape((ROWS, INNER)),
        in_specs=[
            columns(ROWS, BLOCK),
            whole((ROWS, 256)),
            whole((ROWS, LANES)),
            whole((ROWS, LANES)),
            whole((8, LANES)),
        ],
        out_specs=columns(ROWS, BLOCK),
        scratch_shapes=[pltpu.VMEM((LANES, ROWS), F32), pltpu.VMEM((2, HALF, HALF), F32)],
        compiler_params=params(),
        cost_estimate=pl.CostEstimate(
            flops=4 * HEADS * HALF * HALF * LANES, bytes_accessed=6_500_000, transcendentals=1_600_000
        ),
        name="inside",
    )(xa, bca, cum, dt, hpar)


def scan_body(backward, info, msg, out_ref):
    carry = jnp.zeros((STATE, BLOCK), F32)
    for k in reversed(range(GROUPS)) if backward else range(GROUPS):
        keep = info[2 + k].astype(F32)
        if not backward:
            carry = carry * keep
        out_ref[k] = carry.astype(BF16)
        damp = msg[k, STATE : STATE + 1, :].astype(F32) + msg[k, STATE + 1 : STATE + 2, :].astype(F32)
        carry = damp * carry + msg[k, :STATE, :].astype(F32)
        if backward:
            carry = carry * keep


def scan_call(info, msg, backward):
    return pl.pallas_call(
        functools.partial(scan_body, backward),
        out_shape=shape((GROUPS, STATE, BLOCK), BF16),
        in_specs=[SMEM, whole((GROUPS, STATE + 16, BLOCK))],
        out_specs=whole((GROUPS, STATE, BLOCK)),
        compiler_params=params(),
        name="chunk_scan",
    )(info, msg)


def out_proj_body(
    plan, refs, info, y_in, bca, cum, hin, s0, gate, gain, h_ref, *rest,
):
    w_refs, (y_ref, n_ref, res_ref, buffer, sems, sums) = rest[:refs], rest[refs:]
    parts = WIDTH // 384

    def start(part, _):
        for c in copies_of(plan, w_refs, buffer, sems, info, part, 384, False):
            c.start()
        return 0

    lax.fori_loop(0, parts, start, 0)
    c_all = bca[:, STATE:].astype(BF16)
    grow = jnp.exp(cum[...])
    sums[...] = jnp.zeros((ROWS, LANES), F32)

    def group(g, _):
        lanes = pl.ds(pl.multiple_of(g * BLOCK, LANES), BLOCK)
        factor = rolled(grow, g)
        first = hin[g]
        second = spread(factor[HALF - 1 : HALF]) * first.astype(F32) + s0[g]
        carried = jnp.concatenate(
            [dot(half(c_all, 0), first), dot(half(c_all, 1), second.astype(BF16))], axis=0
        )
        y = y_in[:, lanes] + spread(factor) * carried
        y_ref[:, lanes] = y
        z = gate[:, lanes]
        gated = y * z * sigmoid(z)
        square = gated * gated
        sums[...] += sum(square[:, i * LANES : (i + 1) * LANES] for i in range(BLOCK // LANES))
        return 0

    lax.fori_loop(0, GROUPS, group, 0)
    scale = lax.rsqrt(jnp.sum(sums[...], axis=1, keepdims=True) / INNER + EPSILON)

    def norm(g, _):
        lanes = pl.ds(pl.multiple_of(g * BLOCK, LANES), BLOCK)
        z = gate[:, lanes]
        gated = y_ref[:, lanes] * z * sigmoid(z)
        n_ref[:, lanes] = (gated * scale * gain[:, lanes]).astype(BF16)
        return 0

    lax.fori_loop(0, GROUPS, norm, 0)
    usable = usable_rows(info)

    def one(part, _):
        for c in copies_of(plan, w_refs, buffer, sems, info, part, 384, False):
            c.wait()
        cols = pl.ds(pl.multiple_of(part * 384, LANES), 384)
        branch = dot(n_ref[...], buffer[:, cols])
        res_ref[:, cols] = h_ref[:, cols].astype(F32) + usable * branch
        return 0

    lax.fori_loop(0, parts, one, 0)


def out_proj(info, y_in, bca, cum, hin, s0, gate, gain, h, weights, plan, count):
    return pl.pallas_call(
        functools.partial(out_proj_body, plan, len(weights)),
        out_shape=(shape((ROWS, INNER)), shape((ROWS, INNER), BF16), shape((ROWS, WIDTH))),
        in_specs=[
            SMEM,
            whole((ROWS, INNER)),
            whole((ROWS, 256)),
            whole((ROWS, LANES)),
            whole((GROUPS, STATE, BLOCK)),
            whole((GROUPS, STATE, BLOCK)),
            whole((ROWS, INNER)),
            whole((1, INNER)),
            whole((ROWS, WIDTH)),
        ]
        + [ANYWHERE] * len(weights),
        out_specs=(whole((ROWS, INNER)), whole((ROWS, INNER)), whole((ROWS, WIDTH))),
        scratch_shapes=[
            pltpu.VMEM((INNER, WIDTH), BF16),
            pltpu.SemaphoreType.DMA((count, WIDTH // 384)),
            pltpu.VMEM((ROWS, LANES), F32),
        ],
        compiler_params=params(),
        cost_estimate=pl.CostEstimate(
            flops=2 * ROWS * WIDTH * INNER, bytes_accessed=26_000_000, transcendentals=1_600_000
        ),
        name="out_proj",
    )(info, y_in, bca, cum, hin, s0, gate, gain, h, *weights)


def gate_back_body(plan, refs, info, cot, y, gate, gain, *rest):
    w_refs, (bg_ref, dy_ref, dz_ref, dgain_ref, buffer, sems, dn, sums) = rest[:refs], rest[refs:]
    blocks = 4
    size = INNER // blocks

    for b in range(blocks):
        for c in copies_of(plan(b), w_refs, buffer, sems, info, b, None, True):
            c.start()
    bg_ref[...] = (usable_rows(info) * cot[...].astype(F32)).astype(BF16)
    sums[...] = jnp.zeros((2, ROWS, LANES), F32)
    for b in range(blocks):
        for c in copies_of(plan(b), w_refs, buffer, sems, info, b, None, True):
            c.wait()
        dn[:, b * size : (b + 1) * size] = dot_nt(bg_ref[...], buffer[b * size : (b + 1) * size, :])

        def first(i, _, b=b):
            lanes = pl.ds(pl.multiple_of(b * size + i * LANES, LANES), LANES)
            z = gate[:, lanes]
            gated = y[:, lanes] * z * sigmoid(z)
            sums[0] += gated * gated
            sums[1] += gated * dn[:, lanes] * gain[:, lanes]
            return 0

        lax.fori_loop(0, size // LANES, first, 0)
    scale = lax.rsqrt(jnp.sum(sums[0], axis=1, keepdims=True) / INNER + EPSILON)
    inner = jnp.sum(sums[1], axis=1, keepdims=True) * scale * scale * scale / INNER

    def second(i, _):
        lanes = pl.ds(pl.multiple_of(i * LANES, LANES), LANES)
        z = gate[:, lanes]
        sig = sigmoid(z)
        silu = z * sig
        y_here = y[:, lanes]
        gated = y_here * silu
        d_norm = dn[:, lanes]
        d_gated = scale * d_norm * gain[:, lanes] - gated * inner
        total = jnp.sum(d_norm * gated * scale, axis=0, keepdims=True)
        dgain_ref[:, lanes] = jnp.broadcast_to(total, (8, LANES))
        dy_ref[:, lanes] = (d_gated * silu).astype(BF16)
        dz_ref[:, lanes] = (d_gated * y_here * sig * (1.0 + z * (1.0 - sig))).astype(BF16)
        return 0

    lax.fori_loop(0, INNER // LANES, second, 0)


def gate_back(info, cot, y, gate, gain, weights, plan, count):
    return pl.pallas_call(
        functools.partial(gate_back_body, plan, len(weights)),
        out_shape=(
            shape((ROWS, WIDTH), BF16),
            shape((ROWS, INNER), BF16),
            shape((ROWS, INNER), BF16),
            shape((8, INNER)),
        ),
        in_specs=[
            SMEM,
            whole((ROWS, WIDTH)),
            whole((ROWS, INNER)),
            whole((ROWS, INNER)),
            whole((1, INNER)),
        ]
        + [ANYWHERE] * len(weights),
        out_specs=(
            whole((ROWS, WIDTH)),
            whole((ROWS, INNER)),
            whole((ROWS, INNER)),
            whole((8, INNER)),
        ),
        scratch_shapes=[
            pltpu.VMEM((INNER, WIDTH), BF16),
            pltpu.SemaphoreType.DMA((count, 4)),
            pltpu.VMEM((ROWS, INNER), F32),
            pltpu.VMEM((2, ROWS, LANES), F32),
        ],
        compiler_params=params(),
        cost_estimate=pl.CostEstimate(
            flops=2 * ROWS * WIDTH * INNER, bytes_accessed=20_000_000, transcendentals=1_600_000
        ),
        name="gate_back",
    )(info, cot, y, gate, gain, *weights)


def own_grad_body(dy, bca, cum, msg_in, own1_ref, msg_ref, ct, grow):
    g = pl.program_id(0)

    @pl.when(g == 0)
    def _():
        ct[...] = bca[:, STATE:].T.astype(BF16)
        grow[...] = jnp.exp(cum[...])

    factor = rolled(grow[...], g)
    weighted = (dy[...].astype(F32) * spread(factor)).astype(BF16)
    own0 = dot(ct[:, :HALF], half(weighted, 0))
    own1 = dot(ct[:, HALF:], half(weighted, 1))
    own1_ref[0] = own1
    msg_ref[0, :STATE, :] = (spread(factor[HALF - 1 : HALF]) * own1 + own0).astype(BF16)
    msg_ref[0, STATE:, :] = msg_in[0]


def own_grad(dy, bca, cum, msg):
    return pl.pallas_call(
        own_grad_body,
        grid=(GROUPS,),
        out_shape=(
            shape((GROUPS, STATE, BLOCK)),
            shape((GROUPS, STATE + 16, BLOCK), BF16),
        ),
        in_specs=[
            columns(ROWS, BLOCK),
            whole((ROWS, 256)),
            whole((ROWS, LANES)),
            pl.BlockSpec((1, 16, BLOCK), lambda g: (g, STATE // 16, 0)),
        ],
        out_specs=(grouped(STATE), grouped(STATE + 16)),
        scratch_shapes=[pltpu.VMEM((STATE, ROWS), BF16), pltpu.VMEM((ROWS, LANES), F32)],
        compiler_params=params(),
        cost_estimate=pl.CostEstimate(
            flops=2 * ROWS * STATE * INNER, bytes_accessed=5_000_000, transcendentals=0
        ),
        name="own_grad",
    )(dy, bca, cum, msg)


def inside_back_body(
    dy, xa, bca, cum, dt, hpar,
    dx_ref, dskip_ref, gsum_ref, u_ref, dbc_ref, cum_t, scores, dscores,
):
    g = pl.program_id(0)

    @pl.when(g == 0)
    def _():
        tri = lower_triangle()
        for q in range(2):
            b, c = half(bca[:, :STATE], q).astype(BF16), half(bca[:, STATE:], q).astype(BF16)
            scores[q] = dot_nt(b, c) * tri.T
            cum_t[:, q * HALF : (q + 1) * HALF] = half(cum[...], q).T
        dscores[...] = jnp.zeros((2, HALF, HALF), F32)
        u_ref[...] = jnp.zeros((ROWS, LANES), F32)

    cols = rolled(cum[...], g)
    rows = cum_t[pl.ds(pl.multiple_of(8 * g, 8), 8), :]
    steps = rolled(dt[...], g)
    skips = rolled(hpar[...], g)[2:3, :]
    low = lane_of((HALF, LANES)) < HEADDIM
    lane = lane_of((HALF, LANES))
    gsum_ref[...] = jnp.zeros((8, ROWS), F32)
    for q in range(2):
        here = slice(q * HALF, (q + 1) * HALF)
        u_here = u_ref[here, :]
        for p in range(OWN // 2):
            lanes = slice(p * LANES, (p + 1) * LANES)
            dy_pair = dy[here, lanes]
            x = xa[here, lanes]
            zero = jnp.zeros_like(dy_pair)
            both = jnp.concatenate(
                [jnp.where(low, dy_pair, zero), jnp.where(low, zero, dy_pair)], axis=0
            )
            dw = dot_nt(x.astype(BF16), both)
            mats = []
            for n, i in enumerate((2 * p, 2 * p + 1)):
                gap = rows[i : i + 1, here] - half(cols, q)[:, i : i + 1]
                decay = jnp.exp(jnp.minimum(gap, 0.0))
                step = half(steps, q)[:, i : i + 1]
                weight = decay * scores[q]
                mats.append(weight.astype(BF16))
                dw_here = dw[:, n * HALF : (n + 1) * HALF]
                dscores[q] += decay * dw_here * step
                direct = weight * dw_here
                total = jnp.sum(direct, axis=1, keepdims=True)
                u_here = jnp.where(lane == 8 * g + i, total, u_here)
                gsum_ref[i : i + 1, here] = jnp.sum(direct * step, axis=0, keepdims=True)
            dx = dot(jnp.concatenate(mats, axis=1), both)
            dy_wide = dy_pair.astype(F32)
            dx_ref[here, lanes] = dx * pair_lanes(half(steps, q), p) + dy_wide * pair_lanes(skips, p)
            skip_sum = jnp.sum(dy_wide * x, axis=0, keepdims=True)
            if q == 0:
                dskip_ref[:, lanes] = jnp.broadcast_to(skip_sum, (8, LANES))
            else:
                dskip_ref[:, lanes] += skip_sum
        u_ref[here, :] = u_here

    @pl.when(g == GROUPS - 1)
    def _():
        tri = lower_triangle()
        for q in range(2):
            b, c = half(bca[:, :STATE], q).astype(BF16), half(bca[:, STATE:], q).astype(BF16)
            ds_t = dscores[q] * tri.T
            dbc_ref[q * HALF : (q + 1) * HALF, :STATE] = dot(ds_t.astype(BF16), c)
            dbc_ref[q * HALF : (q + 1) * HALF, STATE:] = dot(ds_t.T.astype(BF16), b)


def inside_back(dy, xa, bca, cum, dt, hpar):
    return pl.pallas_call(
        inside_back_body,
        grid=(GROUPS,),
        out_shape=(
            shape((ROWS, INNER)),
            shape((8, INNER)),
            shape((8 * GROUPS, ROWS)),
            shape((ROWS, LANES)),
            shape((ROWS, 256)),
        ),
        in_specs=[
            columns(ROWS, BLOCK),
            columns(ROWS, BLOCK),
            whole((ROWS, 256)),
            whole((ROWS, LANES)),
            whole((ROWS, LANES)),
            whole((8, LANES)),
        ],
        out_specs=(
            columns(ROWS, BLOCK),
            columns(8, BLOCK),
            pl.BlockSpec((8, ROWS), lambda g: (g, 0)),
            whole((ROWS, LANES)),
            whole((ROWS, 256)),
        ),
        scratch_shapes=[
            pltpu.VMEM((LANES, ROWS), F32),
            pltpu.VMEM((2, HALF, HALF), F32),
            pltpu.VMEM((2, HALF, HALF), F32),
        ],
        compiler_params=params(),
        cost_estimate=pl.CostEstimate(
            flops=8 * HEADS * HALF * HALF * LANES, bytes_accessed=9_000_000, transcendentals=1_600_000
        ),
        name="inside_back",
    )(dy, xa, bca, cum, dt, hpar)


def conv_back(d_active, values, halo, cpar, keep, ext, ext_d):
    width = values.shape[1]
    total = conv_sum_of(values, halo, cpar, keep, ext)
    sig = sigmoid(total)
    d_sum = d_active * sig * (1.0 + total * (1.0 - sig))
    ext_d[0:16, :width] = jnp.zeros((16, width), F32)
    ext_d[16 : 16 + ROWS, :width] = d_sum
    ext_d[16 + ROWS :, :width] = jnp.zeros((16, width), F32)
    d_in = jnp.zeros((ROWS + 16, width), F32)
    for k in range(KERNEL):
        d_in = d_in + cpar[k : k + 1, :] * ext_d[3 - k : 3 - k + ROWS + 16, :width]
    row = row_of((8, width))
    d_par = jnp.where(row == 4, jnp.sum(d_sum, axis=0, keepdims=True), 0.0)
    for k in range(KERNEL):
        tap = jnp.sum(d_sum * ext[13 + k : 13 + k + ROWS, :width], axis=0, keepdims=True)
        d_par = jnp.where(row == k, tap, d_par)
    return d_in, d_par


def finish_body(
    info, xa, dxi, dy, mixed, halo, cpar, bc, halo_bc, cpar_bc, bca, cum, dt, rate, hpar, lam, hin, s0, own1, u, gsum, dbc,
    dmx_ref, dmbc_ref, tailx_ref, tailbc_ref, edgex_ref, edgebc_ref, dcx_ref, dcbc_ref, dhead_ref,
    ext, ext_d, grow, tail, v_sum, q_sum, end_sum, dbc_sum,
):
    g = pl.program_id(0)
    keep = info[1].astype(F32)

    @pl.when(g == 0)
    def _():
        grow[...] = jnp.exp(cum[...])
        for q in range(2):
            here = half(cum[...], q)
            tail[q * HALF : (q + 1) * HALF, :] = jnp.exp(here[HALF - 1 :, :] - here)
        v_sum[...] = jnp.zeros((ROWS, LANES), F32)
        q_sum[...] = jnp.zeros((ROWS, LANES), F32)
        end_sum[...] = jnp.zeros((16, LANES), F32)
        dbc_sum[...] = dbc[...]

    sums = head_sum_matrix(g)
    factor = rolled(grow[...], g)
    tails = rolled(tail[...], g)
    steps = rolled(dt[...], g)
    ends = [spread(factor[HALF - 1 : HALF]), spread(factor[ROWS - 1 : ROWS])]
    lam1 = lam[0].astype(F32)
    lams = [ends[1] * lam1 + own1[0], lam1]
    first = hin[0].astype(F32)
    states = [first, ends[0] * first + s0[0]]
    d_x = []
    for q in range(2):
        here = slice(q * HALF, (q + 1) * HALF)
        b, c = bca[here, :STATE].astype(BF16), bca[here, STATE:].astype(BF16)
        lam_q, state_q = lams[q].astype(BF16), states[q].astype(BF16)
        tail_wide = spread(half(tails, q))
        tail_step = tail_wide * spread(half(steps, q))
        x, dy_q = xa[here, :], dy[here, :].astype(F32)
        lb = dot(b, lam_q) * tail_wide
        d_x.append(dxi[here, :] + lb * spread(half(steps, q)))
        v_sum[here, :] += dot((x * lb).astype(BF16), sums)
        grow_wide = spread(half(factor, q))
        dy_grow = (dy_q * grow_wide).astype(BF16)
        carried = dot(c, state_q)
        q_sum[here, :] += dot((dy_q * grow_wide * carried).astype(BF16), sums)
        dbc_sum[here, :STATE] += dot_nt((x * tail_step).astype(BF16), lam_q)
        dbc_sum[here, STATE:] += dot_nt(dy_grow, state_q)
        last = jnp.sum(lams[q] * states[q], axis=0, keepdims=True) * ends[q]
        end_sum[8 * q : 8 * q + 8, :] += exact_dot(
            jnp.broadcast_to(last, (8, BLOCK)), sums.astype(F32)
        )
    d_in, d_par = conv_back(
        jnp.concatenate(d_x, axis=0), mixed[...], halo[...], cpar[...], keep, ext, ext_d
    )
    dmx_ref[...] = d_in[16:].astype(BF16)
    tailx_ref[...] = d_in[ROWS:]
    edgex_ref[...] = (d_in[:16] * keep).astype(BF16)
    dcx_ref[...] = d_par

    @pl.when(g == GROUPS - 1)
    def _():
        d_bc, d_par_bc = conv_back(
            dbc_sum[...], bc[...], halo_bc[...], cpar_bc[...], keep, ext, ext_d
        )
        dmbc_ref[:, :256] = d_bc[16:].astype(BF16)
        tailbc_ref[...] = d_bc[ROWS:]
        edgebc_ref[...] = (d_bc[:16] * keep).astype(BF16)
        dcbc_ref[...] = d_par_bc
        rates = -jnp.exp(hpar[1:2, :])
        logit = rate[...] + hpar[0:1, :]
        upper = lower_triangle().T
        before = lower_triangle(True)
        d_bias = jnp.zeros((1, LANES), F32)
        d_log = jnp.zeros((1, LANES), F32)
        usable = usable_rows(info)
        for q in range(2):
            here = slice(q * HALF, (q + 1) * HALF)
            step = dt[here, :]
            gs = gsum[...][:, here].T
            gs = jnp.concatenate([gs, jnp.zeros((HALF, LANES - 8 * GROUPS), F32)], axis=1)
            d_decay = exact_dot(upper, gs - step * u[here, :] + q_sum[here, :])
            d_decay = d_decay + exact_dot(before, step * v_sum[here, :])
            d_decay = d_decay + end_sum[8 * q : 8 * q + 1, :]
            d_step = u[here, :] + v_sum[here, :] + rates * d_decay
            d_rate = half(usable, q) * d_step * sigmoid(half(logit, q))
            d_bias += jnp.sum(d_rate, axis=0, keepdims=True)
            d_log += jnp.sum(d_decay * step * rates, axis=0, keepdims=True)
            dmbc_ref[here, 256:] = d_rate.astype(BF16)
        row = row_of((8, LANES))
        dhead_ref[...] = jnp.where(row == 0, d_bias, jnp.where(row == 1, d_log, 0.0))


def finish_call(
    info, xa, dxi, dy, mixed, halo, cpar, bca, cum, dt, rate, hpar, lam, hin, s0, own1, u, gsum, dbc
):
    bc_at = INNER // 256
    wide = whole((ROWS, LANES))
    return pl.pallas_call(
        finish_body,
        grid=(GROUPS,),
        out_shape=(
            shape((ROWS, INNER), BF16),
            shape((ROWS, 384), BF16),
            shape((16, INNER)),
            shape((16, 256)),
            shape((16, INNER), BF16),
            shape((16, 256), BF16),
            shape((8, INNER)),
            shape((8, 256)),
            shape((8, LANES)),
        ),
        in_specs=[
            SMEM,
            columns(ROWS, BLOCK),
            columns(ROWS, BLOCK),
            columns(ROWS, BLOCK),
            columns(ROWS, BLOCK),
            columns(16, BLOCK),
            columns(8, BLOCK),
            pl.BlockSpec((ROWS, 256), lambda g: (0, bc_at)),
            pl.BlockSpec((16, 256), lambda g: (0, bc_at)),
            pl.BlockSpec((8, 256), lambda g: (0, bc_at)),
            whole((ROWS, 256)),
            wide,
            wide,
            wide,
            whole((8, LANES)),
            grouped(STATE),
            grouped(STATE),
            grouped(STATE),
            grouped(STATE),
            wide,
            whole((8 * GROUPS, ROWS)),
            whole((ROWS, 256)),
        ],
        out_specs=(
            columns(ROWS, BLOCK),
            whole((ROWS, 384)),
            columns(16, BLOCK),
            whole((16, 256)),
            columns(16, BLOCK),
            whole((16, 256)),
            columns(8, BLOCK),
            whole((8, 256)),
            whole((8, LANES)),
        ),
        scratch_shapes=[
            pltpu.VMEM((ROWS + 32, BLOCK), F32),
            pltpu.VMEM((ROWS + 32, BLOCK), F32),
            pltpu.VMEM((ROWS, LANES), F32),
            pltpu.VMEM((ROWS, LANES), F32),
            pltpu.VMEM((ROWS, LANES), F32),
            pltpu.VMEM((ROWS, LANES), F32),
            pltpu.VMEM((16, LANES), F32),
            pltpu.VMEM((ROWS, 256), F32),
        ],
        compiler_params=params(),
        cost_estimate=pl.CostEstimate(
            flops=10 * ROWS * STATE * INNER, bytes_accessed=15_000_000, transcendentals=1_600_000
        ),
        name="finish_back",
    )(
        info, xa, dxi, dy, mixed, halo, cpar, mixed, halo, cpar, bca, cum, dt, rate, hpar,
        lam, hin, s0, own1, u, gsum, dbc,
    )


def gate_in_back_body(plan, refs, info, dz, *rest):
    w_refs, (out_ref, buffer, sems) = rest[:refs], rest[refs:]
    size = WIDTH // 4
    for b in range(4):
        for c in copies_of(plan(b), w_refs, buffer, sems, info, b, None, True):
            c.start()
    for b in range(4):
        for c in copies_of(plan(b), w_refs, buffer, sems, info, b, None, True):
            c.wait()
        out_ref[:, b * size : (b + 1) * size] = dot_nt(dz[...], buffer[b * size : (b + 1) * size, :])


def gate_in_back(info, dz, weights, plan, count):
    return pl.pallas_call(
        functools.partial(gate_in_back_body, plan, len(weights)),
        out_shape=shape((ROWS, WIDTH)),
        in_specs=[SMEM, whole((ROWS, INNER))] + [ANYWHERE] * len(weights),
        out_specs=whole((ROWS, WIDTH)),
        scratch_shapes=[
            pltpu.VMEM((WIDTH, INNER), BF16),
            pltpu.SemaphoreType.DMA((count, 4)),
        ],
        compiler_params=params(),
        cost_estimate=pl.CostEstimate(
            flops=2 * ROWS * WIDTH * INNER, bytes_accessed=13_000_000, transcendentals=0
        ),
        name="gate_in_back",
    )(info, dz, *weights)


def mixed_back_body(
    plan, refs, info, dmx, dmbc, tailx, tailbc, edge, part, h_ref, cot, gain, *rest
):
    w_refs, (dh_ref, dxc_ref, dgain_ref, buffer, sems) = rest[:refs], rest[refs:]
    size = WIDTH // 4
    for b in range(4):
        for c in copies_of(plan(b), w_refs, buffer, sems, info, b, None, True):
            c.start()
    dxc_ref[:, :INNER] = dmx[...]
    dxc_ref[:, INNER:] = dmbc[...]
    late = edge[...].astype(F32)
    dxc_ref[ROWS - 16 :, :INNER] = (tailx[...] + late[:, :INNER]).astype(BF16)
    dxc_ref[ROWS - 16 :, INNER:CONV_CH] = (tailbc[...] + late[:, INNER:]).astype(BF16)
    for b in range(4):
        cols = slice(b * size, (b + 1) * size)
        for c in copies_of(plan(b), w_refs, buffer, sems, info, b, None, True):
            c.wait()
        dh_ref[:, cols] = part[:, cols] + dot_nt(dxc_ref[...], buffer[cols, :])
    h = h_ref[...].astype(F32)
    scale = lax.rsqrt(jnp.mean(h * h, axis=1, keepdims=True) + EPSILON)
    d_norm = dh_ref[...]
    inner = jnp.mean(d_norm * gain[...] * h, axis=1, keepdims=True) * scale * scale * scale
    dgain_ref[...] = jnp.broadcast_to(
        jnp.sum(d_norm * h * scale, axis=0, keepdims=True), (8, WIDTH)
    )
    dh_ref[...] = cot[...].astype(F32) + scale * d_norm * gain[...] - h * inner


def mixed_back(info, dmx, dmbc, tailx, tailbc, edge, part, h, cot, gain, weights, plan, count):
    return pl.pallas_call(
        functools.partial(mixed_back_body, plan, len(weights)),
        out_shape=(shape((ROWS, WIDTH)), shape((ROWS, PACKED), BF16), shape((8, WIDTH))),
        in_specs=[
            SMEM,
            whole((ROWS, INNER)),
            whole((ROWS, 384)),
            whole((16, INNER)),
            whole((16, 256)),
            whole((16, CONV_CH)),
            whole((ROWS, WIDTH)),
            whole((ROWS, WIDTH)),
            whole((ROWS, WIDTH)),
            whole((1, WIDTH)),
        ]
        + [ANYWHERE] * len(weights),
        out_specs=(whole((ROWS, WIDTH)), whole((ROWS, PACKED)), whole((8, WIDTH))),
        scratch_shapes=[
            pltpu.VMEM((WIDTH, PACKED), BF16),
            pltpu.SemaphoreType.DMA((count, 4)),
        ],
        compiler_params=params(),
        cost_estimate=pl.CostEstimate(
            flops=2 * ROWS * WIDTH * PACKED, bytes_accessed=18_000_000, transcendentals=0
        ),
        name="mixed_back",
    )(info, dmx, dmbc, tailx, tailbc, edge, part, h, cot, gain, *weights)


def z_shift(r):
    return "dp", [(z, (z + r) % 4) for z in range(4)]


def y_shift(r):
    return "ctx", [(j, (j + 4 * r) % 16) for j in range(16)]


def x_shift(r):
    return "ctx", [(j, j - j % 4 + (j + r) % 4) for j in range(16)]


SHIFTS = {"z": z_shift, "y": y_shift, "x": x_shift}


def send(value, axis, r, section=None):
    name, pairs = SHIFTS[axis](r)
    if section is None:
        return lax.ppermute(value, name, pairs)
    base = section * lax.axis_size(name)
    return lax.ppermute(value, ("section", name), [(base + a, base + b) for a, b in pairs])


def swapped(value, section_from=None):
    pairs = [(0, 1), (1, 0)] if section_from is None else [(section_from, 1 - section_from)]
    return lax.ppermute(value, "section", pairs)


def reduced(first, order, place, section):
    axes = ["z", "y", "x"]
    axis = order[0]
    terms = [first((place[axis] + r) % 4) for r in range(4)]
    total = terms[0].astype(F32)
    for r in range(1, 4):
        total = total + send(terms[r].astype(BF16), axis, r, section).astype(F32)
    axes.remove(axis)
    for axis in order[1:]:
        at = axes.index(axis)
        parts = [
            lax.dynamic_index_in_dim(total, (place[axis] + r) % 4, at, False) for r in range(4)
        ]
        total = parts[0]
        for r in range(1, 4):
            total = total + send(parts[r].astype(BF16), axis, r, section).astype(F32)
        axes.remove(axis)
    return total


PARITY = [[j for j in range(16) if j % 2 == e] for e in range(2)]


def exchange(value):
    return lax.all_to_all(value, "ctx", 0, 0, axis_index_groups=PARITY)


def halo_shift(value, step):
    pairs = [(j, j + 2 * step) for j in range(16) if 0 <= j + 2 * step < 16]
    return lax.ppermute(value, "ctx", pairs)


def head_lanes(values):
    rows = values.shape[0]
    grid = jnp.pad(values.reshape(rows, GROUPS, OWN), ((0, 0), (0, 0), (0, 8 - OWN)))
    return jnp.pad(grid.reshape(rows, 8 * GROUPS), ((0, 0), (0, LANES - 8 * GROUPS)))


def lanes_heads(values):
    rows = values.shape[0]
    return values[:, : 8 * GROUPS].reshape(rows, GROUPS, 8)[:, :, :OWN].reshape(rows, HEADS)


def block_plan(rows):
    def plan(b):
        return lambda info: [(0, None, b * rows, rows, b * rows)]

    return plan


def on_device(
    boundary,
    lengths,
    norm_gain,
    w_z,
    w_xbc,
    w_dt,
    conv_weight,
    conv_bias,
    dt_bias,
    a_log,
    d_skip,
    gate_gain,
    w_out,
):
    section = lax.axis_index("section")
    group = lax.axis_index("dp")
    ctx = lax.axis_index("ctx")
    place = {"z": group, "y": ctx // 4, "x": ctx % 4}
    micro = ctx % 2
    chunk = ctx // 2

    own_rows = lax.dynamic_index_in_dim(boundary[0], micro, 0, False)
    other_rows = lax.dynamic_index_in_dim(boundary[0], 1 - micro, 0, False)
    pairs = [(j, j ^ 1) for j in range(16)]
    came = lax.ppermute(other_rows, "ctx", pairs)
    block = jnp.where(
        micro == 0, jnp.concatenate([own_rows, came]), jnp.concatenate([came, own_rows])
    )

    pair = lengths[group, micro]
    padded = (pair[0] + SPAN - 1) // SPAN * SPAN
    offset = chunk * ROWS
    begin = jnp.where(offset >= padded, padded, 0)
    length = jnp.where(offset >= padded, pair[1], pair[0])
    live = jnp.clip(length - (offset - begin), 0, ROWS)
    offsets = jnp.arange(GROUPS, dtype=jnp.int32) * ROWS
    keeps = ((offsets != 0) & (offsets != padded)).astype(jnp.int32)
    keep = ((offset != 0) & (offset != padded)).astype(jnp.int32)
    info = jnp.concatenate([jnp.stack([live, keep]).astype(jnp.int32), keeps])

    packed = jnp.concatenate([w_xbc[0], head_lanes(w_dt[0])], axis=1)
    small = jnp.zeros((8, 832), BF16)
    small = small.at[:4].set(conv_weight[0]).at[4].set(conv_bias[0])
    small = small.at[5, :384].set(norm_gain[0]).at[6, :768].set(gate_gain[0])
    smalls = lax.all_gather(small, "dp").astype(F32)
    cpar = jnp.transpose(smalls, (1, 0, 2)).reshape(8, CONV_CH)
    gain_one = smalls[:, 5, :384].reshape(1, WIDTH)
    gain_two = smalls[:, 6, :768].reshape(1, INNER)
    hpar = jnp.pad(
        jnp.concatenate([head_lanes(dt_bias), head_lanes(a_log), head_lanes(d_skip)]),
        ((0, 5), (0, 0)),
    )
    full_x = lax.all_gather(packed, "dp", axis=0, tiled=True)
    full_z = lax.all_gather(w_z[0], "dp", axis=0, tiled=True)
    full_o = lax.all_gather(w_out[0], "dp", axis=0, tiled=True)

    def forward(h):
        normed, mixed, rate = in_proj(info, h, gain_one, [full_x], whole_plan(WIDTH), 1)
        halo = halo_shift(mixed[ROWS - 16 :], 1)
        gate = gate_proj(info, normed, [full_z], whole_plan(WIDTH), 1)
        xa, bca, cum, dt, s0, msg = state_call(info, mixed, halo, cpar, rate, hpar)
        came = exchange(msg)
        y_in = inside_call(xa, bca, cum, dt, hpar)
        hin = exchange(scan_call(info, came, False))
        y, normed_two, result = out_proj(
            info, y_in, bca, cum, hin, s0, gate, gain_two, h, [full_o], whole_plan(INNER), 1
        )
        saved = (h, normed, mixed, halo, rate, gate, xa, bca, cum, dt, s0, msg, hin, y, normed_two)
        return result, saved

    def backward(cot, saved, own):
        h, normed, mixed, halo, rate, gate, xa, bca, cum, dt, s0, msg, hin, y, normed_two = saved
        bg, dy, dz, d_gain_two = gate_back(
            info, cot, y, gate, gain_two, [full_o], block_plan(INNER // 4), 1
        )
        own1, msg_back = own_grad(dy, bca, cum, msg)
        came = exchange(msg_back)
        normed_two_t = normed_two.T.reshape(4, 4, 4, 48, ROWS)
        normed_t = normed.T.reshape(4, 4, 4, 24, ROWS)

        def product(source, axis, other):
            at = "zyx".index(axis)

            def term(n):
                rows = lax.dynamic_index_in_dim(source, n, at, False)
                lead = rows.shape[:3]
                value = jnp.dot(rows.reshape(-1, ROWS), other, preferred_element_type=F32)
                return value.reshape(lead + (other.shape[1],))

            return term

        sum_out = reduced(product(normed_two_t, "x", bg), "xzy", place, own)
        sum_z = reduced(product(normed_t, "z", dz), "zyx", place, own)
        dxi, d_skips, gsum, u, dbc = inside_back(dy, xa, bca, cum, dt, hpar)
        lam = exchange(scan_call(info, came, True))
        part = gate_in_back(info, dz, [full_z], block_plan(WIDTH // 4), 1)
        dmx, dmbc, tailx, tailbc, edgex, edgebc, d_parx, d_parbc, d_heads = finish_call(
            info, xa, dxi, dy, mixed, halo, cpar, bca, cum, dt, rate, hpar, lam, hin, s0, own1, u, gsum, dbc
        )
        edge = halo_shift(jnp.concatenate([edgex, edgebc], axis=1), -1)
        dh, dxc, d_gain_one = mixed_back(
            info, dmx, dmbc, tailx, tailbc, edge, part, h, cot, gain_one, [full_x],
            block_plan(WIDTH // 4), 1,
        )
        third = PACKED // 3
        sum_x = jnp.concatenate(
            [
                reduced(product(normed_t, order[0], dxc[:, i * third : (i + 1) * third]), order, place, own)
                for i, order in enumerate(("zyx", "yxz", "xzy"))
            ],
            axis=1,
        )
        d_skip_row = jnp.sum(d_skips[0].reshape(HEADS, HEADDIM), axis=1)
        wide = jnp.zeros((16, CONV_CH), F32)
        wide = wide.at[:8, :INNER].set(d_parx).at[:8, INNER:].set(d_parbc)
        wide = wide.at[8, :WIDTH].set(d_gain_one[0]).at[9, :INNER].set(d_gain_two[0])
        wide = wide.at[10, :LANES].set(d_heads[0]).at[11, :LANES].set(d_heads[1])
        wide = wide.at[12, :HEADS].set(d_skip_row)
        return dh, (sum_z, sum_x, sum_out, wide)

    out_low, saved_low = forward(block)
    out_high, saved_high = forward(swapped(out_low.astype(BF16), 0))
    dh_high, sums_high = backward(block, saved_high, 1)
    dh_low, sums_low = backward(swapped(dh_high.astype(BF16), 1), saved_low, 0)

    sum_z, sum_x, sum_out, wide = jax.tree.map(
        lambda a, b: jnp.where(section == 0, a, b), sums_low, sums_high
    )
    wide = lax.psum(wide, ("dp", "ctx"))
    index = group * 16 + ctx
    d_conv = lax.dynamic_slice(wide, (0, index * 52), (8, 52))
    d_gain_one = lax.dynamic_slice(wide, (8, index * 24), (1, 24))
    d_gain_two = lax.dynamic_slice(wide, (9, index * 48), (1, 48))
    d_bias, d_log = lanes_heads(wide[10:11, :LANES]), lanes_heads(wide[11:12, :LANES])

    rows = jnp.where(section == 0, dh_low, out_high)
    mine = jnp.where(micro == 0, rows[:HALF], rows[HALF:])
    other = lax.ppermute(jnp.where(micro == 0, rows[HALF:], rows[:HALF]), "ctx", pairs)
    top = jnp.where(micro == 0, jnp.stack([mine, other]), jnp.stack([other, mine]))
    return (
        top[None],
        d_gain_one,
        sum_z[None],
        sum_x[None, :, :CONV_CH],
        lanes_heads(sum_x[:, CONV_CH:])[None],
        d_conv[None, :4],
        d_conv[4:5],
        d_bias,
        d_log,
        wide[12:13, :HEADS],
        d_gain_two,
        sum_out[None],
    )


def solution(mesh):
    in_specs = (
        P("section", None, ("dp", "ctx"), None),
        P(),
        P("section", "dp"),
        P("section", "dp", None),
        P("section", "dp", None),
        P("section", "dp", None),
        P("section", None, "dp"),
        P("section", "dp"),
        P("section", None),
        P("section", None),
        P("section", None),
        P("section", "dp"),
        P("section", "dp", None),
    )
    out_specs = (
        P("section", None, ("dp", "ctx"), None),
        P("section", ("dp", "ctx")),
        P("section", ("dp", "ctx"), None),
        P("section", ("dp", "ctx"), None),
        P("section", ("dp", "ctx"), None),
        P("section", None, ("dp", "ctx")),
        P("section", ("dp", "ctx")),
        P("section", None),
        P("section", None),
        P("section", None),
        P("section", ("dp", "ctx")),
        P("section", ("dp", "ctx"), None),
    )
    return jax.shard_map(
        on_device, mesh=mesh, in_specs=in_specs, out_specs=out_specs, check_vma=False
    )
```

time: 2920 us -> 1280 us (0.44)
  waiting for transfers between devices: 1590 us -> 487 us
  other arithmetic: 384 us -> 41.2 us
  matrix products: 425 us -> 83.2 us
  Pallas kernels: 0 us -> 271 us
  starting transfers between devices: 34.8 us -> 268 us
  blocking collectives: 230 us -> 31.2 us
  local copies, waits for them, and re-layouts: 210 us -> 60.9 us
    reduce_scatter x3 -> x0, waiting for transfers between devices: 726 us -> none  [the longest x1 244 us: on_device(): lax.psum_scatter(big_sums[2][None], ('dp', 'ctx'), scatter_dimension=1, t...]
    unnamed x18 -> x4, waiting for transfers between devices: 355 us -> 1.41 us
    dot_general x81 -> x40, matrix products: 425 us -> 83.2 us  [term(): value = jnp.dot(rows.reshape(-1, ROWS), other, preferred_element_type=F32)]
    all_gather x9 -> x3, waiting for transfers between devices: 502 us -> 195 us  [the longest x1 79.6 us: on_device(): full_x = lax.all_gather(packed, 'dp', axis=0, tiled=True)]
    pallas_call x0 -> x26, Pallas kernels: none -> 271 us  [the longest x2 43.1 us: finish_call(): pl.pallas_call(finish_body, grid=(GROUPS,), out_shape=(shape((ROWS, INNER...]
    psum x0 -> x1, waiting for transfers between devices: none -> 216 us  [on_device(): wide = lax.psum(wide, ('dp', 'ctx'))]
    all_gather x10 -> x1, blocking collectives: 220 us -> 13.1 us  [on_device(): smalls = lax.all_gather(small, 'dp').astype(F32)]
    ppermute x10 -> x98, starting transfers between devices: 33.7 us -> 218 us  [the longest x90 198 us: send(): lax.ppermute(value, ('section', name), [(base + a, base + b) for a, b in...]
  transfers between devices with their start and end apart: 25 -> 109, of which waited for: 17 -> 16; matrix products, arithmetic and copies ran while one was open for 25% -> 13% of each run, Pallas kernels for 0% -> 16%
where the time goes in v1:
time: 1280 us; the launch traced here: 1260 us
  waiting for transfers between devices  487 us (38%)
  Pallas kernels  271 us (21%)
  starting transfers between devices  268 us (21%)
  matrix products  83.2 us (6%)
  local copies, waits for them, and re-layouts  60.9 us (5%)
  other arithmetic  41.2 us (3%)
  blocking collectives  31.2 us (2%)
  between operations  18.8 us (1%)
    psum x1, waiting for transfers between devices, on_device(): wide = lax.psum(wide, ('dp', 'ctx'))  216 us
    ppermute x90, starting transfers between devices, send(): lax.ppermute(value, ('section', name), [(base + a, base + b) for a, b in...  198 us
    dot_general x40, matrix products, term(): value = jnp.dot(rows.reshape(-1, ROWS), other, preferred_element_type=F32)  83.2 us
    all_gather x1, waiting for transfers between devices, on_device(): full_x = lax.all_gather(packed, 'dp', axis=0, tiled=True)  79.6 us
    all_gather x1, waiting for transfers between devices, on_device(): full_o = lax.all_gather(w_out[0], 'dp', axis=0, tiled=True)  76.9 us
    all_to_all x7, starting transfers between devices, exchange(): return lax.all_to_all(value, 'ctx', 0, 0, axis_index_groups=PARITY)  50.5 us
    pallas_call x2, Pallas kernels, finish_call(): pl.pallas_call(finish_body, grid=(GROUPS,), out_shape=(shape((ROWS, INNER...  43.1 us
    all_gather x1, waiting for transfers between devices, on_device(): full_z = lax.all_gather(w_z[0], 'dp', axis=0, tiled=True)  38.1 us
  transfers between devices with their start and end apart: 109, of which 16 were waited for; matrix products, arithmetic and copies ran while one was open for 13% of the time, Pallas kernels for 16%

profile of v1, /device:TPU:12, one launch (start us, length us, event | category | flops | bytes accessed | tf_op | source)
XLA Modules:
  0.0 1261.4 jit_solution(10899415546987767574)
XLA Ops:
  18.1 13.1 %all_gather.25 = bf16[4,8,832]{2,1,0:T(8,128)(2,1)S(1)} all-gather(bf16[1,8,832]{2,1,0:T(8,128)(2,1)S(1)} %scatter.65), channel_id=1, replica_groups=mesh['section'=2,'dp'=4,'ctx'=16] {'dp'}, dimensions={0}, use_global_device_ids=true | all-gather | bytes 66560 | tf_op jit(solution)/shard_map/all_gather | solution.py:1111
  36.5 79.6 %all-gather.6.cloned.1.call-done.rest_0_ = bf16[1536,3456]{1,0:T(8,128)(2,1)} async-done(((bf16[384,3456]{1,0:T(8,128)(2,1)}), bf16[1536,3456]{1,0:T(8,128)(2,1)}) %all-gather.6.cloned.1.call-update) | async-done | bytes 10616848 | tf_op jit(solution)/shard_map/all_gather | solution.py:1119
  116.1 9.4 in_proj.2
  135.2 9.3 conv_state.2
  144.5 18.1 %all_to_all.40.msg = bf16[8,144,384]{2,1,0:T(8,128)(2,1)} all-to-all(bf16[8,144,384]{2,1,0:T(8,128)(2,1)} %get-tuple-element.304.msg_in), channel_id=1, replica_groups={{0,2,4,6,8,10,12,14},{1,3,5,7,9,11,13,15},{16,18,20,22,24,26,28,30},{17..., dimensions={0} | all-to-all | bytes 1769472 | tf_op jit(solution)/shard_map/all_to_all | solution.py:1040
  164.9 7.1 all-to-all-start.1
  172.7 38.1 %all-gather.8.cloned.1.call-done = bf16[1,1536,3072]{2,1,0:T(8,128)(2,1)} async-done(((bf16[1,384,3072]{2,1,0:T(8,128)(2,1)}), bf16[1,1536,3072]{2,1,0:T(8,128)(2,1)}) %all-gather.8.cloned.1.call-update) | async-done | bytes 9437200 | tf_op jit(solution)/shard_map/all_gather | solution.py:1120
  210.8 7.9 gate_proj.2.gate
  218.7 10.0 inside.2.y_in
  228.6 76.9 %all-gather.10.cloned.1.call-done = bf16[1,3072,1536]{2,1,0:T(8,128)(2,1)} async-done(((bf16[1,768,1536]{2,1,0:T(8,128)(2,1)}), bf16[1,3072,1536]{2,1,0:T(8,128)(2,1)}) %all-gather.10.cloned.1.call-update) | async-done | bytes 9437200 | tf_op jit(solution)/shard_map/all_gather | solution.py:1121
  306.4 14.3 %out_proj.2 = (f32[256,3072]{1,0:T(8,128)}, bf16[256,3072]{1,0:T(8,128)(2,1)}, f32[256,1536]{1,0:T(8,128)}) custom-call(s32[10]{0:T(128)} %pad_add_fusion.info, f32[256,3072]{1,0:T(8,128)} %inside.2.y_in, f32[256,256]{1,0:T(8,128)} %get-tuple-element.301.bca, f32[256,128]{1,0:T(8,128)} %get-tuple-element.302.cum, bf16[8,128,384]{2,1,0:T(8,128)(2,1)} %copy-done.22, ...), custom_call_target="tpu_custom_call" | custom-call | flops 2415919104 | bytes 26000000 | tf_op jit(solution)/shard_map/out_proj/pallas_call | solution.py:457
  326.8 9.4 in_proj.3
  340.5 5.2 collective-permute-done.3.halo.halo_bc
  346.4 9.3 conv_state.3
  355.7 7.2 all-to-all-start.2
  362.9 11.6 all-to-all-done.2.msg
  377.8 7.3 all-to-all-start.3
  391.5 7.9 gate_proj.3.gate
  399.3 9.8 inside.3.y_in
  410.1 14.5 %out_proj.3 = (f32[256,3072]{1,0:T(8,128)}, bf16[256,3072]{1,0:T(8,128)(2,1)}, f32[256,1536]{1,0:T(8,128)}) custom-call(s32[10]{0:T(128)} %pad_add_fusion.info, f32[256,3072]{1,0:T(8,128)} %inside.3.y_in, f32[256,256]{1,0:T(8,128)} %get-tuple-element.311.bca, f32[256,128]{1,0:T(8,128)} %get-tuple-element.312.cum, bf16[8,128,384]{2,1,0:T(8,128)(2,1)} %copy-done.23, ...), custom_call_target="tpu_custom_call" | custom-call | flops 2415919104 | bytes 26000000 | tf_op jit(solution)/shard_map/out_proj/pallas_call | solution.py:457
  424.6 16.2 %gate_back.2 = (bf16[256,1536]{1,0:T(8,128)(2,1)}, bf16[256,3072]{1,0:T(8,128)(2,1)}, bf16[256,3072]{1,0:T(8,128)(2,1)}, f32[8,3072]{1,0:T(8,128)}) custom-call(s32[10]{0:T(128)} %pad_add_fusion.info, bf16[256,1536]{1,0:T(8,128)(2,1)} %maximum_select_fusion.1.h_ref.cot, f32[256,3072]{1,0:T(8,128)} %get-tuple-element.317.y, f32[256,3072]{1,0:T(8,128)} %gate_proj.3.gate, ...), custom_call_target="tpu_custom_call" | custom-call | flops 2415919104 | bytes 20000000 | tf_op jit(solution)/shard_map/gate_back/pallas_call | solution.py:532
  440.8 8.0 own_grad.2
  448.8 7.2 all-to-all-start.4
  475.7 8.3 gate_in_back.2.part
  488.5 7.2 all-to-all-start.5
  495.7 14.8 %inside_back.2 = (f32[256,3072]{1,0:T(8,128)}, f32[8,3072]{1,0:T(8,128)}, f32[64,256]{1,0:T(8,128)}, f32[256,128]{1,0:T(8,128)}, f32[256,256]{1,0:T(8,128)}) custom-call(bf16[256,3072]{1,0:T(8,128)(2,1)} %get-tuple-element.318.dy, f32[256,3072]{1,0:T(8,128)} %get-tuple-element.310.xa, f32[256,256]{1,0:T(8,128)} %get-tuple-element.311.bca, ...), custom_call_target="tpu_custom_call" | custom-call | flops 805306368 | bytes 9000000 | tf_op jit(solution)/shard_map/inside_back/pallas_call | solution.py:678
  517.6 21.6 %finish_back.2 = (bf16[256,3072]{1,0:T(8,128)(2,1)}, bf16[256,384]{1,0:T(8,128)(2,1)}, f32[16,3072]{1,0:T(8,128)}, f32[16,256]{1,0:T(8,128)}, bf16[16,3072]{1,0:...) custom-call(s32[10]{0:T(128)} %pad_add_fusion.info, ...), custom_call_target="tpu_custom_call" | custom-call | flops 1006632960 | bytes 15000000 | tf_op jit(solution)/shard_map/finish_back/pallas_call | solution.py:830
  549.7 10.6 mixed_back.2
  585.5 16.2 %gate_back.3 = (bf16[256,1536]{1,0:T(8,128)(2,1)}, bf16[256,3072]{1,0:T(8,128)(2,1)}, bf16[256,3072]{1,0:T(8,128)(2,1)}, f32[8,3072]{1,0:T(8,128)}) custom-call(s32[10]{0:T(128)} %pad_add_fusion.info, bf16[256,1536]{1,0:T(8,128)(2,1)} %copy-done.27, f32[256,3072]{1,0:T(8,128)} %get-tuple-element.333.y, f32[256,3072]{1,0:T(8,128)} %gate_proj.2.gate, ...), custom_call_target="tpu_custom_call" | custom-call | flops 2415919104 | bytes 20000000 | tf_op jit(solution)/shard_map/gate_back/pallas_call | solution.py:532
  601.7 7.9 own_grad.3
  609.7 7.2 all-to-all-start.6
  616.9 14.8 %inside_back.3 = (f32[256,3072]{1,0:T(8,128)}, f32[8,3072]{1,0:T(8,128)}, f32[64,256]{1,0:T(8,128)}, f32[256,128]{1,0:T(8,128)}, f32[256,256]{1,0:T(8,128)}) custom-call(bf16[256,3072]{1,0:T(8,128)(2,1)} %get-tuple-element.334.dy, f32[256,3072]{1,0:T(8,128)} %get-tuple-element.300.xa, f32[256,256]{1,0:T(8,128)} %get-tuple-element.301.bca, ...), custom_call_target="tpu_custom_call" | custom-call | flops 805306368 | bytes 9000000 | tf_op jit(solution)/shard_map/inside_back/pallas_call | solution.py:678
  631.7 8.4 gate_in_back.3.part
  714.9 7.2 all-to-all-start.7
  724.4 4.8 collective-permute-start.9
  733.3 21.6 %all-to-all-done.7.lam = bf16[8,128,384]{2,1,0:T(8,128)(2,1)S(1)} async-done(((bf16[8,128,384]{2,1,0:T(8,128)(2,1)}), bf16[8,128,384]{2,1,0:T(8,128)(2,1)S(1)}, u32[]{:S(2)}, u32[]{:S(2)}) %all-to-all-start.7) | async-done | bytes 786464 | tf_op jit(solution)/shard_map/all_to_all | solution.py:1040
  755.8 21.6 %finish_back.3 = (bf16[256,3072]{1,0:T(8,128)(2,1)}, bf16[256,384]{1,0:T(8,128)(2,1)}, f32[16,3072]{1,0:T(8,128)}, f32[16,256]{1,0:T(8,128)}, bf16[16,3072]{1,0:...) custom-call(s32[10]{0:T(128)} %pad_add_fusion.info, ...), custom_call_target="tpu_custom_call" | custom-call | flops 1006632960 | bytes 15000000 | tf_op jit(solution)/shard_map/finish_back/pallas_call | solution.py:830
  778.3 5.7 collective-permute-start.6
  791.4 10.7 mixed_back.3
  828.8 5.3 collective-permute-start.82
  837.9 215.6 %all-reduce.14.cloned.1.call-done = f32[16,3328]{1,0:T(8,128)} async-done(((f32[16,3328]{1,0:T(8,128)}), f32[16,3328]{1,0:T(8,128)}) %all-reduce.14.cloned.1.call-update) | async-done | bytes 213008 | tf_op jit(solution)/shard_map/psum | solution.py:1195
  1066.8 4.6 collective-permute-start.27
  1082.8 4.7 collective-permute-start.36
  1115.0 8.5 collective-permute-done.45
  1147.3 4.5 collective-permute-start.49
  1176.1 5.7 collective-permute-start.51
  1195.3 8.2 collective-permute-done.83
  1215.0 6.3 collective-permute-done.11
  (548 shorter events, 392.9 us)
Async XLA Ops:
  7.2 108.9 %all-gather.6.cloned.1.call-start = ((), (), s32[]{:S(2)}) async-start(), calls=%async_computation.8 | async-start | bytes 13271040 | tf_op jit(solution)/shard_map/all_gather | solution.py:1119
  11.6 199.2 %all-gather.8.cloned.1.call-start = ((), (), s32[]{:S(2)}) async-start(), calls=%async_computation.10 | async-start | bytes 11796480 | tf_op jit(solution)/shard_map/all_gather | solution.py:1120
  12.5 293.1 %all-gather.10.cloned.1.call-start = ((), (), s32[]{:S(2)}) async-start(), calls=%async_computation.11 | async-start | bytes 11796480 | tf_op jit(solution)/shard_map/all_gather | solution.py:1121
  13.6 21.9 %collective-permute-start = (bf16[128,1536]{1,0:T(8,128)(2,1)S(1)}, bf16[128,1536]{1,0:T(8,128)(2,1)S(1)}, u32[]{:S(2)}, u32[]{:S(2)}) collective-permute-start(bf16[128,1536]{1,0:T(8,128)(2,1)S(1)} %get-tuple-element.447), channel_id=1, source_target_pairs={{0,1},{1,0},{2,3},{3,2},{4,5},{5,4},{6,7},{7,6},{8,9},{9,8},{10,11... | collective-permute-start | bytes 1179656 | tf_op jit(solution)/shard_map/ppermute | solution.py:1091
  164.9 140.6 %all-to-all-start.1 = ((bf16[8,128,384]{2,1,0:T(8,128)(2,1)}), bf16[8,128,384]{2,1,0:T(8,128)(2,1)S(1)}, u32[]{:S(2)}, u32[]{:S(2)}) async-start(bf16[8,128,384]{2,1,0:T(8,128)(2,1)} %chunk_scan.4), calls=%async_computation.1 | async-start | bytes 1572864 | tf_op jit(solution)/shard_map/all_to_all | solution.py:1040
  355.7 18.8 %all-to-all-start.2 = ((bf16[8,144,384]{2,1,0:T(8,128)(2,1)}), bf16[8,144,384]{2,1,0:T(8,128)(2,1)S(1)}, u32[]{:S(2)}, u32[]{:S(2)}) async-start(bf16[8,144,384]{2,1,0:T(8,128)(2,1)} %get-tuple-element.314.msg_in), calls=%async_computation.2 | async-start | bytes 1769472 | tf_op jit(solution)/shard_map/all_to_all | solution.py:1040
  377.8 31.4 %all-to-all-start.3 = ((bf16[8,128,384]{2,1,0:T(8,128)(2,1)}), bf16[8,128,384]{2,1,0:T(8,128)(2,1)S(1)}, u32[]{:S(2)}, u32[]{:S(2)}) async-start(bf16[8,128,384]{2,1,0:T(8,128)(2,1)} %chunk_scan.5), calls=%async_computation.3 | async-start | bytes 1572864 | tf_op jit(solution)/shard_map/all_to_all | solution.py:1040
  448.8 37.4 %all-to-all-start.4 = ((bf16[8,144,384]{2,1,0:T(8,128)(2,1)}), bf16[8,144,384]{2,1,0:T(8,128)(2,1)}, u32[]{:S(2)}, u32[]{:S(2)}) async-start(bf16[8,144,384]{2,1,0:T(8,128)(2,1)} %get-tuple-element.320), calls=%async_computation.4 | async-start | bytes 1769472 | tf_op jit(solution)/shard_map/all_to_all | solution.py:1040
  460.0 184.6 %collective-permute-start.89 = (bf16[4,4,48,1536]{3,2,1,0:T(8,128)(2,1)}, bf16[4,4,48,1536]{3,2,1,0:T(8,128)(2,1)}, u32[]{:S(2)}, u32[]{:S(2)}) collective-permute-start(bf16[4,4,48,1536]{3,2,1,0:T(8,128)(2,1)} %convolution_convert_fusion.8), channel_id=1, source_target_pairs={{64,65},{65,66},{66,67},{67,64},{68,69},{69,70},{70,71},{71,68},{7... | collective-permute-start | bytes 7077896 | tf_op jit(solution)/shard_map/ppermute | solution.py:1008
  464.3 195.4 %collective-permute-start.90 = (bf16[4,4,48,1536]{3,2,1,0:T(8,128)(2,1)}, bf16[4,4,48,1536]{3,2,1,0:T(8,128)(2,1)}, u32[]{:S(2)}, u32[]{:S(2)}) collective-permute-start(bf16[4,4,48,1536]{3,2,1,0:T(8,128)(2,1)} %convolution_convert_fusion.7), channel_id=1, source_target_pairs={{64,66},{65,67},{66,64},{67,65},{68,70},{69,71},{70,68},{71,69},{7... | collective-permute-start | bytes 7077896 | tf_op jit(solution)/shard_map/ppermute | solution.py:1008
  468.9 192.6 %collective-permute-start.91 = (bf16[4,4,48,1536]{3,2,1,0:T(8,128)(2,1)}, bf16[4,4,48,1536]{3,2,1,0:T(8,128)(2,1)}, u32[]{:S(2)}, u32[]{:S(2)}) collective-permute-start(bf16[4,4,48,1536]{3,2,1,0:T(8,128)(2,1)} %convolution_convert_fusion.6), channel_id=1, source_target_pairs={{64,67},{65,64},{66,65},{67,66},{68,71},{69,68},{70,69},{71,70},{7... | collective-permute-start | bytes 7077896 | tf_op jit(solution)/shard_map/ppermute | solution.py:1008
  473.1 194.4 %collective-permute-start.17 = (bf16[4,4,24,3072]{3,2,1,0:T(8,128)(2,1)}, bf16[4,4,24,3072]{3,2,1,0:T(8,128)(2,1)}, u32[]{:S(2)}, u32[]{:S(2)}) collective-permute-start(bf16[4,4,24,3072]{3,2,1,0:T(8,128)(2,1)} %convolution_convert_fusion.2), channel_id=1, source_target_pairs={{64,80},{80,96},{96,112},{112,64},{65,81},{81,97},{97,113},{113,65... | collective-permute-start | bytes 7077896 | tf_op jit(solution)/shard_map/ppermute | solution.py:1008
  488.5 29.1 %all-to-all-start.5 = ((bf16[8,128,384]{2,1,0:T(8,128)(2,1)}), bf16[8,128,384]{2,1,0:T(8,128)(2,1)}, u32[]{:S(2)}, u32[]{:S(2)}) async-start(bf16[8,128,384]{2,1,0:T(8,128)(2,1)} %chunk_scan.6), calls=%async_computation.5 | async-start | bytes 1572864 | tf_op jit(solution)/shard_map/all_to_all | solution.py:1040
  583.2 85.1 %collective-permute-start.18 = (bf16[4,4,24,3072]{3,2,1,0:T(8,128)(2,1)}, bf16[4,4,24,3072]{3,2,1,0:T(8,128)(2,1)}, u32[]{:S(2)}, u32[]{:S(2)}) collective-permute-start(bf16[4,4,24,3072]{3,2,1,0:T(8,128)(2,1)} %convolution_convert_fusion.1), channel_id=1, source_target_pairs={{64,96},{80,112},{96,64},{112,80},{65,97},{81,113},{97,65},{113,81... | collective-permute-start | bytes 7077896 | tf_op jit(solution)/shard_map/ppermute | solution.py:1008
  609.7 102.5 %all-to-all-start.6 = ((bf16[8,144,384]{2,1,0:T(8,128)(2,1)}), bf16[8,144,384]{2,1,0:T(8,128)(2,1)}, u32[]{:S(2)}, u32[]{:S(2)}) async-start(bf16[8,144,384]{2,1,0:T(8,128)(2,1)} %get-tuple-element.336), calls=%async_computation.6 | async-start | bytes 1769472 | tf_op jit(solution)/shard_map/all_to_all | solution.py:1040
  644.6 24.4 %collective-permute-start.19 = (bf16[4,4,24,3072]{3,2,1,0:T(8,128)(2,1)}, bf16[4,4,24,3072]{3,2,1,0:T(8,128)(2,1)}, u32[]{:S(2)}, u32[]{:S(2)}) collective-permute-start(bf16[4,4,24,3072]{3,2,1,0:T(8,128)(2,1)} %convolution_convert_fusion), channel_id=1, source_target_pairs={{64,112},{80,64},{96,80},{112,96},{65,113},{81,65},{97,81},{113,97... | collective-permute-start | bytes 7077896 | tf_op jit(solution)/shard_map/ppermute | solution.py:1008
  661.5 16.0 %collective-permute-start.54 = (bf16[4,4,24,1152]{3,2,1,0:T(8,128)(2,1)S(1)}, bf16[4,4,24,1152]{3,2,1,0:T(8,128)(2,1)}, u32[]{:S(2)}, u32[]{:S(2)}) collective-permute-start(bf16[4,4,24,1152]{3,2,1,0:T(8,128)(2,1)S(1)} %copy-done.46), channel_id=1, source_target_pairs={{64,96},{80,112},{96,64},{112,80},{65,97},{81,113},{97,65},{113,81... | collective-permute-start | bytes 2654216 | tf_op jit(solution)/shard_map/ppermute | solution.py:1008
  681.9 25.5 %collective-permute-start.20 = (bf16[4,24,3072]{2,1,0:T(8,128)(2,1)S(1)}, bf16[4,24,3072]{2,1,0:T(8,128)(2,1)S(1)}, u32[]{:S(2)}, u32[]{:S(2)}) collective-permute-start(bf16[4,24,3072]{2,1,0:T(8,128)(2,1)S(1)} %get-tuple-element.403), channel_id=1, source_target_pairs={{64,68},{65,69},{66,70},{67,71},{68,72},{69,73},{70,74},{71,75},{7... | collective-permute-start | bytes 1769480 | tf_op jit(solution)/shard_map/ppermute | solution.py:1008
  699.7 376.1 %collective-permute-start.80 = (bf16[4,4,48,1536]{3,2,1,0:T(8,128)(2,1)}, bf16[4,4,48,1536]{3,2,1,0:T(8,128)(2,1)}, u32[]{:S(2)}, u32[]{:S(2)}) collective-permute-start(bf16[4,4,48,1536]{3,2,1,0:T(8,128)(2,1)} %convolution_convert_fusion.11), channel_id=1, source_target_pairs={{0,1},{1,2},{2,3},{3,0},{4,5},{5,6},{6,7},{7,4},{8,9},{9,10},{10,1... | collective-permute-start | bytes 7077896 | tf_op jit(solution)/shard_map/ppermute | solution.py:1008
  703.1 125.7 %collective-permute-start.10 = (bf16[4,4,24,3072]{3,2,1,0:T(8,128)(2,1)}, bf16[4,4,24,3072]{3,2,1,0:T(8,128)(2,1)}, u32[]{:S(2)}, u32[]{:S(2)}) collective-permute-start(bf16[4,4,24,3072]{3,2,1,0:T(8,128)(2,1)} %convolution_convert_fusion.3), channel_id=1, source_target_pairs={{0,48},{16,0},{32,16},{48,32},{1,49},{17,1},{33,17},{49,33},{2,50}... | collective-permute-start | bytes 7077896 | tf_op jit(solution)/shard_map/ppermute | solution.py:1008
  708.9 15.4 %collective-permute-start.93 = (bf16[4,48,1536]{2,1,0:T(8,128)(2,1)}, bf16[4,48,1536]{2,1,0:T(8,128)(2,1)}, u32[]{:S(2)}, u32[]{:S(2)}) collective-permute-start(bf16[4,48,1536]{2,1,0:T(8,128)(2,1)} %get-tuple-element.399), channel_id=1, source_target_pairs={{64,96},{80,112},{96,64},{112,80},{65,97},{81,113},{97,65},{113,81... | collective-permute-start | bytes 1769480 | tf_op jit(solution)/shard_map/ppermute | solution.py:1008
  710.4 18.7 %collective-permute-start.94 = (bf16[4,48,1536]{2,1,0:T(8,128)(2,1)}, bf16[4,48,1536]{2,1,0:T(8,128)(2,1)}, u32[]{:S(2)}, u32[]{:S(2)}) collective-permute-start(bf16[4,48,1536]{2,1,0:T(8,128)(2,1)} %get-tuple-element.398), channel_id=1, source_target_pairs={{64,112},{80,64},{96,80},{112,96},{65,113},{81,65},{97,81},{113,97... | collective-permute-start | bytes 1769480 | tf_op jit(solution)/shard_map/ppermute | solution.py:1008
  714.9 40.0 %all-to-all-start.7 = ((bf16[8,128,384]{2,1,0:T(8,128)(2,1)}), bf16[8,128,384]{2,1,0:T(8,128)(2,1)S(1)}, u32[]{:S(2)}, u32[]{:S(2)}) async-start(bf16[8,128,384]{2,1,0:T(8,128)(2,1)} %chunk_scan.7), calls=%async_computation.7 | async-start | bytes 1572864 | tf_op jit(solution)/shard_map/all_to_all | solution.py:1040
  722.1 331.4 %all-reduce.14.cloned.1.call-start = ((), (), s32[]{:S(2)}) async-start(), calls=%async_computation.9 | async-start | bytes 425984 | tf_op jit(solution)/shard_map/psum | solution.py:1195
  722.1 341.5 %collective-permute-start.8 = (bf16[4,4,24,3072]{3,2,1,0:T(8,128)(2,1)}, bf16[4,4,24,3072]{3,2,1,0:T(8,128)(2,1)}, u32[]{:S(2)}, u32[]{:S(2)}) collective-permute-start(bf16[4,4,24,3072]{3,2,1,0:T(8,128)(2,1)} %convolution_convert_fusion.5), channel_id=1, source_target_pairs={{0,16},{16,32},{32,48},{48,0},{1,17},{17,33},{33,49},{49,1},{2,18}... | collective-permute-start | bytes 7077896 | tf_op jit(solution)/shard_map/ppermute | solution.py:1008
  724.4 342.4 %collective-permute-start.9 = (bf16[4,4,24,3072]{3,2,1,0:T(8,128)(2,1)}, bf16[4,4,24,3072]{3,2,1,0:T(8,128)(2,1)}, u32[]{:S(2)}, u32[]{:S(2)}) collective-permute-start(bf16[4,4,24,3072]{3,2,1,0:T(8,128)(2,1)} %convolution_convert_fusion.4), channel_id=1, source_target_pairs={{0,32},{16,48},{32,0},{48,16},{1,33},{17,49},{33,1},{49,17},{2,34}... | collective-permute-start | bytes 7077896 | tf_op jit(solution)/shard_map/ppermute | solution.py:1008
  825.5 253.2 %collective-permute-start.81 = (bf16[4,4,48,1536]{3,2,1,0:T(8,128)(2,1)}, bf16[4,4,48,1536]{3,2,1,0:T(8,128)(2,1)}, u32[]{:S(2)}, u32[]{:S(2)}) collective-permute-start(bf16[4,4,48,1536]{3,2,1,0:T(8,128)(2,1)} %convolution_convert_fusion.10), channel_id=1, source_target_pairs={{0,2},{1,3},{2,0},{3,1},{4,6},{5,7},{6,4},{7,5},{8,10},{9,11},{10,... | collective-permute-start | bytes 7077896 | tf_op jit(solution)/shard_map/ppermute | solution.py:1008
  828.8 253.9 %collective-permute-start.82 = (bf16[4,4,48,1536]{3,2,1,0:T(8,128)(2,1)}, bf16[4,4,48,1536]{3,2,1,0:T(8,128)(2,1)}, u32[]{:S(2)}, u32[]{:S(2)}) collective-permute-start(bf16[4,4,48,1536]{3,2,1,0:T(8,128)(2,1)} %convolution_convert_fusion.9), channel_id=1, source_target_pairs={{0,3},{1,0},{2,1},{3,2},{4,7},{5,4},{6,5},{7,6},{8,11},{9,8},{10,9... | collective-permute-start | bytes 7077896 | tf_op jit(solution)/shard_map/ppermute | solution.py:1008
  1063.6 28.3 %collective-permute-start.26 = (bf16[4,4,24,1152]{3,2,1,0:T(8,128)(2,1)S(1)}, bf16[4,4,24,1152]{3,2,1,0:T(8,128)(2,1)S(1)}, u32[]{:S(2)}, u32[]{:S(2)}) collective-permute-start(bf16[4,4,24,1152]{3,2,1,0:T(8,128)(2,1)S(1)} %copy-done.50), channel_id=1, source_target_pairs={{0,16},{16,32},{32,48},{48,0},{1,17},{17,33},{33,49},{49,1},{2,18}... | collective-permute-start | bytes 2654216 | tf_op jit(solution)/shard_map/ppermute | solution.py:1008
  1066.8 29.9 %collective-permute-start.27 = (bf16[4,4,24,1152]{3,2,1,0:T(8,128)(2,1)S(1)}, bf16[4,4,24,1152]{3,2,1,0:T(8,128)(2,1)S(1)}, u32[]{:S(2)}, u32[]{:S(2)}) collective-permute-start(bf16[4,4,24,1152]{3,2,1,0:T(8,128)(2,1)S(1)} %copy-done.52), channel_id=1, source_target_pairs={{0,32},{16,48},{32,0},{48,16},{1,33},{17,49},{33,1},{49,17},{2,34}... | collective-permute-start | bytes 2654216 | tf_op jit(solution)/shard_map/ppermute | solution.py:1008
  1075.9 24.1 %collective-permute-start.28 = (bf16[4,4,24,1152]{3,2,1,0:T(8,128)(2,1)S(1)}, bf16[4,4,24,1152]{3,2,1,0:T(8,128)(2,1)S(1)}, u32[]{:S(2)}, u32[]{:S(2)}) collective-permute-start(bf16[4,4,24,1152]{3,2,1,0:T(8,128)(2,1)S(1)} %copy-done.51), channel_id=1, source_target_pairs={{0,48},{16,0},{32,16},{48,32},{1,49},{17,1},{33,17},{49,33},{2,50}... | collective-permute-start | bytes 2654216 | tf_op jit(solution)/shard_map/ppermute | solution.py:1008
  1078.8 24.5 %collective-permute-start.35 = (bf16[4,4,24,1152]{3,2,0,1:T(8,128)(2,1)S(1)}, bf16[4,4,24,1152]{3,2,0,1:T(8,128)(2,1)S(1)}, u32[]{:S(2)}, u32[]{:S(2)}) collective-permute-start(bf16[4,4,24,1152]{3,2,0,1:T(8,128)(2,1)S(1)} %copy-done.40), channel_id=1, source_target_pairs={{0,4},{1,5},{2,6},{3,7},{4,8},{5,9},{6,10},{7,11},{8,12},{9,13},{1... | collective-permute-start | bytes 2654216 | tf_op jit(solution)/shard_map/ppermute | solution.py:1008
  1082.8 24.5 %collective-permute-start.36 = (bf16[4,4,24,1152]{3,2,0,1:T(8,128)(2,1)S(1)}, bf16[4,4,24,1152]{3,2,0,1:T(8,128)(2,1)S(1)}, u32[]{:S(2)}, u32[]{:S(2)}) collective-permute-start(bf16[4,4,24,1152]{3,2,0,1:T(8,128)(2,1)S(1)} %copy-done.47), channel_id=1, source_target_pairs={{0,8},{1,9},{2,10},{3,11},{4,12},{5,13},{6,14},{7,15},{8,0},{9,1},... | collective-permute-start | bytes 2654216 | tf_op jit(solution)/shard_map/ppermute | solution.py:1008
  1091.9 18.5 %collective-permute-start.37 = (bf16[4,4,24,1152]{3,2,0,1:T(8,128)(2,1)S(1)}, bf16[4,4,24,1152]{3,2,0,1:T(8,128)(2,1)S(1)}, u32[]{:S(2)}, u32[]{:S(2)}) collective-permute-start(bf16[4,4,24,1152]{3,2,0,1:T(8,128)(2,1)S(1)} %copy-done.48), channel_id=1, source_target_pairs={{0,12},{1,13},{2,14},{3,15},{4,0},{5,1},{6,2},{7,3},{8,4},{9,5},{1... | collective-permute-start | bytes 2654216 | tf_op jit(solution)/shard_map/ppermute | solution.py:1008
  1096.7 15.7 %collective-permute-start.44 = (bf16[4,4,24,1152]{3,2,1,0:T(8,128)(2,1)S(1)}, bf16[4,4,24,1152]{3,2,1,0:T(8,128)(2,1)S(1)}, u32[]{:S(2)}, u32[]{:S(2)}) collective-permute-start(bf16[4,4,24,1152]{3,2,1,0:T(8,128)(2,1)S(1)} %copy-done.43), channel_id=1, source_target_pairs={{0,1},{1,2},{2,3},{3,0},{4,5},{5,6},{6,7},{7,4},{8,9},{9,10},{10,1... | collective-permute-start | bytes 2654216 | tf_op jit(solution)/shard_map/ppermute | solution.py:1008
  1100.0 23.5 %collective-permute-start.45 = (bf16[4,4,24,1152]{3,2,1,0:T(8,128)(2,1)S(1)}, bf16[4,4,24,1152]{3,2,1,0:T(8,128)(2,1)S(1)}, u32[]{:S(2)}, u32[]{:S(2)}) collective-permute-start(bf16[4,4,24,1152]{3,2,1,0:T(8,128)(2,1)S(1)} %copy-done.45), channel_id=1, source_target_pairs={{0,2},{1,3},{2,0},{3,1},{4,6},{5,7},{6,4},{7,5},{8,10},{9,11},{10,... | collective-permute-start | bytes 2654216 | tf_op jit(solution)/shard_map/ppermute | solution.py:1008
  1103.4 22.4 %collective-permute-start.46 = (bf16[4,4,24,1152]{3,2,1,0:T(8,128)(2,1)S(1)}, bf16[4,4,24,1152]{3,2,1,0:T(8,128)(2,1)S(1)}, u32[]{:S(2)}, u32[]{:S(2)}) collective-permute-start(bf16[4,4,24,1152]{3,2,1,0:T(8,128)(2,1)S(1)} %copy-done.44), channel_id=1, source_target_pairs={{0,3},{1,0},{2,1},{3,2},{4,7},{5,4},{6,5},{7,6},{8,11},{9,8},{10,9... | collective-permute-start | bytes 2654216 | tf_op jit(solution)/shard_map/ppermute | solution.py:1008
  1107.4 123.7 %collective-permute-start.95 = (bf16[48,1536]{1,0:T(8,128)(2,1)}, bf16[48,1536]{1,0:T(8,128)(2,1)S(1)}, u32[]{:S(2)}, u32[]{:S(2)}) collective-permute-start(bf16[48,1536]{1,0:T(8,128)(2,1)} %get-tuple-element.429), channel_id=1, source_target_pairs={{64,68},{65,69},{66,70},{67,71},{68,72},{69,73},{70,74},{71,75},{7... | collective-permute-start | bytes 442376 | tf_op jit(solution)/shard_map/ppermute | solution.py:1008
  1110.4 123.8 %collective-permute-start.96 = (bf16[48,1536]{1,0:T(8,128)(2,1)}, bf16[48,1536]{1,0:T(8,128)(2,1)}, u32[]{:S(2)}, u32[]{:S(2)}) collective-permute-start(bf16[48,1536]{1,0:T(8,128)(2,1)} %get-tuple-element.431), channel_id=1, source_target_pairs={{64,72},{65,73},{66,74},{67,75},{68,76},{69,77},{70,78},{71,79},{7... | collective-permute-start | bytes 442376 | tf_op jit(solution)/shard_map/ppermute | solution.py:1008
  1112.4 18.2 %collective-permute-start.29 = (bf16[4,24,1152]{2,1,0:T(8,128)(2,1)S(1)}, bf16[4,24,1152]{2,1,0:T(8,128)(2,1)S(1)}, u32[]{:S(2)}, u32[]{:S(2)}) collective-permute-start(bf16[4,24,1152]{2,1,0:T(8,128)(2,1)S(1)} %get-tuple-element.415), channel_id=1, source_target_pairs={{0,4},{1,5},{2,6},{3,7},{4,8},{5,9},{6,10},{7,11},{8,12},{9,13},{1... | collective-permute-start | bytes 663560 | tf_op jit(solution)/shard_map/ppermute | solution.py:1008
  1184.0 19.5 %collective-permute-start.83 = (bf16[4,48,1536]{2,1,0:T(8,128)(2,1)}, bf16[4,48,1536]{2,1,0:T(8,128)(2,1)S(1)}, u32[]{:S(2)}, u32[]{:S(2)}) collective-permute-start(bf16[4,48,1536]{2,1,0:T(8,128)(2,1)} %get-tuple-element.394), channel_id=1, source_target_pairs={{0,16},{16,32},{32,48},{48,0},{1,17},{17,33},{33,49},{49,1},{2,18}... | collective-permute-start | bytes 1769480 | tf_op jit(solution)/shard_map/ppermute | solution.py:1008
  1186.0 21.3 %collective-permute-start.84 = (bf16[4,48,1536]{2,1,0:T(8,128)(2,1)}, bf16[4,48,1536]{2,1,0:T(8,128)(2,1)S(1)}, u32[]{:S(2)}, u32[]{:S(2)}) collective-permute-start(bf16[4,48,1536]{2,1,0:T(8,128)(2,1)} %get-tuple-element.396), channel_id=1, source_target_pairs={{0,32},{16,48},{32,0},{48,16},{1,33},{17,49},{33,1},{49,17},{2,34}... | collective-permute-start | bytes 1769480 | tf_op jit(solution)/shard_map/ppermute | solution.py:1008
  1189.3 21.1 %collective-permute-start.85 = (bf16[4,48,1536]{2,1,0:T(8,128)(2,1)}, bf16[4,48,1536]{2,1,0:T(8,128)(2,1)S(1)}, u32[]{:S(2)}, u32[]{:S(2)}) collective-permute-start(bf16[4,48,1536]{2,1,0:T(8,128)(2,1)} %get-tuple-element.395), channel_id=1, source_target_pairs={{0,48},{16,0},{32,16},{48,32},{1,49},{17,1},{33,17},{49,33},{2,50}... | collective-permute-start | bytes 1769480 | tf_op jit(solution)/shard_map/ppermute | solution.py:1008
  1203.5 17.8 %collective-permute-start.11 = (bf16[4,24,3072]{2,1,0:T(8,128)(2,1)}, bf16[4,24,3072]{2,1,0:T(8,128)(2,1)S(1)}, u32[]{:S(2)}, u32[]{:S(2)}) collective-permute-start(bf16[4,24,3072]{2,1,0:T(8,128)(2,1)} %get-tuple-element.400), channel_id=1, source_target_pairs={{0,4},{1,5},{2,6},{3,7},{4,8},{5,9},{6,10},{7,11},{8,12},{9,13},{1... | collective-permute-start | bytes 1769480 | tf_op jit(solution)/shard_map/ppermute | solution.py:1008
  1207.3 14.7 %collective-permute-start.12 = (bf16[4,24,3072]{2,1,0:T(8,128)(2,1)S(1)}, bf16[4,24,3072]{2,1,0:T(8,128)(2,1)S(1)}, u32[]{:S(2)}, u32[]{:S(2)}) collective-permute-start(bf16[4,24,3072]{2,1,0:T(8,128)(2,1)S(1)} %copy-done.65), channel_id=1, source_target_pairs={{0,8},{1,9},{2,10},{3,11},{4,12},{5,13},{6,14},{7,15},{8,0},{9,1},... | collective-permute-start | bytes 1769480 | tf_op jit(solution)/shard_map/ppermute | solution.py:1008
  1210.5 16.4 %collective-permute-start.13 = (bf16[4,24,3072]{2,1,0:T(8,128)(2,1)S(1)}, bf16[4,24,3072]{2,1,0:T(8,128)(2,1)S(1)}, u32[]{:S(2)}, u32[]{:S(2)}) collective-permute-start(bf16[4,24,3072]{2,1,0:T(8,128)(2,1)S(1)} %copy-done.64), channel_id=1, source_target_pairs={{0,12},{1,13},{2,14},{3,15},{4,0},{5,1},{6,2},{7,3},{8,4},{9,5},{1... | collective-permute-start | bytes 1769480 | tf_op jit(solution)/shard_map/ppermute | solution.py:1008
  1221.3 16.9 %collective-permute-start.97 = (bf16[48,1536]{1,0:T(8,128)(2,1)S(1)}, bf16[48,1536]{1,0:T(8,128)(2,1)S(1)}, u32[]{:S(2)}, u32[]{:S(2)}) collective-permute-start(bf16[48,1536]{1,0:T(8,128)(2,1)S(1)} %copy-done.72), channel_id=1, source_target_pairs={{64,76},{65,77},{66,78},{67,79},{68,64},{69,65},{70,66},{71,67},{7... | collective-permute-start | bytes 442376 | tf_op jit(solution)/shard_map/ppermute | solution.py:1008
  1222.0 16.9 %collective-permute-start.23 = (bf16[24,3072]{1,0:T(8,128)(2,1)S(1)}, bf16[24,3072]{1,0:T(8,128)(2,1)S(1)}, u32[]{:S(2)}, u32[]{:S(2)}) collective-permute-start(bf16[24,3072]{1,0:T(8,128)(2,1)S(1)} %copy-done.71), channel_id=1, source_target_pairs={{64,65},{65,66},{66,67},{67,64},{68,69},{69,70},{70,71},{71,68},{7... | collective-permute-start | bytes 442376 | tf_op jit(solution)/shard_map/ppermute | solution.py:1008
  (146 other events, 1502.0 us)
Sparse Core Ops, SparseCore 0:
  11.8 104.2 all-gather.5
  117.7 93.0 all-gather.7
  212.5 93.0 all-gather.9
  835.7 217.8 all-reduce.13

commit v2 on v1

v2 whole, which is shorter than its diff:
```python
import functools

import jax
import jax.numpy as jnp
from jax import lax
from jax.experimental import pallas as pl
from jax.experimental.pallas import tpu as pltpu
from jax.sharding import PartitionSpec as P

HEADS = 48
HEADDIM = 64
STATE = 128
KERNEL = 4
SPAN = 256
MICRO = 2
WIDTH = 1536
INNER = 3072
CONV_CH = 3328
LANES = 128
CHUNKS = 8
GROUPS = 4
OWN = 6
BLOCK = OWN * HEADDIM
LOCAL = GROUPS * BLOCK
MIXED = LOCAL + 2 * STATE
PACKED = MIXED + LANES
ROWS = 256
HALF = 128
SHARD = 384
PIECE = 48
STATE_HALF = STATE // 2
MESSAGE = STATE_HALF + 16
EPSILON = 1e-05
PRECISE = lax.Precision.HIGHEST
F32 = jnp.float32
BF16 = jnp.bfloat16
VMEM_LIMIT = 56 * 1024 * 1024


def params(**more):
    return pltpu.CompilerParams(vmem_limit_bytes=VMEM_LIMIT, **more)


def whole(shape):
    return pl.BlockSpec(shape, lambda *_: (0,) * len(shape))


def columns(rows, width):
    return pl.BlockSpec((rows, width), lambda g: (0, g))


def grouped(rows):
    return pl.BlockSpec((1, rows, BLOCK), lambda g: (g, 0, 0))


MESSAGES = pl.BlockSpec((2, MESSAGE, BLOCK), lambda g: (g, 0, 0))
SMEM = pl.BlockSpec(memory_space=pltpu.SMEM)
ANYWHERE = pl.BlockSpec(memory_space=pl.ANY)


def shape(dims, kind=F32):
    return jax.ShapeDtypeStruct(dims, kind)


def dot(a, b):
    return jnp.dot(a, b, preferred_element_type=F32)


def dot_nt(a, b):
    return lax.dot_general(a, b, (((1,), (1,)), ((), ())), preferred_element_type=F32)


def exact_dot(a, b):
    return jnp.dot(a, b, precision=PRECISE, preferred_element_type=F32)


def lane_of(dims):
    return lax.broadcasted_iota(jnp.int32, dims, len(dims) - 1)


def row_of(dims):
    return lax.broadcasted_iota(jnp.int32, dims, len(dims) - 2)


def sigmoid(v):
    return 1.0 / (1.0 + jnp.exp(-v))


def softplus(v):
    return jnp.maximum(v, 0.0) + jnp.log1p(jnp.exp(-jnp.abs(v)))


def rolled(values, g):
    return pltpu.roll(values, lax.rem(LANES - 8 * g, LANES), axis=1)


def pair_lanes(values, p):
    low = lane_of((values.shape[0], LANES)) < HEADDIM
    return jnp.where(low, values[:, 2 * p : 2 * p + 1], values[:, 2 * p + 1 : 2 * p + 2])


def spread(values):
    return jnp.concatenate([pair_lanes(values, p) for p in range(OWN // 2)], axis=1)


def head_sum_matrix(g):
    head = row_of((BLOCK, LANES)) // HEADDIM
    return (lane_of((BLOCK, LANES)) == head + 8 * g).astype(BF16)


def lower_triangle(strict=False):
    i, j = row_of((HALF, HALF)), lane_of((HALF, HALF))
    return ((i > j) if strict else (i >= j)).astype(F32)


def usable_rows(info):
    return (row_of((ROWS, 1)) < info[0]).astype(F32)


def half(values, q):
    return values[q * HALF : (q + 1) * HALF]


class Weight:
    def __init__(self, arrays, layer, width, first=0):
        self.arrays = arrays
        self.layer = layer
        self.width = width
        self.columns = pl.ds(first, width)

    def block(self, info, b):
        return lax.rem(info[10] + b, 4) * SHARD

    def parts(self, refs, info, b):
        start = self.block(info, b)
        if len(refs) == 1:
            return [(refs[0].at[pl.ds(pl.multiple_of(start, SHARD), SHARD)], start, SHARD)]
        out = []
        for side in range(2):
            mine = info[12 - side]
            for step in range(4):
                source = refs[2 + 4 * side + step].at[pl.ds((b - 1) * PIECE, PIECE)]
                row = start + side * (SHARD // 2) + lax.rem(mine + step, 4) * PIECE
                out.append((source, row, PIECE))
        return out

    def copies(self, refs, info, b, buffer, sems):
        return [
            pltpu.make_async_copy(
                source.at[:, self.columns],
                buffer.at[pl.ds(pl.multiple_of(row, 16), count)],
                sems.at[b, n],
            )
            for n, (source, row, count) in enumerate(self.parts(refs, info, b))
        ]

    def own_copy(self, source, info, buffer, sems):
        rows = pl.ds(pl.multiple_of(self.block(info, 0), SHARD), SHARD)
        return pltpu.make_async_copy(source.at[:, self.columns], buffer.at[rows], sems.at[0, 0])

    def start(self, refs, info, buffer, sems):
        whole_array = len(refs) == 1
        if not whole_array:
            for n in range(2):

                @pl.when((info[13] == self.layer) == (n == 0))
                def _(n=n):
                    self.own_copy(refs[n], info, buffer, sems).start()

        for b in range(0 if whole_array else 1, 4):
            for c in self.copies(refs, info, b, buffer, sems):
                c.start()

    def wait(self, refs, info, b, buffer, sems):
        if b == 0 and len(refs) > 1:
            self.own_copy(refs[0], info, buffer, sems).wait()
        else:
            for c in self.copies(refs, info, b, buffer, sems):
                c.wait()
        return pl.ds(pl.multiple_of(self.block(info, b), SHARD), SHARD)

    def specs(self):
        return [ANYWHERE] * len(self.arrays)

    def scratch(self):
        return [pltpu.VMEM((4 * SHARD, self.width), BF16), pltpu.SemaphoreType.DMA((4, 8))]

    def product(self, refs, info, left, buffer, sems, total):
        for b in range(4):
            self.wait(refs, info, b, buffer, sems)
        step = 512 if self.width % 512 == 0 else 640
        for at in range(0, self.width, step):
            total[:, at : at + step] = dot(left[...], buffer[:, at : at + step])


def in_proj_body(weight, info, h_ref, gain_ref, *rest):
    refs = len(weight.arrays)
    w_refs, (normed_ref, mixed_ref, rate_ref, buffer, sems, total) = rest[:refs], rest[refs:]
    weight.start(w_refs, info, buffer, sems)
    h = h_ref[...].astype(F32)
    scale = lax.rsqrt(jnp.mean(h * h, axis=1, keepdims=True) + EPSILON)
    normed_ref[...] = (h * scale * gain_ref[...]).astype(BF16)
    weight.product(w_refs, info, normed_ref, buffer, sems, total)
    mixed_ref[...] = total[:, :MIXED].astype(BF16)
    rate_ref[...] = total[:, MIXED:]


def in_proj(info, h, gain, weight):
    return pl.pallas_call(
        functools.partial(in_proj_body, weight),
        out_shape=(shape((ROWS, WIDTH), BF16), shape((ROWS, MIXED), BF16), shape((ROWS, LANES))),
        in_specs=[SMEM, whole((ROWS, WIDTH)), whole((1, WIDTH))] + weight.specs(),
        out_specs=(whole((ROWS, WIDTH)), whole((ROWS, MIXED)), whole((ROWS, LANES))),
        scratch_shapes=weight.scratch() + [pltpu.VMEM((ROWS, PACKED), F32)],
        compiler_params=params(),
        cost_estimate=pl.CostEstimate(
            flops=2 * ROWS * WIDTH * PACKED, bytes_accessed=8_000_000, transcendentals=0
        ),
        name="in_proj",
    )(info, h, gain, *weight.arrays)


def gate_proj_body(weight, info, normed_ref, *rest):
    refs = len(weight.arrays)
    w_refs, (gate_ref, buffer, sems) = rest[:refs], rest[refs:]
    weight.start(w_refs, info, buffer, sems)
    weight.product(w_refs, info, normed_ref, buffer, sems, gate_ref)


def gate_proj(info, normed, weight):
    return pl.pallas_call(
        functools.partial(gate_proj_body, weight),
        out_shape=shape((ROWS, LOCAL)),
        in_specs=[SMEM, whole((ROWS, WIDTH))] + weight.specs(),
        out_specs=whole((ROWS, LOCAL)),
        scratch_shapes=weight.scratch(),
        compiler_params=params(),
        cost_estimate=pl.CostEstimate(
            flops=2 * ROWS * WIDTH * LOCAL, bytes_accessed=7_000_000, transcendentals=0
        ),
        name="gate_proj",
    )(info, normed, *weight.arrays)


def conv_sum_of(values, halo, cpar, keep, ext):
    width = values.shape[1]
    ext[0:16, :width] = halo.astype(F32) * keep
    ext[16 : 16 + ROWS, :width] = values.astype(F32)
    total = cpar[4:5, :]
    for k in range(KERNEL):
        total = total + cpar[k : k + 1, :] * ext[13 + k : 13 + k + ROWS, :width]
    return total


def state_body(
    info, mixed, halo, cpar, bc, halo_bc, cpar_bc, rate, hpar,
    xa_ref, bca_ref, cum_ref, dt_ref, s0_ref, msg_ref, ext, bt, tail,
):
    g = pl.program_id(0)
    keep = info[1].astype(F32)

    @pl.when(g == 0)
    def _():
        total = conv_sum_of(bc[...], halo_bc[...], cpar_bc[...], keep, ext)
        active = total * sigmoid(total)
        bca_ref[...] = active
        bt[...] = active[:, :STATE].T.astype(BF16)
        dt = usable_rows(info) * softplus(rate[...] + hpar[0:1, :])
        log_decay = dt * -jnp.exp(hpar[1:2, :])
        dt_ref[...] = dt
        tri = lower_triangle()
        for q in range(2):
            rows = pl.ds(q * HALF, HALF)
            cum = exact_dot(tri, half(log_decay, q))
            cum_ref[rows, :] = cum
            tail[rows, :] = jnp.exp(cum[HALF - 1 :, :] - cum) * half(dt, q)

    total = conv_sum_of(mixed[...], halo[...], cpar[...], keep, ext)
    xa = total * sigmoid(total)
    xa_ref[...] = xa
    weighted = (xa * spread(rolled(tail[...], g))).astype(BF16)
    ends = rolled(cum_ref[...], g)
    end0, end1 = ends[HALF - 1 : HALF], ends[ROWS - 1 : ROWS]
    s0 = dot(bt[:, :HALF], half(weighted, 0))
    s1 = dot(bt[:, HALF:], half(weighted, 1))
    s0_ref[0] = s0
    state = (spread(jnp.exp(end1)) * s0 + s1).astype(BF16)
    damp = spread(jnp.exp(end0 + end1))
    high = damp.astype(BF16)
    low = (damp - high.astype(F32)).astype(BF16)
    row = row_of((16, BLOCK))
    damps = jnp.where(row == 0, high.astype(F32), low.astype(F32)).astype(BF16)
    for r in range(2):
        msg_ref[r, :STATE_HALF, :] = state[r * STATE_HALF : (r + 1) * STATE_HALF]
        msg_ref[r, STATE_HALF:, :] = damps


def state_call(info, mixed, halo, cpar, rate, hpar):
    bc_at = LOCAL // 256
    return pl.pallas_call(
        state_body,
        grid=(GROUPS,),
        out_shape=(
            shape((ROWS, LOCAL)),
            shape((ROWS, 256)),
            shape((ROWS, LANES)),
            shape((ROWS, LANES)),
            shape((GROUPS, STATE, BLOCK)),
            shape((CHUNKS, MESSAGE, BLOCK), BF16),
        ),
        in_specs=[
            SMEM,
            columns(ROWS, BLOCK),
            columns(16, BLOCK),
            columns(8, BLOCK),
            pl.BlockSpec((ROWS, 256), lambda g: (0, bc_at)),
            pl.BlockSpec((16, 256), lambda g: (0, bc_at)),
            pl.BlockSpec((8, 256), lambda g: (0, bc_at)),
            whole((ROWS, LANES)),
            whole((8, LANES)),
        ],
        out_specs=(
            columns(ROWS, BLOCK),
            whole((ROWS, 256)),
            whole((ROWS, LANES)),
            whole((ROWS, LANES)),
            grouped(STATE),
            MESSAGES,
        ),
        scratch_shapes=[
            pltpu.VMEM((ROWS + 32, BLOCK), F32),
            pltpu.VMEM((STATE, ROWS), BF16),
            pltpu.VMEM((ROWS, LANES), F32),
        ],
        compiler_params=params(),
        cost_estimate=pl.CostEstimate(
            flops=2 * ROWS * STATE * LOCAL, bytes_accessed=4_500_000, transcendentals=400_000
        ),
        name="conv_state",
    )(info, mixed, halo, cpar, mixed, halo, cpar, rate, hpar)


def inside_body(xa, bca, cum, dt, hpar, y_ref, cum_t, scores):
    g = pl.program_id(0)

    @pl.when(g == 0)
    def _():
        tri = lower_triangle()
        for q in range(2):
            b, c = half(bca[:, :STATE], q).astype(BF16), half(bca[:, STATE:], q).astype(BF16)
            scores[q] = dot_nt(c, b) * tri
            cum_t[:, q * HALF : (q + 1) * HALF] = half(cum[...], q).T

    cols = rolled(cum[...], g)
    rows = cum_t[pl.ds(pl.multiple_of(8 * g, 8), 8), :]
    steps = rolled(dt[...], g)
    skips = rolled(hpar[...], g)[2:3, :]
    low = lane_of((HALF, LANES)) < HEADDIM
    for q in range(2):
        for p in range(OWN // 2):
            lanes = slice(p * LANES, (p + 1) * LANES)
            x = xa[q * HALF : (q + 1) * HALF, lanes]
            xdt = x * pair_lanes(half(steps, q), p)
            both = jnp.concatenate([jnp.where(low, xdt, 0.0), jnp.where(low, 0.0, xdt)], axis=0)
            mats = []
            for i in (2 * p, 2 * p + 1):
                gap = half(cols, q)[:, i : i + 1] - rows[i : i + 1, q * HALF : (q + 1) * HALF]
                mats.append((jnp.exp(jnp.minimum(gap, 0.0)) * scores[q]).astype(BF16))
            y = dot(jnp.concatenate(mats, axis=1), both.astype(BF16))
            y_ref[q * HALF : (q + 1) * HALF, lanes] = y + x * pair_lanes(skips, p)


def inside_call(xa, bca, cum, dt, hpar):
    return pl.pallas_call(
        inside_body,
        grid=(GROUPS,),
        out_shape=shape((ROWS, LOCAL)),
        in_specs=[
            columns(ROWS, BLOCK),
            whole((ROWS, 256)),
            whole((ROWS, LANES)),
            whole((ROWS, LANES)),
            whole((8, LANES)),
        ],
        out_specs=columns(ROWS, BLOCK),
        scratch_shapes=[pltpu.VMEM((LANES, ROWS), F32), pltpu.VMEM((2, HALF, HALF), F32)],
        compiler_params=params(),
        cost_estimate=pl.CostEstimate(
            flops=2 * HEADS * HALF * HALF * LANES, bytes_accessed=3_300_000, transcendentals=800_000
        ),
        name="inside",
    )(xa, bca, cum, dt, hpar)


def scan_body(backward, info, msg, token, out_ref):
    carry = jnp.zeros((STATE_HALF, BLOCK), F32)
    for k in reversed(range(CHUNKS)) if backward else range(CHUNKS):
        keep = info[2 + k].astype(F32)
        if not backward:
            carry = carry * keep
        out_ref[k] = carry.astype(BF16)
        damps = msg[k, STATE_HALF:, :].astype(F32)
        carry = (damps[0:1] + damps[1:2]) * carry + msg[k, :STATE_HALF, :].astype(F32)
        if backward:
            carry = carry * keep


def scan_call(info, msg, backward, token):
    return pl.pallas_call(
        functools.partial(scan_body, backward),
        out_shape=shape((CHUNKS, STATE_HALF, BLOCK), BF16),
        in_specs=[SMEM, whole((CHUNKS, MESSAGE, BLOCK)), ANYWHERE],
        out_specs=whole((CHUNKS, STATE_HALF, BLOCK)),
        compiler_params=params(),
        name="chunk_scan",
    )(info, msg, token)


def out_proj_body(weight, info, y_in, bca, cum, hin, s0, gate, gain, *rest):
    refs = len(weight.arrays)
    w_refs, (y_ref, part_ref, buffer, sems, sums, gained) = rest[:refs], rest[refs:]
    weight.start(w_refs, info, buffer, sems)
    c_all = bca[:, STATE:].astype(BF16)
    grow = jnp.exp(cum[...])
    sums[...] = jnp.zeros((ROWS, LANES), F32)

    def group(g, _):
        lanes = pl.ds(pl.multiple_of(g * BLOCK, LANES), BLOCK)
        factor = rolled(grow, g)
        first = hin[g]
        second = spread(factor[HALF - 1 : HALF]) * first.astype(F32) + s0[g]
        carried = jnp.concatenate(
            [dot(half(c_all, 0), first), dot(half(c_all, 1), second.astype(BF16))], axis=0
        )
        y = y_in[:, lanes] + spread(factor) * carried
        y_ref[:, lanes] = y
        z = gate[:, lanes]
        gated = y * z * sigmoid(z)
        square = gated * gated
        sums[...] += sum(square[:, i * LANES : (i + 1) * LANES] for i in range(BLOCK // LANES))
        gained[:, lanes] = (gated * gain[:, lanes]).astype(BF16)
        return 0

    lax.fori_loop(0, GROUPS, group, 0)
    part_ref[:, WIDTH:] = sums[...]
    weight.product(w_refs, info, gained, buffer, sems, part_ref)


def out_proj(info, y_in, bca, cum, hin, s0, gate, gain, weight):
    return pl.pallas_call(
        functools.partial(out_proj_body, weight),
        out_shape=(shape((ROWS, LOCAL)), shape((ROWS, WIDTH + LANES))),
        in_specs=[
            SMEM,
            whole((ROWS, LOCAL)),
            whole((ROWS, 256)),
            whole((ROWS, LANES)),
            whole((GROUPS, STATE, BLOCK)),
            whole((GROUPS, STATE, BLOCK)),
            whole((ROWS, LOCAL)),
            whole((1, LOCAL)),
        ]
        + weight.specs(),
        out_specs=(whole((ROWS, LOCAL)), whole((ROWS, WIDTH + LANES))),
        scratch_shapes=weight.scratch()
        + [pltpu.VMEM((ROWS, LANES), F32), pltpu.VMEM((ROWS, LOCAL), BF16)],
        compiler_params=params(),
        cost_estimate=pl.CostEstimate(
            flops=2 * ROWS * WIDTH * LOCAL, bytes_accessed=13_000_000, transcendentals=800_000
        ),
        name="out_proj",
    )(info, y_in, bca, cum, hin, s0, gate, gain, *weight.arrays)


def join_body(info, h_ref, own, came, res_ref, low_ref, branch_ref, scale_ref):
    squares = jnp.sum(own[:, WIDTH:] + came[:, WIDTH:], axis=1, keepdims=True)
    scale = lax.rsqrt(squares / INNER + EPSILON)
    branch = scale * (own[:, :WIDTH] + came[:, :WIDTH])
    branch_ref[...] = branch
    scale_ref[...] = jnp.broadcast_to(scale, (ROWS, LANES))
    result = h_ref[...].astype(F32) + usable_rows(info) * branch
    res_ref[...] = result
    low_ref[...] = result.astype(BF16)


def join(info, h, own, came):
    wide = whole((ROWS, WIDTH))
    parts = whole((ROWS, WIDTH + LANES))
    return pl.pallas_call(
        join_body,
        out_shape=(
            shape((ROWS, WIDTH)),
            shape((ROWS, WIDTH), BF16),
            shape((ROWS, WIDTH)),
            shape((ROWS, LANES)),
        ),
        in_specs=[SMEM, wide, parts, parts],
        out_specs=(wide, wide, wide, whole((ROWS, LANES))),
        compiler_params=params(),
        cost_estimate=pl.CostEstimate(flops=2_000_000, bytes_accessed=8_000_000, transcendentals=0),
        name="join",
    )(info, h, own, came)


def gate_back_body(weight, info, cot, y, gate, gain, branch, scale_ref, *rest):
    refs = len(weight.arrays)
    w_refs, rest = rest[:refs], rest[refs:]
    bg_ref, dy_ref, dz_ref, n_ref, dgain_ref, buffer, sems, dn = rest
    weight.start(w_refs, info, buffer, sems)
    bg = usable_rows(info) * cot[...].astype(F32)
    bg_ref[...] = bg.astype(BF16)
    scale = scale_ref[:, :1]
    inner = jnp.sum(bg_ref[...].astype(F32) * branch[...], axis=1, keepdims=True)
    inner = inner * scale * scale / INNER
    for b in range(4):
        rows = weight.wait(w_refs, info, b, buffer, sems)
        dn[...] = dot_nt(bg_ref[...], buffer[rows, :])

        def one(i, _, rows=rows):
            here = pl.ds(pl.multiple_of(i * LANES, LANES), LANES)
            lanes = pl.ds(pl.multiple_of(rows.start + i * LANES, LANES), LANES)
            z = gate[:, lanes]
            sig = sigmoid(z)
            silu = z * sig
            y_here = y[:, lanes]
            gated = y_here * silu
            d_norm = dn[:, here]
            gained = scale * gain[:, lanes]
            n_ref[:, lanes] = (gated * gained).astype(BF16)
            d_gated = d_norm * gained - gated * inner
            total = jnp.sum(d_norm * gated * scale, axis=0, keepdims=True)
            dgain_ref[:, lanes] = jnp.broadcast_to(total, (8, LANES))
            dy_ref[:, lanes] = (d_gated * silu).astype(BF16)
            dz_ref[:, lanes] = (d_gated * y_here * sig * (1.0 + z * (1.0 - sig))).astype(BF16)
            return 0

        lax.fori_loop(0, SHARD // LANES, one, 0)


def gate_back(info, cot, y, gate, gain, branch, scale, weight):
    wide, local = whole((ROWS, WIDTH)), whole((ROWS, LOCAL))
    return pl.pallas_call(
        functools.partial(gate_back_body, weight),
        out_shape=(
            shape((ROWS, WIDTH), BF16),
            shape((ROWS, LOCAL), BF16),
            shape((ROWS, LOCAL), BF16),
            shape((ROWS, LOCAL), BF16),
            shape((8, LOCAL)),
        ),
        in_specs=[SMEM, wide, local, local, whole((1, LOCAL)), wide, whole((ROWS, LANES))]
        + weight.specs(),
        out_specs=(wide, local, local, local, whole((8, LOCAL))),
        scratch_shapes=weight.scratch() + [pltpu.VMEM((ROWS, SHARD), F32)],
        compiler_params=params(),
        cost_estimate=pl.CostEstimate(
            flops=2 * ROWS * WIDTH * LOCAL, bytes_accessed=13_000_000, transcendentals=800_000
        ),
        name="gate_back",
    )(info, cot, y, gate, gain, branch, scale, *weight.arrays)


def own_grad_body(dy, bca, cum, msg_in, own1_ref, msg_ref, ct, grow):
    g = pl.program_id(0)

    @pl.when(g == 0)
    def _():
        ct[...] = bca[:, STATE:].T.astype(BF16)
        grow[...] = jnp.exp(cum[...])

    factor = rolled(grow[...], g)
    weighted = (dy[...].astype(F32) * spread(factor)).astype(BF16)
    own0 = dot(ct[:, :HALF], half(weighted, 0))
    own1 = dot(ct[:, HALF:], half(weighted, 1))
    own1_ref[0] = own1
    grad = (spread(factor[HALF - 1 : HALF]) * own1 + own0).astype(BF16)
    for r in range(2):
        msg_ref[r, :STATE_HALF, :] = grad[r * STATE_HALF : (r + 1) * STATE_HALF]
        msg_ref[r, STATE_HALF:, :] = msg_in[r, STATE_HALF:, :]


def own_grad(dy, bca, cum, msg):
    return pl.pallas_call(
        own_grad_body,
        grid=(GROUPS,),
        out_shape=(
            shape((GROUPS, STATE, BLOCK)),
            shape((CHUNKS, MESSAGE, BLOCK), BF16),
        ),
        in_specs=[columns(ROWS, BLOCK), whole((ROWS, 256)), whole((ROWS, LANES)), MESSAGES],
        out_specs=(grouped(STATE), MESSAGES),
        scratch_shapes=[pltpu.VMEM((STATE, ROWS), BF16), pltpu.VMEM((ROWS, LANES), F32)],
        compiler_params=params(),
        cost_estimate=pl.CostEstimate(
            flops=2 * ROWS * STATE * LOCAL, bytes_accessed=2_500_000, transcendentals=0
        ),
        name="own_grad",
    )(dy, bca, cum, msg)


def inside_back_body(
    dy, xa, bca, cum, dt, hpar,
    dx_ref, dskip_ref, gsum_ref, u_ref, dbc_ref, cum_t, scores, dscores,
):
    g = pl.program_id(0)

    @pl.when(g == 0)
    def _():
        tri = lower_triangle()
        for q in range(2):
            b, c = half(bca[:, :STATE], q).astype(BF16), half(bca[:, STATE:], q).astype(BF16)
            scores[q] = dot_nt(b, c) * tri.T
            cum_t[:, q * HALF : (q + 1) * HALF] = half(cum[...], q).T
        dscores[...] = jnp.zeros((2, HALF, HALF), F32)
        u_ref[...] = jnp.zeros((ROWS, LANES), F32)

    cols = rolled(cum[...], g)
    rows = cum_t[pl.ds(pl.multiple_of(8 * g, 8), 8), :]
    steps = rolled(dt[...], g)
    skips = rolled(hpar[...], g)[2:3, :]
    low = lane_of((HALF, LANES)) < HEADDIM
    lane = lane_of((HALF, LANES))
    gsum_ref[...] = jnp.zeros((8, ROWS), F32)
    for q in range(2):
        here = slice(q * HALF, (q + 1) * HALF)
        u_here = u_ref[here, :]
        for p in range(OWN // 2):
            lanes = slice(p * LANES, (p + 1) * LANES)
            dy_pair = dy[here, lanes]
            x = xa[here, lanes]
            zero = jnp.zeros_like(dy_pair)
            both = jnp.concatenate(
                [jnp.where(low, dy_pair, zero), jnp.where(low, zero, dy_pair)], axis=0
            )
            dw = dot_nt(x.astype(BF16), both)
            mats = []
            for n, i in enumerate((2 * p, 2 * p + 1)):
                gap = rows[i : i + 1, here] - half(cols, q)[:, i : i + 1]
                decay = jnp.exp(jnp.minimum(gap, 0.0))
                step = half(steps, q)[:, i : i + 1]
                weight = decay * scores[q]
                mats.append(weight.astype(BF16))
                dw_here = dw[:, n * HALF : (n + 1) * HALF]
                dscores[q] += decay * dw_here * step
                direct = weight * dw_here
                total = jnp.sum(direct, axis=1, keepdims=True)
                u_here = jnp.where(lane == 8 * g + i, total, u_here)
                gsum_ref[i : i + 1, here] = jnp.sum(direct * step, axis=0, keepdims=True)
            dx = dot(jnp.concatenate(mats, axis=1), both)
            dy_wide = dy_pair.astype(F32)
            dx_ref[here, lanes] = dx * pair_lanes(half(steps, q), p) + dy_wide * pair_lanes(skips, p)
            skip_sum = jnp.sum(dy_wide * x, axis=0, keepdims=True)
            if q == 0:
                dskip_ref[:, lanes] = jnp.broadcast_to(skip_sum, (8, LANES))
            else:
                dskip_ref[:, lanes] += skip_sum
        u_ref[here, :] = u_here

    @pl.when(g == GROUPS - 1)
    def _():
        tri = lower_triangle()
        for q in range(2):
            b, c = half(bca[:, :STATE], q).astype(BF16), half(bca[:, STATE:], q).astype(BF16)
            ds_t = dscores[q] * tri.T
            dbc_ref[q * HALF : (q + 1) * HALF, :STATE] = dot(ds_t.astype(BF16), c)
            dbc_ref[q * HALF : (q + 1) * HALF, STATE:] = dot(ds_t.T.astype(BF16), b)


def inside_back(dy, xa, bca, cum, dt, hpar):
    return pl.pallas_call(
        inside_back_body,
        grid=(GROUPS,),
        out_shape=(
            shape((ROWS, LOCAL)),
            shape((8, LOCAL)),
            shape((8 * GROUPS, ROWS)),
            shape((ROWS, LANES)),
            shape((ROWS, 256)),
        ),
        in_specs=[
            columns(ROWS, BLOCK),
            columns(ROWS, BLOCK),
            whole((ROWS, 256)),
            whole((ROWS, LANES)),
            whole((ROWS, LANES)),
            whole((8, LANES)),
        ],
        out_specs=(
            columns(ROWS, BLOCK),
            columns(8, BLOCK),
            pl.BlockSpec((8, ROWS), lambda g: (g, 0)),
            whole((ROWS, LANES)),
            whole((ROWS, 256)),
        ),
        scratch_shapes=[
            pltpu.VMEM((LANES, ROWS), F32),
            pltpu.VMEM((2, HALF, HALF), F32),
            pltpu.VMEM((2, HALF, HALF), F32),
        ],
        compiler_params=params(),
        cost_estimate=pl.CostEstimate(
            flops=4 * HEADS * HALF * HALF * LANES, bytes_accessed=4_500_000, transcendentals=800_000
        ),
        name="inside_back",
    )(dy, xa, bca, cum, dt, hpar)


def conv_back(d_active, values, halo, cpar, keep, ext, ext_d):
    width = values.shape[1]
    total = conv_sum_of(values, halo, cpar, keep, ext)
    sig = sigmoid(total)
    d_sum = d_active * sig * (1.0 + total * (1.0 - sig))
    ext_d[0:16, :width] = jnp.zeros((16, width), F32)
    ext_d[16 : 16 + ROWS, :width] = d_sum
    ext_d[16 + ROWS :, :width] = jnp.zeros((16, width), F32)
    d_in = jnp.zeros((ROWS + 16, width), F32)
    for k in range(KERNEL):
        d_in = d_in + cpar[k : k + 1, :] * ext_d[3 - k : 3 - k + ROWS + 16, :width]
    row = row_of((8, width))
    d_par = jnp.where(row == 4, jnp.sum(d_sum, axis=0, keepdims=True), 0.0)
    for k in range(KERNEL):
        tap = jnp.sum(d_sum * ext[13 + k : 13 + k + ROWS, :width], axis=0, keepdims=True)
        d_par = jnp.where(row == k, tap, d_par)
    return d_in, d_par


def finish_body(
    info, xa, dxi, dy, mixed, halo, cpar, bc, halo_bc, cpar_bc, bca, cum, dt, rate, hpar, lam, hin, s0, own1, u, gsum, dbc,
    dmx_ref, dmbc_ref, tailx_ref, tailbc_ref, edgex_ref, edgebc_ref, dcx_ref, dcbc_ref, dhead_ref,
    ext, ext_d, grow, tail, v_sum, q_sum, end_sum, dbc_sum,
):
    g = pl.program_id(0)
    keep = info[1].astype(F32)

    @pl.when(g == 0)
    def _():
        grow[...] = jnp.exp(cum[...])
        for q in range(2):
            here = half(cum[...], q)
            tail[q * HALF : (q + 1) * HALF, :] = jnp.exp(here[HALF - 1 :, :] - here)
        v_sum[...] = jnp.zeros((ROWS, LANES), F32)
        q_sum[...] = jnp.zeros((ROWS, LANES), F32)
        end_sum[...] = jnp.zeros((16, LANES), F32)
        dbc_sum[...] = dbc[...]

    sums = head_sum_matrix(g)
    factor = rolled(grow[...], g)
    tails = rolled(tail[...], g)
    steps = rolled(dt[...], g)
    ends = [spread(factor[HALF - 1 : HALF]), spread(factor[ROWS - 1 : ROWS])]
    lam1 = lam[0].astype(F32)
    lams = [ends[1] * lam1 + own1[0], lam1]
    first = hin[0].astype(F32)
    states = [first, ends[0] * first + s0[0]]
    d_x = []
    for q in range(2):
        here = slice(q * HALF, (q + 1) * HALF)
        b, c = bca[here, :STATE].astype(BF16), bca[here, STATE:].astype(BF16)
        lam_q, state_q = lams[q].astype(BF16), states[q].astype(BF16)
        tail_wide = spread(half(tails, q))
        tail_step = tail_wide * spread(half(steps, q))
        x, dy_q = xa[here, :], dy[here, :].astype(F32)
        lb = dot(b, lam_q) * tail_wide
        d_x.append(dxi[here, :] + lb * spread(half(steps, q)))
        v_sum[here, :] += dot((x * lb).astype(BF16), sums)
        grow_wide = spread(half(factor, q))
        dy_grow = (dy_q * grow_wide).astype(BF16)
        carried = dot(c, state_q)
        q_sum[here, :] += dot((dy_q * grow_wide * carried).astype(BF16), sums)
        dbc_sum[here, :STATE] += dot_nt((x * tail_step).astype(BF16), lam_q)
        dbc_sum[here, STATE:] += dot_nt(dy_grow, state_q)
        last = jnp.sum(lams[q] * states[q], axis=0, keepdims=True) * ends[q]
        end_sum[8 * q : 8 * q + 8, :] += exact_dot(
            jnp.broadcast_to(last, (8, BLOCK)), sums.astype(F32)
        )
    d_in, d_par = conv_back(
        jnp.concatenate(d_x, axis=0), mixed[...], halo[...], cpar[...], keep, ext, ext_d
    )
    dmx_ref[...] = d_in[16:].astype(BF16)
    tailx_ref[...] = d_in[ROWS:]
    edgex_ref[...] = (d_in[:16] * keep).astype(BF16)
    dcx_ref[...] = d_par

    @pl.when(g == GROUPS - 1)
    def _():
        d_bc, d_par_bc = conv_back(
            dbc_sum[...], bc[...], halo_bc[...], cpar_bc[...], keep, ext, ext_d
        )
        dmbc_ref[:, :256] = d_bc[16:].astype(BF16)
        tailbc_ref[...] = d_bc[ROWS:]
        edgebc_ref[...] = (d_bc[:16] * keep).astype(BF16)
        dcbc_ref[...] = d_par_bc
        rates = -jnp.exp(hpar[1:2, :])
        logit = rate[...] + hpar[0:1, :]
        upper = lower_triangle().T
        before = lower_triangle(True)
        d_bias = jnp.zeros((1, LANES), F32)
        d_log = jnp.zeros((1, LANES), F32)
        usable = usable_rows(info)
        for q in range(2):
            here = slice(q * HALF, (q + 1) * HALF)
            step = dt[here, :]
            gs = gsum[...][:, here].T
            gs = jnp.concatenate([gs, jnp.zeros((HALF, LANES - 8 * GROUPS), F32)], axis=1)
            d_decay = exact_dot(upper, gs - step * u[here, :] + q_sum[here, :])
            d_decay = d_decay + exact_dot(before, step * v_sum[here, :])
            d_decay = d_decay + end_sum[8 * q : 8 * q + 1, :]
            d_step = u[here, :] + v_sum[here, :] + rates * d_decay
            d_rate = half(usable, q) * d_step * sigmoid(half(logit, q))
            d_bias += jnp.sum(d_rate, axis=0, keepdims=True)
            d_log += jnp.sum(d_decay * step * rates, axis=0, keepdims=True)
            dmbc_ref[here, 256:] = d_rate.astype(BF16)
        row = row_of((8, LANES))
        dhead_ref[...] = jnp.where(row == 0, d_bias, jnp.where(row == 1, d_log, 0.0))


def finish_call(
    info, xa, dxi, dy, mixed, halo, cpar, bca, cum, dt, rate, hpar, lam, hin, s0, own1, u, gsum, dbc
):
    bc_at = LOCAL // 256
    wide = whole((ROWS, LANES))
    return pl.pallas_call(
        finish_body,
        grid=(GROUPS,),
        out_shape=(
            shape((ROWS, LOCAL), BF16),
            shape((ROWS, 384), BF16),
            shape((16, LOCAL)),
            shape((16, 256)),
            shape((16, LOCAL), BF16),
            shape((16, 256), BF16),
            shape((8, LOCAL)),
            shape((8, 256)),
            shape((8, LANES)),
        ),
        in_specs=[
            SMEM,
            columns(ROWS, BLOCK),
            columns(ROWS, BLOCK),
            columns(ROWS, BLOCK),
            columns(ROWS, BLOCK),
            columns(16, BLOCK),
            columns(8, BLOCK),
            pl.BlockSpec((ROWS, 256), lambda g: (0, bc_at)),
            pl.BlockSpec((16, 256), lambda g: (0, bc_at)),
            pl.BlockSpec((8, 256), lambda g: (0, bc_at)),
            whole((ROWS, 256)),
            wide,
            wide,
            wide,
            whole((8, LANES)),
            grouped(STATE),
            grouped(STATE),
            grouped(STATE),
            grouped(STATE),
            wide,
            whole((8 * GROUPS, ROWS)),
            whole((ROWS, 256)),
        ],
        out_specs=(
            columns(ROWS, BLOCK),
            whole((ROWS, 384)),
            columns(16, BLOCK),
            whole((16, 256)),
            columns(16, BLOCK),
            whole((16, 256)),
            columns(8, BLOCK),
            whole((8, 256)),
            whole((8, LANES)),
        ),
        scratch_shapes=[
            pltpu.VMEM((ROWS + 32, BLOCK), F32),
            pltpu.VMEM((ROWS + 32, BLOCK), F32),
            pltpu.VMEM((ROWS, LANES), F32),
            pltpu.VMEM((ROWS, LANES), F32),
            pltpu.VMEM((ROWS, LANES), F32),
            pltpu.VMEM((ROWS, LANES), F32),
            pltpu.VMEM((16, LANES), F32),
            pltpu.VMEM((ROWS, 256), F32),
        ],
        compiler_params=params(),
        cost_estimate=pl.CostEstimate(
            flops=10 * ROWS * STATE * LOCAL, bytes_accessed=7_500_000, transcendentals=800_000
        ),
        name="finish_back",
    )(
        info, xa, dxi, dy, mixed, halo, cpar, mixed, halo, cpar, bca, cum, dt, rate, hpar,
        lam, hin, s0, own1, u, gsum, dbc,
    )


def gate_in_back_body(weight, info, dz, *rest):
    refs = len(weight.arrays)
    w_refs, (out_ref, buffer, sems) = rest[:refs], rest[refs:]
    weight.start(w_refs, info, buffer, sems)
    for b in range(4):
        rows = weight.wait(w_refs, info, b, buffer, sems)
        out_ref[:, rows] = dot_nt(dz[...], buffer[rows, :])


def gate_in_back(info, dz, weight):
    return pl.pallas_call(
        functools.partial(gate_in_back_body, weight),
        out_shape=shape((ROWS, WIDTH)),
        in_specs=[SMEM, whole((ROWS, LOCAL))] + weight.specs(),
        out_specs=whole((ROWS, WIDTH)),
        scratch_shapes=weight.scratch(),
        compiler_params=params(),
        cost_estimate=pl.CostEstimate(
            flops=2 * ROWS * WIDTH * LOCAL, bytes_accessed=7_000_000, transcendentals=0
        ),
        name="gate_in_back",
    )(info, dz, *weight.arrays)


def patch_body(dmx, dmbc, tailx, tailbc, edge, token, dxc_ref):
    dxc_ref[:, :LOCAL] = dmx[...]
    dxc_ref[:, LOCAL:] = dmbc[...]
    late = edge[...].astype(F32)
    dxc_ref[ROWS - 16 :, :LOCAL] = (tailx[...] + late[:, :LOCAL]).astype(BF16)
    dxc_ref[ROWS - 16 :, LOCAL:MIXED] = (tailbc[...] + late[:, LOCAL:]).astype(BF16)


def patch(dmx, dmbc, tailx, tailbc, edge, token):
    arrays = (dmx, dmbc, tailx, tailbc, edge)
    return pl.pallas_call(
        patch_body,
        out_shape=shape((ROWS, PACKED), BF16),
        in_specs=[whole(v.shape) for v in arrays] + [ANYWHERE],
        out_specs=whole((ROWS, PACKED)),
        compiler_params=params(),
        cost_estimate=pl.CostEstimate(flops=100_000, bytes_accessed=2_000_000, transcendentals=0),
        name="patch",
    )(*arrays, token)


def mixed_back_body(weight, info, dxc, part, *rest):
    refs = len(weight.arrays)
    w_refs, (out_ref, buffer, sems) = rest[:refs], rest[refs:]
    weight.start(w_refs, info, buffer, sems)
    for b in range(4):
        rows = weight.wait(w_refs, info, b, buffer, sems)
        out_ref[:, rows] = part[:, rows] + dot_nt(dxc[...], buffer[rows, :])


def mixed_back(info, dxc, part, weight):
    return pl.pallas_call(
        functools.partial(mixed_back_body, weight),
        out_shape=shape((ROWS, WIDTH)),
        in_specs=[SMEM, whole((ROWS, PACKED)), whole((ROWS, WIDTH))] + weight.specs(),
        out_specs=whole((ROWS, WIDTH)),
        scratch_shapes=weight.scratch(),
        compiler_params=params(),
        cost_estimate=pl.CostEstimate(
            flops=2 * ROWS * WIDTH * PACKED, bytes_accessed=9_000_000, transcendentals=0
        ),
        name="mixed_back",
    )(info, dxc, part, *weight.arrays)


def norm_back_body(own, came, h_ref, cot, gain, dh_ref, low_ref, dgain_ref):
    h = h_ref[...].astype(F32)
    scale = lax.rsqrt(jnp.mean(h * h, axis=1, keepdims=True) + EPSILON)
    d_norm = own[...] + came[...]
    inner = jnp.mean(d_norm * gain[...] * h, axis=1, keepdims=True) * scale * scale * scale
    dgain_ref[...] = jnp.broadcast_to(
        jnp.sum(d_norm * h * scale, axis=0, keepdims=True), (8, WIDTH)
    )
    dh = cot[...].astype(F32) + scale * d_norm * gain[...] - h * inner
    dh_ref[...] = dh
    low_ref[...] = dh.astype(BF16)


def norm_back(own, came, h, cot, gain):
    return pl.pallas_call(
        norm_back_body,
        out_shape=(shape((ROWS, WIDTH)), shape((ROWS, WIDTH), BF16), shape((8, WIDTH))),
        compiler_params=params(),
        cost_estimate=pl.CostEstimate(flops=3_000_000, bytes_accessed=8_000_000, transcendentals=0),
        name="norm_back",
    )(own, came, h, cot, gain)


def z_shift(r):
    return "dp", [(z, (z + r) % 4) for z in range(4)]


def y_shift(r):
    return "ctx", [(j, (j + 4 * r) % 16) for j in range(16)]


def x_shift(r):
    return "ctx", [(j, j - j % 4 + (j + r) % 4) for j in range(16)]


SHIFTS = {"z": z_shift, "y": y_shift, "x": x_shift}


def send(value, axis, r):
    name, pairs = SHIFTS[axis](r % 4)
    return lax.ppermute(value, name, pairs)


def swapped(value):
    return lax.ppermute(value, "section", [(0, 1), (1, 0)])


def after(values, place):
    nothing = jnp.int32(0)
    for value in values:
        corner = lax.slice(value, (0,) * value.ndim, (1,) * value.ndim).reshape(())
        nothing = nothing + (corner != corner).astype(jnp.int32)
    return {axis: n + nothing for axis, n in place.items()}


def pieces(mine, came, layer, section, place):
    rows = SHARD // 2

    def piece(source, side, axis):
        return lax.dynamic_slice_in_dim(source, side * rows + place[axis] * PIECE, PIECE, 0)

    first = jnp.concatenate(
        [
            jnp.where(section == layer, piece(mine, side, axis), piece(came, side, axis))
            for side, axis in enumerate("xy")
        ]
    )
    got = [send(first, "z", -r) for r in range(1, 4)]
    out = [mine, came]
    for side, axis in enumerate("xy"):
        stack = jnp.concatenate([g[side * PIECE : (side + 1) * PIECE] for g in got])
        out += [stack] + [send(stack, axis, -r) for r in range(1, 4)]
    return out, got


def summed(terms):
    a, b, c, d = (t.astype(F32) for t in terms)
    return (a + c) + (b + d)


def arrived(terms, axis):
    return [terms[0]] + [send(terms[r], axis, r) for r in range(1, 4)]


def total_of(value):
    for axis in "xyz":
        low = value.astype(BF16)
        value = summed([low] + [send(low, axis, r) for r in range(1, 4)])
    return value


def fold_body(slot, counts, outer, inner, info, *rest):
    refs, outs, total = rest[: sum(counts)], rest[sum(counts) + 1 : -1], rest[-1]
    column = 0
    for count in counts:
        arrays, refs = refs[:count], refs[count:]
        cols = slice(column, column + arrays[0].shape[1])
        total[:, cols] = summed([a[...] for a in arrays]) if count == 4 else arrays[0][...].astype(F32)
        column = cols.stop
    for r in range(4):
        first = lax.rem(info[slot] + r, 4) * inner
        parts = [
            total[pl.ds(pl.multiple_of(n * 4 * inner + first, 8), inner), :] for n in range(outer)
        ]
        outs[r][...] = jnp.concatenate(parts, axis=0).astype(BF16)


def fold(info, axis, groups, outer, inner, token):
    slot = 10 + "zyx".index(axis)
    arrays = [a for group in groups for a in group]
    rows, width = arrays[0].shape[0], sum(group[0].shape[1] for group in groups)
    return pl.pallas_call(
        functools.partial(fold_body, slot, [len(group) for group in groups], outer, inner),
        out_shape=[shape((rows // 4, width), BF16)] * 4,
        in_specs=[SMEM] + [whole(a.shape) for a in arrays] + [ANYWHERE],
        out_specs=[whole((rows // 4, width))] * 4,
        scratch_shapes=[pltpu.VMEM((rows, width), F32)],
        compiler_params=params(),
        cost_estimate=pl.CostEstimate(flops=2_000_000, bytes_accessed=8_000_000, transcendentals=0),
        name="fold",
    )(info, *arrays, token)


PARITY = [[j for j in range(16) if j % 2 == e] for e in range(2)]
NEIGHBOURS = [(j, j ^ 1) for j in range(16)]


def exchange(value):
    return lax.all_to_all(value, "ctx", 0, 0, axis_index_groups=PARITY)


def halo_shift(value, step):
    pairs = [(j, j + 2 * step) for j in range(16) if 0 <= j + 2 * step < 16]
    return lax.ppermute(value, "ctx", pairs)


def halves(values, section):
    grid = values.reshape(values.shape[0], GROUPS, 2, -1)
    size = values.shape[1] // 2
    return [
        lax.dynamic_index_in_dim(grid, i, 2, False).reshape(-1, size)
        for i in (section, 1 - section)
    ]


def turns(low, high):
    rows = low.shape[0]
    parts = [v.reshape(rows, GROUPS, 1, -1) for v in (low, high)]
    return jnp.concatenate(parts, axis=2).reshape(rows, -1)


def pick_x_body(info, x_ref, dt_ref, *outs):
    head, lane = row_of((HEADS, LANES)), lane_of((HEADS, LANES))
    for out, side in zip(outs, (info[0], 1 - info[0]), strict=True):
        for d in range(GROUPS):
            cols = pl.ds(pl.multiple_of((2 * d + side) * BLOCK, LANES), BLOCK)
            out[:, d * BLOCK : (d + 1) * BLOCK] = x_ref[:, cols]
        out[:, LOCAL:MIXED] = x_ref[:, INNER:]
        here = (head // OWN == 2 * (lane // 8) + side) & (head % OWN == lane % 8)
        out[:, MIXED:] = dot(dt_ref[...], here.astype(BF16)).astype(BF16)


def pick_x(section, x, dt):
    return pl.pallas_call(
        pick_x_body,
        out_shape=[shape((SHARD, PACKED), BF16)] * 2,
        in_specs=[SMEM, whole((SHARD, CONV_CH)), whole((SHARD, HEADS))],
        out_specs=[whole((SHARD, PACKED))] * 2,
        compiler_params=params(),
        cost_estimate=pl.CostEstimate(flops=0, bytes_accessed=6_000_000, transcendentals=0),
        name="pick_x",
    )(section, x, dt)


def pick_zo_body(info, z_ref, o_ref, token, *outs):
    for out, side in zip(outs, (info[0], 1 - info[0]), strict=True):
        for d in range(GROUPS):
            cols = pl.ds(pl.multiple_of((2 * d + side) * BLOCK, LANES), BLOCK)
            out[:, d * BLOCK : (d + 1) * BLOCK] = z_ref[:, cols]
        rows = pl.ds(pl.multiple_of(side * SHARD, SHARD), SHARD)
        out[:, LOCAL:] = o_ref[rows, :]


def pick_zo(section, z, o, token):
    return pl.pallas_call(
        pick_zo_body,
        out_shape=[shape((SHARD, LOCAL + WIDTH), BF16)] * 2,
        in_specs=[SMEM, whole((SHARD, INNER)), whole((2 * SHARD, WIDTH)), ANYWHERE],
        out_specs=[whole((SHARD, LOCAL + WIDTH))] * 2,
        compiler_params=params(),
        cost_estimate=pl.CostEstimate(flops=0, bytes_accessed=9_000_000, transcendentals=0),
        name="pick_zo",
    )(section, z, o, token)


def head_lanes(values):
    rows = values.shape[0]
    grid = jnp.pad(values.reshape(rows, GROUPS, OWN), ((0, 0), (0, 0), (0, 8 - OWN)))
    return jnp.pad(grid.reshape(rows, 8 * GROUPS), ((0, 0), (0, LANES - 8 * GROUPS)))


def lanes_heads(values):
    rows = values.shape[0]
    return values[:, : 8 * GROUPS].reshape(rows, GROUPS, 8)[:, :, :OWN].reshape(rows, -1)


def on_device(
    boundary,
    lengths,
    norm_gain,
    w_z,
    w_xbc,
    w_dt,
    conv_weight,
    conv_bias,
    dt_bias,
    a_log,
    d_skip,
    gate_gain,
    w_out,
):
    section = lax.axis_index("section")
    group = lax.axis_index("dp")
    ctx = lax.axis_index("ctx")
    place = {"z": group, "y": ctx // 4, "x": ctx % 4}
    micro = ctx % 2
    chunk = ctx // 2

    def ordered(mine, came):
        return jnp.where(section == 0, mine, came), jnp.where(section == 0, came, mine)

    at = section.reshape(1).astype(jnp.int32)
    mine_x, other_x = pick_x(at, w_xbc[0], w_dt[0])
    came_x = swapped(other_x)
    mine_zo, other_zo = pick_zo(at, w_z[0], w_out[0], mine_x)
    came_zo = swapped(other_zo)
    low_x, got = pieces(mine_x, came_x, 0, section, place)
    low_zo, got = pieces(mine_zo, came_zo, 0, section, after(got, place))
    here = after(got, {"section": section})["section"]
    high_x = [lax.all_gather(jnp.where(here == 1, mine_x, came_x), "dp", tiled=True)]
    high_zo = [lax.all_gather(jnp.where(here == 1, mine_zo, came_zo), "dp", tiled=True)]
    weights_x = [Weight(v, n, PACKED) for n, v in enumerate((low_x, high_x))]
    weights_z = [Weight(v, n, LOCAL) for n, v in enumerate((low_zo, high_zo))]
    weights_o = [Weight(v, n, WIDTH, LOCAL) for n, v in enumerate((low_zo, high_zo))]

    small = jnp.zeros((16, 832), F32)
    small = small.at[:4].set(conv_weight[0].astype(F32)).at[4].set(conv_bias[0].astype(F32))
    small = small.at[5, :384].set(norm_gain[0].astype(F32))
    small = small.at[6, :768].set(gate_gain[0].astype(F32))
    small = small.at[8, :HEADS].set(dt_bias[0]).at[9, :HEADS].set(a_log[0])
    small = small.at[10, :HEADS].set(d_skip[0])
    smalls = jnp.stack([small] + [send(small, "z", -r) for r in range(1, 4)])
    smalls = lax.dynamic_slice_in_dim(jnp.concatenate([smalls, smalls]), (4 - group) % 4, 4)
    cpars, gains_one, gains_two, hpars = [], [], [], []
    for values in ordered(smalls, swapped(smalls)):
        full = jnp.transpose(values[:, :8], (1, 0, 2)).reshape(8, CONV_CH)
        local = halves(full[:, :INNER], section)[0]
        cpars.append(jnp.concatenate([local, full[:, INNER:]], axis=1))
        gains_one.append(values[:, 5, :384].reshape(1, WIDTH))
        gains_two.append(halves(values[:, 6, :768].reshape(1, INNER), section)[0])
        hpars.append(jnp.pad(head_lanes(halves(values[0, 8:11, :HEADS], section)[0]), ((0, 5), (0, 0))))

    own_rows = lax.dynamic_index_in_dim(boundary[0], micro, 0, False)
    other_rows = lax.dynamic_index_in_dim(boundary[0], 1 - micro, 0, False)
    came = lax.ppermute(other_rows, "ctx", NEIGHBOURS)
    block = jnp.where(
        micro == 0, jnp.concatenate([own_rows, came]), jnp.concatenate([came, own_rows])
    )
    hidden, cotangent = ordered(block, swapped(block))

    pair = lengths[group, micro]
    padded = (pair[0] + SPAN - 1) // SPAN * SPAN
    offset = chunk * ROWS
    begin = jnp.where(offset >= padded, padded, 0)
    length = jnp.where(offset >= padded, pair[1], pair[0])
    live = jnp.clip(length - (offset - begin), 0, ROWS)
    offsets = jnp.arange(CHUNKS, dtype=jnp.int32) * ROWS
    keeps = ((offsets != 0) & (offsets != padded)).astype(jnp.int32)
    keep = (offset != 0) & (offset != padded)
    at = [place["z"], place["y"], place["x"], section]
    info = jnp.concatenate(
        [jnp.stack([live, keep]).astype(jnp.int32), keeps, jnp.stack(at).astype(jnp.int32)]
    )

    def forward(h, layer):
        cpar, hpar = cpars[layer], hpars[layer]
        normed, mixed, rate = in_proj(info, h, gains_one[layer], weights_x[layer])
        halo = halo_shift(mixed[ROWS - 16 :], 1)
        gate = gate_proj(info, normed, weights_z[layer])
        xa, bca, cum, dt, s0, msg = state_call(info, mixed, halo, cpar, rate, hpar)
        came = exchange(msg)
        y_in = inside_call(xa, bca, cum, dt, hpar)
        hin = exchange(scan_call(info, came, False, gate)).reshape(GROUPS, STATE, BLOCK)
        y, part = out_proj(
            info, y_in, bca, cum, hin, s0, gate, gains_two[layer], weights_o[layer]
        )
        result, low, branch, scale = join(info, h, part, swapped(part))
        saved = (h, normed, mixed, halo, rate, gate, xa, bca, cum, dt, s0, msg, hin, y, branch, scale)
        return result, low, saved

    def backward(cot, saved, layer, higher=None):
        h, normed, mixed, halo, rate, gate, xa, bca, cum, dt, s0, msg, hin, y, branch, scale = saved
        cpar, hpar = cpars[layer], hpars[layer]
        bg, dy, dz, normed_two, d_gain_two = gate_back(
            info, cot, y, gate, gains_two[layer], branch, scale, weights_o[layer]
        )
        own1, msg_back = own_grad(dy, bca, cum, msg)
        came = exchange(msg_back)
        normed_two_t, normed_t = normed_two.T, normed.T

        def terms(source, axis, other, place):
            grid = source.reshape((4, 4, 96, ROWS) if axis == "y" else (4, 4, 4, 24, ROWS))
            out = []
            for r in range(4):
                rows = lax.dynamic_index_in_dim(
                    grid, (place[axis] + r) % 4, "zyx".index(axis), False
                )
                out.append(dot(rows.reshape(SHARD, ROWS), other).astype(BF16))
            return out

        def first_stage(source, other):
            return lax.psum_scatter(dot(source, other).astype(BF16), "dp", tiled=True)

        if layer == 1:
            sums = [first_stage(normed_two_t, bg), first_stage(normed_t, dz)]
        dxi, d_skips, gsum, u, dbc = inside_back(dy, xa, bca, cum, dt, hpar)
        part = gate_in_back(info, dz, weights_z[layer])
        lam = exchange(scan_call(info, came, True, part)).reshape(GROUPS, STATE, BLOCK)
        if layer == 0:
            here = after([lam], place)
            sent_z = arrived(terms(normed_t, "y", dz, here), "y")
            sent_o = arrived(terms(normed_two_t, "x", bg, here), "x")
        dmx, dmbc, tailx, tailbc, edgex, edgebc, d_parx, d_parbc, d_heads = finish_call(
            info, xa, dxi, dy, mixed, halo, cpar, bca, cum, dt, rate, hpar, lam, hin, s0, own1, u, gsum, dbc
        )
        edge = halo_shift(jnp.concatenate([edgex, edgebc], axis=1), -1)
        token = d_heads
        if layer == 0:
            higher = fold(info, "y", [[v] for v in higher], 1, 96, d_heads)
            token = higher[0]
        dxc = patch(dmx, dmbc, tailx, tailbc, edge, token)
        part = mixed_back(info, dxc, part, weights_x[layer])
        dh, dh_low, d_gain_one = norm_back(part, swapped(part), h, cot, gains_one[layer])

        if layer == 0:
            middle = PACKED // 2
            sent_l = arrived(terms(normed_t, "y", dxc[:, :middle], place), "y")
            sent_r = arrived(terms(normed_t, "x", dxc[:, middle:], place), "x")
            left = arrived(fold(info, "x", [sent_z, sent_l], 4, 24, dh_low), "x")
            right = arrived(fold(info, "y", [sent_o, sent_r], 4, 24, dh_low), "y")
            sums = higher, summed(arrived(fold(info, "z", [left, right], 1, 24, dh_low), "z"))
        else:
            sums.append(first_stage(normed_t, dxc))
        d_skip_row = jnp.sum(d_skips[0:1].reshape(1, 4 * OWN, HEADDIM), axis=2)
        rows = jnp.where(jnp.arange(8)[:, None] == 5, d_gain_two, d_parx)
        rows = jnp.concatenate([rows, d_parbc], axis=1)
        more = jnp.concatenate(
            [
                d_gain_one[:1],
                jnp.pad(d_heads[:2], ((0, 0), (0, WIDTH - LANES))),
                jnp.pad(head_lanes(d_skip_row), ((0, 4), (0, WIDTH - LANES))),
            ]
        )
        rows = jnp.concatenate([rows, jnp.pad(more, ((0, 0), (0, 2 * STATE)))])
        return dh, dh_low, sums, rows

    _, middle, saved_low = forward(hidden, 0)
    out_high, _, saved_high = forward(middle, 1)
    _, back, higher, rows_high = backward(cotangent, saved_high, 1)
    dh_low, back, (higher, low), rows_low = backward(back, saved_low, 0, higher)

    higher = fold(info, "x", [arrived(higher, "y")], 1, 24, back)
    high = summed(arrived(higher, "x"))
    high_o, high_z, high_x = jnp.split(high, (WIDTH, WIDTH + LOCAL), axis=1)
    at = (LOCAL, LOCAL + PACKED // 2, LOCAL + PACKED // 2 + WIDTH)
    low_z, low_l, low_o, low_r = jnp.split(low, at, axis=1)

    rows = total_of(jnp.concatenate([rows_low, rows_high]))
    own, given = ordered(rows[:16], rows[16:])
    rows_0, rows_1 = ordered(own, swapped(given))
    wide = jnp.concatenate(
        [turns(rows_0[:8, :LOCAL], rows_1[:8, :LOCAL]), rows_0[:8, LOCAL:] + rows_1[:8, LOCAL:]],
        axis=1,
    )
    head_rows = turns(lanes_heads(rows_0[9:12, :LANES]), lanes_heads(rows_1[9:12, :LANES]))
    index = group * 16 + ctx
    d_conv = lax.dynamic_slice(wide, (0, index * 52), (5, 52))
    d_gain_two = lax.dynamic_slice(wide, (5, index * 48), (1, 48))
    d_gain_one = lax.dynamic_slice(rows_0, (8, index * 24), (1, 24))

    own, given = ordered(
        jnp.concatenate([low_z, low_l, low_r], axis=1), jnp.concatenate([high_z, high_x], axis=1)
    )
    first, second = ordered(own, swapped(given))
    sum_z = turns(first[:, :LOCAL], second[:, :LOCAL])
    at_x, at_bc, at_dt = LOCAL, LOCAL + LOCAL, LOCAL + MIXED
    sum_x = turns(first[:, at_x:at_bc], second[:, at_x:at_bc])
    sum_bc = first[:, at_bc:at_dt] + second[:, at_bc:at_dt]
    sum_dt = turns(lanes_heads(first[:, at_dt:]), lanes_heads(second[:, at_dt:]))

    trips = []
    for flip in range(2):
        pairs = [
            (c * 16 + j, (flip ^ (j % 2)) * 16 + 8 * c + j // 2) for c in range(2) for j in range(16)
        ]
        value = jnp.where(micro == flip, low_o, high_o)
        trips.append(lax.ppermute(value, ("section", "ctx"), pairs))
    sum_o = jnp.concatenate(ordered(*trips))

    def returned(rows, layer):
        pairs = [(layer * 16 + a, layer * 16 + b) for a, b in NEIGHBOURS]
        other = lax.ppermute(
            jnp.where(micro == 0, rows[HALF:], rows[:HALF]), ("section", "ctx"), pairs
        )
        mine = jnp.where(micro == 0, rows[:HALF], rows[HALF:])
        return jnp.where(micro == 0, jnp.stack([mine, other]), jnp.stack([other, mine]))

    top = jnp.where(section == 0, returned(dh_low, 0), returned(out_high, 1))
    return (
        top[None],
        d_gain_one,
        sum_z[None],
        jnp.concatenate([sum_x, sum_bc], axis=1)[None],
        sum_dt[None],
        d_conv[None, :4],
        d_conv[4:5],
        head_rows[0:1],
        head_rows[1:2],
        head_rows[2:3],
        d_gain_two,
        sum_o[None],
    )


def solution(mesh):
    in_specs = (
        P("section", None, ("dp", "ctx"), None),
        P(),
        P("section", "dp"),
        P("section", "dp", None),
        P("section", "dp", None),
        P("section", "dp", None),
        P("section", None, "dp"),
        P("section", "dp"),
        P("section", None),
        P("section", None),
        P("section", None),
        P("section", "dp"),
        P("section", "dp", None),
    )
    out_specs = (
        P("section", None, ("dp", "ctx"), None),
        P("section", ("dp", "ctx")),
        P("section", ("dp", "ctx"), None),
        P("section", ("dp", "ctx"), None),
        P("section", ("dp", "ctx"), None),
        P("section", None, ("dp", "ctx")),
        P("section", ("dp", "ctx")),
        P("section", None),
        P("section", None),
        P("section", None),
        P("section", ("dp", "ctx")),
        P("section", ("dp", "ctx"), None),
    )
    return jax.shard_map(
        on_device, mesh=mesh, in_specs=in_specs, out_specs=out_specs, check_vma=False
    )
```

time: 1280 us -> 818 us (0.64)
  waiting for transfers between devices: 487 us -> 176 us
  matrix products: 83.2 us -> 34.4 us
  Pallas kernels: 271 us -> 232 us
  starting transfers between devices: 268 us -> 233 us
  blocking collectives: 31.2 us -> 0 us
  local copies, waits for them, and re-layouts: 60.9 us -> 73.7 us
    psum x1 -> x0, waiting for transfers between devices: 216 us -> none  [on_device(): wide = lax.psum(wide, ('dp', 'ctx'))]
    all_gather x3 -> x2, waiting for transfers between devices: 195 us -> 0.01 us  [the longest x1 0.01 us: on_device(): lax.all_gather(jnp.where(here == 1, mine_x, came_x), 'dp', tiled=True)]
    ppermute x94 -> x72, waiting for transfers between devices: 33.7 us -> 164 us  [the longest x57 139 us: send(): return lax.ppermute(value, name, pairs)]
    dot_general x40 -> x19, matrix products: 83.2 us -> 34.4 us  [dot(): return jnp.dot(a, b, preferred_element_type=F32)]
    ppermute x94 -> x72, starting transfers between devices: 203 us -> 161 us  [the longest x57 148 us: send(): return lax.ppermute(value, name, pairs)]
    all_to_all x7 -> x8, waiting for transfers between devices: 33.2 us -> 2.16 us  [exchange(): return lax.all_to_all(value, 'ctx', 0, 0, axis_index_groups=PARITY)]
    pallas_call x22 -> x35, Pallas kernels: 225 us -> 205 us  [the longest x5 26 us: fold(): pl.pallas_call(functools.partial(fold_body, slot, [len(group) for group i...]
    all_to_all x1 -> x0, blocking collectives: 18.1 us -> none  [exchange(): return lax.all_to_all(value, 'ctx', 0, 0, axis_index_groups=PARITY)]
  transfers between devices with their start and end apart: 109 -> 89, of which waited for: 16 -> 33; matrix products, arithmetic and copies ran while one was open for 13% -> 13% of each run, Pallas kernels for 16% -> 25%
where the time goes in v2:
time: 818 us; the launch traced here: 806 us
  starting transfers between devices  233 us (28%)
  Pallas kernels  232 us (28%)
  waiting for transfers between devices  176 us (22%)
  local copies, waits for them, and re-layouts  73.7 us (9%)
  matrix products  34.4 us (4%)
  other arithmetic  30.2 us (4%)
  between operations  27.3 us (3%)
    ppermute x57, starting transfers between devices, send(): return lax.ppermute(value, name, pairs)  148 us
    ppermute x57, waiting for transfers between devices, send(): return lax.ppermute(value, name, pairs)  139 us
    all_to_all x8, starting transfers between devices, exchange(): return lax.all_to_all(value, 'ctx', 0, 0, axis_index_groups=PARITY)  57.3 us
    dot_general x19, matrix products, dot(): return jnp.dot(a, b, preferred_element_type=F32)  34.4 us
    pallas_call x5, Pallas kernels, fold(): pl.pallas_call(functools.partial(fold_body, slot, [len(group) for group i...  26 us
    pallas_call x2, Pallas kernels, finish_call(): pl.pallas_call(finish_body, grid=(GROUPS,), out_shape=(shape((ROWS, LOCAL...  25.4 us
    pallas_call x2, Pallas kernels, gate_back(): pl.pallas_call(functools.partial(gate_back_body, weight), out_shape=(shap...  20.6 us
    unnamed x209, local copies, waits for them, and re-layouts  20.4 us
  transfers between devices with their start and end apart: 89, of which 33 were waited for; matrix products, arithmetic and copies ran while one was open for 13% of the time, Pallas kernels for 25%

profile of v2, /device:TPU:12, one launch (start us, length us, event | category | flops | bytes accessed | tf_op | source)
XLA Modules:
  0.0 806.4 jit_solution(2476585183504702828)
XLA Ops:
  17.8 6.1 collective-permute-done.6.rest_1_
  30.6 15.0 %collective-permute-done.7 = bf16[96,1920]{1,0:T(8,128)(2,1)S(1)} collective-permute-done((bf16[96,1920]{1,0:T(8,128)(2,1)S(1)}, bf16[96,1920]{1,0:T(8,128)(2,1)S(1)}, u32[]{:S(2)}, u32[]{:S(2)}) %collective-permute-start.7) | collective-permute-done | bytes 368672 | tf_op jit(solution)/shard_map/ppermute | solution.py:1001
  59.8 24.0 %collective-permute-done.18 = bf16[96,3072]{1,0:T(8,128)(2,1)S(1)} collective-permute-done((bf16[96,3072]{1,0:T(8,128)(2,1)S(1)}, bf16[96,3072]{1,0:T(8,128)(2,1)S(1)}, u32[]{:S(2)}, u32[]{:S(2)}) %collective-permute-start.18) | collective-permute-done | bytes 589856 | tf_op jit(solution)/shard_map/ppermute | solution.py:1001
  124.0 6.5 collective-permute-done.10.rest_3_
  132.6 10.4 %collective-permute-start.21 = (bf16[144,3072]{1,0:T(8,128)(2,1)S(1)}, bf16[144,3072]{1,0:T(8,128)(2,1)S(1)}, u32[]{:S(2)}, u32[]{:S(2)}) collective-permute-start(bf16[144,3072]{1,0:T(8,128)(2,1)S(1)} %pad_maximum_fusion.rest_2_), channel_id=1, source_target_pairs={{0,3},{1,0},{2,1},{3,2},{4,7},{5,4},{6,5},{7,6},{8,11},{9,8},{10,9... | collective-permute-start | bytes 2654216 | tf_op jit(solution)/shard_map/ppermute | solution.py:1001
  149.3 6.9 in_proj.2
  157.1 6.1 collective-permute-start.16
  163.4 8.3 %collective-permute-start.23 = (bf16[144,3072]{1,0:T(8,128)(2,1)S(1)}, bf16[144,3072]{1,0:T(8,128)(2,1)}, u32[]{:S(2)}, u32[]{:S(2)}) collective-permute-start(bf16[144,3072]{1,0:T(8,128)(2,1)S(1)} %pad_maximum_fusion.rest_2_), channel_id=1, source_target_pairs={{0,1},{1,2},{2,3},{3,0},{4,5},{5,6},{6,7},{7,4},{8,9},{9,10},{10,1... | collective-permute-start | bytes 2654216 | tf_op jit(solution)/shard_map/ppermute | solution.py:1001
  187.6 5.7 conv_state.2
  193.4 6.6 all-to-all-start
  204.7 11.0 %collective-permute-done.25.rest_8_ = bf16[144,3072]{1,0:T(8,128)(2,1)} collective-permute-done((bf16[144,3072]{1,0:T(8,128)(2,1)S(1)}, bf16[144,3072]{1,0:T(8,128)(2,1)}, u32[]{:S(2)}, u32[]{:S(2)}) %collective-permute-start.25) | collective-permute-done | bytes 884768 | tf_op jit(solution)/shard_map/ppermute | solution.py:1001
  215.9 6.4 gate_proj.2.token.gate
  225.0 7.5 all-to-all-start.1
  234.1 5.8 inside.2.y_in
  240.6 7.5 out_proj.2
  258.5 6.9 in_proj.3
  274.4 5.7 conv_state.3
  280.2 7.2 all-to-all-start.2
  287.4 6.3 gate_proj.3.token.gate
  296.9 6.9 all-to-all-start.3
  304.5 5.8 inside.3.y_in
  311.1 7.6 out_proj.3
  328.7 10.2 %gate_back.2 = (bf16[256,1536]{1,0:T(8,128)(2,1)}, bf16[256,1536]{1,0:T(8,128)(2,1)}, bf16[256,1536]{1,0:T(8,128)(2,1)}, bf16[256,1536]{1,0:T(8,128)(2,1)}, f32[8,1536]{1,0:T(8,128)}) custom-call(s32[14]{0:T(128)} %concatenate.136.info, bf16[256,1536]{1,0:T(8,128)(2,1)} %get-tuple-element.338.cot, f32[256,1536]{1,0:T(8,128)} %get-tuple-element.219.y, ...), custom_call_target="tpu_custom_call" | custom-call | flops 1207959552 | bytes 13000000 | tf_op jit(solution)/shard_map/gate_back/pallas_call | solution.py:542
  353.8 7.2 all-to-all-start.4
  361.0 6.3 gate_in_back.2.token.part
  371.7 6.9 all-to-all-start.5
  378.8 8.7 %inside_back.2 = (f32[256,1536]{1,0:T(8,128)}, f32[8,1536]{1,0:T(8,128)}, f32[32,256]{1,0:T(8,128)}, f32[256,128]{1,0:T(8,128)}, f32[256,256]{1,0:T(8,128)}) custom-call(bf16[256,1536]{1,0:T(8,128)(2,1)} %get-tuple-element.223.dy, f32[256,1536]{1,0:T(8,128)} %get-tuple-element.212.xa, f32[256,256]{1,0:T(8,128)} %get-tuple-element.213.bca, ...), custom_call_target="tpu_custom_call" | custom-call | flops 402653184 | bytes 4500000 | tf_op jit(solution)/shard_map/inside_back/pallas_call | solution.py:670
  388.3 12.7 %finish_back.2 = (bf16[256,1536]{1,0:T(8,128)(2,1)}, bf16[256,384]{1,0:T(8,128)(2,1)}, f32[16,1536]{1,0:T(8,128)}, f32[16,256]{1,0:T(8,128)}, bf16[16,1536]{1,0:...) custom-call(s32[14]{0:T(128)} %concatenate.136.info, ...), custom_call_target="tpu_custom_call" | custom-call | flops 503316480 | bytes 7500000 | tf_op jit(solution)/shard_map/finish_back/pallas_call | solution.py:822
  404.3 6.0 collective-permute-done.30.edge
  418.9 7.6 mixed_back.2.own
  436.7 10.4 %gate_back.3 = (bf16[256,1536]{1,0:T(8,128)(2,1)}, bf16[256,1536]{1,0:T(8,128)(2,1)}, bf16[256,1536]{1,0:T(8,128)(2,1)}, bf16[256,1536]{1,0:T(8,128)(2,1)}, f32[8,1536]{1,0:T(8,128)}) custom-call(s32[14]{0:T(128)} %concatenate.136.info, bf16[256,1536]{1,0:T(8,128)(2,1)} %get-tuple-element.238.cot, f32[256,1536]{1,0:T(8,128)} %get-tuple-element.239.y, ...), custom_call_target="tpu_custom_call" | custom-call | flops 1207959552 | bytes 13000000 | tf_op jit(solution)/shard_map/gate_back/pallas_call | solution.py:542
  452.0 7.2 all-to-all-start.6
  461.9 6.3 gate_in_back.3.token.part
  470.9 7.7 all-to-all-start.7
  478.7 8.7 %inside_back.3 = (f32[256,1536]{1,0:T(8,128)}, f32[8,1536]{1,0:T(8,128)}, f32[32,256]{1,0:T(8,128)}, f32[256,128]{1,0:T(8,128)}, f32[256,256]{1,0:T(8,128)}) custom-call(bf16[256,1536]{1,0:T(8,128)(2,1)} %get-tuple-element.242.dy, f32[256,1536]{1,0:T(8,128)} %get-tuple-element.199.xa, f32[256,256]{1,0:T(8,128)} %get-tuple-element.200.bca, ...), custom_call_target="tpu_custom_call" | custom-call | flops 402653184 | bytes 4500000 | tf_op jit(solution)/shard_map/inside_back/pallas_call | solution.py:670
  494.0 12.7 %finish_back.3 = (bf16[256,1536]{1,0:T(8,128)(2,1)}, bf16[256,384]{1,0:T(8,128)(2,1)}, f32[16,1536]{1,0:T(8,128)}, f32[16,256]{1,0:T(8,128)}, bf16[16,1536]{1,0:...) custom-call(s32[14]{0:T(128)} %concatenate.136.info, ...), custom_call_target="tpu_custom_call" | custom-call | flops 503316480 | bytes 7500000 | tf_op jit(solution)/shard_map/finish_back/pallas_call | solution.py:822
  531.6 7.5 mixed_back.3.own
  557.2 22.8 %collective-permute-start.50 = (bf16[384,960]{0,1:T(8,128)(2,1)}, bf16[384,960]{0,1:T(8,128)(2,1)}, u32[]{:S(2)}, u32[]{:S(2)}) collective-permute-start(bf16[384,960]{0,1:T(8,128)(2,1)} %convolution_convert_fusion.16), channel_id=1, source_target_pairs={{0,8},{1,9},{2,10},{3,11},{4,12},{5,13},{6,14},{7,15},{8,0},{9,1},... | collective-permute-start | bytes 2211848 | tf_op jit(solution)/shard_map/ppermute | solution.py:1001
  586.1 8.7 %collective-permute-done.49 = bf16[384,960]{0,1:T(8,128)(2,1)S(1)} collective-permute-done((bf16[384,960]{0,1:T(8,128)(2,1)}, bf16[384,960]{0,1:T(8,128)(2,1)S(1)}, u32[]{:S(2)}, u32[]{:S(2)}) %collective-permute-start.49) | collective-permute-done | bytes 737312 | tf_op jit(solution)/shard_map/ppermute | solution.py:1001
  594.7 16.2 %collective-permute-start.51 = (bf16[384,960]{0,1:T(8,128)(2,1)}, bf16[384,960]{0,1:T(8,128)(2,1)S(1)}, u32[]{:S(2)}, u32[]{:S(2)}) collective-permute-start(bf16[384,960]{0,1:T(8,128)(2,1)} %convolution_convert_fusion.15), channel_id=1, source_target_pairs={{0,12},{1,13},{2,14},{3,15},{4,0},{5,1},{6,2},{7,3},{8,4},{9,5},{1... | collective-permute-start | bytes 2211848 | tf_op jit(solution)/shard_map/ppermute | solution.py:1001
  617.9 10.3 %collective-permute-done.51 = bf16[384,960]{0,1:T(8,128)(2,1)S(1)} collective-permute-done((bf16[384,960]{0,1:T(8,128)(2,1)}, bf16[384,960]{0,1:T(8,128)(2,1)S(1)}, u32[]{:S(2)}, u32[]{:S(2)}) %collective-permute-start.51) | collective-permute-done | bytes 737312 | tf_op jit(solution)/shard_map/ppermute | solution.py:1001
  628.2 11.6 %collective-permute-start.68 = (bf16[96,4992]{1,0:T(8,128)(2,1)}, bf16[96,4992]{1,0:T(8,128)(2,1)}, u32[]{:S(2)}, u32[]{:S(2)}) collective-permute-start(bf16[96,4992]{1,0:T(8,128)(2,1)} %get-tuple-element.288), channel_id=1, source_target_pairs={{0,8},{1,9},{2,10},{3,11},{4,12},{5,13},{6,14},{7,15},{8,0},{9,1},... | collective-permute-start | bytes 2875400 | tf_op jit(solution)/shard_map/ppermute | solution.py:1001
  646.3 14.6 %collective-permute-done.40 = bf16[32,1792]{1,0:T(8,128)(2,1)S(1)} collective-permute-done((bf16[32,1792]{1,0:T(8,128)(2,1)S(1)}, bf16[32,1792]{1,0:T(8,128)(2,1)S(1)}, u32[]{:S(2)}, u32[]{:S(2)}) %collective-permute-start.40) | collective-permute-done | bytes 114720 | tf_op jit(solution)/shard_map/ppermute | solution.py:1001
  687.8 6.8 fold.6
  695.3 11.8 %collective-permute-done.57.rest_3_ = bf16[384,1536]{1,0:T(8,128)(2,1)} collective-permute-done((bf16[384,1536]{1,0:T(8,128)(2,1)}, bf16[384,1536]{1,0:T(8,128)(2,1)}, u32[]{:S(2)}, u32[]{:S(2)}) %collective-permute-start.57) | collective-permute-done | bytes 1179680 | tf_op jit(solution)/shard_map/ppermute | solution.py:1001
  711.3 6.7 fold.7
  744.0 9.9 %collective-permute-done.63.rest_7_ = bf16[96,2496]{1,0:T(8,128)(2,1)} collective-permute-done((bf16[96,2496]{1,0:T(8,128)(2,1)}, bf16[96,2496]{1,0:T(8,128)(2,1)}, u32[]{:S(2)}, u32[]{:S(2)}) %collective-permute-start.63) | collective-permute-done | bytes 479264 | tf_op jit(solution)/shard_map/ppermute | solution.py:1001
  787.2 7.7 collective-permute-done.75
  (584 shorter events, 345.2 us)
Async XLA Ops:
  7.2 251.3 %all-gather.3.cloned.1.call-start = ((), (), s32[]{:S(2)}) async-start(), calls=%async_computation.11 | async-start | bytes 7372800 | tf_op jit(solution)/shard_map/all_gather | solution.py:1200
  17.2 36.1 %collective-permute-start.17 = (bf16[384,3072]{1,0:T(8,128)(2,1)}, bf16[384,3072]{1,0:T(8,128)(2,1)S(1)}, u32[]{:S(2)}, u32[]{:S(2)}) collective-permute-start(bf16[384,3072]{1,0:T(8,128)(2,1)} %get-tuple-element.206), channel_id=1, source_target_pairs={{0,64},{64,0},{1,65},{65,1},{2,66},{66,2},{3,67},{67,3},{4,68},{68... | collective-permute-start | bytes 7077896 | tf_op jit(solution)/shard_map/ppermute | solution.py:1005
  29.3 21.4 %collective-permute-start.9 = (bf16[96,1920]{1,0:T(8,128)(2,1)S(1)}, bf16[96,1920]{1,0:T(8,128)(2,1)S(1)}, u32[]{:S(2)}, u32[]{:S(2)}) collective-permute-start(bf16[96,1920]{1,0:T(8,128)(2,1)S(1)} %pad_maximum_fusion.5), channel_id=1, source_target_pairs={{0,16},{16,32},{32,48},{48,0},{1,17},{17,33},{33,49},{49,1},{2,18}... | collective-permute-start | bytes 1105928 | tf_op jit(solution)/shard_map/ppermute | solution.py:1001
  55.1 28.7 %collective-permute-start.18 = (bf16[96,3072]{1,0:T(8,128)(2,1)S(1)}, bf16[96,3072]{1,0:T(8,128)(2,1)S(1)}, u32[]{:S(2)}, u32[]{:S(2)}) collective-permute-start(bf16[96,3072]{1,0:T(8,128)(2,1)S(1)} %pad_maximum_fusion.2), channel_id=1, source_target_pairs={{0,48},{16,0},{32,16},{48,32},{1,49},{17,1},{33,17},{49,33},{2,50}... | collective-permute-start | bytes 1769480 | tf_op jit(solution)/shard_map/ppermute | solution.py:1001
  58.8 26.8 %collective-permute-start.19 = (bf16[96,3072]{1,0:T(8,128)(2,1)S(1)}, bf16[96,3072]{1,0:T(8,128)(2,1)S(1)}, u32[]{:S(2)}, u32[]{:S(2)}) collective-permute-start(bf16[96,3072]{1,0:T(8,128)(2,1)S(1)} %pad_maximum_fusion.2), channel_id=1, source_target_pairs={{0,32},{16,48},{32,0},{48,16},{1,33},{17,49},{33,1},{49,17},{2,34}... | collective-permute-start | bytes 1769480 | tf_op jit(solution)/shard_map/ppermute | solution.py:1001
  58.9 28.6 %collective-permute-start.20 = (bf16[96,3072]{1,0:T(8,128)(2,1)S(1)}, bf16[96,3072]{1,0:T(8,128)(2,1)S(1)}, u32[]{:S(2)}, u32[]{:S(2)}) collective-permute-start(bf16[96,3072]{1,0:T(8,128)(2,1)S(1)} %pad_maximum_fusion.2), channel_id=1, source_target_pairs={{0,16},{16,32},{32,48},{48,0},{1,17},{17,33},{33,49},{49,1},{2,18}... | collective-permute-start | bytes 1769480 | tf_op jit(solution)/shard_map/ppermute | solution.py:1001
  93.0 194.4 %all-gather.5.cloned.1.call-start = ((), (), s32[]{:S(2)}) async-start(), calls=%async_computation.12 | async-start | bytes 11796480 | tf_op jit(solution)/shard_map/all_gather | solution.py:1201
  118.4 26.0 %collective-permute-start.12 = (bf16[144,1920]{1,0:T(8,128)(2,1)S(1)}, bf16[144,1920]{1,0:T(8,128)(2,1)S(1)}, u32[]{:S(2)}, u32[]{:S(2)}) collective-permute-start(bf16[144,1920]{1,0:T(8,128)(2,1)S(1)} %pad_maximum_fusion.3.rest_2_), channel_id=1, source_target_pairs={{0,1},{1,2},{2,3},{3,0},{4,5},{5,6},{6,7},{7,4},{8,9},{9,10},{10,1... | collective-permute-start | bytes 1658888 | tf_op jit(solution)/shard_map/ppermute | solution.py:1001
  118.4 25.9 %collective-permute-start.13 = (bf16[144,1920]{1,0:T(8,128)(2,1)S(1)}, bf16[144,1920]{1,0:T(8,128)(2,1)S(1)}, u32[]{:S(2)}, u32[]{:S(2)}) collective-permute-start(bf16[144,1920]{1,0:T(8,128)(2,1)S(1)} %pad_maximum_fusion.4.rest_6_), channel_id=1, source_target_pairs={{0,12},{1,13},{2,14},{3,15},{4,0},{5,1},{6,2},{7,3},{8,4},{9,5},{1... | collective-permute-start | bytes 1658888 | tf_op jit(solution)/shard_map/ppermute | solution.py:1001
  121.3 24.0 %collective-permute-start.14 = (bf16[144,1920]{1,0:T(8,128)(2,1)S(1)}, bf16[144,1920]{1,0:T(8,128)(2,1)S(1)}, u32[]{:S(2)}, u32[]{:S(2)}) collective-permute-start(bf16[144,1920]{1,0:T(8,128)(2,1)S(1)} %pad_maximum_fusion.4.rest_6_), channel_id=1, source_target_pairs={{0,8},{1,9},{2,10},{3,11},{4,12},{5,13},{6,14},{7,15},{8,0},{9,1},... | collective-permute-start | bytes 1658888 | tf_op jit(solution)/shard_map/ppermute | solution.py:1001
  132.6 42.3 %collective-permute-start.21 = (bf16[144,3072]{1,0:T(8,128)(2,1)S(1)}, bf16[144,3072]{1,0:T(8,128)(2,1)S(1)}, u32[]{:S(2)}, u32[]{:S(2)}) collective-permute-start(bf16[144,3072]{1,0:T(8,128)(2,1)S(1)} %pad_maximum_fusion.rest_2_), channel_id=1, source_target_pairs={{0,3},{1,0},{2,1},{3,2},{4,7},{5,4},{6,5},{7,6},{8,11},{9,8},{10,9... | collective-permute-start | bytes 2654216 | tf_op jit(solution)/shard_map/ppermute | solution.py:1001
  163.3 36.7 %collective-permute-start.22 = (bf16[144,3072]{1,0:T(8,128)(2,1)S(1)}, bf16[144,3072]{1,0:T(8,128)(2,1)S(1)}, u32[]{:S(2)}, u32[]{:S(2)}) collective-permute-start(bf16[144,3072]{1,0:T(8,128)(2,1)S(1)} %pad_maximum_fusion.rest_2_), channel_id=1, source_target_pairs={{0,2},{1,3},{2,0},{3,1},{4,6},{5,7},{6,4},{7,5},{8,10},{9,11},{10,... | collective-permute-start | bytes 2654216 | tf_op jit(solution)/shard_map/ppermute | solution.py:1001
  163.4 41.3 %collective-permute-start.23 = (bf16[144,3072]{1,0:T(8,128)(2,1)S(1)}, bf16[144,3072]{1,0:T(8,128)(2,1)}, u32[]{:S(2)}, u32[]{:S(2)}) collective-permute-start(bf16[144,3072]{1,0:T(8,128)(2,1)S(1)} %pad_maximum_fusion.rest_2_), channel_id=1, source_target_pairs={{0,1},{1,2},{2,3},{3,0},{4,5},{5,6},{6,7},{7,4},{8,9},{9,10},{10,1... | collective-permute-start | bytes 2654216 | tf_op jit(solution)/shard_map/ppermute | solution.py:1001
  171.8 32.9 %collective-permute-start.24 = (bf16[144,3072]{1,0:T(8,128)(2,1)S(1)}, bf16[144,3072]{1,0:T(8,128)(2,1)}, u32[]{:S(2)}, u32[]{:S(2)}) collective-permute-start(bf16[144,3072]{1,0:T(8,128)(2,1)S(1)} %pad_maximum_fusion.1.rest_6_), channel_id=1, source_target_pairs={{0,12},{1,13},{2,14},{3,15},{4,0},{5,1},{6,2},{7,3},{8,4},{9,5},{1... | collective-permute-start | bytes 2654216 | tf_op jit(solution)/shard_map/ppermute | solution.py:1001
  173.6 42.1 %collective-permute-start.25 = (bf16[144,3072]{1,0:T(8,128)(2,1)S(1)}, bf16[144,3072]{1,0:T(8,128)(2,1)}, u32[]{:S(2)}, u32[]{:S(2)}) collective-permute-start(bf16[144,3072]{1,0:T(8,128)(2,1)S(1)} %pad_maximum_fusion.1.rest_6_), channel_id=1, source_target_pairs={{0,8},{1,9},{2,10},{3,11},{4,12},{5,13},{6,14},{7,15},{8,0},{9,1},... | collective-permute-start | bytes 2654216 | tf_op jit(solution)/shard_map/ppermute | solution.py:1001
  174.9 41.0 %collective-permute-start.26 = (bf16[144,3072]{1,0:T(8,128)(2,1)S(1)}, bf16[144,3072]{1,0:T(8,128)(2,1)}, u32[]{:S(2)}, u32[]{:S(2)}) collective-permute-start(bf16[144,3072]{1,0:T(8,128)(2,1)S(1)} %pad_maximum_fusion.1.rest_6_), channel_id=1, source_target_pairs={{0,4},{1,5},{2,6},{3,7},{4,8},{5,9},{6,10},{7,11},{8,12},{9,13},{1... | collective-permute-start | bytes 2654216 | tf_op jit(solution)/shard_map/ppermute | solution.py:1001
  193.4 28.9 %all-to-all-start = ((bf16[8,80,384]{2,1,0:T(8,128)(2,1)}), bf16[8,80,384]{2,1,0:T(8,128)(2,1)S(1)}, u32[]{:S(2)}, u32[]{:S(2)}) async-start(bf16[8,80,384]{2,1,0:T(8,128)(2,1)} %get-tuple-element.203.msg_in), calls=%async_computation | async-start | bytes 983040 | tf_op jit(solution)/shard_map/all_to_all | solution.py:1089
  303.9 220.8 %reduce-scatter.4.cloned.1.call-start = ((), (), s32[]{:S(2)}) async-start(), calls=%async_computation.13 | async-start | bytes 5898240 | tf_op jit(solution)/shard_map/reduce_scatter | solution.py:1282
  343.9 180.9 %reduce-scatter.6.cloned.1.call-start = ((), (), s32[]{:S(2)}) async-start(), calls=%async_computation.14 | async-start | bytes 5898240 | tf_op jit(solution)/shard_map/reduce_scatter | solution.py:1282
  378.6 146.1 %reduce-scatter.8.cloned.1.call-start = ((), (), s32[]{:S(2)}) async-start(), calls=%async_computation.15 | async-start | bytes 7372800 | tf_op jit(solution)/shard_map/reduce_scatter | solution.py:1282
  470.9 21.0 %all-to-all-start.7 = ((bf16[8,64,384]{2,1,0:T(8,128)(2,1)}), bf16[8,64,384]{2,1,0:T(8,128)(2,1)S(1)}, u32[]{:S(2)}, u32[]{:S(2)}) async-start(bf16[8,64,384]{2,1,0:T(8,128)(2,1)} %chunk_scan.7), calls=%async_computation.7 | async-start | bytes 786432 | tf_op jit(solution)/shard_map/all_to_all | solution.py:1089
  508.1 21.2 %collective-permute-start.32 = (bf16[16,1792]{1,0:T(8,128)(2,1)}, bf16[16,1792]{1,0:T(8,128)(2,1)}, u32[]{:S(2)}, u32[]{:S(2)}) collective-permute-start(bf16[16,1792]{1,0:T(8,128)(2,1)} %pad_maximum_fusion.13), channel_id=1, source_target_pairs={{2,0},{3,1},{4,2},{5,3},{6,4},{7,5},{8,6},{9,7},{10,8},{11,9},{12,... | collective-permute-start | bytes 172040 | tf_op jit(solution)/shard_map/ppermute | solution.py:1094
  514.4 67.3 %collective-permute-start.48 = (bf16[384,1536]{1,0:T(8,128)(2,1)}, bf16[384,1536]{1,0:T(8,128)(2,1)}, u32[]{:S(2)}, u32[]{:S(2)}) collective-permute-start(bf16[384,1536]{1,0:T(8,128)(2,1)} %convolution_convert_fusion.7), channel_id=1, source_target_pairs={{0,12},{1,13},{2,14},{3,15},{4,0},{5,1},{6,2},{7,3},{8,4},{9,5},{1... | collective-permute-start | bytes 3538952 | tf_op jit(solution)/shard_map/ppermute | solution.py:1001
  515.9 67.3 %collective-permute-start.55 = (bf16[384,1536]{1,0:T(8,128)(2,1)}, bf16[384,1536]{1,0:T(8,128)(2,1)}, u32[]{:S(2)}, u32[]{:S(2)}) collective-permute-start(bf16[384,1536]{1,0:T(8,128)(2,1)} %convolution_convert_fusion.5), channel_id=1, source_target_pairs={{0,1},{1,2},{2,3},{3,0},{4,5},{5,6},{6,7},{7,4},{8,9},{9,10},{10,1... | collective-permute-start | bytes 3538952 | tf_op jit(solution)/shard_map/ppermute | solution.py:1001
  522.5 34.7 %collective-permute-start.46 = (bf16[384,1536]{1,0:T(8,128)(2,1)}, bf16[384,1536]{1,0:T(8,128)(2,1)}, u32[]{:S(2)}, u32[]{:S(2)}) collective-permute-start(bf16[384,1536]{1,0:T(8,128)(2,1)} %convolution_convert_fusion.9), channel_id=1, source_target_pairs={{0,4},{1,5},{2,6},{3,7},{4,8},{5,9},{6,10},{7,11},{8,12},{9,13},{1... | collective-permute-start | bytes 3538952 | tf_op jit(solution)/shard_map/ppermute | solution.py:1001
  539.8 40.2 %collective-permute-start.47 = (bf16[384,1536]{1,0:T(8,128)(2,1)S(1)}, bf16[384,1536]{1,0:T(8,128)(2,1)S(1)}, u32[]{:S(2)}, u32[]{:S(2)}) collective-permute-start(bf16[384,1536]{1,0:T(8,128)(2,1)S(1)} %convolution_convert_fusion.8), channel_id=1, source_target_pairs={{0,8},{1,9},{2,10},{3,11},{4,12},{5,13},{6,14},{7,15},{8,0},{9,1},... | collective-permute-start | bytes 3538952 | tf_op jit(solution)/shard_map/ppermute | solution.py:1001
  549.6 45.1 %collective-permute-start.49 = (bf16[384,960]{0,1:T(8,128)(2,1)}, bf16[384,960]{0,1:T(8,128)(2,1)S(1)}, u32[]{:S(2)}, u32[]{:S(2)}) collective-permute-start(bf16[384,960]{0,1:T(8,128)(2,1)} %convolution_convert_fusion.17), channel_id=1, source_target_pairs={{0,4},{1,5},{2,6},{3,7},{4,8},{5,9},{6,10},{7,11},{8,12},{9,13},{1... | collective-permute-start | bytes 2211848 | tf_op jit(solution)/shard_map/ppermute | solution.py:1001
  557.2 59.1 %collective-permute-start.50 = (bf16[384,960]{0,1:T(8,128)(2,1)}, bf16[384,960]{0,1:T(8,128)(2,1)}, u32[]{:S(2)}, u32[]{:S(2)}) collective-permute-start(bf16[384,960]{0,1:T(8,128)(2,1)} %convolution_convert_fusion.16), channel_id=1, source_target_pairs={{0,8},{1,9},{2,10},{3,11},{4,12},{5,13},{6,14},{7,15},{8,0},{9,1},... | collective-permute-start | bytes 2211848 | tf_op jit(solution)/shard_map/ppermute | solution.py:1001
  580.0 30.9 %collective-permute-start.38 = (bf16[32,1792]{1,0:T(8,128)(2,1)S(1)}, bf16[32,1792]{1,0:T(8,128)(2,1)S(1)}, u32[]{:S(2)}, u32[]{:S(2)}) collective-permute-start(bf16[32,1792]{1,0:T(8,128)(2,1)S(1)} %fusion.14), channel_id=1, source_target_pairs={{0,3},{1,0},{2,1},{3,2},{4,7},{5,4},{6,5},{7,6},{8,11},{9,8},{10,9... | collective-permute-start | bytes 344072 | tf_op jit(solution)/shard_map/ppermute | solution.py:1001
  581.6 32.6 %collective-permute-start.37 = (bf16[32,1792]{1,0:T(8,128)(2,1)S(1)}, bf16[32,1792]{1,0:T(8,128)(2,1)S(1)}, u32[]{:S(2)}, u32[]{:S(2)}) collective-permute-start(bf16[32,1792]{1,0:T(8,128)(2,1)S(1)} %fusion.14), channel_id=1, source_target_pairs={{0,1},{1,2},{2,3},{3,0},{4,5},{5,6},{6,7},{7,4},{8,9},{9,10},{10,1... | collective-permute-start | bytes 344072 | tf_op jit(solution)/shard_map/ppermute | solution.py:1001
  583.2 31.0 %collective-permute-start.36 = (bf16[32,1792]{1,0:T(8,128)(2,1)S(1)}, bf16[32,1792]{1,0:T(8,128)(2,1)S(1)}, u32[]{:S(2)}, u32[]{:S(2)}) collective-permute-start(bf16[32,1792]{1,0:T(8,128)(2,1)S(1)} %fusion.14), channel_id=1, source_target_pairs={{0,2},{1,3},{2,0},{3,1},{4,6},{5,7},{6,4},{7,5},{8,10},{9,11},{10,... | collective-permute-start | bytes 344072 | tf_op jit(solution)/shard_map/ppermute | solution.py:1001
  594.7 33.5 %collective-permute-start.51 = (bf16[384,960]{0,1:T(8,128)(2,1)}, bf16[384,960]{0,1:T(8,128)(2,1)S(1)}, u32[]{:S(2)}, u32[]{:S(2)}) collective-permute-start(bf16[384,960]{0,1:T(8,128)(2,1)} %convolution_convert_fusion.15), channel_id=1, source_target_pairs={{0,12},{1,13},{2,14},{3,15},{4,0},{5,1},{6,2},{7,3},{8,4},{9,5},{1... | collective-permute-start | bytes 2211848 | tf_op jit(solution)/shard_map/ppermute | solution.py:1001
  614.2 25.6 %collective-permute-start.59 = (bf16[384,960]{0,1:T(8,128)(2,1)S(1)}, bf16[384,960]{0,1:T(8,128)(2,1)S(1)}, u32[]{:S(2)}, u32[]{:S(2)}) collective-permute-start(bf16[384,960]{0,1:T(8,128)(2,1)S(1)} %copy-done.53), channel_id=1, source_target_pairs={{0,2},{1,3},{2,0},{3,1},{4,6},{5,7},{6,4},{7,5},{8,10},{9,11},{10,... | collective-permute-start | bytes 2211848 | tf_op jit(solution)/shard_map/ppermute | solution.py:1001
  614.3 28.1 %collective-permute-start.60 = (bf16[384,960]{0,1:T(8,128)(2,1)S(1)}, bf16[384,960]{0,1:T(8,128)(2,1)S(1)}, u32[]{:S(2)}, u32[]{:S(2)}) collective-permute-start(bf16[384,960]{0,1:T(8,128)(2,1)S(1)} %convolution_convert_fusion.11), channel_id=1, source_target_pairs={{0,3},{1,0},{2,1},{3,2},{4,7},{5,4},{6,5},{7,6},{8,11},{9,8},{10,9... | collective-permute-start | bytes 2211848 | tf_op jit(solution)/shard_map/ppermute | solution.py:1001
  616.3 26.2 %collective-permute-start.41 = (bf16[32,1792]{1,0:T(8,128)(2,1)S(1)}, bf16[32,1792]{1,0:T(8,128)(2,1)S(1)}, u32[]{:S(2)}, u32[]{:S(2)}) collective-permute-start(bf16[32,1792]{1,0:T(8,128)(2,1)S(1)} %add_convert_fusion.1), channel_id=1, source_target_pairs={{0,12},{1,13},{2,14},{3,15},{4,0},{5,1},{6,2},{7,3},{8,4},{9,5},{1... | collective-permute-start | bytes 344072 | tf_op jit(solution)/shard_map/ppermute | solution.py:1001
  628.2 49.8 %collective-permute-start.67 = (bf16[96,4992]{1,0:T(8,128)(2,1)}, bf16[96,4992]{1,0:T(8,128)(2,1)}, u32[]{:S(2)}, u32[]{:S(2)}) collective-permute-start(bf16[96,4992]{1,0:T(8,128)(2,1)} %get-tuple-element.287), channel_id=1, source_target_pairs={{0,4},{1,5},{2,6},{3,7},{4,8},{5,9},{6,10},{7,11},{8,12},{9,13},{1... | collective-permute-start | bytes 2875400 | tf_op jit(solution)/shard_map/ppermute | solution.py:1001
  628.2 50.2 %collective-permute-start.68 = (bf16[96,4992]{1,0:T(8,128)(2,1)}, bf16[96,4992]{1,0:T(8,128)(2,1)}, u32[]{:S(2)}, u32[]{:S(2)}) collective-permute-start(bf16[96,4992]{1,0:T(8,128)(2,1)} %get-tuple-element.288), channel_id=1, source_target_pairs={{0,8},{1,9},{2,10},{3,11},{4,12},{5,13},{6,14},{7,15},{8,0},{9,1},... | collective-permute-start | bytes 2875400 | tf_op jit(solution)/shard_map/ppermute | solution.py:1001
  639.9 40.2 %collective-permute-start.69 = (bf16[96,4992]{1,0:T(8,128)(2,1)}, bf16[96,4992]{1,0:T(8,128)(2,1)}, u32[]{:S(2)}, u32[]{:S(2)}) collective-permute-start(bf16[96,4992]{1,0:T(8,128)(2,1)} %get-tuple-element.289), channel_id=1, source_target_pairs={{0,12},{1,13},{2,14},{3,15},{4,0},{5,1},{6,2},{7,3},{8,4},{9,5},{1... | collective-permute-start | bytes 2875400 | tf_op jit(solution)/shard_map/ppermute | solution.py:1001
  642.4 21.5 %collective-permute-start.39 = (bf16[32,1792]{1,0:T(8,128)(2,1)S(1)}, bf16[32,1792]{1,0:T(8,128)(2,1)S(1)}, u32[]{:S(2)}, u32[]{:S(2)}) collective-permute-start(bf16[32,1792]{1,0:T(8,128)(2,1)S(1)} %add_convert_fusion.1), channel_id=1, source_target_pairs={{0,8},{1,9},{2,10},{3,11},{4,12},{5,13},{6,14},{7,15},{8,0},{9,1},... | collective-permute-start | bytes 344072 | tf_op jit(solution)/shard_map/ppermute | solution.py:1001
  660.9 33.7 %collective-permute-start.56 = (bf16[384,1536]{1,0:T(8,128)(2,1)}, bf16[384,1536]{1,0:T(8,128)(2,1)}, u32[]{:S(2)}, u32[]{:S(2)}) collective-permute-start(bf16[384,1536]{1,0:T(8,128)(2,1)} %convolution_convert_fusion.4), channel_id=1, source_target_pairs={{0,2},{1,3},{2,0},{3,1},{4,6},{5,7},{6,4},{7,5},{8,10},{9,11},{10,... | collective-permute-start | bytes 3538952 | tf_op jit(solution)/shard_map/ppermute | solution.py:1001
  663.9 43.2 %collective-permute-start.57 = (bf16[384,1536]{1,0:T(8,128)(2,1)}, bf16[384,1536]{1,0:T(8,128)(2,1)}, u32[]{:S(2)}, u32[]{:S(2)}) collective-permute-start(bf16[384,1536]{1,0:T(8,128)(2,1)} %convolution_convert_fusion.3), channel_id=1, source_target_pairs={{0,3},{1,0},{2,1},{3,2},{4,7},{5,4},{6,5},{7,6},{8,11},{9,8},{10,9... | collective-permute-start | bytes 3538952 | tf_op jit(solution)/shard_map/ppermute | solution.py:1001
  678.0 40.0 %collective-permute-start.44 = (bf16[32,1792]{1,0:T(8,128)(2,1)S(1)}, bf16[32,1792]{1,0:T(8,128)(2,1)S(1)}, u32[]{:S(2)}, u32[]{:S(2)}) collective-permute-start(bf16[32,1792]{1,0:T(8,128)(2,1)S(1)} %add_convert_fusion), channel_id=1, source_target_pairs={{0,48},{16,0},{32,16},{48,32},{1,49},{17,1},{33,17},{49,33},{2,50}... | collective-permute-start | bytes 344072 | tf_op jit(solution)/shard_map/ppermute | solution.py:1001
  678.4 39.7 %collective-permute-start.43 = (bf16[32,1792]{1,0:T(8,128)(2,1)S(1)}, bf16[32,1792]{1,0:T(8,128)(2,1)S(1)}, u32[]{:S(2)}, u32[]{:S(2)}) collective-permute-start(bf16[32,1792]{1,0:T(8,128)(2,1)S(1)} %add_convert_fusion), channel_id=1, source_target_pairs={{0,16},{16,32},{32,48},{48,0},{1,17},{17,33},{33,49},{49,1},{2,18}... | collective-permute-start | bytes 344072 | tf_op jit(solution)/shard_map/ppermute | solution.py:1001
  680.1 38.4 %collective-permute-start.42 = (bf16[32,1792]{1,0:T(8,128)(2,1)S(1)}, bf16[32,1792]{1,0:T(8,128)(2,1)S(1)}, u32[]{:S(2)}, u32[]{:S(2)}) collective-permute-start(bf16[32,1792]{1,0:T(8,128)(2,1)S(1)} %add_convert_fusion), channel_id=1, source_target_pairs={{0,32},{16,48},{32,0},{48,16},{1,33},{17,49},{33,1},{49,17},{2,34}... | collective-permute-start | bytes 344072 | tf_op jit(solution)/shard_map/ppermute | solution.py:1001
  694.5 27.3 %collective-permute-start.72 = (bf16[24,4992]{1,0:T(8,128)(2,1)S(1)}, bf16[24,4992]{1,0:T(8,128)(2,1)S(1)}, u32[]{:S(2)}, u32[]{:S(2)}) collective-permute-start(bf16[24,4992]{1,0:T(8,128)(2,1)S(1)} %copy-done.99), channel_id=1, source_target_pairs={{0,3},{1,0},{2,1},{3,2},{4,7},{5,4},{6,5},{7,6},{8,11},{9,8},{10,9... | collective-permute-start | bytes 718856 | tf_op jit(solution)/shard_map/ppermute | solution.py:1001
  736.3 43.0 %collective-permute-start.35 = (f32[128,1536]{1,0:T(8,128)}, f32[128,1536]{1,0:T(8,128)}, u32[]{:S(2)}, u32[]{:S(2)}) collective-permute-start(f32[128,1536]{1,0:T(8,128)} %get-tuple-element.335), channel_id=1, source_target_pairs={{64,65},{65,64},{66,67},{67,66},{68,69},{69,68},{70,71},{71,70},{7... | collective-permute-start | bytes 2359304 | tf_op jit(solution)/shard_map/ppermute | solution.py:1372
  737.9 41.4 %collective-permute-start.34 = (f32[128,1536]{1,0:T(8,128)}, f32[128,1536]{1,0:T(8,128)}, u32[]{:S(2)}, u32[]{:S(2)}) collective-permute-start(f32[128,1536]{1,0:T(8,128)} %get-tuple-element.337), channel_id=1, source_target_pairs={{0,1},{1,0},{2,3},{3,2},{4,5},{5,4},{6,7},{7,6},{8,9},{9,8},{10,11... | collective-permute-start | bytes 2359304 | tf_op jit(solution)/shard_map/ppermute | solution.py:1372
  774.3 21.3 %collective-permute-start.73 = (f32[24,3456]{1,0:T(8,128)S(1)}, f32[24,3456]{1,0:T(8,128)S(1)}, u32[]{:S(2)}, u32[]{:S(2)}) collective-permute-start(f32[24,3456]{1,0:T(8,128)S(1)} %slice_select_fusion.2), channel_id=1, source_target_pairs={{0,64},{64,0},{1,65},{65,1},{2,66},{66,2},{3,67},{67,3},{4,68},{68... | collective-permute-start | bytes 995336 | tf_op jit(solution)/shard_map/ppermute | solution.py:1005
  (143 other events, 1590.2 us)
Sparse Core Ops, SparseCore 0:
  93.1 64.5 all-gather.2
  159.4 92.4 all-gather.4
  344.0 50.8 reduce-scatter.3
  397.1 50.8 reduce-scatter.5
  450.3 60.5 reduce-scatter.7

commit v3 on v2

--- a/solution.py
+++ b/solution.py
@@ -27,9 +27,11 @@
 ROWS = 256
 HALF = 128
 SHARD = 384
+TALL = SHARD + 16
 PIECE = 48
 STATE_HALF = STATE // 2
 MESSAGE = STATE_HALF + 16
+SMALL = 64
 EPSILON = 1e-05
 PRECISE = lax.Precision.HIGHEST
 F32 = jnp.float32
@@ -124,6 +126,7 @@
 class Weight:
     def __init__(self, arrays, layer, width, first=0):
         self.arrays = arrays
+        self.stride = arrays[0].shape[0] // 4
         self.layer = layer
         self.width = width
         self.columns = pl.ds(first, width)
@@ -134,7 +137,8 @@
     def parts(self, refs, info, b):
         start = self.block(info, b)
         if len(refs) == 1:
-            return [(refs[0].at[pl.ds(pl.multiple_of(start, SHARD), SHARD)], start, SHARD)]
+            there = pl.multiple_of(start // SHARD * self.stride, 16)
+            return [(refs[0].at[pl.ds(there, SHARD)], start, SHARD)]
         out = []
         for side in range(2):
             mine = info[12 - side]
@@ -156,7 +160,8 @@
 
     def own_copy(self, source, info, buffer, sems):
         rows = pl.ds(pl.multiple_of(self.block(info, 0), SHARD), SHARD)
-        return pltpu.make_async_copy(source.at[:, self.columns], buffer.at[rows], sems.at[0, 0])
+        source = source.at[pl.ds(0, SHARD), self.columns]
+        return pltpu.make_async_copy(source, buffer.at[rows], sems.at[0, 0])
 
     def start(self, refs, info, buffer, sems):
         whole_array = len(refs) == 1
@@ -193,9 +198,10 @@
             total[:, at : at + step] = dot(left[...], buffer[:, at : at + step])
 
 
-def in_proj_body(weight, info, h_ref, gain_ref, *rest):
+def in_proj_body(weight, tokens, info, h_ref, gain_ref, *rest):
     refs = len(weight.arrays)
-    w_refs, (normed_ref, mixed_ref, rate_ref, buffer, sems, total) = rest[:refs], rest[refs:]
+    w_refs, rest = rest[:refs], rest[refs + tokens :]
+    (normed_ref, mixed_ref, rate_ref, buffer, sems, total) = rest
     weight.start(w_refs, info, buffer, sems)
     h = h_ref[...].astype(F32)
     scale = lax.rsqrt(jnp.mean(h * h, axis=1, keepdims=True) + EPSILON)
@@ -205,11 +211,13 @@
     rate_ref[...] = total[:, MIXED:]
 
 
-def in_proj(info, h, gain, weight):
-    return pl.pallas_call(
-        functools.partial(in_proj_body, weight),
+def in_proj(info, h, gain, weight, tokens):
+    return pl.pallas_call(
+        functools.partial(in_proj_body, weight, len(tokens)),
         out_shape=(shape((ROWS, WIDTH), BF16), shape((ROWS, MIXED), BF16), shape((ROWS, LANES))),
-        in_specs=[SMEM, whole((ROWS, WIDTH)), whole((1, WIDTH))] + weight.specs(),
+        in_specs=[SMEM, whole((ROWS, WIDTH)), whole((1, WIDTH))]
+        + weight.specs()
+        + [ANYWHERE] * len(tokens),
         out_specs=(whole((ROWS, WIDTH)), whole((ROWS, MIXED)), whole((ROWS, LANES))),
         scratch_shapes=weight.scratch() + [pltpu.VMEM((ROWS, PACKED), F32)],
         compiler_params=params(),
@@ -217,21 +225,21 @@
             flops=2 * ROWS * WIDTH * PACKED, bytes_accessed=8_000_000, transcendentals=0
         ),
         name="in_proj",
-    )(info, h, gain, *weight.arrays)
-
-
-def gate_proj_body(weight, info, normed_ref, *rest):
+    )(info, h, gain, *weight.arrays, *tokens)
+
+
+def gate_proj_body(weight, tokens, info, normed_ref, *rest):
     refs = len(weight.arrays)
-    w_refs, (gate_ref, buffer, sems) = rest[:refs], rest[refs:]
+    w_refs, (gate_ref, buffer, sems) = rest[:refs], rest[refs + tokens :]
     weight.start(w_refs, info, buffer, sems)
     weight.product(w_refs, info, normed_ref, buffer, sems, gate_ref)
 
 
-def gate_proj(info, normed, weight):
-    return pl.pallas_call(
-        functools.partial(gate_proj_body, weight),
+def gate_proj(info, normed, weight, tokens):
+    return pl.pallas_call(
+        functools.partial(gate_proj_body, weight, len(tokens)),
         out_shape=shape((ROWS, LOCAL)),
-        in_specs=[SMEM, whole((ROWS, WIDTH))] + weight.specs(),
+        in_specs=[SMEM, whole((ROWS, WIDTH))] + weight.specs() + [ANYWHERE] * len(tokens),
         out_specs=whole((ROWS, LOCAL)),
         scratch_shapes=weight.scratch(),
         compiler_params=params(),
@@ -239,7 +247,7 @@
             flops=2 * ROWS * WIDTH * LOCAL, bytes_accessed=7_000_000, transcendentals=0
         ),
         name="gate_proj",
-    )(info, normed, *weight.arrays)
+    )(info, normed, *weight.arrays, *tokens)
 
 
 def conv_sum_of(values, halo, cpar, keep, ext):
@@ -392,7 +400,8 @@
     )(xa, bca, cum, dt, hpar)
 
 
-def scan_body(backward, info, msg, token, out_ref):
+def scan_body(backward, info, msg, *rest):
+    out_ref = rest[-1]
     carry = jnp.zeros((STATE_HALF, BLOCK), F32)
     for k in reversed(range(CHUNKS)) if backward else range(CHUNKS):
         keep = info[2 + k].astype(F32)
@@ -405,15 +414,15 @@
             carry = carry * keep
 
 
-def scan_call(info, msg, backward, token):
+def scan_call(info, msg, backward, *tokens):
     return pl.pallas_call(
         functools.partial(scan_body, backward),
         out_shape=shape((CHUNKS, STATE_HALF, BLOCK), BF16),
-        in_specs=[SMEM, whole((CHUNKS, MESSAGE, BLOCK)), ANYWHERE],
+        in_specs=[SMEM, whole((CHUNKS, MESSAGE, BLOCK))] + [ANYWHERE] * len(tokens),
         out_specs=whole((CHUNKS, STATE_HALF, BLOCK)),
         compiler_params=params(),
         name="chunk_scan",
-    )(info, msg, token)
+    )(info, msg, *tokens)
 
 
 def out_proj_body(weight, info, y_in, bca, cum, hin, s0, gate, gain, *rest):
@@ -472,30 +481,28 @@
     )(info, y_in, bca, cum, hin, s0, gate, gain, *weight.arrays)
 
 
-def join_body(info, h_ref, own, came, res_ref, low_ref, branch_ref, scale_ref):
+def join_body(info, h_ref, own, came, res_ref, branch_ref, scale_ref):
     squares = jnp.sum(own[:, WIDTH:] + came[:, WIDTH:], axis=1, keepdims=True)
     scale = lax.rsqrt(squares / INNER + EPSILON)
     branch = scale * (own[:, :WIDTH] + came[:, :WIDTH])
-    branch_ref[...] = branch
-    scale_ref[...] = jnp.broadcast_to(scale, (ROWS, LANES))
-    result = h_ref[...].astype(F32) + usable_rows(info) * branch
-    res_ref[...] = result
-    low_ref[...] = result.astype(BF16)
-
-
-def join(info, h, own, came):
-    wide = whole((ROWS, WIDTH))
-    parts = whole((ROWS, WIDTH + LANES))
+    branch_ref[...] = branch.astype(BF16)
+    scale_ref[...] = jnp.broadcast_to(scale, (HALF // 2, LANES))
+    first = pl.program_id(0) * (HALF // 2)
+    usable = (row_of((HALF // 2, 1)) + first < info[0]).astype(F32)
+    result = h_ref[...].astype(F32) + usable * branch
+    res_ref[...] = result.astype(res_ref.dtype)
+
+
+def join(info, h, own, came, kind):
+    def rows(width):
+        return pl.BlockSpec((HALF // 2, width), lambda i: (i, 0))
+
     return pl.pallas_call(
         join_body,
-        out_shape=(
-            shape((ROWS, WIDTH)),
-            shape((ROWS, WIDTH), BF16),
-            shape((ROWS, WIDTH)),
-            shape((ROWS, LANES)),
-        ),
-        in_specs=[SMEM, wide, parts, parts],
-        out_specs=(wide, wide, wide, whole((ROWS, LANES))),
+        grid=(4,),
+        out_shape=(shape((ROWS, WIDTH), kind), shape((ROWS, WIDTH), BF16), shape((ROWS, LANES))),
+        in_specs=[SMEM, rows(WIDTH), rows(WIDTH + LANES), rows(WIDTH + LANES)],
+        out_specs=(rows(WIDTH), rows(WIDTH), rows(LANES)),
         compiler_params=params(),
         cost_estimate=pl.CostEstimate(flops=2_000_000, bytes_accessed=8_000_000, transcendentals=0),
         name="join",
@@ -510,7 +517,7 @@
     bg = usable_rows(info) * cot[...].astype(F32)
     bg_ref[...] = bg.astype(BF16)
     scale = scale_ref[:, :1]
-    inner = jnp.sum(bg_ref[...].astype(F32) * branch[...], axis=1, keepdims=True)
+    inner = jnp.sum(bg_ref[...].astype(F32) * branch[...].astype(F32), axis=1, keepdims=True)
     inner = inner * scale * scale / INNER
     for b in range(4):
         rows = weight.wait(w_refs, info, b, buffer, sems)
@@ -934,51 +941,59 @@
     )(*arrays, token)
 
 
-def mixed_back_body(weight, info, dxc, part, *rest):
+def mixed_back_body(weight, tokens, info, dxc, part, h_ref, *rest):
     refs = len(weight.arrays)
-    w_refs, (out_ref, buffer, sems) = rest[:refs], rest[refs:]
+    w_refs, (out_ref, dgain_ref, buffer, sems) = rest[:refs], rest[refs + tokens :]
     weight.start(w_refs, info, buffer, sems)
+    h = h_ref[...].astype(F32)
+    scale = lax.rsqrt(jnp.mean(h * h, axis=1, keepdims=True) + EPSILON)
     for b in range(4):
         rows = weight.wait(w_refs, info, b, buffer, sems)
-        out_ref[:, rows] = part[:, rows] + dot_nt(dxc[...], buffer[rows, :])
-
-
-def mixed_back(info, dxc, part, weight):
-    return pl.pallas_call(
-        functools.partial(mixed_back_body, weight),
-        out_shape=shape((ROWS, WIDTH)),
-        in_specs=[SMEM, whole((ROWS, PACKED)), whole((ROWS, WIDTH))] + weight.specs(),
-        out_specs=whole((ROWS, WIDTH)),
+        d_norm = part[:, rows] + dot_nt(dxc[...], buffer[rows, :])
+        out_ref[:, rows] = d_norm
+        total = jnp.sum(d_norm * h_ref[:, rows].astype(F32) * scale, axis=0, keepdims=True)
+        dgain_ref[:, rows] = jnp.broadcast_to(total, (8, SHARD))
+
+
+def mixed_back(info, dxc, part, h, weight, tokens):
+    return pl.pallas_call(
+        functools.partial(mixed_back_body, weight, len(tokens)),
+        out_shape=(shape((ROWS, WIDTH)), shape((8, WIDTH))),
+        in_specs=[SMEM, whole((ROWS, PACKED)), whole((ROWS, WIDTH)), whole((ROWS, WIDTH))]
+        + weight.specs()
+        + [ANYWHERE] * len(tokens),
+        out_specs=(whole((ROWS, WIDTH)), whole((8, WIDTH))),
         scratch_shapes=weight.scratch(),
         compiler_params=params(),
         cost_estimate=pl.CostEstimate(
             flops=2 * ROWS * WIDTH * PACKED, bytes_accessed=9_000_000, transcendentals=0
         ),
         name="mixed_back",
-    )(info, dxc, part, *weight.arrays)
-
-
-def norm_back_body(own, came, h_ref, cot, gain, dh_ref, low_ref, dgain_ref):
+    )(info, dxc, part, h, *weight.arrays, *tokens)
+
+
+def norm_back_body(own, came, h_ref, cot, gain, token, dh_ref, low_ref):
     h = h_ref[...].astype(F32)
     scale = lax.rsqrt(jnp.mean(h * h, axis=1, keepdims=True) + EPSILON)
     d_norm = own[...] + came[...]
     inner = jnp.mean(d_norm * gain[...] * h, axis=1, keepdims=True) * scale * scale * scale
-    dgain_ref[...] = jnp.broadcast_to(
-        jnp.sum(d_norm * h * scale, axis=0, keepdims=True), (8, WIDTH)
-    )
     dh = cot[...].astype(F32) + scale * d_norm * gain[...] - h * inner
     dh_ref[...] = dh
     low_ref[...] = dh.astype(BF16)
 
 
-def norm_back(own, came, h, cot, gain):
+def norm_back(own, came, h, cot, gain, token):
+    rows = pl.BlockSpec((HALF // 2, WIDTH), lambda i: (i, 0))
     return pl.pallas_call(
         norm_back_body,
-        out_shape=(shape((ROWS, WIDTH)), shape((ROWS, WIDTH), BF16), shape((8, WIDTH))),
+        grid=(4,),
+        out_shape=(shape((ROWS, WIDTH)), shape((ROWS, WIDTH), BF16)),
+        in_specs=[rows] * 4 + [whole((1, WIDTH)), ANYWHERE],
+        out_specs=(rows, rows),
         compiler_params=params(),
         cost_estimate=pl.CostEstimate(flops=3_000_000, bytes_accessed=8_000_000, transcendentals=0),
         name="norm_back",
-    )(own, came, h, cot, gain)
+    )(own, came, h, cot, gain, token)
 
 
 def z_shift(r):
@@ -1005,32 +1020,47 @@
     return lax.ppermute(value, "section", [(0, 1), (1, 0)])
 
 
+def nothing_body(*refs):
+    refs[-1][...] = jnp.zeros((8, LANES), jnp.int32)
+
+
 def after(values, place):
-    nothing = jnp.int32(0)
-    for value in values:
-        corner = lax.slice(value, (0,) * value.ndim, (1,) * value.ndim).reshape(())
-        nothing = nothing + (corner != corner).astype(jnp.int32)
+    nothing = pl.pallas_call(
+        nothing_body,
+        out_shape=shape((8, LANES), jnp.int32),
+        in_specs=[ANYWHERE] * len(values),
+        out_specs=whole((8, LANES)),
+        compiler_params=params(),
+        cost_estimate=pl.CostEstimate(flops=0, bytes_accessed=4096, transcendentals=0),
+        name="after",
+    )(*values)[0, 0]
     return {axis: n + nothing for axis, n in place.items()}
 
 
-def pieces(mine, came, layer, section, place):
+def fetched(mine, came, layer, section, place):
     rows = SHARD // 2
 
     def piece(source, side, axis):
         return lax.dynamic_slice_in_dim(source, side * rows + place[axis] * PIECE, PIECE, 0)
 
-    first = jnp.concatenate(
-        [
-            jnp.where(section == layer, piece(mine, side, axis), piece(came, side, axis))
-            for side, axis in enumerate("xy")
-        ]
-    )
-    got = [send(first, "z", -r) for r in range(1, 4)]
+    parts = [
+        jnp.where(section == layer, piece(mine, side, axis), piece(came, side, axis))
+        for side, axis in enumerate("xy")
+    ]
+    if mine.shape[0] == TALL:
+        parts.append(jnp.where(section == layer, mine[SHARD:], came[SHARD:]))
+    return jnp.concatenate(parts)
+
+
+def pieces(mine, came, got, late):
     out = [mine, came]
     for side, axis in enumerate("xy"):
-        stack = jnp.concatenate([g[side * PIECE : (side + 1) * PIECE] for g in got])
+        rows = slice(side * PIECE, (side + 1) * PIECE)
+        stack = jnp.concatenate(
+            [lax.dynamic_slice_in_dim(g, rows.start + late, PIECE, 0) for g in got[1:]]
+        )
         out += [stack] + [send(stack, axis, -r) for r in range(1, 4)]
-    return out, got
+    return out
 
 
 def summed(terms):
@@ -1042,14 +1072,40 @@
     return [terms[0]] + [send(terms[r], axis, r) for r in range(1, 4)]
 
 
-def total_of(value):
-    for axis in "xyz":
-        low = value.astype(BF16)
-        value = summed([low] + [send(low, axis, r) for r in range(1, 4)])
-    return value
-
-
-def fold_body(slot, counts, outer, inner, info, *rest):
+def terms_body(axis, width, info, source, other, *rest):
+    small, outs, total = rest[:-5], rest[-5:-1], rest[-1]
+    total[...] = dot(source[...], other[...])
+    count = 96 if axis == "y" else 24
+    for r in range(4):
+        first = lax.rem(info[11 if axis == "y" else 12] + r, 4) * count
+        starts = [z * SHARD for z in range(4)]
+        if axis == "x":
+            starts = [start + y * 96 for start in starts for y in range(4)]
+        parts = [total[pl.ds(pl.multiple_of(start + first, 8), count), :] for start in starts]
+        outs[r][:SHARD, :] = jnp.concatenate(parts, axis=0).astype(BF16)
+        for ref in small:
+            outs[r][SHARD:, :] = ref[...]
+
+
+def terms(info, axis, source, other, small=()):
+    width = other.shape[1]
+    rows = SHARD + sum(v.shape[0] for v in small)
+    arrays = (source, other, *small)
+    return pl.pallas_call(
+        functools.partial(terms_body, axis, width),
+        out_shape=[shape((rows, width), BF16)] * 4,
+        in_specs=[SMEM] + [whole(v.shape) for v in arrays],
+        out_specs=[whole((rows, width))] * 4,
+        scratch_shapes=[pltpu.VMEM((4 * SHARD, width), F32)],
+        compiler_params=params(),
+        cost_estimate=pl.CostEstimate(
+            flops=8 * SHARD * ROWS * width, bytes_accessed=5_000_000, transcendentals=0
+        ),
+        name="terms",
+    )(info, *arrays)
+
+
+def fold_body(slot, counts, outer, inner, rest_rows, info, *rest):
     refs, outs, total = rest[: sum(counts)], rest[sum(counts) + 1 : -1], rest[-1]
     column = 0
     for count in counts:
@@ -1062,6 +1118,8 @@
         parts = [
             total[pl.ds(pl.multiple_of(n * 4 * inner + first, 8), inner), :] for n in range(outer)
         ]
+        if rest_rows:
+            parts.append(total[4 * outer * inner :, :])
         outs[r][...] = jnp.concatenate(parts, axis=0).astype(BF16)
 
 
@@ -1069,15 +1127,48 @@
     slot = 10 + "zyx".index(axis)
     arrays = [a for group in groups for a in group]
     rows, width = arrays[0].shape[0], sum(group[0].shape[1] for group in groups)
-    return pl.pallas_call(
-        functools.partial(fold_body, slot, [len(group) for group in groups], outer, inner),
-        out_shape=[shape((rows // 4, width), BF16)] * 4,
+    more = rows - 4 * outer * inner
+    out = shape((outer * inner + more, width), BF16)
+    counts = [len(group) for group in groups]
+    return pl.pallas_call(
+        functools.partial(fold_body, slot, counts, outer, inner, more),
+        out_shape=[out] * 4,
         in_specs=[SMEM] + [whole(a.shape) for a in arrays] + [ANYWHERE],
-        out_specs=[whole((rows // 4, width))] * 4,
+        out_specs=[whole(out.shape)] * 4,
         scratch_shapes=[pltpu.VMEM((rows, width), F32)],
         compiler_params=params(),
         cost_estimate=pl.CostEstimate(flops=2_000_000, bytes_accessed=8_000_000, transcendentals=0),
         name="fold",
+    )(info, *arrays, token)
+
+
+def last_fold_body(info, *rest):
+    left, right, outs, total = rest[:4], rest[4:8], rest[9:13], rest[13]
+    width = left[0].shape[1]
+    rows = 96 + SMALL // 2
+    total[:96, :width] = summed([a[...] for a in left])
+    total[:96, width:] = summed([a[:96, :] for a in right])
+    total[96:, :width] = summed([a[96:rows, :width] for a in right])
+    total[96:, width:] = summed([a[rows:, :] for a in right])
+    for r in range(4):
+        first = pl.multiple_of(lax.rem(info[10] + r, 4) * 24, 8)
+        parts = [total[pl.ds(first, 24), :], total[96:, :]]
+        outs[r][...] = jnp.concatenate(parts, axis=0).astype(BF16)
+
+
+def last_fold(info, left, right, token):
+    width = left[0].shape[1] + right[0].shape[1]
+    out = shape((24 + SMALL // 2, width), BF16)
+    arrays = (*left, *right)
+    return pl.pallas_call(
+        last_fold_body,
+        out_shape=[out] * 4,
+        in_specs=[SMEM] + [whole(a.shape) for a in arrays] + [ANYWHERE],
+        out_specs=[whole(out.shape)] * 4,
+        scratch_shapes=[pltpu.VMEM((96 + SMALL // 2, width), F32)],
+        compiler_params=params(),
+        cost_estimate=pl.CostEstimate(flops=500_000, bytes_accessed=2_000_000, transcendentals=0),
+        name="last_fold",
     )(info, *arrays, token)
 
 
@@ -1109,27 +1200,94 @@
     return jnp.concatenate(parts, axis=2).reshape(rows, -1)
 
 
-def pick_x_body(info, x_ref, dt_ref, *outs):
+def pick_x_body(info, x_ref, dt_ref, *rest):
+    smalls, outs, small = rest[:7], rest[7:9], rest[9]
+    small[...] = jnp.zeros((16, PACKED), F32)
+    row = 0
+    for ref in smalls[:4]:
+        count, width = ref.shape
+        small[row : row + count, :width] = ref[...].astype(F32)
+        row += count
+    for ref in smalls[4:]:
+        left = ref[...]
+        for _ in range(3):
+            part = left.astype(BF16).astype(F32)
+            small[row : row + 1, :HEADS] = part
+            left = left - part
+            row += 1
     head, lane = row_of((HEADS, LANES)), lane_of((HEADS, LANES))
     for out, side in zip(outs, (info[0], 1 - info[0]), strict=True):
         for d in range(GROUPS):
             cols = pl.ds(pl.multiple_of((2 * d + side) * BLOCK, LANES), BLOCK)
-            out[:, d * BLOCK : (d + 1) * BLOCK] = x_ref[:, cols]
-        out[:, LOCAL:MIXED] = x_ref[:, INNER:]
+            out[:SHARD, d * BLOCK : (d + 1) * BLOCK] = x_ref[:, cols]
+        out[:SHARD, LOCAL:MIXED] = x_ref[:, INNER:]
         here = (head // OWN == 2 * (lane // 8) + side) & (head % OWN == lane % 8)
-        out[:, MIXED:] = dot(dt_ref[...], here.astype(BF16)).astype(BF16)
-
-
-def pick_x(section, x, dt):
+        out[:SHARD, MIXED:] = dot(dt_ref[...], here.astype(BF16)).astype(BF16)
+        out[SHARD:, :] = small[...].astype(BF16)
+
+
+def pick_x(section, x, dt, smalls):
     return pl.pallas_call(
         pick_x_body,
-        out_shape=[shape((SHARD, PACKED), BF16)] * 2,
-        in_specs=[SMEM, whole((SHARD, CONV_CH)), whole((SHARD, HEADS))],
-        out_specs=[whole((SHARD, PACKED))] * 2,
+        out_shape=[shape((TALL, PACKED), BF16)] * 2,
+        in_specs=[SMEM, whole((SHARD, CONV_CH)), whole((SHARD, HEADS))]
+        + [whole(v.shape) for v in smalls],
+        out_specs=[whole((TALL, PACKED))] * 2,
+        scratch_shapes=[pltpu.VMEM((16, PACKED), F32)],
         compiler_params=params(),
         cost_estimate=pl.CostEstimate(flops=0, bytes_accessed=6_000_000, transcendentals=0),
         name="pick_x",
-    )(section, x, dt)
+    )(section, x, dt, *smalls)
+
+
+def unpack_body(count, info, *rest):
+    refs, (cpar, gain_one, gain_two, hpar, held, full, sems) = rest[:count], rest[count:]
+    copies = []
+    for n in range(4):
+        if count == 4:
+            source, to = refs[n].at[pl.ds(2 * PIECE, 16)], lax.rem(info[10] + n, 4)
+        else:
+            source, to = refs[0].at[pl.ds(n * TALL + SHARD, 16)], n
+        copies.append(pltpu.make_async_copy(source, held.at[to], sems.at[n]))
+    for c in copies:
+        c.start()
+    for c in copies:
+        c.wait()
+    section = info[13]
+    half_cols = pl.ds(pl.multiple_of(section * BLOCK, LANES), BLOCK)
+    for z in range(4):
+        values = held[z].astype(F32)
+        full[:, z * 832 : (z + 1) * 832] = values[:8, :832]
+        gain_one[:, z * SHARD : (z + 1) * SHARD] = values[5:6, :SHARD]
+        gain_two[:, z * BLOCK : (z + 1) * BLOCK] = held[z, :, half_cols].astype(F32)[6:7]
+    for d in range(GROUPS):
+        cols = pl.ds(pl.multiple_of((2 * d + section) * BLOCK, LANES), BLOCK)
+        cpar[:, d * BLOCK : (d + 1) * BLOCK] = full[:, cols]
+    cpar[:, LOCAL:] = full[:, INNER:]
+    values = held[0, :, :LANES].astype(F32)
+    heads = [values[n : n + 1] + values[n + 1 : n + 2] + values[n + 2 : n + 3] for n in (7, 10, 13)]
+    heads = jnp.concatenate(heads + [jnp.zeros((5, LANES), F32)], axis=0)
+    head, lane = row_of((LANES, LANES)), lane_of((LANES, LANES))
+    here = (head // OWN == 2 * (lane // 8) + section) & (head % OWN == lane % 8)
+    hpar[...] = exact_dot(heads, here.astype(F32))
+
+
+def unpack(info, arrays):
+    shapes = ((8, MIXED), (1, WIDTH), (1, LOCAL), (8, LANES))
+    return pl.pallas_call(
+        functools.partial(unpack_body, len(arrays)),
+        out_shape=[shape(dims) for dims in shapes],
+        in_specs=[SMEM] + [ANYWHERE] * len(arrays),
+        out_specs=[whole(dims) for dims in shapes],
+        scratch_shapes=[
+            pltpu.VMEM((4, 16, PACKED), BF16),
+            pltpu.VMEM((8, CONV_CH), F32),
+            pltpu.SemaphoreType.DMA((4,)),
+        ],
+        compiler_params=params(),
+        cost_estimate=pl.CostEstimate(flops=0, bytes_accessed=400_000, transcendentals=0),
+        name="unpack",
+    )(info, *arrays)
 
 
 def pick_zo_body(info, z_ref, o_ref, token, *outs):
@@ -1189,37 +1347,6 @@
     def ordered(mine, came):
         return jnp.where(section == 0, mine, came), jnp.where(section == 0, came, mine)
 
-    at = section.reshape(1).astype(jnp.int32)
-    mine_x, other_x = pick_x(at, w_xbc[0], w_dt[0])
-    came_x = swapped(other_x)
-    mine_zo, other_zo = pick_zo(at, w_z[0], w_out[0], mine_x)
-    came_zo = swapped(other_zo)
-    low_x, got = pieces(mine_x, came_x, 0, section, place)
-    low_zo, got = pieces(mine_zo, came_zo, 0, section, after(got, place))
-    here = after(got, {"section": section})["section"]
-    high_x = [lax.all_gather(jnp.where(here == 1, mine_x, came_x), "dp", tiled=True)]
-    high_zo = [lax.all_gather(jnp.where(here == 1, mine_zo, came_zo), "dp", tiled=True)]
-    weights_x = [Weight(v, n, PACKED) for n, v in enumerate((low_x, high_x))]
-    weights_z = [Weight(v, n, LOCAL) for n, v in enumerate((low_zo, high_zo))]
-    weights_o = [Weight(v, n, WIDTH, LOCAL) for n, v in enumerate((low_zo, high_zo))]
-
-    small = jnp.zeros((16, 832), F32)
-    small = small.at[:4].set(conv_weight[0].astype(F32)).at[4].set(conv_bias[0].astype(F32))
-    small = small.at[5, :384].set(norm_gain[0].astype(F32))
-    small = small.at[6, :768].set(gate_gain[0].astype(F32))
-    small = small.at[8, :HEADS].set(dt_bias[0]).at[9, :HEADS].set(a_log[0])
-    small = small.at[10, :HEADS].set(d_skip[0])
-    smalls = jnp.stack([small] + [send(small, "z", -r) for r in range(1, 4)])
-    smalls = lax.dynamic_slice_in_dim(jnp.concatenate([smalls, smalls]), (4 - group) % 4, 4)
-    cpars, gains_one, gains_two, hpars = [], [], [], []
-    for values in ordered(smalls, swapped(smalls)):
-        full = jnp.transpose(values[:, :8], (1, 0, 2)).reshape(8, CONV_CH)
-        local = halves(full[:, :INNER], section)[0]
-        cpars.append(jnp.concatenate([local, full[:, INNER:]], axis=1))
-        gains_one.append(values[:, 5, :384].reshape(1, WIDTH))
-        gains_two.append(halves(values[:, 6, :768].reshape(1, INNER), section)[0])
-        hpars.append(jnp.pad(head_lanes(halves(values[0, 8:11, :HEADS], section)[0]), ((0, 5), (0, 0))))
-
     own_rows = lax.dynamic_index_in_dim(boundary[0], micro, 0, False)
     other_rows = lax.dynamic_index_in_dim(boundary[0], 1 - micro, 0, False)
     came = lax.ppermute(other_rows, "ctx", NEIGHBOURS)
@@ -1244,21 +1371,23 @@
 
     def forward(h, layer):
         cpar, hpar = cpars[layer], hpars[layer]
-        normed, mixed, rate = in_proj(info, h, gains_one[layer], weights_x[layer])
+        normed, mixed, rate = in_proj(
+            info, h, gains_one[layer], weights_x[layer], []
+        )
         halo = halo_shift(mixed[ROWS - 16 :], 1)
-        gate = gate_proj(info, normed, weights_z[layer])
+        gate = gate_proj(info, normed, weights_z[layer], [] if layer else ready)
         xa, bca, cum, dt, s0, msg = state_call(info, mixed, halo, cpar, rate, hpar)
         came = exchange(msg)
         y_in = inside_call(xa, bca, cum, dt, hpar)
-        hin = exchange(scan_call(info, came, False, gate)).reshape(GROUPS, STATE, BLOCK)
+        hin = exchange(scan_call(info, came, False, y_in)).reshape(GROUPS, STATE, BLOCK)
         y, part = out_proj(
             info, y_in, bca, cum, hin, s0, gate, gains_two[layer], weights_o[layer]
         )
-        result, low, branch, scale = join(info, h, part, swapped(part))
+        result, branch, scale = join(info, h, part, swapped(part), F32 if layer else BF16)
         saved = (h, normed, mixed, halo, rate, gate, xa, bca, cum, dt, s0, msg, hin, y, branch, scale)
-        return result, low, saved
-
-    def backward(cot, saved, layer, higher=None):
+        return result, saved
+
+    def backward(cot, saved, layer, higher, tokens):
         h, normed, mixed, halo, rate, gate, xa, bca, cum, dt, s0, msg, hin, y, branch, scale = saved
         cpar, hpar = cpars[layer], hpars[layer]
         bg, dy, dz, normed_two, d_gain_two = gate_back(
@@ -1268,49 +1397,33 @@
         came = exchange(msg_back)
         normed_two_t, normed_t = normed_two.T, normed.T
 
-        def terms(source, axis, other, place):
-            grid = source.reshape((4, 4, 96, ROWS) if axis == "y" else (4, 4, 4, 24, ROWS))
-            out = []
-            for r in range(4):
-                rows = lax.dynamic_index_in_dim(
-                    grid, (place[axis] + r) % 4, "zyx".index(axis), False
-                )
-                out.append(dot(rows.reshape(SHARD, ROWS), other).astype(BF16))
-            return out
-
-        def first_stage(source, other):
-            return lax.psum_scatter(dot(source, other).astype(BF16), "dp", tiled=True)
-
-        if layer == 1:
-            sums = [first_stage(normed_two_t, bg), first_stage(normed_t, dz)]
+        def first_stage(value):
+            return lax.psum_scatter(value, "dp", tiled=True)
+
+        grad_o, grad_z = dot(normed_two_t, bg).astype(BF16), dot(normed_t, dz).astype(BF16)
+        sums = [first_stage(grad_o), first_stage(grad_z)]
         dxi, d_skips, gsum, u, dbc = inside_back(dy, xa, bca, cum, dt, hpar)
         part = gate_in_back(info, dz, weights_z[layer])
-        lam = exchange(scan_call(info, came, True, part)).reshape(GROUPS, STATE, BLOCK)
-        if layer == 0:
-            here = after([lam], place)
-            sent_z = arrived(terms(normed_t, "y", dz, here), "y")
-            sent_o = arrived(terms(normed_two_t, "x", bg, here), "x")
+        lam = exchange(scan_call(info, came, True, part, grad_o, grad_z, *tokens)).reshape(GROUPS, STATE, BLOCK)
         dmx, dmbc, tailx, tailbc, edgex, edgebc, d_parx, d_parbc, d_heads = finish_call(
             info, xa, dxi, dy, mixed, halo, cpar, bca, cum, dt, rate, hpar, lam, hin, s0, own1, u, gsum, dbc
         )
         edge = halo_shift(jnp.concatenate([edgex, edgebc], axis=1), -1)
         token = d_heads
         if layer == 0:
-            higher = fold(info, "y", [[v] for v in higher], 1, 96, d_heads)
+            higher_rows, higher = higher
+            higher = arrived(fold(info, "y", [[v] for v in higher], 1, 96, d_heads), "y")
             token = higher[0]
         dxc = patch(dmx, dmbc, tailx, tailbc, edge, token)
-        part = mixed_back(info, dxc, part, weights_x[layer])
-        dh, dh_low, d_gain_one = norm_back(part, swapped(part), h, cot, gains_one[layer])
-
+        middle = 7 * LANES
+        left, deadline = [], []
         if layer == 0:
-            middle = PACKED // 2
-            sent_l = arrived(terms(normed_t, "y", dxc[:, :middle], place), "y")
-            sent_r = arrived(terms(normed_t, "x", dxc[:, middle:], place), "x")
-            left = arrived(fold(info, "x", [sent_z, sent_l], 4, 24, dh_low), "x")
-            right = arrived(fold(info, "y", [sent_o, sent_r], 4, 24, dh_low), "y")
-            sums = higher, summed(arrived(fold(info, "z", [left, right], 1, 24, dh_low), "z"))
-        else:
-            sums.append(first_stage(normed_t, dxc))
+            left = terms(info, "y", normed_t, dxc[:, :middle])
+            deadline = [left[0]]
+        part, d_gain_one = mixed_back(info, dxc, part, h, weights_x[layer], deadline)
+        grad_x = dot(normed_t, dxc).astype(BF16) if layer == 1 else dxc
+        dh, dh_low = norm_back(part, swapped(part), h, cot, gains_one[layer], grad_x)
+
         d_skip_row = jnp.sum(d_skips[0:1].reshape(1, 4 * OWN, HEADDIM), axis=2)
         rows = jnp.where(jnp.arange(8)[:, None] == 5, d_gain_two, d_parx)
         rows = jnp.concatenate([rows, d_parbc], axis=1)
@@ -1322,20 +1435,70 @@
             ]
         )
         rows = jnp.concatenate([rows, jnp.pad(more, ((0, 0), (0, 2 * STATE)))])
-        return dh, dh_low, sums, rows
-
-    _, middle, saved_low = forward(hidden, 0)
-    out_high, _, saved_high = forward(middle, 1)
-    _, back, higher, rows_high = backward(cotangent, saved_high, 1)
-    dh_low, back, (higher, low), rows_low = backward(back, saved_low, 0, higher)
-
-    higher = fold(info, "x", [arrived(higher, "y")], 1, 24, back)
-    high = summed(arrived(higher, "x"))
-    high_o, high_z, high_x = jnp.split(high, (WIDTH, WIDTH + LOCAL), axis=1)
-    at = (LOCAL, LOCAL + PACKED // 2, LOCAL + PACKED // 2 + WIDTH)
-    low_z, low_l, low_o, low_r = jnp.split(low, at, axis=1)
-
-    rows = total_of(jnp.concatenate([rows_low, rows_high]))
+        if layer == 1:
+            return dh, dh_low, sums + [first_stage(grad_x)], rows
+
+        rows = jnp.concatenate([rows, higher_rows]).astype(BF16)
+        small = jnp.concatenate([rows[:, : MIXED // 2], rows[:, MIXED // 2 :]])
+        small = jnp.pad(small, ((0, 0), (0, LANES)))
+        left = arrived(left, "y")
+        right = arrived(terms(info, "x", normed_t, dxc[:, middle:], (small,)), "x")
+        left = fold(info, "x", [left], 4, 24, dh_low)
+        right = fold(info, "y", [right], 4, 24, dh_low)
+        higher = arrived(fold(info, "x", [higher], 1, 24, left[0]), "x")
+        token = right[0]
+        left, right = arrived(left, "x"), arrived(right, "y")
+        sum_x = summed(arrived(last_fold(info, left, right, higher[0]), "z"))
+        rows = jnp.concatenate(
+            [sum_x[24:, : MIXED // 2], sum_x[24:, middle : middle + MIXED // 2]], axis=1
+        )
+        return dh, [higher, sums, token], sum_x[:24], rows
+
+    at = section.reshape(1).astype(jnp.int32)
+    smalls = (conv_weight[0], conv_bias, norm_gain, gate_gain, dt_bias, a_log, d_skip)
+    mine_x, other_x = pick_x(at, w_xbc[0], w_dt[0], smalls)
+    came_x = swapped(other_x)
+    mine_zo, other_zo = pick_zo(at, w_z[0], w_out[0], mine_x)
+    came_zo = swapped(other_zo)
+    first = fetched(mine_x, came_x, 0, section, after([hidden], place))
+    got = [first] + [send(first, "z", -r) for r in range(1, 4)]
+    small_low = got
+    low_x = pieces(mine_x, came_x, got, 0)
+    got = lax.all_gather(fetched(mine_zo, came_zo, 0, section, after(got[1:], place)), "dp")
+    late = after(low_x[3:6] + low_x[7:10], place)["z"]
+    got = [None] + [lax.dynamic_index_in_dim(got, (late + r) % 4, 0, False) for r in range(1, 4)]
+    low_zo = pieces(mine_zo, came_zo, got, 0)
+    high_x = [lax.all_gather(jnp.where(section == 1, mine_x, came_x), "dp", tiled=True)]
+    high_zo = [lax.all_gather(jnp.where(section == 1, mine_zo, came_zo), "dp", tiled=True)]
+    ready = low_zo[3:6] + low_zo[7:10]
+    weights_x = [Weight(v, n, PACKED) for n, v in enumerate((low_x, high_x))]
+    weights_z = [Weight(v, n, LOCAL) for n, v in enumerate((low_zo, high_zo))]
+    weights_o = [Weight(v, n, WIDTH, LOCAL) for n, v in enumerate((low_zo, high_zo))]
+
+    unpacked = [unpack(info, v) for v in (small_low, high_x)]
+    cpars, gains_one, gains_two, hpars = zip(*unpacked, strict=True)
+
+    def returned(rows, layer):
+        pairs = [(layer * 16 + a, layer * 16 + b) for a, b in NEIGHBOURS]
+        other = lax.ppermute(
+            jnp.where(micro == 0, rows[HALF:], rows[:HALF]), ("section", "ctx"), pairs
+        )
+        mine = jnp.where(micro == 0, rows[:HALF], rows[HALF:])
+        return jnp.where(micro == 0, jnp.stack([mine, other]), jnp.stack([other, mine]))
+
+    middle, saved_low = forward(hidden, 0)
+    out_high, saved_high = forward(middle, 1)
+    top_high = returned(out_high, 1)
+    _, back, higher, rows = backward(cotangent, saved_high, 1, None, [top_high])
+    dh_low, (higher, lower, token), low_x, rows = backward(
+        back, saved_low, 0, (rows, higher), []
+    )
+
+    high_o, high_z, high_x = jnp.split(summed(higher), (WIDTH, WIDTH + LOCAL), axis=1)
+    lower = fold(info, "x", [[v] for v in lower], 4, 24, token)
+    lower = fold(info, "y", [arrived(lower, "x")], 1, 24, token)
+    low_o, low_z = jnp.split(summed(arrived(lower, "y")), 2, axis=1)
+
     own, given = ordered(rows[:16], rows[16:])
     rows_0, rows_1 = ordered(own, swapped(given))
     wide = jnp.concatenate(
@@ -1346,10 +1509,10 @@
     index = group * 16 + ctx
     d_conv = lax.dynamic_slice(wide, (0, index * 52), (5, 52))
     d_gain_two = lax.dynamic_slice(wide, (5, index * 48), (1, 48))
-    d_gain_one = lax.dynamic_slice(rows_0, (8, index * 24), (1, 24))
+    d_gain_one = lax.dynamic_slice(rows_0[8:9] + rows_1[8:9], (0, index * 24), (1, 24))
 
     own, given = ordered(
-        jnp.concatenate([low_z, low_l, low_r], axis=1), jnp.concatenate([high_z, high_x], axis=1)
+        jnp.concatenate([low_z, low_x], axis=1), jnp.concatenate([high_z, high_x], axis=1)
     )
     first, second = ordered(own, swapped(given))
     sum_z = turns(first[:, :LOCAL], second[:, :LOCAL])
@@ -1367,15 +1530,7 @@
         trips.append(lax.ppermute(value, ("section", "ctx"), pairs))
     sum_o = jnp.concatenate(ordered(*trips))
 
-    def returned(rows, layer):
-        pairs = [(layer * 16 + a, layer * 16 + b) for a, b in NEIGHBOURS]
-        other = lax.ppermute(
-            jnp.where(micro == 0, rows[HALF:], rows[:HALF]), ("section", "ctx"), pairs
-        )
-        mine = jnp.where(micro == 0, rows[:HALF], rows[HALF:])
-        return jnp.where(micro == 0, jnp.stack([mine, other]), jnp.stack([other, mine]))
-
-    top = jnp.where(section == 0, returned(dh_low, 0), returned(out_high, 1))
+    top = jnp.where(section == 0, returned(dh_low, 0), top_high)
     return (
         top[None],
         d_gain_one,

time: 818 us -> 728 us (0.89)
  starting transfers between devices: 233 us -> 166 us
  local copies, waits for them, and re-layouts: 73.7 us -> 44 us
  Pallas kernels: 232 us -> 247 us
  matrix products: 34.4 us -> 22.8 us
    ppermute x57 -> x42, starting transfers between devices: 148 us -> 75.6 us  [send(): return lax.ppermute(value, name, pairs)]
    pallas_call x16 -> x25, Pallas kernels: 90.7 us -> 106 us  [the longest x6 22.5 us: fold(): pl.pallas_call(functools.partial(fold_body, slot, counts, outer, inner, m...]
    dot_general x19 -> x5, matrix products: 34.4 us -> 22.8 us  [dot(): return jnp.dot(a, b, preferred_element_type=F32)]
    ppermute x6 -> x0, local copies, waits for them, and re-layouts: 9.52 us -> none  [send(): return lax.ppermute(value, name, pairs)]
    ppermute x57 -> x42, waiting for transfers between devices: 139 us -> 134 us  [send(): return lax.ppermute(value, name, pairs)]
    unnamed x209 -> x142, local copies, waits for them, and re-layouts: 20.4 us -> 20 us
  transfers between devices with their start and end apart: 89 -> 76, of which waited for: 33 -> 31; matrix products, arithmetic and copies ran while one was open for 13% -> 10% of each run, Pallas kernels for 25% -> 31%
where the time goes in v3:
time: 728 us; the launch traced here: 716 us
  Pallas kernels  247 us (34%)
  waiting for transfers between devices  183 us (25%)
  starting transfers between devices  166 us (23%)
  local copies, waits for them, and re-layouts  44 us (6%)
  other arithmetic  31.9 us (4%)
  matrix products  22.8 us (3%)
  between operations  21.1 us (3%)
    ppermute x42, waiting for transfers between devices, send(): return lax.ppermute(value, name, pairs)  134 us
    ppermute x42, starting transfers between devices, send(): return lax.ppermute(value, name, pairs)  75.6 us
    all_to_all x8, starting transfers between devices, exchange(): return lax.all_to_all(value, 'ctx', 0, 0, axis_index_groups=PARITY)  60 us
    pallas_call x2, Pallas kernels, finish_call(): pl.pallas_call(finish_body, grid=(GROUPS,), out_shape=(shape((ROWS, LOCAL...  25.5 us
    dot_general x5, matrix products, dot(): return jnp.dot(a, b, preferred_element_type=F32)  22.8 us
    pallas_call x6, Pallas kernels, fold(): pl.pallas_call(functools.partial(fold_body, slot, counts, outer, inner, m...  22.5 us
    pallas_call x2, Pallas kernels, gate_back(): pl.pallas_call(functools.partial(gate_back_body, weight), out_shape=(shap...  20.1 us
    unnamed x142, local copies, waits for them, and re-layouts  20 us
  transfers between devices with their start and end apart: 76, of which 31 were waited for; matrix products, arithmetic and copies ran while one was open for 10% of the time, Pallas kernels for 31%

profile of v3, /device:TPU:12, one launch (start us, length us, event | category | flops | bytes accessed | tf_op | source)
XLA Modules:
  0.0 715.6 jit_solution(2889364392605572559)
XLA Ops:
  14.2 5.2 collective-permute-done
  37.2 17.3 %collective-permute-done.3.rest_1_.refs_0_ = bf16[112,1920]{1,0:T(8,128)(2,1)S(1)} collective-permute-done((bf16[112,1920]{1,0:T(8,128)(2,1)S(1)}, bf16[112,1920]{1,0:T(8,128)(2,1)S(1)}, u32[]{:S(2)}, u32[]{:S(2)}) %collective-permute-start.3) | collective-permute-done | bytes 430112 | tf_op jit(solution)/shard_map/ppermute | solution.py:1016
  79.5 8.5 %collective-permute-done.6.rest_3_.refs_0_ = bf16[144,1920]{1,0:T(8,128)(2,1)S(1)} collective-permute-done((bf16[144,1920]{1,0:T(8,128)(2,1)}, bf16[144,1920]{1,0:T(8,128)(2,1)S(1)}, u32[]{:S(2)}, u32[]{:S(2)}) %collective-permute-start.6) | collective-permute-done | bytes 552992 | tf_op jit(solution)/shard_map/ppermute | solution.py:1016
  90.0 8.6 %collective-permute-done.8.rest_5_.refs_2_ = bf16[144,1920]{1,0:T(8,128)(2,1)S(1)} collective-permute-done((bf16[144,1920]{1,0:T(8,128)(2,1)}, bf16[144,1920]{1,0:T(8,128)(2,1)S(1)}, u32[]{:S(2)}, u32[]{:S(2)}) %collective-permute-start.8) | collective-permute-done | bytes 552992 | tf_op jit(solution)/shard_map/ppermute | solution.py:1016
  115.8 7.0 in_proj.2
  123.6 9.9 %collective-permute-start.12 = (bf16[16,1792]{1,0:T(8,128)(2,1)S(1)}, bf16[16,1792]{1,0:T(8,128)(2,1)S(1)}, u32[]{:S(2)}, u32[]{:S(2)}) collective-permute-start(bf16[16,1792]{1,0:T(8,128)(2,1)S(1)} %slice.198), channel_id=1, source_target_pairs={{0,2},{1,3},{2,4},{3,5},{4,6},{5,7},{6,8},{7,9},{8,10},{9,11},{10,... | collective-permute-start | bytes 172040 | tf_op jit(solution)/shard_map/ppermute | solution.py:1185
  137.7 14.3 %collective-permute-start.19 = (bf16[144,3072]{1,0:T(8,128)(2,1)S(1)}, bf16[144,3072]{1,0:T(8,128)(2,1)}, u32[]{:S(2)}, u32[]{:S(2)}) collective-permute-start(bf16[144,3072]{1,0:T(8,128)(2,1)S(1)} %pad_maximum_fusion.1.rest_6_), channel_id=1, source_target_pairs={{0,4},{1,5},{2,6},{3,7},{4,8},{5,9},{6,10},{7,11},{8,12},{9,13},{1... | collective-permute-start | bytes 2654216 | tf_op jit(solution)/shard_map/ppermute | solution.py:1016
  151.9 5.7 conv_state.2
  157.7 9.2 %all-to-all-start = ((bf16[8,80,384]{2,1,0:T(8,128)(2,1)}), bf16[8,80,384]{2,1,0:T(8,128)(2,1)}, u32[]{:S(2)}, u32[]{:S(2)}) async-start(bf16[8,80,384]{2,1,0:T(8,128)(2,1)} %get-tuple-element.148.msg_in), calls=%async_computation | async-start | bytes 983040 | tf_op jit(solution)/shard_map/all_to_all | solution.py:1180
  166.9 5.8 inside.2.rest_0_.y_in
  177.5 8.1 %all-to-all-start.1 = ((bf16[8,64,384]{2,1,0:T(8,128)(2,1)}), bf16[8,64,384]{2,1,0:T(8,128)(2,1)S(1)}, u32[]{:S(2)}, u32[]{:S(2)}) async-start(bf16[8,64,384]{2,1,0:T(8,128)(2,1)} %chunk_scan.4), calls=%async_computation.1 | async-start | bytes 786432 | tf_op jit(solution)/shard_map/all_to_all | solution.py:1180
  186.6 6.3 gate_proj.2.gate
  193.7 7.7 %out_proj.2 = (f32[256,1536]{1,0:T(8,128)}, f32[256,1664]{1,0:T(8,128)}) custom-call(s32[14]{0:T(128)} %concatenate.115.info, f32[256,1536]{1,0:T(8,128)} %inside.2.rest_0_.y_in, f32[256,256]{1,0:T(8,128)} %get-tuple-element.145.bca, f32[256,128]{1,0:T(8,128)} %get-tuple-element.146.cum, bf16[4,128,384]{2,1,0:T(8,128)(2,1)} %bitcast.80, ...), custom_call_target="tpu_custom_call" | custom-call | flops 1207959552 | bytes 13000000 | tf_op jit(solution)/shard_map/out_proj/pallas_call | solution.py:459
  213.3 7.1 in_proj.3
  229.4 5.7 conv_state.3
  235.1 7.2 %all-to-all-start.2 = ((bf16[8,80,384]{2,1,0:T(8,128)(2,1)}), bf16[8,80,384]{2,1,0:T(8,128)(2,1)S(1)}, u32[]{:S(2)}, u32[]{:S(2)}) async-start(bf16[8,80,384]{2,1,0:T(8,128)(2,1)} %get-tuple-element.165.msg_in), calls=%async_computation.2 | async-start | bytes 983040 | tf_op jit(solution)/shard_map/all_to_all | solution.py:1180
  242.3 5.8 inside.3.rest_0_.y_in
  252.2 6.9 all-to-all-start.3
  259.1 6.3 gate_proj.3.gate
  266.2 7.6 %out_proj.3 = (f32[256,1536]{1,0:T(8,128)}, f32[256,1664]{1,0:T(8,128)}) custom-call(s32[14]{0:T(128)} %concatenate.115.info, f32[256,1536]{1,0:T(8,128)} %inside.3.rest_0_.y_in, f32[256,256]{1,0:T(8,128)} %get-tuple-element.162.bca, f32[256,128]{1,0:T(8,128)} %get-tuple-element.163.cum, bf16[4,128,384]{2,1,0:T(8,128)(2,1)} %bitcast.78, ...), custom_call_target="tpu_custom_call" | custom-call | flops 1207959552 | bytes 13000000 | tf_op jit(solution)/shard_map/out_proj/pallas_call | solution.py:459
  283.5 9.9 %gate_back.2 = (bf16[256,1536]{1,0:T(8,128)(2,1)}, bf16[256,1536]{1,0:T(8,128)(2,1)}, bf16[256,1536]{1,0:T(8,128)(2,1)}, bf16[256,1536]{1,0:T(8,128)(2,1)}, f32[8,1536]{1,0:T(8,128)}) custom-call(s32[14]{0:T(128)} %concatenate.115.info, bf16[256,1536]{1,0:T(8,128)(2,1)} %get-tuple-element.289.cot, f32[256,1536]{1,0:T(8,128)} %get-tuple-element.169.y, ...), custom_call_target="tpu_custom_call" | custom-call | flops 1207959552 | bytes 13000000 | tf_op jit(solution)/shard_map/gate_back/pallas_call | solution.py:549
  311.8 7.4 %all-to-all-start.4 = ((bf16[8,80,384]{2,1,0:T(8,128)(2,1)}), bf16[8,80,384]{2,1,0:T(8,128)(2,1)}, u32[]{:S(2)}, u32[]{:S(2)}) async-start(bf16[8,80,384]{2,1,0:T(8,128)(2,1)} %get-tuple-element.175), calls=%async_computation.4 | async-start | bytes 983040 | tf_op jit(solution)/shard_map/all_to_all | solution.py:1180
  319.2 6.3 gate_in_back.2.rest_0_.part
  330.3 6.6 all-to-all-start.5
  337.2 8.7 %inside_back.2 = (f32[256,1536]{1,0:T(8,128)}, f32[8,1536]{1,0:T(8,128)}, f32[32,256]{1,0:T(8,128)}, f32[256,128]{1,0:T(8,128)}, f32[256,256]{1,0:T(8,128)}) custom-call(bf16[256,1536]{1,0:T(8,128)(2,1)} %get-tuple-element.173.dy, f32[256,1536]{1,0:T(8,128)} %get-tuple-element.161.xa, f32[256,256]{1,0:T(8,128)} %get-tuple-element.162.bca, ...), custom_call_target="tpu_custom_call" | custom-call | flops 402653184 | bytes 4500000 | tf_op jit(solution)/shard_map/inside_back/pallas_call | solution.py:677
  346.6 12.8 %finish_back.2 = (bf16[256,1536]{1,0:T(8,128)(2,1)}, bf16[256,384]{1,0:T(8,128)(2,1)}, f32[16,1536]{1,0:T(8,128)}, f32[16,256]{1,0:T(8,128)}, bf16[16,1536]{1,0:...) custom-call(s32[14]{0:T(128)} %concatenate.115.info, ...), custom_call_target="tpu_custom_call" | custom-call | flops 503316480 | bytes 7500000 | tf_op jit(solution)/shard_map/finish_back/pallas_call | solution.py:829
  362.7 6.0 collective-permute-done.24.edge
  371.6 5.6 convolution_convert_fusion.token
  377.3 7.8 %mixed_back.2 = (f32[256,1536]{1,0:T(8,128)}, f32[8,1536]{1,0:T(8,128)}) custom-call(s32[14]{0:T(128)} %concatenate.115.info, bf16[256,1920]{1,0:T(8,128)(2,1)} %patch.2.dxc, f32[256,1536]{1,0:T(8,128)} %gate_in_back.2.rest_0_.part, bf16[256,1536]{1,0:T(8,128)(2,1)} %get-tuple-element.155.h_ref, bf16[1600,1920]{1,0:T(8,128)(2,1)} %all-gather.5.cloned.1.call-done.rest_0_), custom_call_target="tpu_custom_call" | custom-call | flops 1509949440 | bytes 9000000 | tf_op jit(solution)/shard_map/mixed_back/pallas_call | solution.py:959
  395.0 10.1 %gate_back.3 = (bf16[256,1536]{1,0:T(8,128)(2,1)}, bf16[256,1536]{1,0:T(8,128)(2,1)}, bf16[256,1536]{1,0:T(8,128)(2,1)}, bf16[256,1536]{1,0:T(8,128)(2,1)}, f32[8,1536]{1,0:T(8,128)}) custom-call(s32[14]{0:T(128)} %concatenate.115.info, bf16[256,1536]{1,0:T(8,128)(2,1)} %get-tuple-element.192.cot, f32[256,1536]{1,0:T(8,128)} %get-tuple-element.193.y, ...), custom_call_target="tpu_custom_call" | custom-call | flops 1207959552 | bytes 13000000 | tf_op jit(solution)/shard_map/gate_back/pallas_call | solution.py:549
  420.0 7.2 %all-to-all-start.6 = ((bf16[8,80,384]{2,1,0:T(8,128)(2,1)}), bf16[8,80,384]{2,1,0:T(8,128)(2,1)S(1)}, u32[]{:S(2)}, u32[]{:S(2)}) async-start(bf16[8,80,384]{2,1,0:T(8,128)(2,1)} %get-tuple-element.198), calls=%async_computation.6 | async-start | bytes 983040 | tf_op jit(solution)/shard_map/all_to_all | solution.py:1180
  427.2 6.3 gate_in_back.3.rest_0_.part
  437.8 7.3 %all-to-all-start.7 = ((bf16[8,64,384]{2,1,0:T(8,128)(2,1)}), bf16[8,64,384]{2,1,0:T(8,128)(2,1)S(1)}, u32[]{:S(2)}, u32[]{:S(2)}) async-start(bf16[8,64,384]{2,1,0:T(8,128)(2,1)} %chunk_scan.7), calls=%async_computation.7 | async-start | bytes 786432 | tf_op jit(solution)/shard_map/all_to_all | solution.py:1180
  448.3 8.7 %inside_back.3 = (f32[256,1536]{1,0:T(8,128)}, f32[8,1536]{1,0:T(8,128)}, f32[32,256]{1,0:T(8,128)}, f32[256,128]{1,0:T(8,128)}, f32[256,256]{1,0:T(8,128)}) custom-call(bf16[256,1536]{1,0:T(8,128)(2,1)} %get-tuple-element.196.dy, f32[256,1536]{1,0:T(8,128)} %get-tuple-element.144.xa, f32[256,256]{1,0:T(8,128)} %get-tuple-element.145.bca, ...), custom_call_target="tpu_custom_call" | custom-call | flops 402653184 | bytes 4500000 | tf_op jit(solution)/shard_map/inside_back/pallas_call | solution.py:677
  459.0 12.7 %finish_back.3 = (bf16[256,1536]{1,0:T(8,128)(2,1)}, bf16[256,384]{1,0:T(8,128)(2,1)}, f32[16,1536]{1,0:T(8,128)}, f32[16,256]{1,0:T(8,128)}, bf16[16,1536]{1,0:...) custom-call(s32[14]{0:T(128)} %concatenate.115.info, ...), custom_call_target="tpu_custom_call" | custom-call | flops 503316480 | bytes 7500000 | tf_op jit(solution)/shard_map/finish_back/pallas_call | solution.py:829
  492.8 7.8 %mixed_back.3 = (f32[256,1536]{1,0:T(8,128)}, f32[8,1536]{1,0:T(8,128)}) custom-call(s32[14]{0:T(128)} %concatenate.115.info, bf16[256,1920]{1,0:T(8,128)(2,1)} %patch.3.dxc.token, f32[256,1536]{1,0:T(8,128)} %gate_in_back.3.rest_0_.part, bf16[256,1536]{1,0:T(8,128)(2,1)} %get-tuple-element.290.refs_0_.h_ref, ...), custom_call_target="tpu_custom_call" | custom-call | flops 1509949440 | bytes 9000000 | tf_op jit(solution)/shard_map/mixed_back/pallas_call | solution.py:959
  513.4 13.5 %collective-permute-done.29.rest_1_ = bf16[384,896]{1,0:T(8,128)(2,1)S(1)} collective-permute-done((bf16[384,896]{1,0:T(8,128)(2,1)S(1)}, bf16[384,896]{1,0:T(8,128)(2,1)S(1)}, u32[]{:S(2)}, u32[]{:S(2)}) %collective-permute-start.29) | collective-permute-done | bytes 688160 | tf_op jit(solution)/shard_map/ppermute | solution.py:1016
  530.7 12.8 %collective-permute-done.31.rest_3_ = bf16[384,896]{1,0:T(8,128)(2,1)S(1)} collective-permute-done((bf16[384,896]{1,0:T(8,128)(2,1)}, bf16[384,896]{1,0:T(8,128)(2,1)S(1)}, u32[]{:S(2)}, u32[]{:S(2)}) %collective-permute-start.31) | collective-permute-done | bytes 688160 | tf_op jit(solution)/shard_map/ppermute | solution.py:1016
  558.3 8.4 %collective-permute-done.36.rest_2_ = bf16[448,1024]{1,0:T(8,128)(2,1)S(1)} collective-permute-done((bf16[448,1024]{1,0:T(8,128)(2,1)}, bf16[448,1024]{1,0:T(8,128)(2,1)S(1)}, u32[]{:S(2)}, u32[]{:S(2)}) %collective-permute-start.36) | collective-permute-done | bytes 917536 | tf_op jit(solution)/shard_map/ppermute | solution.py:1016
  566.6 5.7 collective-permute-start.32
  572.3 14.9 %collective-permute-done.37.rest_3_ = bf16[448,1024]{1,0:T(8,128)(2,1)S(1)} collective-permute-done((bf16[448,1024]{1,0:T(8,128)(2,1)}, bf16[448,1024]{1,0:T(8,128)(2,1)S(1)}, u32[]{:S(2)}, u32[]{:S(2)}) %collective-permute-start.37) | collective-permute-done | bytes 917536 | tf_op jit(solution)/shard_map/ppermute | solution.py:1016
  617.7 5.9 collective-permute-start.28
  632.6 11.8 %collective-permute-done.56 = bf16[24,4992]{1,0:T(8,128)(2,1)S(1)} collective-permute-done((bf16[24,4992]{1,0:T(8,128)(2,1)}, bf16[24,4992]{1,0:T(8,128)(2,1)S(1)}, u32[]{:S(2)}, u32[]{:S(2)}) %collective-permute-start.56) | collective-permute-done | bytes 239648 | tf_op jit(solution)/shard_map/ppermute | solution.py:1016
  645.8 5.2 collective-permute-done.54
  651.1 11.6 %collective-permute-done.48.rest_1_ = bf16[96,3072]{1,0:T(8,128)(2,1)S(1)} collective-permute-done((bf16[96,3072]{1,0:T(8,128)(2,1)}, bf16[96,3072]{1,0:T(8,128)(2,1)S(1)}, u32[]{:S(2)}, u32[]{:S(2)}) %collective-permute-start.48) | collective-permute-done | bytes 589856 | tf_op jit(solution)/shard_map/ppermute | solution.py:1016
  662.8 6.5 collective-permute-done.49.rest_2_
  689.2 7.6 %collective-permute-done.58 = f32[24,1536]{1,0:T(8,128)S(1)} collective-permute-done((f32[24,1536]{1,0:T(8,128)S(1)}, f32[24,1536]{1,0:T(8,128)S(1)}, u32[]{:S(2)}, u32[]{:S(2)}) %collective-permute-start.58) | collective-permute-done | bytes 147488 | tf_op jit(solution)/shard_map/ppermute | solution.py:1530
  696.8 6.9 collective-permute-done.59
  (430 shorter events, 292.4 us)
Async XLA Ops:
  7.2 98.4 %all-gather.9.cloned.1.call-start = ((), (), s32[]{:S(2)}) async-start(), calls=%async_computation.20 | async-start | bytes 2949120 | tf_op jit(solution)/shard_map/all_gather | solution.py:1467
  24.6 37.2 %collective-permute-start.13 = (bf16[384,3072]{1,0:T(8,128)(2,1)}, bf16[384,3072]{1,0:T(8,128)(2,1)}, u32[]{:S(2)}, u32[]{:S(2)}) collective-permute-start(bf16[384,3072]{1,0:T(8,128)(2,1)} %get-tuple-element.152), channel_id=1, source_target_pairs={{0,64},{64,0},{1,65},{65,1},{2,66},{66,2},{3,67},{67,3},{4,68},{68... | collective-permute-start | bytes 7077896 | tf_op jit(solution)/shard_map/ppermute | solution.py:1020
  31.8 22.7 %collective-permute-start.3 = (bf16[112,1920]{1,0:T(8,128)(2,1)S(1)}, bf16[112,1920]{1,0:T(8,128)(2,1)S(1)}, u32[]{:S(2)}, u32[]{:S(2)}) collective-permute-start(bf16[112,1920]{1,0:T(8,128)(2,1)S(1)} %pad_maximum_fusion.5.rest_0_), channel_id=1, source_target_pairs={{0,48},{16,0},{32,16},{48,32},{1,49},{17,1},{33,17},{49,33},{2,50}... | collective-permute-start | bytes 1290248 | tf_op jit(solution)/shard_map/ppermute | solution.py:1016
  35.9 18.6 %collective-permute-start.4 = (bf16[112,1920]{1,0:T(8,128)(2,1)S(1)}, bf16[112,1920]{1,0:T(8,128)(2,1)S(1)}, u32[]{:S(2)}, u32[]{:S(2)}) collective-permute-start(bf16[112,1920]{1,0:T(8,128)(2,1)S(1)} %pad_maximum_fusion.5.rest_0_), channel_id=1, source_target_pairs={{0,32},{16,48},{32,0},{48,16},{1,33},{17,49},{33,1},{49,17},{2,34}... | collective-permute-start | bytes 1290248 | tf_op jit(solution)/shard_map/ppermute | solution.py:1016
  35.9 22.0 %collective-permute-start.5 = (bf16[112,1920]{1,0:T(8,128)(2,1)S(1)}, bf16[112,1920]{1,0:T(8,128)(2,1)S(1)}, u32[]{:S(2)}, u32[]{:S(2)}) collective-permute-start(bf16[112,1920]{1,0:T(8,128)(2,1)S(1)} %pad_maximum_fusion.5.rest_0_), channel_id=1, source_target_pairs={{0,16},{16,32},{32,48},{48,0},{1,17},{17,33},{33,49},{49,1},{2,18}... | collective-permute-start | bytes 1290248 | tf_op jit(solution)/shard_map/ppermute | solution.py:1016
  63.9 146.9 %all-gather.5.cloned.1.call-start = ((), (), s32[]{:S(2)}) async-start(), calls=%async_computation.13 | async-start | bytes 7680000 | tf_op jit(solution)/shard_map/all_gather | solution.py:1471
  66.7 192.4 %all-gather.7.cloned.1.call-start = ((), (), s32[]{:S(2)}) async-start(), calls=%async_computation.14 | async-start | bytes 11796480 | tf_op jit(solution)/shard_map/all_gather | solution.py:1472
  72.8 17.2 %collective-permute-start.7 = (bf16[144,1920]{1,0:T(8,128)(2,1)}, bf16[144,1920]{1,0:T(8,128)(2,1)S(1)}, u32[]{:S(2)}, u32[]{:S(2)}) collective-permute-start(bf16[144,1920]{1,0:T(8,128)(2,1)} %pad_maximum_fusion.3.rest_2_), channel_id=1, source_target_pairs={{0,2},{1,3},{2,0},{3,1},{4,6},{5,7},{6,4},{7,5},{8,10},{9,11},{10,... | collective-permute-start | bytes 1658888 | tf_op jit(solution)/shard_map/ppermute | solution.py:1016
  75.6 23.0 %collective-permute-start.8 = (bf16[144,1920]{1,0:T(8,128)(2,1)}, bf16[144,1920]{1,0:T(8,128)(2,1)S(1)}, u32[]{:S(2)}, u32[]{:S(2)}) collective-permute-start(bf16[144,1920]{1,0:T(8,128)(2,1)} %pad_maximum_fusion.3.rest_2_), channel_id=1, source_target_pairs={{0,1},{1,2},{2,3},{3,0},{4,5},{5,6},{6,7},{7,4},{8,9},{9,10},{10,1... | collective-permute-start | bytes 1658888 | tf_op jit(solution)/shard_map/ppermute | solution.py:1016
  76.4 22.2 %collective-permute-start.9 = (bf16[144,1920]{1,0:T(8,128)(2,1)}, bf16[144,1920]{1,0:T(8,128)(2,1)S(1)}, u32[]{:S(2)}, u32[]{:S(2)}) collective-permute-start(bf16[144,1920]{1,0:T(8,128)(2,1)} %pad_maximum_fusion.4.rest_6_), channel_id=1, source_target_pairs={{0,12},{1,13},{2,14},{3,15},{4,0},{5,1},{6,2},{7,3},{8,4},{9,5},{1... | collective-permute-start | bytes 1658888 | tf_op jit(solution)/shard_map/ppermute | solution.py:1016
  76.9 24.5 %collective-permute-start.10 = (bf16[144,1920]{1,0:T(8,128)(2,1)}, bf16[144,1920]{1,0:T(8,128)(2,1)S(1)}, u32[]{:S(2)}, u32[]{:S(2)}) collective-permute-start(bf16[144,1920]{1,0:T(8,128)(2,1)} %pad_maximum_fusion.4.rest_6_), channel_id=1, source_target_pairs={{0,8},{1,9},{2,10},{3,11},{4,12},{5,13},{6,14},{7,15},{8,0},{9,1},... | collective-permute-start | bytes 1658888 | tf_op jit(solution)/shard_map/ppermute | solution.py:1016
  108.1 29.5 %collective-permute-start.14 = (bf16[144,3072]{1,0:T(8,128)(2,1)S(1)}, bf16[144,3072]{1,0:T(8,128)(2,1)S(1)}, u32[]{:S(2)}, u32[]{:S(2)}) collective-permute-start(bf16[144,3072]{1,0:T(8,128)(2,1)S(1)} %pad_maximum_fusion.rest_2_), channel_id=1, source_target_pairs={{0,3},{1,0},{2,1},{3,2},{4,7},{5,4},{6,5},{7,6},{8,11},{9,8},{10,9... | collective-permute-start | bytes 2654216 | tf_op jit(solution)/shard_map/ppermute | solution.py:1016
  133.5 52.1 %collective-permute-start.15 = (bf16[144,3072]{1,0:T(8,128)(2,1)S(1)}, bf16[144,3072]{1,0:T(8,128)(2,1)S(1)}, u32[]{:S(2)}, u32[]{:S(2)}) collective-permute-start(bf16[144,3072]{1,0:T(8,128)(2,1)S(1)} %pad_maximum_fusion.rest_2_), channel_id=1, source_target_pairs={{0,2},{1,3},{2,0},{3,1},{4,6},{5,7},{6,4},{7,5},{8,10},{9,11},{10,... | collective-permute-start | bytes 2654216 | tf_op jit(solution)/shard_map/ppermute | solution.py:1016
  133.6 52.1 %collective-permute-start.16 = (bf16[144,3072]{1,0:T(8,128)(2,1)S(1)}, bf16[144,3072]{1,0:T(8,128)(2,1)}, u32[]{:S(2)}, u32[]{:S(2)}) collective-permute-start(bf16[144,3072]{1,0:T(8,128)(2,1)S(1)} %pad_maximum_fusion.rest_2_), channel_id=1, source_target_pairs={{0,1},{1,2},{2,3},{3,0},{4,5},{5,6},{6,7},{7,4},{8,9},{9,10},{10,1... | collective-permute-start | bytes 2654216 | tf_op jit(solution)/shard_map/ppermute | solution.py:1016
  134.3 51.4 %collective-permute-start.17 = (bf16[144,3072]{1,0:T(8,128)(2,1)S(1)}, bf16[144,3072]{1,0:T(8,128)(2,1)}, u32[]{:S(2)}, u32[]{:S(2)}) collective-permute-start(bf16[144,3072]{1,0:T(8,128)(2,1)S(1)} %pad_maximum_fusion.1.rest_6_), channel_id=1, source_target_pairs={{0,12},{1,13},{2,14},{3,15},{4,0},{5,1},{6,2},{7,3},{8,4},{9,5},{1... | collective-permute-start | bytes 2654216 | tf_op jit(solution)/shard_map/ppermute | solution.py:1016
  135.9 49.8 %collective-permute-start.18 = (bf16[144,3072]{1,0:T(8,128)(2,1)S(1)}, bf16[144,3072]{1,0:T(8,128)(2,1)}, u32[]{:S(2)}, u32[]{:S(2)}) collective-permute-start(bf16[144,3072]{1,0:T(8,128)(2,1)S(1)} %pad_maximum_fusion.1.rest_6_), channel_id=1, source_target_pairs={{0,8},{1,9},{2,10},{3,11},{4,12},{5,13},{6,14},{7,15},{8,0},{9,1},... | collective-permute-start | bytes 2654216 | tf_op jit(solution)/shard_map/ppermute | solution.py:1016
  137.7 48.0 %collective-permute-start.19 = (bf16[144,3072]{1,0:T(8,128)(2,1)S(1)}, bf16[144,3072]{1,0:T(8,128)(2,1)}, u32[]{:S(2)}, u32[]{:S(2)}) collective-permute-start(bf16[144,3072]{1,0:T(8,128)(2,1)S(1)} %pad_maximum_fusion.1.rest_6_), channel_id=1, source_target_pairs={{0,4},{1,5},{2,6},{3,7},{4,8},{5,9},{6,10},{7,11},{8,12},{9,13},{1... | collective-permute-start | bytes 2654216 | tf_op jit(solution)/shard_map/ppermute | solution.py:1016
  157.7 17.9 %all-to-all-start = ((bf16[8,80,384]{2,1,0:T(8,128)(2,1)}), bf16[8,80,384]{2,1,0:T(8,128)(2,1)}, u32[]{:S(2)}, u32[]{:S(2)}) async-start(bf16[8,80,384]{2,1,0:T(8,128)(2,1)} %get-tuple-element.148.msg_in), calls=%async_computation | async-start | bytes 983040 | tf_op jit(solution)/shard_map/all_to_all | solution.py:1180
  259.1 218.2 %reduce-scatter.6.cloned.1.call-start = ((), (), s32[]{:S(2)}) async-start(), calls=%async_computation.15 | async-start | bytes 5898240 | tf_op jit(solution)/shard_map/reduce_scatter | solution.py:1401
  298.4 178.8 %reduce-scatter.8.cloned.1.call-start = ((), (), s32[]{:S(2)}) async-start(), calls=%async_computation.16 | async-start | bytes 5898240 | tf_op jit(solution)/shard_map/reduce_scatter | solution.py:1401
  306.0 19.5 %collective-permute-start.23 = (f32[128,1536]{1,0:T(8,128)}, f32[128,1536]{1,0:T(8,128)S(1)}, u32[]{:S(2)}, u32[]{:S(2)}) collective-permute-start(f32[128,1536]{1,0:T(8,128)} %get-tuple-element.286), channel_id=1, source_target_pairs={{64,65},{65,64},{66,67},{67,66},{68,69},{69,68},{70,71},{71,70},{7... | collective-permute-start | bytes 2359304 | tf_op jit(solution)/shard_map/ppermute | solution.py:1483
  311.8 16.6 %all-to-all-start.4 = ((bf16[8,80,384]{2,1,0:T(8,128)(2,1)}), bf16[8,80,384]{2,1,0:T(8,128)(2,1)}, u32[]{:S(2)}, u32[]{:S(2)}) async-start(bf16[8,80,384]{2,1,0:T(8,128)(2,1)} %get-tuple-element.175), calls=%async_computation.4 | async-start | bytes 983040 | tf_op jit(solution)/shard_map/all_to_all | solution.py:1180
  336.9 140.3 %reduce-scatter.10.cloned.1.call-start = ((), (), s32[]{:S(2)}) async-start(), calls=%async_computation.17 | async-start | bytes 7372800 | tf_op jit(solution)/shard_map/reduce_scatter | solution.py:1401
  377.2 246.6 %reduce-scatter.12.cloned.1.call-start = ((), (), s32[]{:S(2)}) async-start(), calls=%async_computation.18 | async-start | bytes 5898240 | tf_op jit(solution)/shard_map/reduce_scatter | solution.py:1401
  410.2 213.6 %reduce-scatter.14.cloned.1.call-start = ((), (), s32[]{:S(2)}) async-start(), calls=%async_computation.19 | async-start | bytes 5898240 | tf_op jit(solution)/shard_map/reduce_scatter | solution.py:1401
  437.8 20.4 %all-to-all-start.7 = ((bf16[8,64,384]{2,1,0:T(8,128)(2,1)}), bf16[8,64,384]{2,1,0:T(8,128)(2,1)S(1)}, u32[]{:S(2)}, u32[]{:S(2)}) async-start(bf16[8,64,384]{2,1,0:T(8,128)(2,1)} %chunk_scan.7), calls=%async_computation.7 | async-start | bytes 786432 | tf_op jit(solution)/shard_map/all_to_all | solution.py:1180
  500.6 48.2 %collective-permute-start.27 = (f32[256,1536]{1,0:T(8,128)}, f32[256,1536]{1,0:T(8,128)S(1)}, u32[]{:S(2)}, u32[]{:S(2)}) collective-permute-start(f32[256,1536]{1,0:T(8,128)} %get-tuple-element.215.own), channel_id=1, source_target_pairs={{0,64},{64,0},{1,65},{65,1},{2,66},{66,2},{3,67},{67,3},{4,68},{68... | collective-permute-start | bytes 4718600 | tf_op jit(solution)/shard_map/ppermute | solution.py:1020
  507.6 38.8 %collective-permute-start.35 = (bf16[448,1024]{1,0:T(8,128)(2,1)}, bf16[448,1024]{1,0:T(8,128)(2,1)S(1)}, u32[]{:S(2)}, u32[]{:S(2)}) collective-permute-start(bf16[448,1024]{1,0:T(8,128)(2,1)} %get-tuple-element.236), channel_id=1, source_target_pairs={{0,1},{1,2},{2,3},{3,0},{4,5},{5,6},{6,7},{7,4},{8,9},{9,10},{10,1... | collective-permute-start | bytes 2752520 | tf_op jit(solution)/shard_map/ppermute | solution.py:1016
  508.7 18.3 %collective-permute-start.29 = (bf16[384,896]{1,0:T(8,128)(2,1)S(1)}, bf16[384,896]{1,0:T(8,128)(2,1)S(1)}, u32[]{:S(2)}, u32[]{:S(2)}) collective-permute-start(bf16[384,896]{1,0:T(8,128)(2,1)S(1)} %copy-done.65), channel_id=1, source_target_pairs={{0,4},{1,5},{2,6},{3,7},{4,8},{5,9},{6,10},{7,11},{8,12},{9,13},{1... | collective-permute-start | bytes 2064392 | tf_op jit(solution)/shard_map/ppermute | solution.py:1016
  510.2 19.8 %collective-permute-start.30 = (bf16[384,896]{1,0:T(8,128)(2,1)S(1)}, bf16[384,896]{1,0:T(8,128)(2,1)S(1)}, u32[]{:S(2)}, u32[]{:S(2)}) collective-permute-start(bf16[384,896]{1,0:T(8,128)(2,1)S(1)} %copy-done.64), channel_id=1, source_target_pairs={{0,8},{1,9},{2,10},{3,11},{4,12},{5,13},{6,14},{7,15},{8,0},{9,1},... | collective-permute-start | bytes 2064392 | tf_op jit(solution)/shard_map/ppermute | solution.py:1016
  510.9 32.6 %collective-permute-start.31 = (bf16[384,896]{1,0:T(8,128)(2,1)}, bf16[384,896]{1,0:T(8,128)(2,1)S(1)}, u32[]{:S(2)}, u32[]{:S(2)}) collective-permute-start(bf16[384,896]{1,0:T(8,128)(2,1)} %get-tuple-element.219), channel_id=1, source_target_pairs={{0,12},{1,13},{2,14},{3,15},{4,0},{5,1},{6,2},{7,3},{8,4},{9,5},{1... | collective-permute-start | bytes 2064392 | tf_op jit(solution)/shard_map/ppermute | solution.py:1016
  527.0 66.5 %collective-permute-start.41 = (bf16[96,4992]{1,0:T(8,128)(2,1)}, bf16[96,4992]{1,0:T(8,128)(2,1)S(1)}, u32[]{:S(2)}, u32[]{:S(2)}) collective-permute-start(bf16[96,4992]{1,0:T(8,128)(2,1)} %get-tuple-element.243), channel_id=1, source_target_pairs={{0,4},{1,5},{2,6},{3,7},{4,8},{5,9},{6,10},{7,11},{8,12},{9,13},{1... | collective-permute-start | bytes 2875400 | tf_op jit(solution)/shard_map/ppermute | solution.py:1016
  530.0 65.1 %collective-permute-start.42 = (bf16[96,4992]{1,0:T(8,128)(2,1)}, bf16[96,4992]{1,0:T(8,128)(2,1)S(1)}, u32[]{:S(2)}, u32[]{:S(2)}) collective-permute-start(bf16[96,4992]{1,0:T(8,128)(2,1)} %get-tuple-element.244), channel_id=1, source_target_pairs={{0,8},{1,9},{2,10},{3,11},{4,12},{5,13},{6,14},{7,15},{8,0},{9,1},... | collective-permute-start | bytes 2875400 | tf_op jit(solution)/shard_map/ppermute | solution.py:1016
  543.5 23.2 %collective-permute-start.36 = (bf16[448,1024]{1,0:T(8,128)(2,1)}, bf16[448,1024]{1,0:T(8,128)(2,1)S(1)}, u32[]{:S(2)}, u32[]{:S(2)}) collective-permute-start(bf16[448,1024]{1,0:T(8,128)(2,1)} %get-tuple-element.237), channel_id=1, source_target_pairs={{0,2},{1,3},{2,0},{3,1},{4,6},{5,7},{6,4},{7,5},{8,10},{9,11},{10,... | collective-permute-start | bytes 2752520 | tf_op jit(solution)/shard_map/ppermute | solution.py:1016
  546.4 40.7 %collective-permute-start.37 = (bf16[448,1024]{1,0:T(8,128)(2,1)}, bf16[448,1024]{1,0:T(8,128)(2,1)S(1)}, u32[]{:S(2)}, u32[]{:S(2)}) collective-permute-start(bf16[448,1024]{1,0:T(8,128)(2,1)} %get-tuple-element.238), channel_id=1, source_target_pairs={{0,3},{1,0},{2,1},{3,2},{4,7},{5,4},{6,5},{7,6},{8,11},{9,8},{10,9... | collective-permute-start | bytes 2752520 | tf_op jit(solution)/shard_map/ppermute | solution.py:1016
  548.8 48.3 %collective-permute-start.43 = (bf16[96,4992]{1,0:T(8,128)(2,1)}, bf16[96,4992]{1,0:T(8,128)(2,1)}, u32[]{:S(2)}, u32[]{:S(2)}) collective-permute-start(bf16[96,4992]{1,0:T(8,128)(2,1)} %get-tuple-element.245), channel_id=1, source_target_pairs={{0,12},{1,13},{2,14},{3,15},{4,0},{5,1},{6,2},{7,3},{8,4},{9,5},{1... | collective-permute-start | bytes 2875400 | tf_op jit(solution)/shard_map/ppermute | solution.py:1016
  566.6 33.1 %collective-permute-start.32 = (bf16[96,896]{1,0:T(8,128)(2,1)}, bf16[96,896]{1,0:T(8,128)(2,1)}, u32[]{:S(2)}, u32[]{:S(2)}) collective-permute-start(bf16[96,896]{1,0:T(8,128)(2,1)} %get-tuple-element.222), channel_id=1, source_target_pairs={{0,1},{1,2},{2,3},{3,0},{4,5},{5,6},{6,7},{7,4},{8,9},{9,10},{10,1... | collective-permute-start | bytes 516104 | tf_op jit(solution)/shard_map/ppermute | solution.py:1016
  613.6 15.8 %collective-permute-start.45 = (bf16[56,1920]{1,0:T(8,128)(2,1)}, bf16[56,1920]{1,0:T(8,128)(2,1)S(1)}, u32[]{:S(2)}, u32[]{:S(2)}) collective-permute-start(bf16[56,1920]{1,0:T(8,128)(2,1)} %get-tuple-element.249), channel_id=1, source_target_pairs={{0,16},{16,32},{32,48},{48,0},{1,17},{17,33},{33,49},{49,1},{2,18}... | collective-permute-start | bytes 645128 | tf_op jit(solution)/shard_map/ppermute | solution.py:1016
  617.7 68.5 %collective-permute-start.28 = (f32[128,1536]{1,0:T(8,128)}, f32[128,1536]{1,0:T(8,128)}, u32[]{:S(2)}, u32[]{:S(2)}) collective-permute-start(f32[128,1536]{1,0:T(8,128)} %get-tuple-element.288), channel_id=1, source_target_pairs={{0,1},{1,0},{2,3},{3,2},{4,5},{5,4},{6,7},{7,6},{8,9},{9,8},{10,11... | collective-permute-start | bytes 2359304 | tf_op jit(solution)/shard_map/ppermute | solution.py:1483
  623.7 20.7 %collective-permute-start.56 = (bf16[24,4992]{1,0:T(8,128)(2,1)}, bf16[24,4992]{1,0:T(8,128)(2,1)S(1)}, u32[]{:S(2)}, u32[]{:S(2)}) collective-permute-start(bf16[24,4992]{1,0:T(8,128)(2,1)} %get-tuple-element.261), channel_id=1, source_target_pairs={{0,3},{1,0},{2,1},{3,2},{4,7},{5,4},{6,5},{7,6},{8,11},{9,8},{10,9... | collective-permute-start | bytes 718856 | tf_op jit(solution)/shard_map/ppermute | solution.py:1016
  627.3 18.5 %collective-permute-start.55 = (bf16[24,4992]{1,0:T(8,128)(2,1)S(1)}, bf16[24,4992]{1,0:T(8,128)(2,1)S(1)}, u32[]{:S(2)}, u32[]{:S(2)}) collective-permute-start(bf16[24,4992]{1,0:T(8,128)(2,1)S(1)} %copy-done.69), channel_id=1, source_target_pairs={{0,1},{1,2},{2,3},{3,0},{4,5},{5,6},{6,7},{7,4},{8,9},{9,10},{10,1... | collective-permute-start | bytes 718856 | tf_op jit(solution)/shard_map/ppermute | solution.py:1016
  629.4 21.6 %collective-permute-start.54 = (bf16[24,4992]{1,0:T(8,128)(2,1)S(1)}, bf16[24,4992]{1,0:T(8,128)(2,1)S(1)}, u32[]{:S(2)}, u32[]{:S(2)}) collective-permute-start(bf16[24,4992]{1,0:T(8,128)(2,1)S(1)} %copy-done.68), channel_id=1, source_target_pairs={{0,2},{1,3},{2,0},{3,1},{4,6},{5,7},{6,4},{7,5},{8,10},{9,11},{10,... | collective-permute-start | bytes 718856 | tf_op jit(solution)/shard_map/ppermute | solution.py:1016
  629.5 33.2 %collective-permute-start.48 = (bf16[96,3072]{1,0:T(8,128)(2,1)}, bf16[96,3072]{1,0:T(8,128)(2,1)S(1)}, u32[]{:S(2)}, u32[]{:S(2)}) collective-permute-start(bf16[96,3072]{1,0:T(8,128)(2,1)} %get-tuple-element.252), channel_id=1, source_target_pairs={{0,1},{1,2},{2,3},{3,0},{4,5},{5,6},{6,7},{7,4},{8,9},{9,10},{10,1... | collective-permute-start | bytes 1769480 | tf_op jit(solution)/shard_map/ppermute | solution.py:1016
  644.4 24.9 %collective-permute-start.49 = (bf16[96,3072]{1,0:T(8,128)(2,1)S(1)}, bf16[96,3072]{1,0:T(8,128)(2,1)S(1)}, u32[]{:S(2)}, u32[]{:S(2)}) collective-permute-start(bf16[96,3072]{1,0:T(8,128)(2,1)S(1)} %copy-done.67), channel_id=1, source_target_pairs={{0,2},{1,3},{2,0},{3,1},{4,6},{5,7},{6,4},{7,5},{8,10},{9,11},{10,... | collective-permute-start | bytes 1769480 | tf_op jit(solution)/shard_map/ppermute | solution.py:1016
  645.8 23.5 %collective-permute-start.50 = (bf16[96,3072]{1,0:T(8,128)(2,1)S(1)}, bf16[96,3072]{1,0:T(8,128)(2,1)S(1)}, u32[]{:S(2)}, u32[]{:S(2)}) collective-permute-start(bf16[96,3072]{1,0:T(8,128)(2,1)S(1)} %copy-done.66), channel_id=1, source_target_pairs={{0,3},{1,0},{2,1},{3,2},{4,7},{5,4},{6,5},{7,6},{8,11},{9,8},{10,9... | collective-permute-start | bytes 1769480 | tf_op jit(solution)/shard_map/ppermute | solution.py:1016
  651.0 27.4 %collective-permute-start.47 = (f32[16,1792]{1,0:T(8,128)S(1)}, f32[16,1792]{1,0:T(8,128)S(1)}, u32[]{:S(2)}, u32[]{:S(2)}) collective-permute-start(f32[16,1792]{1,0:T(8,128)S(1)} %slice_select_fusion.7), channel_id=1, source_target_pairs={{0,64},{64,0},{1,65},{65,1},{2,66},{66,2},{3,67},{67,3},{4,68},{68... | collective-permute-start | bytes 344072 | tf_op jit(solution)/shard_map/ppermute | solution.py:1020
  684.1 20.3 %collective-permute-start.57 = (f32[24,3456]{1,0:T(8,128)S(1)}, f32[24,3456]{1,0:T(8,128)S(1)}, u32[]{:S(2)}, u32[]{:S(2)}) collective-permute-start(f32[24,3456]{1,0:T(8,128)S(1)} %slice_select_fusion.3), channel_id=1, source_target_pairs={{0,64},{64,0},{1,65},{65,1},{2,66},{66,2},{3,67},{67,3},{4,68},{68... | collective-permute-start | bytes 995336 | tf_op jit(solution)/shard_map/ppermute | solution.py:1020
  686.2 17.6 %collective-permute-start.59 = (f32[24,1536]{1,0:T(8,128)S(1)}, f32[24,1536]{1,0:T(8,128)S(1)}, u32[]{:S(2)}, u32[]{:S(2)}) collective-permute-start(f32[24,1536]{1,0:T(8,128)S(1)} %get-tuple-element.296), channel_id=1, source_target_pairs={{0,64},{1,0},{2,65},{3,1},{4,66},{5,2},{6,67},{7,3},{8,68},{9,4},{... | collective-permute-start | bytes 442376 | tf_op jit(solution)/shard_map/ppermute | solution.py:1530
  (100 other events, 1039.9 us)
Sparse Core Ops, SparseCore 0:
  64.1 32.6 all-gather.8
  98.4 64.5 all-gather.4
  164.7 92.5 all-gather.6
  298.6 50.3 reduce-scatter.5
  351.2 50.9 reduce-scatter.7
  404.5 60.4 reduce-scatter.9
  467.4 50.8 reduce-scatter.11
  520.8 50.9 reduce-scatter.13

commit v4 on v3

--- a/solution.py
+++ b/solution.py
@@ -31,7 +31,7 @@
 PIECE = 48
 STATE_HALF = STATE // 2
 MESSAGE = STATE_HALF + 16
-SMALL = 64
+SMALL = 32
 EPSILON = 1e-05
 PRECISE = lax.Precision.HIGHEST
 F32 = jnp.float32
@@ -512,63 +512,77 @@
 def gate_back_body(weight, info, cot, y, gate, gain, branch, scale_ref, *rest):
     refs = len(weight.arrays)
     w_refs, rest = rest[:refs], rest[refs:]
-    bg_ref, dy_ref, dz_ref, n_ref, dgain_ref, buffer, sems, dn = rest
-    weight.start(w_refs, info, buffer, sems)
-    bg = usable_rows(info) * cot[...].astype(F32)
-    bg_ref[...] = bg.astype(BF16)
+    bg_ref, dy_ref, dz_ref, grad_ref, dgain_ref, buffer, sems, inner_ref = rest
+    b = pl.program_id(0)
     scale = scale_ref[:, :1]
-    inner = jnp.sum(bg_ref[...].astype(F32) * branch[...].astype(F32), axis=1, keepdims=True)
-    inner = inner * scale * scale / INNER
-    for b in range(4):
-        rows = weight.wait(w_refs, info, b, buffer, sems)
-        dn[...] = dot_nt(bg_ref[...], buffer[rows, :])
-
-        def one(i, _, rows=rows):
-            here = pl.ds(pl.multiple_of(i * LANES, LANES), LANES)
-            lanes = pl.ds(pl.multiple_of(rows.start + i * LANES, LANES), LANES)
-            z = gate[:, lanes]
-            sig = sigmoid(z)
-            silu = z * sig
-            y_here = y[:, lanes]
-            gated = y_here * silu
-            d_norm = dn[:, here]
-            gained = scale * gain[:, lanes]
-            n_ref[:, lanes] = (gated * gained).astype(BF16)
-            d_gated = d_norm * gained - gated * inner
-            total = jnp.sum(d_norm * gated * scale, axis=0, keepdims=True)
-            dgain_ref[:, lanes] = jnp.broadcast_to(total, (8, LANES))
-            dy_ref[:, lanes] = (d_gated * silu).astype(BF16)
-            dz_ref[:, lanes] = (d_gated * y_here * sig * (1.0 + z * (1.0 - sig))).astype(BF16)
-            return 0
-
-        lax.fori_loop(0, SHARD // LANES, one, 0)
-
-
-def gate_back(info, cot, y, gate, gain, branch, scale, weight):
-    wide, local = whole((ROWS, WIDTH)), whole((ROWS, LOCAL))
+
+    @pl.when(b == 0)
+    def _():
+        weight.start(w_refs, info, buffer, sems)
+        bg = (usable_rows(info) * cot[...].astype(F32)).astype(BF16)
+        bg_ref[...] = bg
+        inner = jnp.sum(bg.astype(F32) * branch[...].astype(F32), axis=1, keepdims=True)
+        inner_ref[...] = jnp.broadcast_to(inner * scale * scale / INNER, (ROWS, LANES))
+        for n in range(4):
+            weight.wait(w_refs, info, n, buffer, sems)
+
+    inner = inner_ref[:, :1]
+    bg = bg_ref[...]
+    d_norms = dot_nt(bg, buffer[pl.ds(pl.multiple_of(b * SHARD, SHARD), SHARD), :])
+    norms = []
+    for i in range(SHARD // LANES):
+        lanes = slice(i * LANES, (i + 1) * LANES)
+        z = gate[:, lanes]
+        sig = sigmoid(z)
+        silu = z * sig
+        y_here = y[:, lanes]
+        gated = y_here * silu
+        d_norm = d_norms[:, lanes]
+        gained = scale * gain[:, lanes]
+        norms.append((gated * gained).astype(BF16))
+        d_gated = d_norm * gained - gated * inner
+        total = jnp.sum(d_norm * gated * scale, axis=0, keepdims=True)
+        dgain_ref[:, lanes] = jnp.broadcast_to(total, (8, LANES))
+        dy_ref[:, lanes] = (d_gated * silu).astype(BF16)
+        dz_ref[:, lanes] = (d_gated * y_here * sig * (1.0 + z * (1.0 - sig))).astype(BF16)
+    norm = jnp.concatenate(norms, axis=1)
+    grad_ref[...] = dot(norm.T, bg).astype(BF16) if grad_ref.shape[1] == WIDTH else norm.T
+
+
+def gate_back(info, cot, y, gate, gain, branch, scale, weight, with_grad):
+    wide, local = whole((ROWS, WIDTH)), columns(ROWS, SHARD)
+    grad_width = WIDTH if with_grad else ROWS
     return pl.pallas_call(
         functools.partial(gate_back_body, weight),
+        grid=(4,),
         out_shape=(
             shape((ROWS, WIDTH), BF16),
             shape((ROWS, LOCAL), BF16),
             shape((ROWS, LOCAL), BF16),
-            shape((ROWS, LOCAL), BF16),
+            shape((LOCAL, grad_width), BF16),
             shape((8, LOCAL)),
         ),
-        in_specs=[SMEM, wide, local, local, whole((1, LOCAL)), wide, whole((ROWS, LANES))]
+        in_specs=[SMEM, wide, local, local, columns(1, SHARD), wide, whole((ROWS, LANES))]
         + weight.specs(),
-        out_specs=(wide, local, local, local, whole((8, LOCAL))),
-        scratch_shapes=weight.scratch() + [pltpu.VMEM((ROWS, SHARD), F32)],
+        out_specs=(
+            wide,
+            local,
+            local,
+            pl.BlockSpec((SHARD, grad_width), lambda b: (b, 0)),
+            columns(8, SHARD),
+        ),
+        scratch_shapes=weight.scratch() + [pltpu.VMEM((ROWS, LANES), F32)],
         compiler_params=params(),
         cost_estimate=pl.CostEstimate(
-            flops=2 * ROWS * WIDTH * LOCAL, bytes_accessed=13_000_000, transcendentals=800_000
+            flops=4 * ROWS * WIDTH * LOCAL, bytes_accessed=17_000_000, transcendentals=800_000
         ),
         name="gate_back",
     )(info, cot, y, gate, gain, branch, scale, *weight.arrays)
 
 
-def own_grad_body(dy, bca, cum, msg_in, own1_ref, msg_ref, ct, grow):
+def own_grad_body(dy, bca, cum, msg_in, dz, normed, own1_ref, msg_ref, grad_ref, ct, grow):
     g = pl.program_id(0)
+    grad_ref[...] = dot(normed[...].T, dz[...]).astype(BF16)
 
     @pl.when(g == 0)
     def _():
@@ -586,23 +600,31 @@
         msg_ref[r, STATE_HALF:, :] = msg_in[r, STATE_HALF:, :]
 
 
-def own_grad(dy, bca, cum, msg):
+def own_grad(dy, bca, cum, msg, dz, normed):
     return pl.pallas_call(
         own_grad_body,
         grid=(GROUPS,),
         out_shape=(
             shape((GROUPS, STATE, BLOCK)),
             shape((CHUNKS, MESSAGE, BLOCK), BF16),
-        ),
-        in_specs=[columns(ROWS, BLOCK), whole((ROWS, 256)), whole((ROWS, LANES)), MESSAGES],
-        out_specs=(grouped(STATE), MESSAGES),
+            shape((WIDTH, LOCAL), BF16),
+        ),
+        in_specs=[
+            columns(ROWS, BLOCK),
+            whole((ROWS, 256)),
+            whole((ROWS, LANES)),
+            MESSAGES,
+            whole((ROWS, LOCAL)),
+            columns(ROWS, SHARD),
+        ],
+        out_specs=(grouped(STATE), MESSAGES, pl.BlockSpec((SHARD, LOCAL), lambda b: (b, 0))),
         scratch_shapes=[pltpu.VMEM((STATE, ROWS), BF16), pltpu.VMEM((ROWS, LANES), F32)],
         compiler_params=params(),
         cost_estimate=pl.CostEstimate(
-            flops=2 * ROWS * STATE * LOCAL, bytes_accessed=2_500_000, transcendentals=0
+            flops=2 * ROWS * WIDTH * LOCAL, bytes_accessed=8_000_000, transcendentals=0
         ),
         name="own_grad",
-    )(dy, bca, cum, msg)
+    )(dy, bca, cum, msg, dz, normed)
 
 
 def inside_back_body(
@@ -777,9 +799,10 @@
         dbc_sum[here, :STATE] += dot_nt((x * tail_step).astype(BF16), lam_q)
         dbc_sum[here, STATE:] += dot_nt(dy_grow, state_q)
         last = jnp.sum(lams[q] * states[q], axis=0, keepdims=True) * ends[q]
-        end_sum[8 * q : 8 * q + 8, :] += exact_dot(
-            jnp.broadcast_to(last, (8, BLOCK)), sums.astype(F32)
-        )
+        high = last.astype(BF16).astype(F32)
+        both = jnp.where(row_of((16, BLOCK)) == 0, high, last - high).astype(BF16)
+        both = dot(both, sums)
+        end_sum[8 * q : 8 * q + 8, :] += both[0:1] + both[1:2]
     d_in, d_par = conv_back(
         jnp.concatenate(d_x, axis=0), mixed[...], halo[...], cpar[...], keep, ext, ext_d
     )
@@ -896,28 +919,34 @@
     )
 
 
-def gate_in_back_body(weight, info, dz, *rest):
+def gate_in_back_body(weight, info, dz, token, *rest):
     refs = len(weight.arrays)
     w_refs, (out_ref, buffer, sems) = rest[:refs], rest[refs:]
-    weight.start(w_refs, info, buffer, sems)
-    for b in range(4):
-        rows = weight.wait(w_refs, info, b, buffer, sems)
-        out_ref[:, rows] = dot_nt(dz[...], buffer[rows, :])
-
-
-def gate_in_back(info, dz, weight):
+
+    @pl.when(pl.program_id(0) == 0)
+    def _():
+        weight.start(w_refs, info, buffer, sems)
+        for n in range(4):
+            weight.wait(w_refs, info, n, buffer, sems)
+
+    rows = pl.ds(pl.multiple_of(pl.program_id(0) * SHARD, SHARD), SHARD)
+    out_ref[...] = dot_nt(dz[...], buffer[rows, :])
+
+
+def gate_in_back(info, dz, weight, token):
     return pl.pallas_call(
         functools.partial(gate_in_back_body, weight),
+        grid=(4,),
         out_shape=shape((ROWS, WIDTH)),
-        in_specs=[SMEM, whole((ROWS, LOCAL))] + weight.specs(),
-        out_specs=whole((ROWS, WIDTH)),
+        in_specs=[SMEM, whole((ROWS, LOCAL)), ANYWHERE] + weight.specs(),
+        out_specs=columns(ROWS, SHARD),
         scratch_shapes=weight.scratch(),
         compiler_params=params(),
         cost_estimate=pl.CostEstimate(
             flops=2 * ROWS * WIDTH * LOCAL, bytes_accessed=7_000_000, transcendentals=0
         ),
         name="gate_in_back",
-    )(info, dz, *weight.arrays)
+    )(info, dz, token, *weight.arrays)
 
 
 def patch_body(dmx, dmbc, tailx, tailbc, edge, token, dxc_ref):
@@ -941,38 +970,59 @@
     )(*arrays, token)
 
 
-def mixed_back_body(weight, tokens, info, dxc, part, h_ref, *rest):
+def mixed_back_body(weight, tokens, info, dxc, part, h_ref, normed, *rest):
     refs = len(weight.arrays)
-    w_refs, (out_ref, dgain_ref, buffer, sems) = rest[:refs], rest[refs + tokens :]
-    weight.start(w_refs, info, buffer, sems)
-    h = h_ref[...].astype(F32)
-    scale = lax.rsqrt(jnp.mean(h * h, axis=1, keepdims=True) + EPSILON)
-    for b in range(4):
-        rows = weight.wait(w_refs, info, b, buffer, sems)
-        d_norm = part[:, rows] + dot_nt(dxc[...], buffer[rows, :])
-        out_ref[:, rows] = d_norm
-        total = jnp.sum(d_norm * h_ref[:, rows].astype(F32) * scale, axis=0, keepdims=True)
-        dgain_ref[:, rows] = jnp.broadcast_to(total, (8, SHARD))
-
-
-def mixed_back(info, dxc, part, h, weight, tokens):
+    w_refs, rest = rest[:refs], rest[refs + tokens :]
+    (out_ref, dgain_ref, *grad_ref), (buffer, sems, scale_ref) = rest[:-3], rest[-3:]
+    b = pl.program_id(0)
+    block = pl.ds(pl.multiple_of(b * SHARD, SHARD), SHARD)
+
+    @pl.when(b == 0)
+    def _():
+        weight.start(w_refs, info, buffer, sems)
+        h = h_ref[...].astype(F32)
+        scale = lax.rsqrt(jnp.mean(h * h, axis=1, keepdims=True) + EPSILON)
+        scale_ref[...] = jnp.broadcast_to(scale, (ROWS, LANES))
+
+    for ref in grad_ref:
+        ref[...] = dot(normed[...].T, dxc[...]).astype(BF16)
+
+    @pl.when(b == 0)
+    def _():
+        for n in range(4):
+            weight.wait(w_refs, info, n, buffer, sems)
+
+    d_norm = part[...] + dot_nt(dxc[...], buffer[block, :])
+    out_ref[...] = d_norm
+    total = jnp.sum(d_norm * h_ref[:, block].astype(F32) * scale_ref[:, :1], axis=0, keepdims=True)
+    dgain_ref[...] = jnp.broadcast_to(total, (8, SHARD))
+
+
+def mixed_back(info, dxc, part, h, normed, weight, with_grad, tokens):
+    wide, local = whole((ROWS, WIDTH)), columns(ROWS, SHARD)
+    outs = [shape((ROWS, WIDTH)), shape((8, WIDTH))]
+    specs = [local, columns(8, SHARD)]
+    if with_grad:
+        outs.append(shape((WIDTH, PACKED), BF16))
+        specs.append(pl.BlockSpec((SHARD, PACKED), lambda b: (b, 0)))
     return pl.pallas_call(
         functools.partial(mixed_back_body, weight, len(tokens)),
-        out_shape=(shape((ROWS, WIDTH)), shape((8, WIDTH))),
-        in_specs=[SMEM, whole((ROWS, PACKED)), whole((ROWS, WIDTH)), whole((ROWS, WIDTH))]
+        grid=(4,),
+        out_shape=outs,
+        in_specs=[SMEM, whole((ROWS, PACKED)), local, wide, local]
         + weight.specs()
         + [ANYWHERE] * len(tokens),
-        out_specs=(whole((ROWS, WIDTH)), whole((8, WIDTH))),
-        scratch_shapes=weight.scratch(),
+        out_specs=specs,
+        scratch_shapes=weight.scratch() + [pltpu.VMEM((ROWS, LANES), F32)],
         compiler_params=params(),
         cost_estimate=pl.CostEstimate(
-            flops=2 * ROWS * WIDTH * PACKED, bytes_accessed=9_000_000, transcendentals=0
+            flops=4 * ROWS * WIDTH * PACKED, bytes_accessed=14_000_000, transcendentals=0
         ),
         name="mixed_back",
-    )(info, dxc, part, h, *weight.arrays, *tokens)
-
-
-def norm_back_body(own, came, h_ref, cot, gain, token, dh_ref, low_ref):
+    )(info, dxc, part, h, normed, *weight.arrays, *tokens)
+
+
+def norm_back_body(own, came, h_ref, cot, gain, dh_ref, low_ref):
     h = h_ref[...].astype(F32)
     scale = lax.rsqrt(jnp.mean(h * h, axis=1, keepdims=True) + EPSILON)
     d_norm = own[...] + came[...]
@@ -982,18 +1032,18 @@
     low_ref[...] = dh.astype(BF16)
 
 
-def norm_back(own, came, h, cot, gain, token):
+def norm_back(own, came, h, cot, gain):
     rows = pl.BlockSpec((HALF // 2, WIDTH), lambda i: (i, 0))
     return pl.pallas_call(
         norm_back_body,
         grid=(4,),
         out_shape=(shape((ROWS, WIDTH)), shape((ROWS, WIDTH), BF16)),
-        in_specs=[rows] * 4 + [whole((1, WIDTH)), ANYWHERE],
+        in_specs=[rows] * 4 + [whole((1, WIDTH))],
         out_specs=(rows, rows),
         compiler_params=params(),
         cost_estimate=pl.CostEstimate(flops=3_000_000, bytes_accessed=8_000_000, transcendentals=0),
         name="norm_back",
-    )(own, came, h, cot, gain, token)
+    )(own, came, h, cot, gain)
 
 
 def z_shift(r):
@@ -1072,69 +1122,91 @@
     return [terms[0]] + [send(terms[r], axis, r) for r in range(1, 4)]
 
 
-def terms_body(axis, width, info, source, other, *rest):
-    small, outs, total = rest[:-5], rest[-5:-1], rest[-1]
-    total[...] = dot(source[...], other[...])
+def terms_body(axis, cuts, stacked, info, *rest):
+    factors, rest = rest[: 2 * len(cuts)], rest[2 * len(cuts) :]
+    small, outs, total = rest[:-2] if stacked else rest[:-5], rest[-5:-1], rest[-1]
+    column = 0
+    for n, cols in enumerate(cuts):
+        there = slice(column, column + cols.stop - cols.start)
+        total[:, there] = dot(factors[2 * n][...], factors[2 * n + 1][:, cols])
+        column = there.stop
     count = 96 if axis == "y" else 24
+    starts = [z * SHARD for z in range(4)]
+    if axis == "x":
+        starts = [start + y * 96 for start in starts for y in range(4)]
     for r in range(4):
-        first = lax.rem(info[11 if axis == "y" else 12] + r, 4) * count
-        starts = [z * SHARD for z in range(4)]
-        if axis == "x":
-            starts = [start + y * 96 for start in starts for y in range(4)]
+        first = r * count
+        if not stacked:
+            first = lax.rem(info[11 if axis == "y" else 12] + r, 4) * count
         parts = [total[pl.ds(pl.multiple_of(start + first, 8), count), :] for start in starts]
-        outs[r][:SHARD, :] = jnp.concatenate(parts, axis=0).astype(BF16)
+        out = rest[-2].at[r] if stacked else outs[r]
+        out[:SHARD, :] = jnp.concatenate(parts, axis=0).astype(BF16)
         for ref in small:
-            outs[r][SHARD:, :] = ref[...]
-
-
-def terms(info, axis, source, other, small=()):
-    width = other.shape[1]
+            out[SHARD:, :] = ref[...]
+
+
+def four(dims, stacked):
+    if stacked:
+        return shape((4, *dims), BF16), whole((4, *dims))
+    return [shape(dims, BF16)] * 4, [whole(dims)] * 4
+
+
+def terms(info, axis, products, small=(), stacked=False):
+    cuts = [cols for _, _, cols in products]
+    width = sum(cols.stop - cols.start for cols in cuts)
     rows = SHARD + sum(v.shape[0] for v in small)
-    arrays = (source, other, *small)
-    return pl.pallas_call(
-        functools.partial(terms_body, axis, width),
-        out_shape=[shape((rows, width), BF16)] * 4,
+    arrays = [v for left, right, _ in products for v in (left, right)] + list(small)
+    outs, specs = four((rows, width), stacked)
+    return pl.pallas_call(
+        functools.partial(terms_body, axis, cuts, stacked),
+        out_shape=outs,
         in_specs=[SMEM] + [whole(v.shape) for v in arrays],
-        out_specs=[whole((rows, width))] * 4,
+        out_specs=specs,
         scratch_shapes=[pltpu.VMEM((4 * SHARD, width), F32)],
         compiler_params=params(),
         cost_estimate=pl.CostEstimate(
-            flops=8 * SHARD * ROWS * width, bytes_accessed=5_000_000, transcendentals=0
+            flops=8 * SHARD * ROWS * width, bytes_accessed=8_000_000, transcendentals=0
         ),
         name="terms",
     )(info, *arrays)
 
 
-def fold_body(slot, counts, outer, inner, rest_rows, info, *rest):
+def fold_body(slot, counts, outer, inner, rest_rows, stacked, info, *rest):
     refs, outs, total = rest[: sum(counts)], rest[sum(counts) + 1 : -1], rest[-1]
     column = 0
     for count in counts:
         arrays, refs = refs[:count], refs[count:]
-        cols = slice(column, column + arrays[0].shape[1])
-        total[:, cols] = summed([a[...] for a in arrays]) if count == 4 else arrays[0][...].astype(F32)
+        cols = slice(column, column + arrays[0].shape[-1])
+        if count == 4:
+            total[:, cols] = summed([a[...] for a in arrays])
+        elif len(arrays[0].shape) == 3:
+            total[:, cols] = summed([arrays[0][n] for n in range(4)])
+        else:
+            total[:, cols] = arrays[0][...].astype(F32)
         column = cols.stop
     for r in range(4):
-        first = lax.rem(info[slot] + r, 4) * inner
+        first = r * inner if stacked else lax.rem(info[slot] + r, 4) * inner
         parts = [
             total[pl.ds(pl.multiple_of(n * 4 * inner + first, 8), inner), :] for n in range(outer)
         ]
         if rest_rows:
             parts.append(total[4 * outer * inner :, :])
-        outs[r][...] = jnp.concatenate(parts, axis=0).astype(BF16)
-
-
-def fold(info, axis, groups, outer, inner, token):
+        out = outs[0].at[r] if stacked else outs[r]
+        out[...] = jnp.concatenate(parts, axis=0).astype(BF16)
+
+
+def fold(info, axis, groups, outer, inner, token, stacked=False):
     slot = 10 + "zyx".index(axis)
     arrays = [a for group in groups for a in group]
-    rows, width = arrays[0].shape[0], sum(group[0].shape[1] for group in groups)
+    rows, width = arrays[0].shape[-2], sum(group[0].shape[-1] for group in groups)
     more = rows - 4 * outer * inner
-    out = shape((outer * inner + more, width), BF16)
+    outs, specs = four((outer * inner + more, width), stacked)
     counts = [len(group) for group in groups]
     return pl.pallas_call(
-        functools.partial(fold_body, slot, counts, outer, inner, more),
-        out_shape=[out] * 4,
+        functools.partial(fold_body, slot, counts, outer, inner, more, stacked),
+        out_shape=outs,
         in_specs=[SMEM] + [whole(a.shape) for a in arrays] + [ANYWHERE],
-        out_specs=[whole(out.shape)] * 4,
+        out_specs=specs,
         scratch_shapes=[pltpu.VMEM((rows, width), F32)],
         compiler_params=params(),
         cost_estimate=pl.CostEstimate(flops=2_000_000, bytes_accessed=8_000_000, transcendentals=0),
@@ -1145,11 +1217,9 @@
 def last_fold_body(info, *rest):
     left, right, outs, total = rest[:4], rest[4:8], rest[9:13], rest[13]
     width = left[0].shape[1]
-    rows = 96 + SMALL // 2
     total[:96, :width] = summed([a[...] for a in left])
-    total[:96, width:] = summed([a[:96, :] for a in right])
-    total[96:, :width] = summed([a[96:rows, :width] for a in right])
-    total[96:, width:] = summed([a[rows:, :] for a in right])
+    total[96:, :width] = jnp.zeros((SMALL, width), F32)
+    total[:, width:] = summed([a[...] for a in right])
     for r in range(4):
         first = pl.multiple_of(lax.rem(info[10] + r, 4) * 24, 8)
         parts = [total[pl.ds(first, 24), :], total[96:, :]]
@@ -1158,14 +1228,14 @@
 
 def last_fold(info, left, right, token):
     width = left[0].shape[1] + right[0].shape[1]
-    out = shape((24 + SMALL // 2, width), BF16)
+    out = shape((24 + SMALL, width), BF16)
     arrays = (*left, *right)
     return pl.pallas_call(
         last_fold_body,
         out_shape=[out] * 4,
         in_specs=[SMEM] + [whole(a.shape) for a in arrays] + [ANYWHERE],
         out_specs=[whole(out.shape)] * 4,
-        scratch_shapes=[pltpu.VMEM((96 + SMALL // 2, width), F32)],
+        scratch_shapes=[pltpu.VMEM((96 + SMALL, width), F32)],
         compiler_params=params(),
         cost_estimate=pl.CostEstimate(flops=500_000, bytes_accessed=2_000_000, transcendentals=0),
         name="last_fold",
@@ -1174,6 +1244,14 @@
 
 PARITY = [[j for j in range(16) if j % 2 == e] for e in range(2)]
 NEIGHBOURS = [(j, j ^ 1) for j in range(16)]
+GROUPS_OF = {
+    "y": [[4 * y + x for y in range(4)] for x in range(4)],
+    "x": [[4 * y + x for x in range(4)] for y in range(4)],
+}
+
+
+def traded(value, axis):
+    return lax.all_to_all(value, "ctx", 0, 0, axis_index_groups=GROUPS_OF[axis])
 
 
 def exchange(value):
@@ -1390,40 +1468,38 @@
     def backward(cot, saved, layer, higher, tokens):
         h, normed, mixed, halo, rate, gate, xa, bca, cum, dt, s0, msg, hin, y, branch, scale = saved
         cpar, hpar = cpars[layer], hpars[layer]
-        bg, dy, dz, normed_two, d_gain_two = gate_back(
-            info, cot, y, gate, gains_two[layer], branch, scale, weights_o[layer]
-        )
-        own1, msg_back = own_grad(dy, bca, cum, msg)
-        came = exchange(msg_back)
-        normed_two_t, normed_t = normed_two.T, normed.T
 
         def first_stage(value):
             return lax.psum_scatter(value, "dp", tiled=True)
 
-        grad_o, grad_z = dot(normed_two_t, bg).astype(BF16), dot(normed_t, dz).astype(BF16)
-        sums = [first_stage(grad_o), first_stage(grad_z)]
+        bg, dy, dz, grad_o, d_gain_two = gate_back(
+            info, cot, y, gate, gains_two[layer], branch, scale, weights_o[layer], layer == 1
+        )
+        own1, msg_back, grad_z = own_grad(dy, bca, cum, msg, dz, normed)
+        sums = [first_stage(grad_z)] + ([first_stage(grad_o)] if layer else [])
+        came = exchange(msg_back)
         dxi, d_skips, gsum, u, dbc = inside_back(dy, xa, bca, cum, dt, hpar)
-        part = gate_in_back(info, dz, weights_z[layer])
-        lam = exchange(scan_call(info, came, True, part, grad_o, grad_z, *tokens)).reshape(GROUPS, STATE, BLOCK)
+        part = gate_in_back(info, dz, weights_z[layer], msg_back)
+        lam = exchange(scan_call(info, came, True, part, *tokens)).reshape(GROUPS, STATE, BLOCK)
         dmx, dmbc, tailx, tailbc, edgex, edgebc, d_parx, d_parbc, d_heads = finish_call(
             info, xa, dxi, dy, mixed, halo, cpar, bca, cum, dt, rate, hpar, lam, hin, s0, own1, u, gsum, dbc
         )
         edge = halo_shift(jnp.concatenate([edgex, edgebc], axis=1), -1)
-        token = d_heads
+        dxc = patch(dmx, dmbc, tailx, tailbc, edge, d_heads)
+        middle = 7 * LANES
         if layer == 0:
             higher_rows, higher = higher
-            higher = arrived(fold(info, "y", [[v] for v in higher], 1, 96, d_heads), "y")
-            token = higher[0]
-        dxc = patch(dmx, dmbc, tailx, tailbc, edge, token)
-        middle = 7 * LANES
-        left, deadline = [], []
-        if layer == 0:
-            left = terms(info, "y", normed_t, dxc[:, :middle])
-            deadline = [left[0]]
-        part, d_gain_one = mixed_back(info, dxc, part, h, weights_x[layer], deadline)
-        grad_x = dot(normed_t, dxc).astype(BF16) if layer == 1 else dxc
-        dh, dh_low = norm_back(part, swapped(part), h, cot, gains_one[layer], grad_x)
-
+            normed_t = normed.T
+            cuts = [(normed_t, dxc, slice(0, middle)), (grad_o, bg, slice(0, WIDTH // 2))]
+            left = terms(info, "y", cuts, (), True)
+            part, d_gain_one = mixed_back(
+                info, dxc, part, h, normed, weights_x[layer], False, [left, *higher]
+            )
+        else:
+            part, d_gain_one, grad_x = mixed_back(
+                info, dxc, part, h, normed, weights_x[layer], True, []
+            )
+        dh, dh_low = norm_back(part, swapped(part), h, cot, gains_one[layer])
         d_skip_row = jnp.sum(d_skips[0:1].reshape(1, 4 * OWN, HEADDIM), axis=2)
         rows = jnp.where(jnp.arange(8)[:, None] == 5, d_gain_two, d_parx)
         rows = jnp.concatenate([rows, d_parbc], axis=1)
@@ -1439,20 +1515,22 @@
             return dh, dh_low, sums + [first_stage(grad_x)], rows
 
         rows = jnp.concatenate([rows, higher_rows]).astype(BF16)
-        small = jnp.concatenate([rows[:, : MIXED // 2], rows[:, MIXED // 2 :]])
-        small = jnp.pad(small, ((0, 0), (0, LANES)))
-        left = arrived(left, "y")
-        right = arrived(terms(info, "x", normed_t, dxc[:, middle:], (small,)), "x")
-        left = fold(info, "x", [left], 4, 24, dh_low)
+        cuts = [(normed_t, dxc, slice(middle, PACKED)), (grad_o, bg, slice(WIDTH // 2, WIDTH))]
+        right = arrived(terms(info, "x", cuts, (rows,)), "x")
+        tall = fold(info, "y", [[v] for v in higher + sums], 1, 96, dh_low, True)
+        left = fold(info, "x", [[traded(left, "y")]], 4, 24, tall)
         right = fold(info, "y", [right], 4, 24, dh_low)
-        higher = arrived(fold(info, "x", [higher], 1, 24, left[0]), "x")
-        token = right[0]
+        tall = fold(info, "x", [[traded(tall, "y")]], 1, 24, right[0])
         left, right = arrived(left, "x"), arrived(right, "y")
-        sum_x = summed(arrived(last_fold(info, left, right, higher[0]), "z"))
-        rows = jnp.concatenate(
-            [sum_x[24:, : MIXED // 2], sum_x[24:, middle : middle + MIXED // 2]], axis=1
+        final = summed(arrived(last_fold(info, left, right, tall[0]), "z"))
+        left, right = left[0].shape[1], right[0].shape[1]
+        rows = final[24:, left:]
+        final = final[:24]
+        sum_x = jnp.concatenate(
+            [final[:, :middle], final[:, left : left + PACKED - middle]], axis=1
         )
-        return dh, [higher, sums, token], sum_x[:24], rows
+        sum_o = jnp.concatenate([final[:, middle:left], final[:, left + PACKED - middle :]], axis=1)
+        return dh, [arrived(tall, "x"), sum_o], sum_x, rows
 
     at = section.reshape(1).astype(jnp.int32)
     smalls = (conv_weight[0], conv_bias, norm_gain, gate_gain, dt_bias, a_log, d_skip)
@@ -1480,24 +1558,19 @@
 
     def returned(rows, layer):
         pairs = [(layer * 16 + a, layer * 16 + b) for a, b in NEIGHBOURS]
-        other = lax.ppermute(
-            jnp.where(micro == 0, rows[HALF:], rows[:HALF]), ("section", "ctx"), pairs
+        other, mine = (
+            lax.dynamic_slice_in_dim(rows, n * HALF, HALF, 0) for n in (1 - micro, micro)
         )
-        mine = jnp.where(micro == 0, rows[:HALF], rows[HALF:])
+        other = lax.ppermute(other, ("section", "ctx"), pairs)
         return jnp.where(micro == 0, jnp.stack([mine, other]), jnp.stack([other, mine]))
 
     middle, saved_low = forward(hidden, 0)
     out_high, saved_high = forward(middle, 1)
     top_high = returned(out_high, 1)
     _, back, higher, rows = backward(cotangent, saved_high, 1, None, [top_high])
-    dh_low, (higher, lower, token), low_x, rows = backward(
-        back, saved_low, 0, (rows, higher), []
-    )
-
-    high_o, high_z, high_x = jnp.split(summed(higher), (WIDTH, WIDTH + LOCAL), axis=1)
-    lower = fold(info, "x", [[v] for v in lower], 4, 24, token)
-    lower = fold(info, "y", [arrived(lower, "x")], 1, 24, token)
-    low_o, low_z = jnp.split(summed(arrived(lower, "y")), 2, axis=1)
+    dh_low, (tall, low_o), low_x, rows = backward(back, saved_low, 0, (rows, higher), [])
+    at = (LOCAL, LOCAL + WIDTH, LOCAL + WIDTH + PACKED)
+    high_z, high_o, high_x, low_z = jnp.split(summed(tall), at, axis=1)
 
     own, given = ordered(rows[:16], rows[16:])
     rows_0, rows_1 = ordered(own, swapped(given))

time: 728 us -> 713 us (0.979)
  matrix products: 22.8 us -> 0 us
  Pallas kernels: 247 us -> 261 us
  waiting for transfers between devices: 183 us -> 196 us
  starting transfers between devices: 166 us -> 154 us
  other arithmetic: 31.9 us -> 23.8 us
    ppermute x42 -> x30, starting transfers between devices: 75.6 us -> 38.8 us  [send(): return lax.ppermute(value, name, pairs)]
    dot_general x5 -> x0, matrix products: 22.8 us -> none  [dot(): return jnp.dot(a, b, preferred_element_type=F32)]
    reduce_scatter x5 -> x4, waiting for transfers between devices: 0.04 us -> 21.8 us  [first_stage(): return lax.psum_scatter(value, 'dp', tiled=True)]
    ppermute x42 -> x30, waiting for transfers between devices: 134 us -> 114 us  [send(): return lax.ppermute(value, name, pairs)]
    all_to_all x8, starting transfers between devices: 60 us -> 76.3 us  [exchange(): return lax.all_to_all(value, 'ctx', 0, 0, axis_index_groups=PARITY)]
    all_to_all x0 -> x2, starting transfers between devices: none -> 12 us  [traded(): return lax.all_to_all(value, 'ctx', 0, 0, axis_index_groups=GROUPS_OF[axis])]
    pallas_call x8, Pallas kernels: 57.6 us -> 68.1 us  [the longest x2 20.2 us: mixed_back(): pl.pallas_call(functools.partial(mixed_back_body, weight, len(tokens)), g...]
    all_to_all x0 -> x2, waiting for transfers between devices: none -> 9.95 us  [traded(): return lax.all_to_all(value, 'ctx', 0, 0, axis_index_groups=GROUPS_OF[axis])]
  transfers between devices with their start and end apart: 76 -> 65, of which waited for: 31 -> 30; matrix products, arithmetic and copies ran while one was open for 10% -> 6% of each run, Pallas kernels for 31% -> 34%
where the time goes in v4:
time: 713 us; the launch traced here: 700 us
  Pallas kernels  261 us (37%)
  waiting for transfers between devices  196 us (27%)
  starting transfers between devices  154 us (22%)
  local copies, waits for them, and re-layouts  44 us (6%)
  other arithmetic  23.8 us (3%)
  between operations  21 us (3%)
    ppermute x30, waiting for transfers between devices, send(): return lax.ppermute(value, name, pairs)  114 us
    all_to_all x8, starting transfers between devices, exchange(): return lax.all_to_all(value, 'ctx', 0, 0, axis_index_groups=PARITY)  76.3 us
    ppermute x30, starting transfers between devices, send(): return lax.ppermute(value, name, pairs)  38.8 us
    pallas_call x2, Pallas kernels, finish_call(): pl.pallas_call(finish_body, grid=(GROUPS,), out_shape=(shape((ROWS, LOCAL...  24.5 us
    reduce_scatter x4, waiting for transfers between devices, first_stage(): return lax.psum_scatter(value, 'dp', tiled=True)  21.8 us
    pallas_call x4, Pallas kernels, fold(): pl.pallas_call(functools.partial(fold_body, slot, counts, outer, inner, m...  20.4 us
    unnamed x110, local copies, waits for them, and re-layouts  20.2 us
    pallas_call x2, Pallas kernels, mixed_back(): pl.pallas_call(functools.partial(mixed_back_body, weight, len(tokens)), g...  20.2 us
  transfers between devices with their start and end apart: 65, of which 30 were waited for; matrix products, arithmetic and copies ran while one was open for 6% of the time, Pallas kernels for 34%

profile of v4, /device:TPU:12, one launch (start us, length us, event | category | flops | bytes accessed | tf_op | source)
XLA Modules:
  0.0 699.7 jit_solution(10893849825889399383)
XLA Ops:
  14.2 5.2 collective-permute-done
  19.6 4.9 pick_zo.1
  38.4 7.6 %collective-permute-done.5.rest_3_.refs_2_ = bf16[112,1920]{1,0:T(8,128)(2,1)S(1)} collective-permute-done((bf16[112,1920]{1,0:T(8,128)(2,1)S(1)}, bf16[112,1920]{1,0:T(8,128)(2,1)S(1)}, u32[]{:S(2)}, u32[]{:S(2)}) %collective-permute-start.5) | collective-permute-done | bytes 430112 | tf_op jit(solution)/shard_map/ppermute | solution.py:1066
  46.0 10.4 %collective-permute-done.4.rest_2_.refs_1_ = bf16[112,1920]{1,0:T(8,128)(2,1)S(1)} collective-permute-done((bf16[112,1920]{1,0:T(8,128)(2,1)S(1)}, bf16[112,1920]{1,0:T(8,128)(2,1)S(1)}, u32[]{:S(2)}, u32[]{:S(2)}) %collective-permute-start.4) | collective-permute-done | bytes 430112 | tf_op jit(solution)/shard_map/ppermute | solution.py:1066
  78.1 9.1 %collective-permute-done.8.rest_5_.refs_2_ = bf16[144,1920]{1,0:T(8,128)(2,1)S(1)} collective-permute-done((bf16[144,1920]{1,0:T(8,128)(2,1)}, bf16[144,1920]{1,0:T(8,128)(2,1)S(1)}, u32[]{:S(2)}, u32[]{:S(2)}) %collective-permute-start.8) | collective-permute-done | bytes 552992 | tf_op jit(solution)/shard_map/ppermute | solution.py:1066
  87.7 7.9 %collective-permute-done.7.rest_4_.refs_1_ = bf16[144,1920]{1,0:T(8,128)(2,1)S(1)} collective-permute-done((bf16[144,1920]{1,0:T(8,128)(2,1)}, bf16[144,1920]{1,0:T(8,128)(2,1)S(1)}, u32[]{:S(2)}, u32[]{:S(2)}) %collective-permute-start.7) | collective-permute-done | bytes 552992 | tf_op jit(solution)/shard_map/ppermute | solution.py:1066
  113.7 7.0 in_proj.2
  132.6 5.7 conv_state.2
  138.4 25.9 %all-to-all-start = ((bf16[8,80,384]{2,1,0:T(8,128)(2,1)}), bf16[8,80,384]{2,1,0:T(8,128)(2,1)}, u32[]{:S(2)}, u32[]{:S(2)}) async-start(bf16[8,80,384]{2,1,0:T(8,128)(2,1)} %get-tuple-element.134.msg_in), calls=%async_computation | async-start | bytes 983040 | tf_op jit(solution)/shard_map/all_to_all | solution.py:1258
  164.3 5.8 inside.2.rest_0_.y_in
  175.5 7.3 %all-to-all-start.1 = ((bf16[8,64,384]{2,1,0:T(8,128)(2,1)}), bf16[8,64,384]{2,1,0:T(8,128)(2,1)S(1)}, u32[]{:S(2)}, u32[]{:S(2)}) async-start(bf16[8,64,384]{2,1,0:T(8,128)(2,1)} %chunk_scan.4), calls=%async_computation.1 | async-start | bytes 786432 | tf_op jit(solution)/shard_map/all_to_all | solution.py:1258
  183.7 6.3 gate_proj.2.gate
  190.8 7.8 %out_proj.2 = (f32[256,1536]{1,0:T(8,128)}, f32[256,1664]{1,0:T(8,128)}) custom-call(s32[14]{0:T(128)} %concatenate.114.info, f32[256,1536]{1,0:T(8,128)} %inside.2.rest_0_.y_in, f32[256,256]{1,0:T(8,128)} %get-tuple-element.131.bca, f32[256,128]{1,0:T(8,128)} %get-tuple-element.132.cum, bf16[4,128,384]{2,1,0:T(8,128)(2,1)} %bitcast.70, ...), custom_call_target="tpu_custom_call" | custom-call | flops 1207959552 | bytes 13000000 | tf_op jit(solution)/shard_map/out_proj/pallas_call | solution.py:459
  210.4 7.0 in_proj.3
  226.4 5.7 conv_state.3
  232.1 7.2 %all-to-all-start.2 = ((bf16[8,80,384]{2,1,0:T(8,128)(2,1)}), bf16[8,80,384]{2,1,0:T(8,128)(2,1)S(1)}, u32[]{:S(2)}, u32[]{:S(2)}) async-start(bf16[8,80,384]{2,1,0:T(8,128)(2,1)} %get-tuple-element.151.msg_in), calls=%async_computation.2 | async-start | bytes 983040 | tf_op jit(solution)/shard_map/all_to_all | solution.py:1258
  239.3 5.8 inside.3.rest_0_.y_in
  249.3 6.9 all-to-all-start.3
  256.8 6.3 gate_proj.3.gate
  263.9 7.6 %out_proj.3 = (f32[256,1536]{1,0:T(8,128)}, f32[256,1664]{1,0:T(8,128)}) custom-call(s32[14]{0:T(128)} %concatenate.114.info, f32[256,1536]{1,0:T(8,128)} %inside.3.rest_0_.y_in, f32[256,256]{1,0:T(8,128)} %get-tuple-element.148.bca, f32[256,128]{1,0:T(8,128)} %get-tuple-element.149.cum, bf16[4,128,384]{2,1,0:T(8,128)(2,1)} %bitcast.68, ...), custom_call_target="tpu_custom_call" | custom-call | flops 1207959552 | bytes 13000000 | tf_op jit(solution)/shard_map/out_proj/pallas_call | solution.py:459
  281.5 10.6 %gate_back.2 = (bf16[256,1536]{1,0:T(8,128)(2,1)}, bf16[256,1536]{1,0:T(8,128)(2,1)}, bf16[256,1536]{1,0:T(8,128)(2,1)}, bf16[1536,1536]{1,0:T(8,128)(2,1)}, f32[8,1536]{1,0:T(8,128)}) custom-call(s32[14]{0:T(128)} %concatenate.114.info, bf16[256,1536]{1,0:T(8,128)(2,1)} %get-tuple-element.261.cot, f32[256,1536]{1,0:T(8,128)} %get-tuple-element.155.y, ...), custom_call_target="tpu_custom_call" | custom-call | flops 2415919104 | bytes 17000000 | tf_op jit(solution)/shard_map/gate_back/pallas_call | solution.py:555
  292.2 7.7 %own_grad.2 = (f32[4,128,384]{2,1,0:T(8,128)}, bf16[8,80,384]{2,1,0:T(8,128)(2,1)}, bf16[1536,1536]{1,0:T(8,128)(2,1)}) custom-call(bf16[256,1536]{1,0:T(8,128)(2,1)} %get-tuple-element.159.dy, f32[256,256]{1,0:T(8,128)} %get-tuple-element.148.bca, f32[256,128]{1,0:T(8,128)} %get-tuple-element.149.cum, bf16[8,80,384]{2,1,0:T(8,128)(2,1)} %get-tuple-element.151.msg_in, ...), custom_call_target="tpu_custom_call" | custom-call | flops 1207959552 | bytes 8000000 | tf_op jit(solution)/shard_map/own_grad/pallas_call | solution.py:604
  303.2 7.2 %all-to-all-start.4 = ((bf16[8,80,384]{2,1,0:T(8,128)(2,1)}), bf16[8,80,384]{2,1,0:T(8,128)(2,1)S(1)}, u32[]{:S(2)}, u32[]{:S(2)}) async-start(bf16[8,80,384]{2,1,0:T(8,128)(2,1)} %get-tuple-element.162.token), calls=%async_computation.4 | async-start | bytes 983040 | tf_op jit(solution)/shard_map/all_to_all | solution.py:1258
  310.4 7.3 %gate_in_back.2.rest_0_.part = f32[256,1536]{1,0:T(8,128)} custom-call(s32[14]{0:T(128)} %concatenate.114.info, bf16[256,1536]{1,0:T(8,128)(2,1)} %get-tuple-element.161.dz, bf16[8,80,384]{2,1,0:T(8,128)(2,1)} %get-tuple-element.162.token, bf16[1536,3072]{1,0:T(8,128)(2,1)} %all-gather.7.cloned.1.call-done.rest_0_), custom_call_target="tpu_custom_call" | custom-call | flops 1207959552 | bytes 7000000 | tf_op jit(solution)/shard_map/gate_in_back/pallas_call | solution.py:937
  321.7 7.5 %all-to-all-start.5 = ((bf16[8,64,384]{2,1,0:T(8,128)(2,1)}), bf16[8,64,384]{2,1,0:T(8,128)(2,1)S(1)}, u32[]{:S(2)}, u32[]{:S(2)}) async-start(bf16[8,64,384]{2,1,0:T(8,128)(2,1)} %chunk_scan.6), calls=%async_computation.5 | async-start | bytes 786432 | tf_op jit(solution)/shard_map/all_to_all | solution.py:1258
  329.2 8.7 %inside_back.2 = (f32[256,1536]{1,0:T(8,128)}, f32[8,1536]{1,0:T(8,128)}, f32[32,256]{1,0:T(8,128)}, f32[256,128]{1,0:T(8,128)}, f32[256,256]{1,0:T(8,128)}) custom-call(bf16[256,1536]{1,0:T(8,128)(2,1)} %get-tuple-element.159.dy, f32[256,1536]{1,0:T(8,128)} %get-tuple-element.147.xa, f32[256,256]{1,0:T(8,128)} %get-tuple-element.148.bca, ...), custom_call_target="tpu_custom_call" | custom-call | flops 402653184 | bytes 4500000 | tf_op jit(solution)/shard_map/inside_back/pallas_call | solution.py:699
  338.7 12.3 %finish_back.2 = (bf16[256,1536]{1,0:T(8,128)(2,1)}, bf16[256,384]{1,0:T(8,128)(2,1)}, f32[16,1536]{1,0:T(8,128)}, f32[16,256]{1,0:T(8,128)}, bf16[16,1536]{1,0:...) custom-call(s32[14]{0:T(128)} %concatenate.114.info, ...), custom_call_target="tpu_custom_call" | custom-call | flops 503316480 | bytes 7500000 | tf_op jit(solution)/shard_map/finish_back/pallas_call | solution.py:852
  354.2 6.0 collective-permute-done.24.edge
  363.1 11.3 %mixed_back.2 = (f32[256,1536]{1,0:T(8,128)}, f32[8,1536]{1,0:T(8,128)}, bf16[1536,1920]{1,0:T(8,128)(2,1)}) custom-call(s32[14]{0:T(128)} %concatenate.114.info, bf16[256,1920]{1,0:T(8,128)(2,1)} %patch.2.dxc, f32[256,1536]{1,0:T(8,128)} %gate_in_back.2.rest_0_.part, bf16[256,1536]{1,0:T(8,128)(2,1)} %get-tuple-element.141.h_ref, ...), custom_call_target="tpu_custom_call" | custom-call | flops 3019898880 | bytes 14000000 | tf_op jit(solution)/shard_map/mixed_back/pallas_call | solution.py:1008
  386.1 9.3 %gate_back.3 = (bf16[256,1536]{1,0:T(8,128)(2,1)}, bf16[256,1536]{1,0:T(8,128)(2,1)}, bf16[256,1536]{1,0:T(8,128)(2,1)}, bf16[1536,256]{1,0:T(8,128)(2,1)}, f32[8,1536]{1,0:T(8,128)}) custom-call(s32[14]{0:T(128)} %concatenate.114.info, bf16[256,1536]{1,0:T(8,128)(2,1)} %get-tuple-element.176.cot, f32[256,1536]{1,0:T(8,128)} %get-tuple-element.177.y, ...), custom_call_target="tpu_custom_call" | custom-call | flops 2415919104 | bytes 17000000 | tf_op jit(solution)/shard_map/gate_back/pallas_call | solution.py:555
  395.4 7.7 %own_grad.3 = (f32[4,128,384]{2,1,0:T(8,128)}, bf16[8,80,384]{2,1,0:T(8,128)(2,1)}, bf16[1536,1536]{1,0:T(8,128)(2,1)}) custom-call(bf16[256,1536]{1,0:T(8,128)(2,1)} %get-tuple-element.180.dy, f32[256,256]{1,0:T(8,128)} %get-tuple-element.131.bca, f32[256,128]{1,0:T(8,128)} %get-tuple-element.132.cum, bf16[8,80,384]{2,1,0:T(8,128)(2,1)} %get-tuple-element.134.msg_in, ...), custom_call_target="tpu_custom_call" | custom-call | flops 1207959552 | bytes 8000000 | tf_op jit(solution)/shard_map/own_grad/pallas_call | solution.py:604
  403.1 7.2 %all-to-all-start.6 = ((bf16[8,80,384]{2,1,0:T(8,128)(2,1)}), bf16[8,80,384]{2,1,0:T(8,128)(2,1)S(1)}, u32[]{:S(2)}, u32[]{:S(2)}) async-start(bf16[8,80,384]{2,1,0:T(8,128)(2,1)} %get-tuple-element.183.token), calls=%async_computation.6 | async-start | bytes 983040 | tf_op jit(solution)/shard_map/all_to_all | solution.py:1258
  410.3 7.2 %gate_in_back.3.rest_0_.part = f32[256,1536]{1,0:T(8,128)} custom-call(s32[14]{0:T(128)} %concatenate.114.info, bf16[256,1536]{1,0:T(8,128)(2,1)} %get-tuple-element.182.dz, bf16[8,80,384]{2,1,0:T(8,128)(2,1)} %get-tuple-element.183.token, bf16[384,3072]{1,0:T(8,128)(2,1)} %get-tuple-element.137.rest_0_, bf16[384,3072]{1,0:T(8,128)(2,1)} %collective-permute-done.13.rest_1_, ...), custom_call_target="tpu_custom_call" | custom-call | flops 1207959552 | bytes 7000000 | tf_op jit(solution)/shard_map/gate_in_back/pallas_call | solution.py:937
  421.3 6.9 all-to-all-start.7
  428.2 8.7 %inside_back.3 = (f32[256,1536]{1,0:T(8,128)}, f32[8,1536]{1,0:T(8,128)}, f32[32,256]{1,0:T(8,128)}, f32[256,128]{1,0:T(8,128)}, f32[256,256]{1,0:T(8,128)}) custom-call(bf16[256,1536]{1,0:T(8,128)(2,1)} %get-tuple-element.180.dy, f32[256,1536]{1,0:T(8,128)} %get-tuple-element.130.xa, f32[256,256]{1,0:T(8,128)} %get-tuple-element.131.bca, ...), custom_call_target="tpu_custom_call" | custom-call | flops 402653184 | bytes 4500000 | tf_op jit(solution)/shard_map/inside_back/pallas_call | solution.py:699
  437.7 12.3 %finish_back.3 = (bf16[256,1536]{1,0:T(8,128)(2,1)}, bf16[256,384]{1,0:T(8,128)(2,1)}, f32[16,1536]{1,0:T(8,128)}, f32[16,256]{1,0:T(8,128)}, bf16[16,1536]{1,0:...) custom-call(s32[14]{0:T(128)} %concatenate.114.info, ...), custom_call_target="tpu_custom_call" | custom-call | flops 503316480 | bytes 7500000 | tf_op jit(solution)/shard_map/finish_back/pallas_call | solution.py:852
  462.3 5.7 terms.2.rest_10_
  468.0 5.6 all-to-all-start.8
  473.6 8.9 %mixed_back.3 = (f32[256,1536]{1,0:T(8,128)}, f32[8,1536]{1,0:T(8,128)}) custom-call(s32[14]{0:T(128)} %concatenate.114.info, bf16[256,1920]{1,0:T(8,128)(2,1)} %patch.3.rest_1_.dxc, f32[256,1536]{1,0:T(8,128)} %gate_in_back.3.rest_0_.part, bf16[256,1536]{1,0:T(8,128)(2,1)} %get-tuple-element.262.refs_0_.h_ref, ...), custom_call_target="tpu_custom_call" | custom-call | flops 3019898880 | bytes 14000000 | tf_op jit(solution)/shard_map/mixed_back/pallas_call | solution.py:1008
  492.3 21.8 %reduce-scatter.11.cloned.1.call-done.rest_3_ = bf16[384,1536]{1,0:T(8,128)(2,1)} async-done(((bf16[1536,1536]{1,0:T(8,128)(2,1)}), bf16[384,1536]{1,0:T(8,128)(2,1)}) %reduce-scatter.11.cloned.1.call-update) | async-done | bytes 1179664 | tf_op jit(solution)/shard_map/reduce_scatter | solution.py:1473
  514.1 5.0 fold.4.rest_1_
  519.1 9.9 %all-to-all-done.8.rest_0_ = bf16[4,384,1664]{2,1,0:T(8,128)(2,1)} async-done(((bf16[4,384,1664]{2,1,0:T(8,128)(2,1)}), bf16[4,384,1664]{2,1,0:T(8,128)(2,1)}, u32[]{:S(2)}, u32[]{:S(2)}) %all-to-all-start.8) | async-done | bytes 5111840 | tf_op jit(solution)/shard_map/all_to_all | solution.py:1254
  529.1 6.4 all-to-all-start.9
  540.4 7.9 %terms.3 = (bf16[416,1792]{1,0:T(8,128)(2,1)}, bf16[416,1792]{1,0:T(8,128)(2,1)}, bf16[416,1792]{1,0:T(8,128)(2,1)}, bf16[416,1792]{1,0:T(8,128)(2,1)}) custom-call(s32[14]{0:T(128)} %concatenate.114.info, bf16[1536,256]{1,0:T(8,128)(2,1)} %bitcast.73, bf16[256,1920]{1,0:T(8,128)(2,1)} %patch.3.rest_1_.dxc, bf16[1536,256]{1,0:T(8,128)(2,1)} %get-tuple-element.195.rest_2_, ...), custom_call_target="tpu_custom_call" | custom-call | flops 1409286144 | bytes 8000000 | tf_op jit(solution)/shard_map/terms/pallas_call | solution.py:1160
  560.9 57.0 %collective-permute-done.32.rest_1_ = bf16[416,1792]{1,0:T(8,128)(2,1)S(1)} collective-permute-done((bf16[416,1792]{1,0:T(8,128)(2,1)}, bf16[416,1792]{1,0:T(8,128)(2,1)S(1)}, u32[]{:S(2)}, u32[]{:S(2)}) %collective-permute-start.32) | collective-permute-done | bytes 1490976 | tf_op jit(solution)/shard_map/ppermute | solution.py:1066
  619.5 5.7 fold.6
  657.5 5.2 collective-permute-done.38
  681.6 6.2 collective-permute-done.47
  (362 shorter events, 238.0 us)
Async XLA Ops:
  7.2 97.0 %all-gather.9.cloned.1.call-start = ((), (), s32[]{:S(2)}) async-start(), calls=%async_computation.20 | async-start | bytes 2949120 | tf_op jit(solution)/shard_map/all_gather | solution.py:1545
  14.2 15.2 %collective-permute-start.2 = (bf16[400,1920]{1,0:T(8,128)(2,1)}, bf16[400,1920]{1,0:T(8,128)(2,1)}, u32[]{:S(2)}, u32[]{:S(2)}) collective-permute-start(bf16[400,1920]{1,0:T(8,128)(2,1)} %get-tuple-element.124), channel_id=1, source_target_pairs={{0,64},{64,0},{1,65},{65,1},{2,66},{66,2},{3,67},{67,3},{4,68},{68... | collective-permute-start | bytes 4608008 | tf_op jit(solution)/shard_map/ppermute | solution.py:1070
  24.6 36.5 %collective-permute-start.13 = (bf16[384,3072]{1,0:T(8,128)(2,1)}, bf16[384,3072]{1,0:T(8,128)(2,1)}, u32[]{:S(2)}, u32[]{:S(2)}) collective-permute-start(bf16[384,3072]{1,0:T(8,128)(2,1)} %get-tuple-element.138), channel_id=1, source_target_pairs={{0,64},{64,0},{1,65},{65,1},{2,66},{66,2},{3,67},{67,3},{4,68},{68... | collective-permute-start | bytes 7077896 | tf_op jit(solution)/shard_map/ppermute | solution.py:1070
  31.8 14.2 %collective-permute-start.5 = (bf16[112,1920]{1,0:T(8,128)(2,1)S(1)}, bf16[112,1920]{1,0:T(8,128)(2,1)S(1)}, u32[]{:S(2)}, u32[]{:S(2)}) collective-permute-start(bf16[112,1920]{1,0:T(8,128)(2,1)S(1)} %pad_maximum_fusion.5.rest_0_), channel_id=1, source_target_pairs={{0,16},{16,32},{32,48},{48,0},{1,17},{17,33},{33,49},{49,1},{2,18}... | collective-permute-start | bytes 1290248 | tf_op jit(solution)/shard_map/ppermute | solution.py:1066
  33.8 22.6 %collective-permute-start.4 = (bf16[112,1920]{1,0:T(8,128)(2,1)S(1)}, bf16[112,1920]{1,0:T(8,128)(2,1)S(1)}, u32[]{:S(2)}, u32[]{:S(2)}) collective-permute-start(bf16[112,1920]{1,0:T(8,128)(2,1)S(1)} %pad_maximum_fusion.5.rest_0_), channel_id=1, source_target_pairs={{0,32},{16,48},{32,0},{48,16},{1,33},{17,49},{33,1},{49,17},{2,34}... | collective-permute-start | bytes 1290248 | tf_op jit(solution)/shard_map/ppermute | solution.py:1066
  37.4 19.0 %collective-permute-start.3 = (bf16[112,1920]{1,0:T(8,128)(2,1)S(1)}, bf16[112,1920]{1,0:T(8,128)(2,1)S(1)}, u32[]{:S(2)}, u32[]{:S(2)}) collective-permute-start(bf16[112,1920]{1,0:T(8,128)(2,1)S(1)} %pad_maximum_fusion.5.rest_0_), channel_id=1, source_target_pairs={{0,48},{16,0},{32,16},{48,32},{1,49},{17,1},{33,17},{49,33},{2,50}... | collective-permute-start | bytes 1290248 | tf_op jit(solution)/shard_map/ppermute | solution.py:1066
  63.2 144.8 %all-gather.5.cloned.1.call-start = ((), (), s32[]{:S(2)}) async-start(), calls=%async_computation.14 | async-start | bytes 7680000 | tf_op jit(solution)/shard_map/all_gather | solution.py:1549
  66.0 190.8 %all-gather.7.cloned.1.call-start = ((), (), s32[]{:S(2)}) async-start(), calls=%async_computation.15 | async-start | bytes 11796480 | tf_op jit(solution)/shard_map/all_gather | solution.py:1550
  71.5 15.7 %collective-permute-start.8 = (bf16[144,1920]{1,0:T(8,128)(2,1)}, bf16[144,1920]{1,0:T(8,128)(2,1)S(1)}, u32[]{:S(2)}, u32[]{:S(2)}) collective-permute-start(bf16[144,1920]{1,0:T(8,128)(2,1)} %pad_maximum_fusion.3.rest_2_), channel_id=1, source_target_pairs={{0,1},{1,2},{2,3},{3,0},{4,5},{5,6},{6,7},{7,4},{8,9},{9,10},{10,1... | collective-permute-start | bytes 1658888 | tf_op jit(solution)/shard_map/ppermute | solution.py:1066
  72.7 22.8 %collective-permute-start.7 = (bf16[144,1920]{1,0:T(8,128)(2,1)}, bf16[144,1920]{1,0:T(8,128)(2,1)S(1)}, u32[]{:S(2)}, u32[]{:S(2)}) collective-permute-start(bf16[144,1920]{1,0:T(8,128)(2,1)} %pad_maximum_fusion.3.rest_2_), channel_id=1, source_target_pairs={{0,2},{1,3},{2,0},{3,1},{4,6},{5,7},{6,4},{7,5},{8,10},{9,11},{10,... | collective-permute-start | bytes 1658888 | tf_op jit(solution)/shard_map/ppermute | solution.py:1066
  73.5 23.8 %collective-permute-start.6 = (bf16[144,1920]{1,0:T(8,128)(2,1)}, bf16[144,1920]{1,0:T(8,128)(2,1)S(1)}, u32[]{:S(2)}, u32[]{:S(2)}) collective-permute-start(bf16[144,1920]{1,0:T(8,128)(2,1)} %pad_maximum_fusion.3.rest_2_), channel_id=1, source_target_pairs={{0,3},{1,0},{2,1},{3,2},{4,7},{5,4},{6,5},{7,6},{8,11},{9,8},{10,9... | collective-permute-start | bytes 1658888 | tf_op jit(solution)/shard_map/ppermute | solution.py:1066
  75.6 21.8 %collective-permute-start.11 = (bf16[144,1920]{1,0:T(8,128)(2,1)}, bf16[144,1920]{1,0:T(8,128)(2,1)S(1)}, u32[]{:S(2)}, u32[]{:S(2)}) collective-permute-start(bf16[144,1920]{1,0:T(8,128)(2,1)} %pad_maximum_fusion.4.rest_6_), channel_id=1, source_target_pairs={{0,4},{1,5},{2,6},{3,7},{4,8},{5,9},{6,10},{7,11},{8,12},{9,13},{1... | collective-permute-start | bytes 1658888 | tf_op jit(solution)/shard_map/ppermute | solution.py:1066
  77.2 20.2 %collective-permute-start.10 = (bf16[144,1920]{1,0:T(8,128)(2,1)}, bf16[144,1920]{1,0:T(8,128)(2,1)S(1)}, u32[]{:S(2)}, u32[]{:S(2)}) collective-permute-start(bf16[144,1920]{1,0:T(8,128)(2,1)} %pad_maximum_fusion.4.rest_6_), channel_id=1, source_target_pairs={{0,8},{1,9},{2,10},{3,11},{4,12},{5,13},{6,14},{7,15},{8,0},{9,1},... | collective-permute-start | bytes 1658888 | tf_op jit(solution)/shard_map/ppermute | solution.py:1066
  87.3 14.4 %collective-permute-start.9 = (bf16[144,1920]{1,0:T(8,128)(2,1)}, bf16[144,1920]{1,0:T(8,128)(2,1)}, u32[]{:S(2)}, u32[]{:S(2)}) collective-permute-start(bf16[144,1920]{1,0:T(8,128)(2,1)} %pad_maximum_fusion.4.rest_6_), channel_id=1, source_target_pairs={{0,12},{1,13},{2,14},{3,15},{4,0},{5,1},{6,2},{7,3},{8,4},{9,5},{1... | collective-permute-start | bytes 1658888 | tf_op jit(solution)/shard_map/ppermute | solution.py:1066
  106.7 25.2 %collective-permute-start.16 = (bf16[144,3072]{1,0:T(8,128)(2,1)S(1)}, bf16[144,3072]{1,0:T(8,128)(2,1)S(1)}, u32[]{:S(2)}, u32[]{:S(2)}) collective-permute-start(bf16[144,3072]{1,0:T(8,128)(2,1)S(1)} %pad_maximum_fusion.rest_2_), channel_id=1, source_target_pairs={{0,1},{1,2},{2,3},{3,0},{4,5},{5,6},{6,7},{7,4},{8,9},{9,10},{10,1... | collective-permute-start | bytes 2654216 | tf_op jit(solution)/shard_map/ppermute | solution.py:1066
  125.8 57.0 %collective-permute-start.15 = (bf16[144,3072]{1,0:T(8,128)(2,1)S(1)}, bf16[144,3072]{1,0:T(8,128)(2,1)S(1)}, u32[]{:S(2)}, u32[]{:S(2)}) collective-permute-start(bf16[144,3072]{1,0:T(8,128)(2,1)S(1)} %pad_maximum_fusion.rest_2_), channel_id=1, source_target_pairs={{0,2},{1,3},{2,0},{3,1},{4,6},{5,7},{6,4},{7,5},{8,10},{9,11},{10,... | collective-permute-start | bytes 2654216 | tf_op jit(solution)/shard_map/ppermute | solution.py:1066
  127.0 55.8 %collective-permute-start.14 = (bf16[144,3072]{1,0:T(8,128)(2,1)S(1)}, bf16[144,3072]{1,0:T(8,128)(2,1)}, u32[]{:S(2)}, u32[]{:S(2)}) collective-permute-start(bf16[144,3072]{1,0:T(8,128)(2,1)S(1)} %pad_maximum_fusion.rest_2_), channel_id=1, source_target_pairs={{0,3},{1,0},{2,1},{3,2},{4,7},{5,4},{6,5},{7,6},{8,11},{9,8},{10,9... | collective-permute-start | bytes 2654216 | tf_op jit(solution)/shard_map/ppermute | solution.py:1066
  128.3 54.5 %collective-permute-start.19 = (bf16[144,3072]{1,0:T(8,128)(2,1)S(1)}, bf16[144,3072]{1,0:T(8,128)(2,1)}, u32[]{:S(2)}, u32[]{:S(2)}) collective-permute-start(bf16[144,3072]{1,0:T(8,128)(2,1)S(1)} %pad_maximum_fusion.1.rest_6_), channel_id=1, source_target_pairs={{0,4},{1,5},{2,6},{3,7},{4,8},{5,9},{6,10},{7,11},{8,12},{9,13},{1... | collective-permute-start | bytes 2654216 | tf_op jit(solution)/shard_map/ppermute | solution.py:1066
  131.5 51.3 %collective-permute-start.18 = (bf16[144,3072]{1,0:T(8,128)(2,1)S(1)}, bf16[144,3072]{1,0:T(8,128)(2,1)}, u32[]{:S(2)}, u32[]{:S(2)}) collective-permute-start(bf16[144,3072]{1,0:T(8,128)(2,1)S(1)} %pad_maximum_fusion.1.rest_6_), channel_id=1, source_target_pairs={{0,8},{1,9},{2,10},{3,11},{4,12},{5,13},{6,14},{7,15},{8,0},{9,1},... | collective-permute-start | bytes 2654216 | tf_op jit(solution)/shard_map/ppermute | solution.py:1066
  131.9 50.9 %collective-permute-start.17 = (bf16[144,3072]{1,0:T(8,128)(2,1)S(1)}, bf16[144,3072]{1,0:T(8,128)(2,1)}, u32[]{:S(2)}, u32[]{:S(2)}) collective-permute-start(bf16[144,3072]{1,0:T(8,128)(2,1)S(1)} %pad_maximum_fusion.1.rest_6_), channel_id=1, source_target_pairs={{0,12},{1,13},{2,14},{3,15},{4,0},{5,1},{6,2},{7,3},{8,4},{9,5},{1... | collective-permute-start | bytes 2654216 | tf_op jit(solution)/shard_map/ppermute | solution.py:1066
  138.4 35.1 %all-to-all-start = ((bf16[8,80,384]{2,1,0:T(8,128)(2,1)}), bf16[8,80,384]{2,1,0:T(8,128)(2,1)}, u32[]{:S(2)}, u32[]{:S(2)}) async-start(bf16[8,80,384]{2,1,0:T(8,128)(2,1)} %get-tuple-element.134.msg_in), calls=%async_computation | async-start | bytes 983040 | tf_op jit(solution)/shard_map/all_to_all | solution.py:1258
  175.5 14.6 %all-to-all-start.1 = ((bf16[8,64,384]{2,1,0:T(8,128)(2,1)}), bf16[8,64,384]{2,1,0:T(8,128)(2,1)S(1)}, u32[]{:S(2)}, u32[]{:S(2)}) async-start(bf16[8,64,384]{2,1,0:T(8,128)(2,1)} %chunk_scan.4), calls=%async_computation.1 | async-start | bytes 786432 | tf_op jit(solution)/shard_map/all_to_all | solution.py:1258
  232.1 14.5 %all-to-all-start.2 = ((bf16[8,80,384]{2,1,0:T(8,128)(2,1)}), bf16[8,80,384]{2,1,0:T(8,128)(2,1)S(1)}, u32[]{:S(2)}, u32[]{:S(2)}) async-start(bf16[8,80,384]{2,1,0:T(8,128)(2,1)} %get-tuple-element.151.msg_in), calls=%async_computation.2 | async-start | bytes 983040 | tf_op jit(solution)/shard_map/all_to_all | solution.py:1258
  249.3 13.8 %all-to-all-start.3 = ((bf16[8,64,384]{2,1,0:T(8,128)(2,1)}), bf16[8,64,384]{2,1,0:T(8,128)(2,1)S(1)}, u32[]{:S(2)}, u32[]{:S(2)}) async-start(bf16[8,64,384]{2,1,0:T(8,128)(2,1)} %chunk_scan.5), calls=%async_computation.3 | async-start | bytes 786432 | tf_op jit(solution)/shard_map/all_to_all | solution.py:1258
  256.3 217.4 %reduce-scatter.7.cloned.1.call-start = ((), (), s32[]{:S(2)}) async-start(), calls=%async_computation.17 | async-start | bytes 5898240 | tf_op jit(solution)/shard_map/reduce_scatter | solution.py:1473
  292.1 181.5 %reduce-scatter.5.cloned.1.call-start = ((), (), s32[]{:S(2)}) async-start(), calls=%async_computation.16 | async-start | bytes 5898240 | tf_op jit(solution)/shard_map/reduce_scatter | solution.py:1473
  302.5 15.2 %collective-permute-start.23 = (f32[128,1536]{1,0:T(8,128)}, f32[128,1536]{1,0:T(8,128)S(1)}, u32[]{:S(2)}, u32[]{:S(2)}) collective-permute-start(f32[128,1536]{1,0:T(8,128)} %get-tuple-element.257), channel_id=1, source_target_pairs={{64,65},{65,64},{66,67},{67,66},{68,69},{69,68},{70,71},{71,70},{7... | collective-permute-start | bytes 2359304 | tf_op jit(solution)/shard_map/ppermute | solution.py:1564
  303.2 15.8 %all-to-all-start.4 = ((bf16[8,80,384]{2,1,0:T(8,128)(2,1)}), bf16[8,80,384]{2,1,0:T(8,128)(2,1)S(1)}, u32[]{:S(2)}, u32[]{:S(2)}) async-start(bf16[8,80,384]{2,1,0:T(8,128)(2,1)} %get-tuple-element.162.token), calls=%async_computation.4 | async-start | bytes 983040 | tf_op jit(solution)/shard_map/all_to_all | solution.py:1258
  321.7 16.2 %all-to-all-start.5 = ((bf16[8,64,384]{2,1,0:T(8,128)(2,1)}), bf16[8,64,384]{2,1,0:T(8,128)(2,1)S(1)}, u32[]{:S(2)}, u32[]{:S(2)}) async-start(bf16[8,64,384]{2,1,0:T(8,128)(2,1)} %chunk_scan.6), calls=%async_computation.5 | async-start | bytes 786432 | tf_op jit(solution)/shard_map/all_to_all | solution.py:1258
  329.2 144.4 %reduce-scatter.9.cloned.1.call-start = ((), (), s32[]{:S(2)}) async-start(), calls=%async_computation.18 | async-start | bytes 7372800 | tf_op jit(solution)/shard_map/reduce_scatter | solution.py:1473
  374.5 139.6 %reduce-scatter.11.cloned.1.call-start = ((), (), s32[]{:S(2)}) async-start(), calls=%async_computation.19 | async-start | bytes 5898240 | tf_op jit(solution)/shard_map/reduce_scatter | solution.py:1473
  403.1 15.5 %all-to-all-start.6 = ((bf16[8,80,384]{2,1,0:T(8,128)(2,1)}), bf16[8,80,384]{2,1,0:T(8,128)(2,1)S(1)}, u32[]{:S(2)}, u32[]{:S(2)}) async-start(bf16[8,80,384]{2,1,0:T(8,128)(2,1)} %get-tuple-element.183.token), calls=%async_computation.6 | async-start | bytes 983040 | tf_op jit(solution)/shard_map/all_to_all | solution.py:1258
  421.3 15.6 %all-to-all-start.7 = ((bf16[8,64,384]{2,1,0:T(8,128)(2,1)}), bf16[8,64,384]{2,1,0:T(8,128)(2,1)S(1)}, u32[]{:S(2)}, u32[]{:S(2)}) async-start(bf16[8,64,384]{2,1,0:T(8,128)(2,1)} %chunk_scan.7), calls=%async_computation.7 | async-start | bytes 786432 | tf_op jit(solution)/shard_map/all_to_all | solution.py:1258
  468.0 61.1 %all-to-all-start.8 = ((bf16[4,384,1664]{2,1,0:T(8,128)(2,1)}), bf16[4,384,1664]{2,1,0:T(8,128)(2,1)}, u32[]{:S(2)}, u32[]{:S(2)}) async-start(bf16[4,384,1664]{2,1,0:T(8,128)(2,1)} %terms.2.rest_10_), calls=%async_computation.11 | async-start | bytes 10223616 | tf_op jit(solution)/shard_map/all_to_all | solution.py:1254
  529.1 103.9 %all-to-all-start.9 = ((bf16[4,96,6528]{2,1,0:T(8,128)(2,1)}), bf16[4,96,6528]{2,1,0:T(8,128)(2,1)}, u32[]{:S(2)}, u32[]{:S(2)}) async-start(bf16[4,96,6528]{2,1,0:T(8,128)(2,1)} %fold.4.rest_1_), calls=%async_computation.13 | async-start | bytes 10027008 | tf_op jit(solution)/shard_map/all_to_all | solution.py:1254
  548.3 69.5 %collective-permute-start.32 = (bf16[416,1792]{1,0:T(8,128)(2,1)}, bf16[416,1792]{1,0:T(8,128)(2,1)S(1)}, u32[]{:S(2)}, u32[]{:S(2)}) collective-permute-start(bf16[416,1792]{1,0:T(8,128)(2,1)} %get-tuple-element.219), channel_id=1, source_target_pairs={{0,1},{1,2},{2,3},{3,0},{4,5},{5,6},{6,7},{7,4},{8,9},{9,10},{10,1... | collective-permute-start | bytes 4472840 | tf_op jit(solution)/shard_map/ppermute | solution.py:1066
  549.6 68.2 %collective-permute-start.33 = (bf16[416,1792]{1,0:T(8,128)(2,1)}, bf16[416,1792]{1,0:T(8,128)(2,1)S(1)}, u32[]{:S(2)}, u32[]{:S(2)}) collective-permute-start(bf16[416,1792]{1,0:T(8,128)(2,1)} %get-tuple-element.220), channel_id=1, source_target_pairs={{0,2},{1,3},{2,0},{3,1},{4,6},{5,7},{6,4},{7,5},{8,10},{9,11},{10,... | collective-permute-start | bytes 4472840 | tf_op jit(solution)/shard_map/ppermute | solution.py:1066
  549.6 68.2 %collective-permute-start.34 = (bf16[416,1792]{1,0:T(8,128)(2,1)}, bf16[416,1792]{1,0:T(8,128)(2,1)}, u32[]{:S(2)}, u32[]{:S(2)}) collective-permute-start(bf16[416,1792]{1,0:T(8,128)(2,1)} %get-tuple-element.221), channel_id=1, source_target_pairs={{0,3},{1,0},{2,1},{3,2},{4,7},{5,4},{6,5},{7,6},{8,11},{9,8},{10,9... | collective-permute-start | bytes 4472840 | tf_op jit(solution)/shard_map/ppermute | solution.py:1066
  552.1 89.9 %collective-permute-start.28 = (f32[128,1536]{1,0:T(8,128)}, f32[128,1536]{1,0:T(8,128)S(1)}, u32[]{:S(2)}, u32[]{:S(2)}) collective-permute-start(f32[128,1536]{1,0:T(8,128)} %get-tuple-element.260), channel_id=1, source_target_pairs={{0,1},{1,0},{2,3},{3,2},{4,5},{5,4},{6,7},{7,6},{8,9},{9,8},{10,11... | collective-permute-start | bytes 2359304 | tf_op jit(solution)/shard_map/ppermute | solution.py:1564
  560.1 68.9 %collective-permute-start.29 = (bf16[96,1664]{1,0:T(8,128)(2,1)}, bf16[96,1664]{1,0:T(8,128)(2,1)S(1)}, u32[]{:S(2)}, u32[]{:S(2)}) collective-permute-start(bf16[96,1664]{1,0:T(8,128)(2,1)} %get-tuple-element.205), channel_id=1, source_target_pairs={{0,1},{1,2},{2,3},{3,0},{4,5},{5,6},{6,7},{7,4},{8,9},{9,10},{10,1... | collective-permute-start | bytes 958472 | tf_op jit(solution)/shard_map/ppermute | solution.py:1066
  617.8 14.6 %collective-permute-start.30 = (bf16[96,1664]{1,0:T(8,128)(2,1)}, bf16[96,1664]{1,0:T(8,128)(2,1)}, u32[]{:S(2)}, u32[]{:S(2)}) collective-permute-start(bf16[96,1664]{1,0:T(8,128)(2,1)} %get-tuple-element.206), channel_id=1, source_target_pairs={{0,2},{1,3},{2,0},{3,1},{4,6},{5,7},{6,4},{7,5},{8,10},{9,11},{10,... | collective-permute-start | bytes 958472 | tf_op jit(solution)/shard_map/ppermute | solution.py:1066
  625.2 16.8 %collective-permute-start.35 = (bf16[128,1792]{1,0:T(8,128)(2,1)}, bf16[128,1792]{1,0:T(8,128)(2,1)}, u32[]{:S(2)}, u32[]{:S(2)}) collective-permute-start(bf16[128,1792]{1,0:T(8,128)(2,1)} %get-tuple-element.223), channel_id=1, source_target_pairs={{0,4},{1,5},{2,6},{3,7},{4,8},{5,9},{6,10},{7,11},{8,12},{9,13},{1... | collective-permute-start | bytes 1376264 | tf_op jit(solution)/shard_map/ppermute | solution.py:1066
  629.0 16.4 %collective-permute-start.36 = (bf16[128,1792]{1,0:T(8,128)(2,1)}, bf16[128,1792]{1,0:T(8,128)(2,1)}, u32[]{:S(2)}, u32[]{:S(2)}) collective-permute-start(bf16[128,1792]{1,0:T(8,128)(2,1)} %get-tuple-element.224), channel_id=1, source_target_pairs={{0,8},{1,9},{2,10},{3,11},{4,12},{5,13},{6,14},{7,15},{8,0},{9,1},... | collective-permute-start | bytes 1376264 | tf_op jit(solution)/shard_map/ppermute | solution.py:1066
  637.9 17.2 %collective-permute-start.42 = (bf16[24,6528]{1,0:T(8,128)(2,1)}, bf16[24,6528]{1,0:T(8,128)(2,1)S(1)}, u32[]{:S(2)}, u32[]{:S(2)}) collective-permute-start(bf16[24,6528]{1,0:T(8,128)(2,1)} %get-tuple-element.231), channel_id=1, source_target_pairs={{0,2},{1,3},{2,0},{3,1},{4,6},{5,7},{6,4},{7,5},{8,10},{9,11},{10,... | collective-permute-start | bytes 940040 | tf_op jit(solution)/shard_map/ppermute | solution.py:1066
  642.0 14.2 %collective-permute-start.43 = (bf16[24,6528]{1,0:T(8,128)(2,1)}, bf16[24,6528]{1,0:T(8,128)(2,1)}, u32[]{:S(2)}, u32[]{:S(2)}) collective-permute-start(bf16[24,6528]{1,0:T(8,128)(2,1)} %get-tuple-element.232), channel_id=1, source_target_pairs={{0,1},{1,2},{2,3},{3,0},{4,5},{5,6},{6,7},{7,4},{8,9},{9,10},{10,1... | collective-permute-start | bytes 940040 | tf_op jit(solution)/shard_map/ppermute | solution.py:1066
  642.0 14.2 %collective-permute-start.44 = (bf16[24,6528]{1,0:T(8,128)(2,1)}, bf16[24,6528]{1,0:T(8,128)(2,1)}, u32[]{:S(2)}, u32[]{:S(2)}) collective-permute-start(bf16[24,6528]{1,0:T(8,128)(2,1)} %get-tuple-element.233), channel_id=1, source_target_pairs={{0,3},{1,0},{2,1},{3,2},{4,7},{5,4},{6,5},{7,6},{8,11},{9,8},{10,9... | collective-permute-start | bytes 940040 | tf_op jit(solution)/shard_map/ppermute | solution.py:1066
  655.1 14.4 %collective-permute-start.40 = (bf16[56,3456]{1,0:T(8,128)(2,1)}, bf16[56,3456]{1,0:T(8,128)(2,1)S(1)}, u32[]{:S(2)}, u32[]{:S(2)}) collective-permute-start(bf16[56,3456]{1,0:T(8,128)(2,1)} %get-tuple-element.230), channel_id=1, source_target_pairs={{0,48},{16,0},{32,16},{48,32},{1,49},{17,1},{33,17},{49,33},{2,50}... | collective-permute-start | bytes 1161224 | tf_op jit(solution)/shard_map/ppermute | solution.py:1066
  673.4 14.4 %collective-permute-start.47 = (f32[24,1536]{1,0:T(8,128)S(1)}, f32[24,1536]{1,0:T(8,128)S(1)}, u32[]{:S(2)}, u32[]{:S(2)}) collective-permute-start(f32[24,1536]{1,0:T(8,128)S(1)} %get-tuple-element.270), channel_id=1, source_target_pairs={{0,64},{1,0},{2,65},{3,1},{4,66},{5,2},{6,67},{7,3},{8,68},{9,4},{... | collective-permute-start | bytes 442376 | tf_op jit(solution)/shard_map/ppermute | solution.py:1603
  (71 other events, 680.5 us)
Sparse Core Ops, SparseCore 0:
  63.3 32.9 all-gather.8
  97.9 64.5 all-gather.4
  164.3 92.5 all-gather.6
  292.3 52.3 reduce-scatter.6
  347.0 50.8 reduce-scatter.4
  400.2 60.5 reduce-scatter.8
  463.1 50.8 reduce-scatter.10

commit v5 on v4

--- a/solution.py
+++ b/solution.py
@@ -1457,7 +1457,7 @@
         xa, bca, cum, dt, s0, msg = state_call(info, mixed, halo, cpar, rate, hpar)
         came = exchange(msg)
         y_in = inside_call(xa, bca, cum, dt, hpar)
-        hin = exchange(scan_call(info, came, False, y_in)).reshape(GROUPS, STATE, BLOCK)
+        hin = exchange(scan_call(info, came, False, y_in, *([] if layer else cpars[1:]))).reshape(GROUPS, STATE, BLOCK)
         y, part = out_proj(
             info, y_in, bca, cum, hin, s0, gate, gains_two[layer], weights_o[layer]
         )
@@ -1480,12 +1480,12 @@
         came = exchange(msg_back)
         dxi, d_skips, gsum, u, dbc = inside_back(dy, xa, bca, cum, dt, hpar)
         part = gate_in_back(info, dz, weights_z[layer], msg_back)
-        lam = exchange(scan_call(info, came, True, part, *tokens)).reshape(GROUPS, STATE, BLOCK)
+        lam = exchange(scan_call(info, came, True, part)).reshape(GROUPS, STATE, BLOCK)
         dmx, dmbc, tailx, tailbc, edgex, edgebc, d_parx, d_parbc, d_heads = finish_call(
             info, xa, dxi, dy, mixed, halo, cpar, bca, cum, dt, rate, hpar, lam, hin, s0, own1, u, gsum, dbc
         )
         edge = halo_shift(jnp.concatenate([edgex, edgebc], axis=1), -1)
-        dxc = patch(dmx, dmbc, tailx, tailbc, edge, d_heads)
+        dxc = patch(dmx, dmbc, tailx, tailbc, edge, *tokens)
         middle = 7 * LANES
         if layer == 0:
             higher_rows, higher = higher
@@ -1516,8 +1516,9 @@
 
         rows = jnp.concatenate([rows, higher_rows]).astype(BF16)
         cuts = [(normed_t, dxc, slice(middle, PACKED)), (grad_o, bg, slice(WIDTH // 2, WIDTH))]
-        right = arrived(terms(info, "x", cuts, (rows,)), "x")
-        tall = fold(info, "y", [[v] for v in higher + sums], 1, 96, dh_low, True)
+        right = terms(info, "x", cuts, (rows,))
+        tall = fold(info, "y", [[v] for v in higher + sums], 1, 96, right[0], True)
+        right = arrived(right, "x")
         left = fold(info, "x", [[traded(left, "y")]], 4, 24, tall)
         right = fold(info, "y", [right], 4, 24, dh_low)
         tall = fold(info, "x", [[traded(tall, "y")]], 1, 24, right[0])
@@ -1546,8 +1547,9 @@
     late = after(low_x[3:6] + low_x[7:10], place)["z"]
     got = [None] + [lax.dynamic_index_in_dim(got, (late + r) % 4, 0, False) for r in range(1, 4)]
     low_zo = pieces(mine_zo, came_zo, got, 0)
-    high_x = [lax.all_gather(jnp.where(section == 1, mine_x, came_x), "dp", tiled=True)]
-    high_zo = [lax.all_gather(jnp.where(section == 1, mine_zo, came_zo), "dp", tiled=True)]
+    here = after([low_x[2], low_x[6]], {"section": section})["section"]
+    high_x = [lax.all_gather(jnp.where(here == 1, mine_x, came_x), "dp", tiled=True)]
+    high_zo = [lax.all_gather(jnp.where(here == 1, mine_zo, came_zo), "dp", tiled=True)]
     ready = low_zo[3:6] + low_zo[7:10]
     weights_x = [Weight(v, n, PACKED) for n, v in enumerate((low_x, high_x))]
     weights_z = [Weight(v, n, LOCAL) for n, v in enumerate((low_zo, high_zo))]
@@ -1568,7 +1570,7 @@
     out_high, saved_high = forward(middle, 1)
     top_high = returned(out_high, 1)
     _, back, higher, rows = backward(cotangent, saved_high, 1, None, [top_high])
-    dh_low, (tall, low_o), low_x, rows = backward(back, saved_low, 0, (rows, higher), [])
+    dh_low, (tall, low_o), low_x, rows = backward(back, saved_low, 0, (rows, higher), [rows])
     at = (LOCAL, LOCAL + WIDTH, LOCAL + WIDTH + PACKED)
     high_z, high_o, high_x, low_z = jnp.split(summed(tall), at, axis=1)
 

time: 713 us -> 702 us (0.985)
  waiting for transfers between devices: 196 us -> 180 us
    ppermute x30, waiting for transfers between devices: 114 us -> 106 us  [send(): return lax.ppermute(value, name, pairs)]
    unnamed x110 -> x108, local copies, waits for them, and re-layouts: 20.2 us -> 19.4 us
  transfers between devices with their start and end apart: 65 -> 65, of which waited for: 30 -> 29; matrix products, arithmetic and copies ran while one was open for 6% -> 7% of each run, Pallas kernels for 34% -> 35%
where the time goes in v5:
time: 702 us; the launch traced here: 689 us
  Pallas kernels  261 us (37%)
  waiting for transfers between devices  180 us (26%)
  starting transfers between devices  155 us (22%)
  local copies, waits for them, and re-layouts  46.7 us (7%)
  other arithmetic  24.8 us (4%)
  between operations  21.7 us (3%)
    ppermute x30, waiting for transfers between devices, send(): return lax.ppermute(value, name, pairs)  106 us
    all_to_all x8, starting transfers between devices, exchange(): return lax.all_to_all(value, 'ctx', 0, 0, axis_index_groups=PARITY)  75.9 us
    ppermute x30, starting transfers between devices, send(): return lax.ppermute(value, name, pairs)  39.2 us
    pallas_call x2, Pallas kernels, finish_call(): pl.pallas_call(finish_body, grid=(GROUPS,), out_shape=(shape((ROWS, LOCAL...  24.5 us
    pallas_call x4, Pallas kernels, fold(): pl.pallas_call(functools.partial(fold_body, slot, counts, outer, inner, m...  20.3 us
    pallas_call x2, Pallas kernels, mixed_back(): pl.pallas_call(functools.partial(mixed_back_body, weight, len(tokens)), g...  20.1 us
    pallas_call x2, Pallas kernels, gate_back(): pl.pallas_call(functools.partial(gate_back_body, weight), grid=(4,), out_...  19.5 us
    reduce_scatter x4, waiting for transfers between devices, first_stage(): return lax.psum_scatter(value, 'dp', tiled=True)  19.4 us
  transfers between devices with their start and end apart: 65, of which 29 were waited for; matrix products, arithmetic and copies ran while one was open for 7% of the time, Pallas kernels for 35%

profile of v5, /device:TPU:12, one launch (start us, length us, event | category | flops | bytes accessed | tf_op | source)
XLA Modules:
  0.0 688.5 jit_solution(5079081480604349897)
XLA Ops:
  14.2 5.2 collective-permute-done
  38.4 7.6 %collective-permute-done.5.rest_3_.refs_2_ = bf16[112,1920]{1,0:T(8,128)(2,1)S(1)} collective-permute-done((bf16[112,1920]{1,0:T(8,128)(2,1)S(1)}, bf16[112,1920]{1,0:T(8,128)(2,1)S(1)}, u32[]{:S(2)}, u32[]{:S(2)}) %collective-permute-start.5) | collective-permute-done | bytes 430112 | tf_op jit(solution)/shard_map/ppermute | solution.py:1066
  46.0 10.4 %collective-permute-done.4.rest_2_.refs_1_ = bf16[112,1920]{1,0:T(8,128)(2,1)S(1)} collective-permute-done((bf16[112,1920]{1,0:T(8,128)(2,1)S(1)}, bf16[112,1920]{1,0:T(8,128)(2,1)S(1)}, u32[]{:S(2)}, u32[]{:S(2)}) %collective-permute-start.4) | collective-permute-done | bytes 430112 | tf_op jit(solution)/shard_map/ppermute | solution.py:1066
  81.6 9.8 %collective-permute-done.8.rest_5_.refs_2_ = bf16[144,1920]{1,0:T(8,128)(2,1)S(1)} collective-permute-done((bf16[144,1920]{1,0:T(8,128)(2,1)S(1)}, bf16[144,1920]{1,0:T(8,128)(2,1)S(1)}, u32[]{:S(2)}, u32[]{:S(2)}) %collective-permute-start.8) | collective-permute-done | bytes 552992 | tf_op jit(solution)/shard_map/ppermute | solution.py:1066
  91.9 7.8 %collective-permute-done.7.rest_4_.refs_1_ = bf16[144,1920]{1,0:T(8,128)(2,1)S(1)} collective-permute-done((bf16[144,1920]{1,0:T(8,128)(2,1)S(1)}, bf16[144,1920]{1,0:T(8,128)(2,1)S(1)}, u32[]{:S(2)}, u32[]{:S(2)}) %collective-permute-start.7) | collective-permute-done | bytes 552992 | tf_op jit(solution)/shard_map/ppermute | solution.py:1066
  117.1 7.0 %in_proj.2 = (bf16[256,1536]{1,0:T(8,128)(2,1)}, bf16[256,1792]{1,0:T(8,128)(2,1)}, f32[256,128]{1,0:T(8,128)}) custom-call(s32[14]{0:T(128)} %concatenate.116.info, bf16[256,1536]{1,0:T(8,128)(2,1)} %get-tuple-element.262.refs_0_.h_ref, f32[1,1536]{1,0:T(1,128)} %get-tuple-element.125.gain_ref.gain, bf16[400,1920]{1,0:T(8,128)(2,1)} %get-tuple-element.123.rest_0_.token, ...), custom_call_target="tpu_custom_call" | custom-call | flops 1509949440 | bytes 8000000 | tf_op jit(solution)/shard_map/in_proj/pallas_call | solution.py:215
  136.0 5.7 conv_state.2
  141.8 25.5 %all-to-all-start = ((bf16[8,80,384]{2,1,0:T(8,128)(2,1)}), bf16[8,80,384]{2,1,0:T(8,128)(2,1)}, u32[]{:S(2)}, u32[]{:S(2)}) async-start(bf16[8,80,384]{2,1,0:T(8,128)(2,1)} %get-tuple-element.134.msg_in), calls=%async_computation | async-start | bytes 983040 | tf_op jit(solution)/shard_map/all_to_all | solution.py:1258
  167.3 5.8 inside.2.rest_0_.y_in
  178.6 7.2 %all-to-all-start.1 = ((bf16[8,64,384]{2,1,0:T(8,128)(2,1)}), bf16[8,64,384]{2,1,0:T(8,128)(2,1)S(1)}, u32[]{:S(2)}, u32[]{:S(2)}) async-start(bf16[8,64,384]{2,1,0:T(8,128)(2,1)} %chunk_scan.4), calls=%async_computation.1 | async-start | bytes 786432 | tf_op jit(solution)/shard_map/all_to_all | solution.py:1258
  186.7 6.4 gate_proj.2.gate
  193.9 7.6 %out_proj.2 = (f32[256,1536]{1,0:T(8,128)}, f32[256,1664]{1,0:T(8,128)}) custom-call(s32[14]{0:T(128)} %concatenate.116.info, f32[256,1536]{1,0:T(8,128)} %inside.2.rest_0_.y_in, f32[256,256]{1,0:T(8,128)} %get-tuple-element.131.bca, f32[256,128]{1,0:T(8,128)} %get-tuple-element.132.cum, bf16[4,128,384]{2,1,0:T(8,128)(2,1)} %bitcast.71, ...), custom_call_target="tpu_custom_call" | custom-call | flops 1207959552 | bytes 13000000 | tf_op jit(solution)/shard_map/out_proj/pallas_call | solution.py:459
  211.0 7.0 %in_proj.3 = (bf16[256,1536]{1,0:T(8,128)(2,1)}, bf16[256,1792]{1,0:T(8,128)(2,1)}, f32[256,128]{1,0:T(8,128)}) custom-call(s32[14]{0:T(128)} %concatenate.116.info, bf16[256,1536]{1,0:T(8,128)(2,1)} %get-tuple-element.142.h_ref, f32[1,1536]{1,0:T(1,128)} %get-tuple-element.143.gain_ref.gain, bf16[1600,1920]{1,0:T(8,128)(2,1)} %all-gather.5.cloned.1.call-done.rest_0_), custom_call_target="tpu_custom_call" | custom-call | flops 1509949440 | bytes 8000000 | tf_op jit(solution)/shard_map/in_proj/pallas_call | solution.py:215
  227.0 5.7 conv_state.3
  232.7 7.2 %all-to-all-start.2 = ((bf16[8,80,384]{2,1,0:T(8,128)(2,1)}), bf16[8,80,384]{2,1,0:T(8,128)(2,1)S(1)}, u32[]{:S(2)}, u32[]{:S(2)}) async-start(bf16[8,80,384]{2,1,0:T(8,128)(2,1)} %get-tuple-element.151.msg_in), calls=%async_computation.2 | async-start | bytes 983040 | tf_op jit(solution)/shard_map/all_to_all | solution.py:1258
  239.9 5.8 inside.3.rest_0_.y_in
  249.9 6.9 %all-to-all-start.3 = ((bf16[8,64,384]{2,1,0:T(8,128)(2,1)}), bf16[8,64,384]{2,1,0:T(8,128)(2,1)S(1)}, u32[]{:S(2)}, u32[]{:S(2)}) async-start(bf16[8,64,384]{2,1,0:T(8,128)(2,1)} %chunk_scan.5), calls=%async_computation.3 | async-start | bytes 786432 | tf_op jit(solution)/shard_map/all_to_all | solution.py:1258
  256.9 6.3 gate_proj.3.gate
  264.0 7.7 %out_proj.3 = (f32[256,1536]{1,0:T(8,128)}, f32[256,1664]{1,0:T(8,128)}) custom-call(s32[14]{0:T(128)} %concatenate.116.info, f32[256,1536]{1,0:T(8,128)} %inside.3.rest_0_.y_in, f32[256,256]{1,0:T(8,128)} %get-tuple-element.148.bca, f32[256,128]{1,0:T(8,128)} %get-tuple-element.149.cum, bf16[4,128,384]{2,1,0:T(8,128)(2,1)} %bitcast.69, ...), custom_call_target="tpu_custom_call" | custom-call | flops 1207959552 | bytes 13000000 | tf_op jit(solution)/shard_map/out_proj/pallas_call | solution.py:459
  281.7 10.5 %gate_back.2 = (bf16[256,1536]{1,0:T(8,128)(2,1)}, bf16[256,1536]{1,0:T(8,128)(2,1)}, bf16[256,1536]{1,0:T(8,128)(2,1)}, bf16[1536,1536]{1,0:T(8,128)(2,1)}, f32[8,1536]{1,0:T(8,128)}) custom-call(s32[14]{0:T(128)} %concatenate.116.info, bf16[256,1536]{1,0:T(8,128)(2,1)} %get-tuple-element.261.cot, f32[256,1536]{1,0:T(8,128)} %get-tuple-element.155.y, ...), custom_call_target="tpu_custom_call" | custom-call | flops 2415919104 | bytes 17000000 | tf_op jit(solution)/shard_map/gate_back/pallas_call | solution.py:555
  292.2 7.7 %own_grad.2 = (f32[4,128,384]{2,1,0:T(8,128)}, bf16[8,80,384]{2,1,0:T(8,128)(2,1)}, bf16[1536,1536]{1,0:T(8,128)(2,1)}) custom-call(bf16[256,1536]{1,0:T(8,128)(2,1)} %get-tuple-element.159.dy, f32[256,256]{1,0:T(8,128)} %get-tuple-element.148.bca, f32[256,128]{1,0:T(8,128)} %get-tuple-element.149.cum, bf16[8,80,384]{2,1,0:T(8,128)(2,1)} %get-tuple-element.151.msg_in, ...), custom_call_target="tpu_custom_call" | custom-call | flops 1207959552 | bytes 8000000 | tf_op jit(solution)/shard_map/own_grad/pallas_call | solution.py:604
  300.0 7.2 %all-to-all-start.4 = ((bf16[8,80,384]{2,1,0:T(8,128)(2,1)}), bf16[8,80,384]{2,1,0:T(8,128)(2,1)S(1)}, u32[]{:S(2)}, u32[]{:S(2)}) async-start(bf16[8,80,384]{2,1,0:T(8,128)(2,1)} %get-tuple-element.162.token), calls=%async_computation.4 | async-start | bytes 983040 | tf_op jit(solution)/shard_map/all_to_all | solution.py:1258
  310.4 7.2 %gate_in_back.2.rest_0_.part = f32[256,1536]{1,0:T(8,128)} custom-call(s32[14]{0:T(128)} %concatenate.116.info, bf16[256,1536]{1,0:T(8,128)(2,1)} %get-tuple-element.161.dz, bf16[8,80,384]{2,1,0:T(8,128)(2,1)} %get-tuple-element.162.token, bf16[1536,3072]{1,0:T(8,128)(2,1)} %all-gather.7.cloned.1.call-done.rest_0_), custom_call_target="tpu_custom_call" | custom-call | flops 1207959552 | bytes 7000000 | tf_op jit(solution)/shard_map/gate_in_back/pallas_call | solution.py:937
  320.4 7.2 %all-to-all-start.5 = ((bf16[8,64,384]{2,1,0:T(8,128)(2,1)}), bf16[8,64,384]{2,1,0:T(8,128)(2,1)S(1)}, u32[]{:S(2)}, u32[]{:S(2)}) async-start(bf16[8,64,384]{2,1,0:T(8,128)(2,1)} %chunk_scan.6), calls=%async_computation.5 | async-start | bytes 786432 | tf_op jit(solution)/shard_map/all_to_all | solution.py:1258
  327.6 8.7 %inside_back.2 = (f32[256,1536]{1,0:T(8,128)}, f32[8,1536]{1,0:T(8,128)}, f32[32,256]{1,0:T(8,128)}, f32[256,128]{1,0:T(8,128)}, f32[256,256]{1,0:T(8,128)}) custom-call(bf16[256,1536]{1,0:T(8,128)(2,1)} %get-tuple-element.159.dy, f32[256,1536]{1,0:T(8,128)} %get-tuple-element.147.xa, f32[256,256]{1,0:T(8,128)} %get-tuple-element.148.bca, ...), custom_call_target="tpu_custom_call" | custom-call | flops 402653184 | bytes 4500000 | tf_op jit(solution)/shard_map/inside_back/pallas_call | solution.py:699
  337.1 12.3 %finish_back.2 = (bf16[256,1536]{1,0:T(8,128)(2,1)}, bf16[256,384]{1,0:T(8,128)(2,1)}, f32[16,1536]{1,0:T(8,128)}, f32[16,256]{1,0:T(8,128)}, bf16[16,1536]{1,0:...) custom-call(s32[14]{0:T(128)} %concatenate.116.info, ...), custom_call_target="tpu_custom_call" | custom-call | flops 503316480 | bytes 7500000 | tf_op jit(solution)/shard_map/finish_back/pallas_call | solution.py:852
  362.0 11.0 %mixed_back.2 = (f32[256,1536]{1,0:T(8,128)}, f32[8,1536]{1,0:T(8,128)}, bf16[1536,1920]{1,0:T(8,128)(2,1)}) custom-call(s32[14]{0:T(128)} %concatenate.116.info, bf16[256,1920]{1,0:T(8,128)(2,1)} %patch.2.dxc, f32[256,1536]{1,0:T(8,128)} %gate_in_back.2.rest_0_.part, bf16[256,1536]{1,0:T(8,128)(2,1)} %get-tuple-element.142.h_ref, ...), custom_call_target="tpu_custom_call" | custom-call | flops 3019898880 | bytes 14000000 | tf_op jit(solution)/shard_map/mixed_back/pallas_call | solution.py:1008
  384.0 9.0 %gate_back.3 = (bf16[256,1536]{1,0:T(8,128)(2,1)}, bf16[256,1536]{1,0:T(8,128)(2,1)}, bf16[256,1536]{1,0:T(8,128)(2,1)}, bf16[1536,256]{1,0:T(8,128)(2,1)}, f32[8,1536]{1,0:T(8,128)}) custom-call(s32[14]{0:T(128)} %concatenate.116.info, bf16[256,1536]{1,0:T(8,128)(2,1)} %get-tuple-element.175.cot, f32[256,1536]{1,0:T(8,128)} %get-tuple-element.176.y, ...), custom_call_target="tpu_custom_call" | custom-call | flops 2415919104 | bytes 17000000 | tf_op jit(solution)/shard_map/gate_back/pallas_call | solution.py:555
  393.1 7.8 %own_grad.3 = (f32[4,128,384]{2,1,0:T(8,128)}, bf16[8,80,384]{2,1,0:T(8,128)(2,1)}, bf16[1536,1536]{1,0:T(8,128)(2,1)}) custom-call(bf16[256,1536]{1,0:T(8,128)(2,1)} %get-tuple-element.179.dy, f32[256,256]{1,0:T(8,128)} %get-tuple-element.131.bca, f32[256,128]{1,0:T(8,128)} %get-tuple-element.132.cum, bf16[8,80,384]{2,1,0:T(8,128)(2,1)} %get-tuple-element.134.msg_in, ...), custom_call_target="tpu_custom_call" | custom-call | flops 1207959552 | bytes 8000000 | tf_op jit(solution)/shard_map/own_grad/pallas_call | solution.py:604
  400.8 7.3 %all-to-all-start.6 = ((bf16[8,80,384]{2,1,0:T(8,128)(2,1)}), bf16[8,80,384]{2,1,0:T(8,128)(2,1)S(1)}, u32[]{:S(2)}, u32[]{:S(2)}) async-start(bf16[8,80,384]{2,1,0:T(8,128)(2,1)} %get-tuple-element.182.token), calls=%async_computation.6 | async-start | bytes 983040 | tf_op jit(solution)/shard_map/all_to_all | solution.py:1258
  410.6 7.1 %gate_in_back.3.rest_0_.part = f32[256,1536]{1,0:T(8,128)} custom-call(s32[14]{0:T(128)} %concatenate.116.info, bf16[256,1536]{1,0:T(8,128)(2,1)} %get-tuple-element.181.dz, bf16[8,80,384]{2,1,0:T(8,128)(2,1)} %get-tuple-element.182.token, bf16[384,3072]{1,0:T(8,128)(2,1)} %get-tuple-element.138.rest_0_, bf16[384,3072]{1,0:T(8,128)(2,1)} %collective-permute-done.13.rest_1_, ...), custom_call_target="tpu_custom_call" | custom-call | flops 1207959552 | bytes 7000000 | tf_op jit(solution)/shard_map/gate_in_back/pallas_call | solution.py:937
  420.5 7.2 %all-to-all-start.7 = ((bf16[8,64,384]{2,1,0:T(8,128)(2,1)}), bf16[8,64,384]{2,1,0:T(8,128)(2,1)S(1)}, u32[]{:S(2)}, u32[]{:S(2)}) async-start(bf16[8,64,384]{2,1,0:T(8,128)(2,1)} %chunk_scan.7), calls=%async_computation.7 | async-start | bytes 786432 | tf_op jit(solution)/shard_map/all_to_all | solution.py:1258
  429.3 8.7 %inside_back.3 = (f32[256,1536]{1,0:T(8,128)}, f32[8,1536]{1,0:T(8,128)}, f32[32,256]{1,0:T(8,128)}, f32[256,128]{1,0:T(8,128)}, f32[256,256]{1,0:T(8,128)}) custom-call(bf16[256,1536]{1,0:T(8,128)(2,1)} %get-tuple-element.179.dy, f32[256,1536]{1,0:T(8,128)} %get-tuple-element.130.xa, f32[256,256]{1,0:T(8,128)} %get-tuple-element.131.bca, ...), custom_call_target="tpu_custom_call" | custom-call | flops 402653184 | bytes 4500000 | tf_op jit(solution)/shard_map/inside_back/pallas_call | solution.py:699
  438.8 12.2 %finish_back.3 = (bf16[256,1536]{1,0:T(8,128)(2,1)}, bf16[256,384]{1,0:T(8,128)(2,1)}, f32[16,1536]{1,0:T(8,128)}, f32[16,256]{1,0:T(8,128)}, bf16[16,1536]{1,0:...) custom-call(s32[14]{0:T(128)} %concatenate.116.info, ...), custom_call_target="tpu_custom_call" | custom-call | flops 503316480 | bytes 7500000 | tf_op jit(solution)/shard_map/finish_back/pallas_call | solution.py:852
  455.0 5.3 collective-permute-done.26.edge
  463.3 5.9 terms.2.rest_10_
  469.2 6.3 all-to-all-start.8
  476.9 9.0 %mixed_back.3 = (f32[256,1536]{1,0:T(8,128)}, f32[8,1536]{1,0:T(8,128)}) custom-call(s32[14]{0:T(128)} %concatenate.116.info, bf16[256,1920]{1,0:T(8,128)(2,1)} %patch.3.rest_1_.dxc, f32[256,1536]{1,0:T(8,128)} %gate_in_back.3.rest_0_.part, bf16[256,1536]{1,0:T(8,128)(2,1)} %get-tuple-element.262.refs_0_.h_ref, ...), custom_call_target="tpu_custom_call" | custom-call | flops 3019898880 | bytes 14000000 | tf_op jit(solution)/shard_map/mixed_back/pallas_call | solution.py:1008
  487.4 7.7 %terms.3 = (bf16[416,1792]{1,0:T(8,128)(2,1)}, bf16[416,1792]{1,0:T(8,128)(2,1)}, bf16[416,1792]{1,0:T(8,128)(2,1)}, bf16[416,1792]{1,0:T(8,128)(2,1)}) custom-call(s32[14]{0:T(128)} %concatenate.116.info, bf16[1536,256]{1,0:T(8,128)(2,1)} %bitcast.74, bf16[256,1920]{1,0:T(8,128)(2,1)} %patch.3.rest_1_.dxc, bf16[1536,256]{1,0:T(8,128)(2,1)} %get-tuple-element.199.rest_2_, ...), custom_call_target="tpu_custom_call" | custom-call | flops 1409286144 | bytes 8000000 | tf_op jit(solution)/shard_map/terms/pallas_call | solution.py:1160
  495.1 19.4 %reduce-scatter.11.cloned.1.call-done.rest_3_ = bf16[384,1536]{1,0:T(8,128)(2,1)} async-done(((bf16[1536,1536]{1,0:T(8,128)(2,1)}), bf16[384,1536]{1,0:T(8,128)(2,1)}) %reduce-scatter.11.cloned.1.call-update) | async-done | bytes 1179664 | tf_op jit(solution)/shard_map/reduce_scatter | solution.py:1473
  514.5 5.0 fold.4.rest_1_
  519.5 11.4 %all-to-all-done.8.rest_0_ = bf16[4,384,1664]{2,1,0:T(8,128)(2,1)} async-done(((bf16[4,384,1664]{2,1,0:T(8,128)(2,1)}), bf16[4,384,1664]{2,1,0:T(8,128)(2,1)}, u32[]{:S(2)}, u32[]{:S(2)}) %all-to-all-start.8) | async-done | bytes 5111840 | tf_op jit(solution)/shard_map/all_to_all | solution.py:1254
  530.9 6.4 all-to-all-start.9
  557.7 47.2 %collective-permute-done.32.rest_1_ = bf16[416,1792]{1,0:T(8,128)(2,1)S(1)} collective-permute-done((bf16[416,1792]{1,0:T(8,128)(2,1)}, bf16[416,1792]{1,0:T(8,128)(2,1)S(1)}, u32[]{:S(2)}, u32[]{:S(2)}) %collective-permute-start.32) | collective-permute-done | bytes 1490976 | tf_op jit(solution)/shard_map/ppermute | solution.py:1066
  606.5 5.7 fold.6
  614.1 7.9 %collective-permute-done.29.rest_1_ = bf16[96,1664]{1,0:T(8,128)(2,1)S(1)} collective-permute-done((bf16[96,1664]{1,0:T(8,128)(2,1)}, bf16[96,1664]{1,0:T(8,128)(2,1)S(1)}, u32[]{:S(2)}, u32[]{:S(2)}) %collective-permute-start.29) | collective-permute-done | bytes 319520 | tf_op jit(solution)/shard_map/ppermute | solution.py:1066
  656.8 7.5 %collective-permute-start.46 = (f32[24,1536]{1,0:T(8,128)S(1)}, f32[24,1536]{1,0:T(8,128)S(1)}, u32[]{:S(2)}, u32[]{:S(2)}) collective-permute-start(f32[24,1536]{1,0:T(8,128)S(1)} %get-tuple-element.269), channel_id=1, source_target_pairs={{0,0},{1,64},{2,1},{3,65},{4,2},{5,66},{6,3},{7,67},{8,4},{9,68},{... | collective-permute-start | bytes 442376 | tf_op jit(solution)/shard_map/ppermute | solution.py:1605
  669.4 7.2 %collective-permute-done.47 = f32[24,1536]{1,0:T(8,128)S(1)} collective-permute-done((f32[24,1536]{1,0:T(8,128)S(1)}, f32[24,1536]{1,0:T(8,128)S(1)}, u32[]{:S(2)}, u32[]{:S(2)}) %collective-permute-start.47) | collective-permute-done | bytes 147488 | tf_op jit(solution)/shard_map/ppermute | solution.py:1605
  (365 shorter events, 230.9 us)
Async XLA Ops:
  7.2 100.2 %all-gather.9.cloned.1.call-start = ((), (), s32[]{:S(2)}) async-start(), calls=%async_computation.20 | async-start | bytes 2949120 | tf_op jit(solution)/shard_map/all_gather | solution.py:1546
  14.2 15.3 %collective-permute-start.2 = (bf16[400,1920]{1,0:T(8,128)(2,1)}, bf16[400,1920]{1,0:T(8,128)(2,1)}, u32[]{:S(2)}, u32[]{:S(2)}) collective-permute-start(bf16[400,1920]{1,0:T(8,128)(2,1)} %get-tuple-element.124), channel_id=1, source_target_pairs={{0,64},{64,0},{1,65},{65,1},{2,66},{66,2},{3,67},{67,3},{4,68},{68... | collective-permute-start | bytes 4608008 | tf_op jit(solution)/shard_map/ppermute | solution.py:1070
  24.6 36.5 %collective-permute-start.13 = (bf16[384,3072]{1,0:T(8,128)(2,1)}, bf16[384,3072]{1,0:T(8,128)(2,1)}, u32[]{:S(2)}, u32[]{:S(2)}) collective-permute-start(bf16[384,3072]{1,0:T(8,128)(2,1)} %get-tuple-element.139), channel_id=1, source_target_pairs={{0,64},{64,0},{1,65},{65,1},{2,66},{66,2},{3,67},{67,3},{4,68},{68... | collective-permute-start | bytes 7077896 | tf_op jit(solution)/shard_map/ppermute | solution.py:1070
  31.8 14.2 %collective-permute-start.5 = (bf16[112,1920]{1,0:T(8,128)(2,1)S(1)}, bf16[112,1920]{1,0:T(8,128)(2,1)S(1)}, u32[]{:S(2)}, u32[]{:S(2)}) collective-permute-start(bf16[112,1920]{1,0:T(8,128)(2,1)S(1)} %pad_maximum_fusion.5.rest_0_), channel_id=1, source_target_pairs={{0,16},{16,32},{32,48},{48,0},{1,17},{17,33},{33,49},{49,1},{2,18}... | collective-permute-start | bytes 1290248 | tf_op jit(solution)/shard_map/ppermute | solution.py:1066
  33.8 22.6 %collective-permute-start.4 = (bf16[112,1920]{1,0:T(8,128)(2,1)S(1)}, bf16[112,1920]{1,0:T(8,128)(2,1)S(1)}, u32[]{:S(2)}, u32[]{:S(2)}) collective-permute-start(bf16[112,1920]{1,0:T(8,128)(2,1)S(1)} %pad_maximum_fusion.5.rest_0_), channel_id=1, source_target_pairs={{0,32},{16,48},{32,0},{48,16},{1,33},{17,49},{33,1},{49,17},{2,34}... | collective-permute-start | bytes 1290248 | tf_op jit(solution)/shard_map/ppermute | solution.py:1066
  37.4 19.0 %collective-permute-start.3 = (bf16[112,1920]{1,0:T(8,128)(2,1)S(1)}, bf16[112,1920]{1,0:T(8,128)(2,1)S(1)}, u32[]{:S(2)}, u32[]{:S(2)}) collective-permute-start(bf16[112,1920]{1,0:T(8,128)(2,1)S(1)} %pad_maximum_fusion.5.rest_0_), channel_id=1, source_target_pairs={{0,48},{16,0},{32,16},{48,32},{1,49},{17,1},{33,17},{49,33},{2,50}... | collective-permute-start | bytes 1290248 | tf_op jit(solution)/shard_map/ppermute | solution.py:1066
  63.3 109.8 %all-gather.5.cloned.1.call-start = ((), (), s32[]{:S(2)}) async-start(), calls=%async_computation.14 | async-start | bytes 7680000 | tf_op jit(solution)/shard_map/all_gather | solution.py:1551
  71.3 185.6 %all-gather.7.cloned.1.call-start = ((), (), s32[]{:S(2)}) async-start(), calls=%async_computation.15 | async-start | bytes 11796480 | tf_op jit(solution)/shard_map/all_gather | solution.py:1552
  76.0 15.5 %collective-permute-start.8 = (bf16[144,1920]{1,0:T(8,128)(2,1)S(1)}, bf16[144,1920]{1,0:T(8,128)(2,1)S(1)}, u32[]{:S(2)}, u32[]{:S(2)}) collective-permute-start(bf16[144,1920]{1,0:T(8,128)(2,1)S(1)} %copy-done.8), channel_id=1, source_target_pairs={{0,1},{1,2},{2,3},{3,0},{4,5},{5,6},{6,7},{7,4},{8,9},{9,10},{10,1... | collective-permute-start | bytes 1658888 | tf_op jit(solution)/shard_map/ppermute | solution.py:1066
  77.2 22.5 %collective-permute-start.7 = (bf16[144,1920]{1,0:T(8,128)(2,1)S(1)}, bf16[144,1920]{1,0:T(8,128)(2,1)S(1)}, u32[]{:S(2)}, u32[]{:S(2)}) collective-permute-start(bf16[144,1920]{1,0:T(8,128)(2,1)S(1)} %copy-done.8), channel_id=1, source_target_pairs={{0,2},{1,3},{2,0},{3,1},{4,6},{5,7},{6,4},{7,5},{8,10},{9,11},{10,... | collective-permute-start | bytes 1658888 | tf_op jit(solution)/shard_map/ppermute | solution.py:1066
  78.0 23.5 %collective-permute-start.6 = (bf16[144,1920]{1,0:T(8,128)(2,1)S(1)}, bf16[144,1920]{1,0:T(8,128)(2,1)S(1)}, u32[]{:S(2)}, u32[]{:S(2)}) collective-permute-start(bf16[144,1920]{1,0:T(8,128)(2,1)S(1)} %copy-done.8), channel_id=1, source_target_pairs={{0,3},{1,0},{2,1},{3,2},{4,7},{5,4},{6,5},{7,6},{8,11},{9,8},{10,9... | collective-permute-start | bytes 1658888 | tf_op jit(solution)/shard_map/ppermute | solution.py:1066
  79.1 22.4 %collective-permute-start.11 = (bf16[144,1920]{1,0:T(8,128)(2,1)S(1)}, bf16[144,1920]{1,0:T(8,128)(2,1)}, u32[]{:S(2)}, u32[]{:S(2)}) collective-permute-start(bf16[144,1920]{1,0:T(8,128)(2,1)S(1)} %copy-done.7), channel_id=1, source_target_pairs={{0,4},{1,5},{2,6},{3,7},{4,8},{5,9},{6,10},{7,11},{8,12},{9,13},{1... | collective-permute-start | bytes 1658888 | tf_op jit(solution)/shard_map/ppermute | solution.py:1066
  80.7 20.8 %collective-permute-start.10 = (bf16[144,1920]{1,0:T(8,128)(2,1)S(1)}, bf16[144,1920]{1,0:T(8,128)(2,1)}, u32[]{:S(2)}, u32[]{:S(2)}) collective-permute-start(bf16[144,1920]{1,0:T(8,128)(2,1)S(1)} %copy-done.7), channel_id=1, source_target_pairs={{0,8},{1,9},{2,10},{3,11},{4,12},{5,13},{6,14},{7,15},{8,0},{9,1},... | collective-permute-start | bytes 1658888 | tf_op jit(solution)/shard_map/ppermute | solution.py:1066
  91.5 13.4 %collective-permute-start.9 = (bf16[144,1920]{1,0:T(8,128)(2,1)S(1)}, bf16[144,1920]{1,0:T(8,128)(2,1)}, u32[]{:S(2)}, u32[]{:S(2)}) collective-permute-start(bf16[144,1920]{1,0:T(8,128)(2,1)S(1)} %copy-done.7), channel_id=1, source_target_pairs={{0,12},{1,13},{2,14},{3,15},{4,0},{5,1},{6,2},{7,3},{8,4},{9,5},{1... | collective-permute-start | bytes 1658888 | tf_op jit(solution)/shard_map/ppermute | solution.py:1066
  110.1 25.0 %collective-permute-start.16 = (bf16[144,3072]{1,0:T(8,128)(2,1)S(1)}, bf16[144,3072]{1,0:T(8,128)(2,1)S(1)}, u32[]{:S(2)}, u32[]{:S(2)}) collective-permute-start(bf16[144,3072]{1,0:T(8,128)(2,1)S(1)} %pad_maximum_fusion.rest_2_), channel_id=1, source_target_pairs={{0,1},{1,2},{2,3},{3,0},{4,5},{5,6},{6,7},{7,4},{8,9},{9,10},{10,1... | collective-permute-start | bytes 2654216 | tf_op jit(solution)/shard_map/ppermute | solution.py:1066
  129.2 56.6 %collective-permute-start.15 = (bf16[144,3072]{1,0:T(8,128)(2,1)S(1)}, bf16[144,3072]{1,0:T(8,128)(2,1)S(1)}, u32[]{:S(2)}, u32[]{:S(2)}) collective-permute-start(bf16[144,3072]{1,0:T(8,128)(2,1)S(1)} %pad_maximum_fusion.rest_2_), channel_id=1, source_target_pairs={{0,2},{1,3},{2,0},{3,1},{4,6},{5,7},{6,4},{7,5},{8,10},{9,11},{10,... | collective-permute-start | bytes 2654216 | tf_op jit(solution)/shard_map/ppermute | solution.py:1066
  130.5 55.3 %collective-permute-start.14 = (bf16[144,3072]{1,0:T(8,128)(2,1)S(1)}, bf16[144,3072]{1,0:T(8,128)(2,1)}, u32[]{:S(2)}, u32[]{:S(2)}) collective-permute-start(bf16[144,3072]{1,0:T(8,128)(2,1)S(1)} %pad_maximum_fusion.rest_2_), channel_id=1, source_target_pairs={{0,3},{1,0},{2,1},{3,2},{4,7},{5,4},{6,5},{7,6},{8,11},{9,8},{10,9... | collective-permute-start | bytes 2654216 | tf_op jit(solution)/shard_map/ppermute | solution.py:1066
  131.7 54.1 %collective-permute-start.19 = (bf16[144,3072]{1,0:T(8,128)(2,1)S(1)}, bf16[144,3072]{1,0:T(8,128)(2,1)}, u32[]{:S(2)}, u32[]{:S(2)}) collective-permute-start(bf16[144,3072]{1,0:T(8,128)(2,1)S(1)} %pad_maximum_fusion.1.rest_6_), channel_id=1, source_target_pairs={{0,4},{1,5},{2,6},{3,7},{4,8},{5,9},{6,10},{7,11},{8,12},{9,13},{1... | collective-permute-start | bytes 2654216 | tf_op jit(solution)/shard_map/ppermute | solution.py:1066
  134.8 51.0 %collective-permute-start.18 = (bf16[144,3072]{1,0:T(8,128)(2,1)S(1)}, bf16[144,3072]{1,0:T(8,128)(2,1)}, u32[]{:S(2)}, u32[]{:S(2)}) collective-permute-start(bf16[144,3072]{1,0:T(8,128)(2,1)S(1)} %pad_maximum_fusion.1.rest_6_), channel_id=1, source_target_pairs={{0,8},{1,9},{2,10},{3,11},{4,12},{5,13},{6,14},{7,15},{8,0},{9,1},... | collective-permute-start | bytes 2654216 | tf_op jit(solution)/shard_map/ppermute | solution.py:1066
  135.1 50.8 %collective-permute-start.17 = (bf16[144,3072]{1,0:T(8,128)(2,1)S(1)}, bf16[144,3072]{1,0:T(8,128)(2,1)}, u32[]{:S(2)}, u32[]{:S(2)}) collective-permute-start(bf16[144,3072]{1,0:T(8,128)(2,1)S(1)} %pad_maximum_fusion.1.rest_6_), channel_id=1, source_target_pairs={{0,12},{1,13},{2,14},{3,15},{4,0},{5,1},{6,2},{7,3},{8,4},{9,5},{1... | collective-permute-start | bytes 2654216 | tf_op jit(solution)/shard_map/ppermute | solution.py:1066
  141.8 34.8 %all-to-all-start = ((bf16[8,80,384]{2,1,0:T(8,128)(2,1)}), bf16[8,80,384]{2,1,0:T(8,128)(2,1)}, u32[]{:S(2)}, u32[]{:S(2)}) async-start(bf16[8,80,384]{2,1,0:T(8,128)(2,1)} %get-tuple-element.134.msg_in), calls=%async_computation | async-start | bytes 983040 | tf_op jit(solution)/shard_map/all_to_all | solution.py:1258
  178.6 14.6 %all-to-all-start.1 = ((bf16[8,64,384]{2,1,0:T(8,128)(2,1)}), bf16[8,64,384]{2,1,0:T(8,128)(2,1)S(1)}, u32[]{:S(2)}, u32[]{:S(2)}) async-start(bf16[8,64,384]{2,1,0:T(8,128)(2,1)} %chunk_scan.4), calls=%async_computation.1 | async-start | bytes 786432 | tf_op jit(solution)/shard_map/all_to_all | solution.py:1258
  232.7 14.5 %all-to-all-start.2 = ((bf16[8,80,384]{2,1,0:T(8,128)(2,1)}), bf16[8,80,384]{2,1,0:T(8,128)(2,1)S(1)}, u32[]{:S(2)}, u32[]{:S(2)}) async-start(bf16[8,80,384]{2,1,0:T(8,128)(2,1)} %get-tuple-element.151.msg_in), calls=%async_computation.2 | async-start | bytes 983040 | tf_op jit(solution)/shard_map/all_to_all | solution.py:1258
  249.9 13.4 %all-to-all-start.3 = ((bf16[8,64,384]{2,1,0:T(8,128)(2,1)}), bf16[8,64,384]{2,1,0:T(8,128)(2,1)S(1)}, u32[]{:S(2)}, u32[]{:S(2)}) async-start(bf16[8,64,384]{2,1,0:T(8,128)(2,1)} %chunk_scan.5), calls=%async_computation.3 | async-start | bytes 786432 | tf_op jit(solution)/shard_map/all_to_all | solution.py:1258
  256.8 220.0 %reduce-scatter.7.cloned.1.call-start = ((), (), s32[]{:S(2)}) async-start(), calls=%async_computation.17 | async-start | bytes 5898240 | tf_op jit(solution)/shard_map/reduce_scatter | solution.py:1473
  292.2 184.6 %reduce-scatter.5.cloned.1.call-start = ((), (), s32[]{:S(2)}) async-start(), calls=%async_computation.16 | async-start | bytes 5898240 | tf_op jit(solution)/shard_map/reduce_scatter | solution.py:1473
  300.0 17.7 %all-to-all-start.4 = ((bf16[8,80,384]{2,1,0:T(8,128)(2,1)}), bf16[8,80,384]{2,1,0:T(8,128)(2,1)S(1)}, u32[]{:S(2)}, u32[]{:S(2)}) async-start(bf16[8,80,384]{2,1,0:T(8,128)(2,1)} %get-tuple-element.162.token), calls=%async_computation.4 | async-start | bytes 983040 | tf_op jit(solution)/shard_map/all_to_all | solution.py:1258
  309.7 43.1 %collective-permute-start.24 = (f32[128,1536]{1,0:T(8,128)}, f32[128,1536]{1,0:T(8,128)S(1)}, u32[]{:S(2)}, u32[]{:S(2)}) collective-permute-start(f32[128,1536]{1,0:T(8,128)} %get-tuple-element.257), channel_id=1, source_target_pairs={{64,65},{65,64},{66,67},{67,66},{68,69},{69,68},{70,71},{71,70},{7... | collective-permute-start | bytes 2359304 | tf_op jit(solution)/shard_map/ppermute | solution.py:1566
  320.4 15.9 %all-to-all-start.5 = ((bf16[8,64,384]{2,1,0:T(8,128)(2,1)}), bf16[8,64,384]{2,1,0:T(8,128)(2,1)S(1)}, u32[]{:S(2)}, u32[]{:S(2)}) async-start(bf16[8,64,384]{2,1,0:T(8,128)(2,1)} %chunk_scan.6), calls=%async_computation.5 | async-start | bytes 786432 | tf_op jit(solution)/shard_map/all_to_all | solution.py:1258
  327.6 149.2 %reduce-scatter.9.cloned.1.call-start = ((), (), s32[]{:S(2)}) async-start(), calls=%async_computation.18 | async-start | bytes 7372800 | tf_op jit(solution)/shard_map/reduce_scatter | solution.py:1473
  373.1 141.4 %reduce-scatter.11.cloned.1.call-start = ((), (), s32[]{:S(2)}) async-start(), calls=%async_computation.19 | async-start | bytes 5898240 | tf_op jit(solution)/shard_map/reduce_scatter | solution.py:1473
  400.8 16.9 %all-to-all-start.6 = ((bf16[8,80,384]{2,1,0:T(8,128)(2,1)}), bf16[8,80,384]{2,1,0:T(8,128)(2,1)S(1)}, u32[]{:S(2)}, u32[]{:S(2)}) async-start(bf16[8,80,384]{2,1,0:T(8,128)(2,1)} %get-tuple-element.182.token), calls=%async_computation.6 | async-start | bytes 983040 | tf_op jit(solution)/shard_map/all_to_all | solution.py:1258
  420.5 17.6 %all-to-all-start.7 = ((bf16[8,64,384]{2,1,0:T(8,128)(2,1)}), bf16[8,64,384]{2,1,0:T(8,128)(2,1)S(1)}, u32[]{:S(2)}, u32[]{:S(2)}) async-start(bf16[8,64,384]{2,1,0:T(8,128)(2,1)} %chunk_scan.7), calls=%async_computation.7 | async-start | bytes 786432 | tf_op jit(solution)/shard_map/all_to_all | solution.py:1258
  469.2 61.7 %all-to-all-start.8 = ((bf16[4,384,1664]{2,1,0:T(8,128)(2,1)}), bf16[4,384,1664]{2,1,0:T(8,128)(2,1)}, u32[]{:S(2)}, u32[]{:S(2)}) async-start(bf16[4,384,1664]{2,1,0:T(8,128)(2,1)} %terms.2.rest_10_), calls=%async_computation.11 | async-start | bytes 10223616 | tf_op jit(solution)/shard_map/all_to_all | solution.py:1254
  530.9 94.9 %all-to-all-start.9 = ((bf16[4,96,6528]{2,1,0:T(8,128)(2,1)}), bf16[4,96,6528]{2,1,0:T(8,128)(2,1)}, u32[]{:S(2)}, u32[]{:S(2)}) async-start(bf16[4,96,6528]{2,1,0:T(8,128)(2,1)} %fold.4.rest_1_), calls=%async_computation.13 | async-start | bytes 10027008 | tf_op jit(solution)/shard_map/all_to_all | solution.py:1254
  537.3 67.6 %collective-permute-start.32 = (bf16[416,1792]{1,0:T(8,128)(2,1)}, bf16[416,1792]{1,0:T(8,128)(2,1)S(1)}, u32[]{:S(2)}, u32[]{:S(2)}) collective-permute-start(bf16[416,1792]{1,0:T(8,128)(2,1)} %get-tuple-element.218), channel_id=1, source_target_pairs={{0,1},{1,2},{2,3},{3,0},{4,5},{5,6},{6,7},{7,4},{8,9},{9,10},{10,1... | collective-permute-start | bytes 4472840 | tf_op jit(solution)/shard_map/ppermute | solution.py:1066
  538.4 66.5 %collective-permute-start.33 = (bf16[416,1792]{1,0:T(8,128)(2,1)}, bf16[416,1792]{1,0:T(8,128)(2,1)S(1)}, u32[]{:S(2)}, u32[]{:S(2)}) collective-permute-start(bf16[416,1792]{1,0:T(8,128)(2,1)} %get-tuple-element.219), channel_id=1, source_target_pairs={{0,2},{1,3},{2,0},{3,1},{4,6},{5,7},{6,4},{7,5},{8,10},{9,11},{10,... | collective-permute-start | bytes 4472840 | tf_op jit(solution)/shard_map/ppermute | solution.py:1066
  538.4 68.0 %collective-permute-start.34 = (bf16[416,1792]{1,0:T(8,128)(2,1)}, bf16[416,1792]{1,0:T(8,128)(2,1)}, u32[]{:S(2)}, u32[]{:S(2)}) collective-permute-start(bf16[416,1792]{1,0:T(8,128)(2,1)} %get-tuple-element.220), channel_id=1, source_target_pairs={{0,3},{1,0},{2,1},{3,2},{4,7},{5,4},{6,5},{7,6},{8,11},{9,8},{10,9... | collective-permute-start | bytes 4472840 | tf_op jit(solution)/shard_map/ppermute | solution.py:1066
  548.9 85.8 %collective-permute-start.28 = (f32[128,1536]{1,0:T(8,128)}, f32[128,1536]{1,0:T(8,128)S(1)}, u32[]{:S(2)}, u32[]{:S(2)}) collective-permute-start(f32[128,1536]{1,0:T(8,128)} %get-tuple-element.260), channel_id=1, source_target_pairs={{0,1},{1,0},{2,3},{3,2},{4,5},{5,4},{6,7},{7,6},{8,9},{9,8},{10,11... | collective-permute-start | bytes 2359304 | tf_op jit(solution)/shard_map/ppermute | solution.py:1566
  556.8 65.2 %collective-permute-start.29 = (bf16[96,1664]{1,0:T(8,128)(2,1)}, bf16[96,1664]{1,0:T(8,128)(2,1)S(1)}, u32[]{:S(2)}, u32[]{:S(2)}) collective-permute-start(bf16[96,1664]{1,0:T(8,128)(2,1)} %get-tuple-element.215), channel_id=1, source_target_pairs={{0,1},{1,2},{2,3},{3,0},{4,5},{5,6},{6,7},{7,4},{8,9},{9,10},{10,1... | collective-permute-start | bytes 958472 | tf_op jit(solution)/shard_map/ppermute | solution.py:1066
  604.9 20.6 %collective-permute-start.30 = (bf16[96,1664]{1,0:T(8,128)(2,1)}, bf16[96,1664]{1,0:T(8,128)(2,1)}, u32[]{:S(2)}, u32[]{:S(2)}) collective-permute-start(bf16[96,1664]{1,0:T(8,128)(2,1)} %get-tuple-element.216), channel_id=1, source_target_pairs={{0,2},{1,3},{2,0},{3,1},{4,6},{5,7},{6,4},{7,5},{8,10},{9,11},{10,... | collective-permute-start | bytes 958472 | tf_op jit(solution)/shard_map/ppermute | solution.py:1066
  612.1 22.6 %collective-permute-start.35 = (bf16[128,1792]{1,0:T(8,128)(2,1)}, bf16[128,1792]{1,0:T(8,128)(2,1)}, u32[]{:S(2)}, u32[]{:S(2)}) collective-permute-start(bf16[128,1792]{1,0:T(8,128)(2,1)} %get-tuple-element.223), channel_id=1, source_target_pairs={{0,4},{1,5},{2,6},{3,7},{4,8},{5,9},{6,10},{7,11},{8,12},{9,13},{1... | collective-permute-start | bytes 1376264 | tf_op jit(solution)/shard_map/ppermute | solution.py:1066
  613.6 17.0 %collective-permute-start.31 = (bf16[96,1664]{1,0:T(8,128)(2,1)}, bf16[96,1664]{1,0:T(8,128)(2,1)}, u32[]{:S(2)}, u32[]{:S(2)}) collective-permute-start(bf16[96,1664]{1,0:T(8,128)(2,1)} %get-tuple-element.217), channel_id=1, source_target_pairs={{0,3},{1,0},{2,1},{3,2},{4,7},{5,4},{6,5},{7,6},{8,11},{9,8},{10,9... | collective-permute-start | bytes 958472 | tf_op jit(solution)/shard_map/ppermute | solution.py:1066
  622.0 16.1 %collective-permute-start.36 = (bf16[128,1792]{1,0:T(8,128)(2,1)}, bf16[128,1792]{1,0:T(8,128)(2,1)}, u32[]{:S(2)}, u32[]{:S(2)}) collective-permute-start(bf16[128,1792]{1,0:T(8,128)(2,1)} %get-tuple-element.224), channel_id=1, source_target_pairs={{0,8},{1,9},{2,10},{3,11},{4,12},{5,13},{6,14},{7,15},{8,0},{9,1},... | collective-permute-start | bytes 1376264 | tf_op jit(solution)/shard_map/ppermute | solution.py:1066
  630.6 15.7 %collective-permute-start.42 = (bf16[24,6528]{1,0:T(8,128)(2,1)}, bf16[24,6528]{1,0:T(8,128)(2,1)S(1)}, u32[]{:S(2)}, u32[]{:S(2)}) collective-permute-start(bf16[24,6528]{1,0:T(8,128)(2,1)} %get-tuple-element.231), channel_id=1, source_target_pairs={{0,2},{1,3},{2,0},{3,1},{4,6},{5,7},{6,4},{7,5},{8,10},{9,11},{10,... | collective-permute-start | bytes 940040 | tf_op jit(solution)/shard_map/ppermute | solution.py:1066
  634.7 13.6 %collective-permute-start.43 = (bf16[24,6528]{1,0:T(8,128)(2,1)}, bf16[24,6528]{1,0:T(8,128)(2,1)}, u32[]{:S(2)}, u32[]{:S(2)}) collective-permute-start(bf16[24,6528]{1,0:T(8,128)(2,1)} %get-tuple-element.232), channel_id=1, source_target_pairs={{0,1},{1,2},{2,3},{3,0},{4,5},{5,6},{6,7},{7,4},{8,9},{9,10},{10,1... | collective-permute-start | bytes 940040 | tf_op jit(solution)/shard_map/ppermute | solution.py:1066
  634.7 13.6 %collective-permute-start.44 = (bf16[24,6528]{1,0:T(8,128)(2,1)}, bf16[24,6528]{1,0:T(8,128)(2,1)}, u32[]{:S(2)}, u32[]{:S(2)}) collective-permute-start(bf16[24,6528]{1,0:T(8,128)(2,1)} %get-tuple-element.233), channel_id=1, source_target_pairs={{0,3},{1,0},{2,1},{3,2},{4,7},{5,4},{6,5},{7,6},{8,11},{9,8},{10,9... | collective-permute-start | bytes 940040 | tf_op jit(solution)/shard_map/ppermute | solution.py:1066
  664.5 12.9 %collective-permute-start.45 = (f32[24,3456]{1,0:T(8,128)S(1)}, f32[24,3456]{1,0:T(8,128)S(1)}, u32[]{:S(2)}, u32[]{:S(2)}) collective-permute-start(f32[24,3456]{1,0:T(8,128)S(1)} %fusion.1), channel_id=1, source_target_pairs={{0,64},{64,0},{1,65},{65,1},{2,66},{66,2},{3,67},{67,3},{4,68},{68... | collective-permute-start | bytes 995336 | tf_op jit(solution)/shard_map/ppermute | solution.py:1070
  (70 other events, 576.9 us)
Sparse Core Ops, SparseCore 0:
  63.4 32.9 all-gather.8
  98.0 64.5 all-gather.4
  164.3 92.5 all-gather.6
  292.3 52.7 reduce-scatter.6
  347.4 50.9 reduce-scatter.4
  400.6 60.4 reduce-scatter.8
  463.6 50.8 reduce-scatter.10

commit v6 on v5

--- a/solution.py
+++ b/solution.py
@@ -1516,9 +1516,8 @@
 
         rows = jnp.concatenate([rows, higher_rows]).astype(BF16)
         cuts = [(normed_t, dxc, slice(middle, PACKED)), (grad_o, bg, slice(WIDTH // 2, WIDTH))]
-        right = terms(info, "x", cuts, (rows,))
-        tall = fold(info, "y", [[v] for v in higher + sums], 1, 96, right[0], True)
-        right = arrived(right, "x")
+        right = arrived(terms(info, "x", cuts, (rows,)), "x")
+        tall = fold(info, "y", [[v] for v in higher + sums], 1, 96, right[1], True)
         left = fold(info, "x", [[traded(left, "y")]], 4, 24, tall)
         right = fold(info, "y", [right], 4, 24, dh_low)
         tall = fold(info, "x", [[traded(tall, "y")]], 1, 24, right[0])
@@ -1547,7 +1546,7 @@
     late = after(low_x[3:6] + low_x[7:10], place)["z"]
     got = [None] + [lax.dynamic_index_in_dim(got, (late + r) % 4, 0, False) for r in range(1, 4)]
     low_zo = pieces(mine_zo, came_zo, got, 0)
-    here = after([low_x[2], low_x[6]], {"section": section})["section"]
+    here = after([low_x[3], low_x[7]], {"section": section})["section"]
     high_x = [lax.all_gather(jnp.where(here == 1, mine_x, came_x), "dp", tiled=True)]
     high_zo = [lax.all_gather(jnp.where(here == 1, mine_zo, came_zo), "dp", tiled=True)]
     ready = low_zo[3:6] + low_zo[7:10]

time: 702 us -> 719 us (1.024)
  waiting for transfers between devices: 180 us -> 192 us
    ppermute x30, waiting for transfers between devices: 106 us -> 129 us  [send(): return lax.ppermute(value, name, pairs)]
    all_to_all x2, waiting for transfers between devices: 11.4 us -> 0.01 us  [traded(): return lax.all_to_all(value, 'ctx', 0, 0, axis_index_groups=GROUPS_OF[axis])]
    unnamed x108 -> x116, local copies, waits for them, and re-layouts: 19.4 us -> 24.1 us
  transfers between devices with their start and end apart: 65 -> 65, of which waited for: 29 -> 27; matrix products, arithmetic and copies ran while one was open for 7% -> 6% of each run, Pallas kernels for 35% -> 34%
where the time goes in v6:
time: 719 us; the launch traced here: 706 us
  Pallas kernels  260 us (36%)
  waiting for transfers between devices  192 us (27%)
  starting transfers between devices  157 us (22%)
  local copies, waits for them, and re-layouts  51.4 us (7%)
  other arithmetic  23.9 us (3%)
  between operations  21.7 us (3%)
    ppermute x30, waiting for transfers between devices, send(): return lax.ppermute(value, name, pairs)  129 us
    all_to_all x8, starting transfers between devices, exchange(): return lax.all_to_all(value, 'ctx', 0, 0, axis_index_groups=PARITY)  73.5 us
    ppermute x30, starting transfers between devices, send(): return lax.ppermute(value, name, pairs)  43.3 us
    pallas_call x2, Pallas kernels, finish_call(): pl.pallas_call(finish_body, grid=(GROUPS,), out_shape=(shape((ROWS, LOCAL...  24.5 us
    unnamed x116, local copies, waits for them, and re-layouts  24.1 us
    pallas_call x4, Pallas kernels, fold(): pl.pallas_call(functools.partial(fold_body, slot, counts, outer, inner, m...  20.2 us
    pallas_call x2, Pallas kernels, mixed_back(): pl.pallas_call(functools.partial(mixed_back_body, weight, len(tokens)), g...  20.1 us
    reduce_scatter x4, waiting for transfers between devices, first_stage(): return lax.psum_scatter(value, 'dp', tiled=True)  19.7 us
  transfers between devices with their start and end apart: 65, of which 27 were waited for; matrix products, arithmetic and copies ran while one was open for 6% of the time, Pallas kernels for 34%

profile of v6, /device:TPU:12, one launch (start us, length us, event | category | flops | bytes accessed | tf_op | source)
XLA Modules:
  0.0 706.3 jit_solution(3970410727347661424)
XLA Ops:
  38.4 7.6 %collective-permute-done.5.rest_3_.refs_2_ = bf16[112,1920]{1,0:T(8,128)(2,1)S(1)} collective-permute-done((bf16[112,1920]{1,0:T(8,128)(2,1)S(1)}, bf16[112,1920]{1,0:T(8,128)(2,1)S(1)}, u32[]{:S(2)}, u32[]{:S(2)}) %collective-permute-start.5) | collective-permute-done | bytes 430112 | tf_op jit(solution)/shard_map/ppermute | solution.py:1066
  46.0 10.4 %collective-permute-done.4.rest_2_.refs_1_ = bf16[112,1920]{1,0:T(8,128)(2,1)S(1)} collective-permute-done((bf16[112,1920]{1,0:T(8,128)(2,1)S(1)}, bf16[112,1920]{1,0:T(8,128)(2,1)S(1)}, u32[]{:S(2)}, u32[]{:S(2)}) %collective-permute-start.4) | collective-permute-done | bytes 430112 | tf_op jit(solution)/shard_map/ppermute | solution.py:1066
  66.4 11.8 %collective-permute-done.6.rest_3_.refs_0_ = bf16[144,1920]{1,0:T(8,128)(2,1)S(1)} collective-permute-done((bf16[144,1920]{1,0:T(8,128)(2,1)S(1)}, bf16[144,1920]{1,0:T(8,128)(2,1)S(1)}, u32[]{:S(2)}, u32[]{:S(2)}) %collective-permute-start.6) | collective-permute-done | bytes 552992 | tf_op jit(solution)/shard_map/ppermute | solution.py:1066
  96.3 8.6 %collective-permute-done.8.rest_5_.refs_2_ = bf16[144,1920]{1,0:T(8,128)(2,1)S(1)} collective-permute-done((bf16[144,1920]{1,0:T(8,128)(2,1)S(1)}, bf16[144,1920]{1,0:T(8,128)(2,1)S(1)}, u32[]{:S(2)}, u32[]{:S(2)}) %collective-permute-start.8) | collective-permute-done | bytes 552992 | tf_op jit(solution)/shard_map/ppermute | solution.py:1066
  105.0 8.8 %collective-permute-done.7.rest_4_.refs_1_ = bf16[144,1920]{1,0:T(8,128)(2,1)S(1)} collective-permute-done((bf16[144,1920]{1,0:T(8,128)(2,1)S(1)}, bf16[144,1920]{1,0:T(8,128)(2,1)S(1)}, u32[]{:S(2)}, u32[]{:S(2)}) %collective-permute-start.7) | collective-permute-done | bytes 552992 | tf_op jit(solution)/shard_map/ppermute | solution.py:1066
  126.5 7.0 in_proj.2
  134.3 8.0 %collective-permute-start.12 = (bf16[16,1792]{1,0:T(8,128)(2,1)S(1)}, bf16[16,1792]{1,0:T(8,128)(2,1)S(1)}, u32[]{:S(2)}, u32[]{:S(2)}) collective-permute-start(bf16[16,1792]{1,0:T(8,128)(2,1)S(1)} %slice.182), channel_id=1, source_target_pairs={{0,2},{1,3},{2,4},{3,5},{4,6},{5,7},{6,8},{7,9},{8,10},{9,11},{10,... | collective-permute-start | bytes 172040 | tf_op jit(solution)/shard_map/ppermute | solution.py:1263
  148.9 5.7 conv_state.2
  154.7 22.8 %all-to-all-start = ((bf16[8,80,384]{2,1,0:T(8,128)(2,1)}), bf16[8,80,384]{2,1,0:T(8,128)(2,1)}, u32[]{:S(2)}, u32[]{:S(2)}) async-start(bf16[8,80,384]{2,1,0:T(8,128)(2,1)} %get-tuple-element.134.msg_in), calls=%async_computation | async-start | bytes 983040 | tf_op jit(solution)/shard_map/all_to_all | solution.py:1258
  177.5 5.9 inside.2.rest_0_.y_in
  189.2 7.6 %all-to-all-start.1 = ((bf16[8,64,384]{2,1,0:T(8,128)(2,1)}), bf16[8,64,384]{2,1,0:T(8,128)(2,1)S(1)}, u32[]{:S(2)}, u32[]{:S(2)}) async-start(bf16[8,64,384]{2,1,0:T(8,128)(2,1)} %chunk_scan.4), calls=%async_computation.1 | async-start | bytes 786432 | tf_op jit(solution)/shard_map/all_to_all | solution.py:1258
  197.7 6.3 gate_proj.2.gate
  204.7 7.6 %out_proj.2 = (f32[256,1536]{1,0:T(8,128)}, f32[256,1664]{1,0:T(8,128)}) custom-call(s32[14]{0:T(128)} %concatenate.116.info, f32[256,1536]{1,0:T(8,128)} %inside.2.rest_0_.y_in, f32[256,256]{1,0:T(8,128)} %get-tuple-element.131.bca, f32[256,128]{1,0:T(8,128)} %get-tuple-element.132.cum, bf16[4,128,384]{2,1,0:T(8,128)(2,1)} %bitcast.71, ...), custom_call_target="tpu_custom_call" | custom-call | flops 1207959552 | bytes 13000000 | tf_op jit(solution)/shard_map/out_proj/pallas_call | solution.py:459
  221.8 6.9 in_proj.3
  237.7 5.7 conv_state.3
  243.4 7.2 %all-to-all-start.2 = ((bf16[8,80,384]{2,1,0:T(8,128)(2,1)}), bf16[8,80,384]{2,1,0:T(8,128)(2,1)S(1)}, u32[]{:S(2)}, u32[]{:S(2)}) async-start(bf16[8,80,384]{2,1,0:T(8,128)(2,1)} %get-tuple-element.151.msg_in), calls=%async_computation.2 | async-start | bytes 983040 | tf_op jit(solution)/shard_map/all_to_all | solution.py:1258
  250.6 5.8 inside.3.rest_0_.y_in
  260.5 6.9 all-to-all-start.3
  267.5 6.3 gate_proj.3.gate
  274.6 7.6 %out_proj.3 = (f32[256,1536]{1,0:T(8,128)}, f32[256,1664]{1,0:T(8,128)}) custom-call(s32[14]{0:T(128)} %concatenate.116.info, f32[256,1536]{1,0:T(8,128)} %inside.3.rest_0_.y_in, f32[256,256]{1,0:T(8,128)} %get-tuple-element.148.bca, f32[256,128]{1,0:T(8,128)} %get-tuple-element.149.cum, bf16[4,128,384]{2,1,0:T(8,128)(2,1)} %bitcast.69, ...), custom_call_target="tpu_custom_call" | custom-call | flops 1207959552 | bytes 13000000 | tf_op jit(solution)/shard_map/out_proj/pallas_call | solution.py:459
  292.2 10.5 %gate_back.2 = (bf16[256,1536]{1,0:T(8,128)(2,1)}, bf16[256,1536]{1,0:T(8,128)(2,1)}, bf16[256,1536]{1,0:T(8,128)(2,1)}, bf16[1536,1536]{1,0:T(8,128)(2,1)}, f32[8,1536]{1,0:T(8,128)}) custom-call(s32[14]{0:T(128)} %concatenate.116.info, bf16[256,1536]{1,0:T(8,128)(2,1)} %get-tuple-element.261.cot, f32[256,1536]{1,0:T(8,128)} %get-tuple-element.155.y, ...), custom_call_target="tpu_custom_call" | custom-call | flops 2415919104 | bytes 17000000 | tf_op jit(solution)/shard_map/gate_back/pallas_call | solution.py:555
  302.7 7.7 %own_grad.2 = (f32[4,128,384]{2,1,0:T(8,128)}, bf16[8,80,384]{2,1,0:T(8,128)(2,1)}, bf16[1536,1536]{1,0:T(8,128)(2,1)}) custom-call(bf16[256,1536]{1,0:T(8,128)(2,1)} %get-tuple-element.159.dy, f32[256,256]{1,0:T(8,128)} %get-tuple-element.148.bca, f32[256,128]{1,0:T(8,128)} %get-tuple-element.149.cum, bf16[8,80,384]{2,1,0:T(8,128)(2,1)} %get-tuple-element.151.msg_in, ...), custom_call_target="tpu_custom_call" | custom-call | flops 1207959552 | bytes 8000000 | tf_op jit(solution)/shard_map/own_grad/pallas_call | solution.py:604
  310.5 7.2 %all-to-all-start.4 = ((bf16[8,80,384]{2,1,0:T(8,128)(2,1)}), bf16[8,80,384]{2,1,0:T(8,128)(2,1)S(1)}, u32[]{:S(2)}, u32[]{:S(2)}) async-start(bf16[8,80,384]{2,1,0:T(8,128)(2,1)} %get-tuple-element.162.token), calls=%async_computation.4 | async-start | bytes 983040 | tf_op jit(solution)/shard_map/all_to_all | solution.py:1258
  321.0 7.2 %gate_in_back.2.rest_0_.part = f32[256,1536]{1,0:T(8,128)} custom-call(s32[14]{0:T(128)} %concatenate.116.info, bf16[256,1536]{1,0:T(8,128)(2,1)} %get-tuple-element.161.dz, bf16[8,80,384]{2,1,0:T(8,128)(2,1)} %get-tuple-element.162.token, bf16[1536,3072]{1,0:T(8,128)(2,1)} %all-gather.7.cloned.1.call-done.rest_0_), custom_call_target="tpu_custom_call" | custom-call | flops 1207959552 | bytes 7000000 | tf_op jit(solution)/shard_map/gate_in_back/pallas_call | solution.py:937
  331.0 7.2 %all-to-all-start.5 = ((bf16[8,64,384]{2,1,0:T(8,128)(2,1)}), bf16[8,64,384]{2,1,0:T(8,128)(2,1)S(1)}, u32[]{:S(2)}, u32[]{:S(2)}) async-start(bf16[8,64,384]{2,1,0:T(8,128)(2,1)} %chunk_scan.6), calls=%async_computation.5 | async-start | bytes 786432 | tf_op jit(solution)/shard_map/all_to_all | solution.py:1258
  338.2 8.7 %inside_back.2 = (f32[256,1536]{1,0:T(8,128)}, f32[8,1536]{1,0:T(8,128)}, f32[32,256]{1,0:T(8,128)}, f32[256,128]{1,0:T(8,128)}, f32[256,256]{1,0:T(8,128)}) custom-call(bf16[256,1536]{1,0:T(8,128)(2,1)} %get-tuple-element.159.dy, f32[256,1536]{1,0:T(8,128)} %get-tuple-element.147.xa, f32[256,256]{1,0:T(8,128)} %get-tuple-element.148.bca, ...), custom_call_target="tpu_custom_call" | custom-call | flops 402653184 | bytes 4500000 | tf_op jit(solution)/shard_map/inside_back/pallas_call | solution.py:699
  347.6 12.3 %finish_back.2 = (bf16[256,1536]{1,0:T(8,128)(2,1)}, bf16[256,384]{1,0:T(8,128)(2,1)}, f32[16,1536]{1,0:T(8,128)}, f32[16,256]{1,0:T(8,128)}, bf16[16,1536]{1,0:...) custom-call(s32[14]{0:T(128)} %concatenate.116.info, ...), custom_call_target="tpu_custom_call" | custom-call | flops 503316480 | bytes 7500000 | tf_op jit(solution)/shard_map/finish_back/pallas_call | solution.py:852
  372.7 11.1 %mixed_back.2 = (f32[256,1536]{1,0:T(8,128)}, f32[8,1536]{1,0:T(8,128)}, bf16[1536,1920]{1,0:T(8,128)(2,1)}) custom-call(s32[14]{0:T(128)} %concatenate.116.info, bf16[256,1920]{1,0:T(8,128)(2,1)} %patch.2.dxc, f32[256,1536]{1,0:T(8,128)} %gate_in_back.2.rest_0_.part, bf16[256,1536]{1,0:T(8,128)(2,1)} %get-tuple-element.142.h_ref, ...), custom_call_target="tpu_custom_call" | custom-call | flops 3019898880 | bytes 14000000 | tf_op jit(solution)/shard_map/mixed_back/pallas_call | solution.py:1008
  394.8 9.1 %gate_back.3 = (bf16[256,1536]{1,0:T(8,128)(2,1)}, bf16[256,1536]{1,0:T(8,128)(2,1)}, bf16[256,1536]{1,0:T(8,128)(2,1)}, bf16[1536,256]{1,0:T(8,128)(2,1)}, f32[8,1536]{1,0:T(8,128)}) custom-call(s32[14]{0:T(128)} %concatenate.116.info, bf16[256,1536]{1,0:T(8,128)(2,1)} %get-tuple-element.175.cot, f32[256,1536]{1,0:T(8,128)} %get-tuple-element.176.y, ...), custom_call_target="tpu_custom_call" | custom-call | flops 2415919104 | bytes 17000000 | tf_op jit(solution)/shard_map/gate_back/pallas_call | solution.py:555
  403.9 7.8 %own_grad.3 = (f32[4,128,384]{2,1,0:T(8,128)}, bf16[8,80,384]{2,1,0:T(8,128)(2,1)}, bf16[1536,1536]{1,0:T(8,128)(2,1)}) custom-call(bf16[256,1536]{1,0:T(8,128)(2,1)} %get-tuple-element.179.dy, f32[256,256]{1,0:T(8,128)} %get-tuple-element.131.bca, f32[256,128]{1,0:T(8,128)} %get-tuple-element.132.cum, bf16[8,80,384]{2,1,0:T(8,128)(2,1)} %get-tuple-element.134.msg_in, ...), custom_call_target="tpu_custom_call" | custom-call | flops 1207959552 | bytes 8000000 | tf_op jit(solution)/shard_map/own_grad/pallas_call | solution.py:604
  411.6 7.4 %all-to-all-start.6 = ((bf16[8,80,384]{2,1,0:T(8,128)(2,1)}), bf16[8,80,384]{2,1,0:T(8,128)(2,1)S(1)}, u32[]{:S(2)}, u32[]{:S(2)}) async-start(bf16[8,80,384]{2,1,0:T(8,128)(2,1)} %get-tuple-element.182.token), calls=%async_computation.6 | async-start | bytes 983040 | tf_op jit(solution)/shard_map/all_to_all | solution.py:1258
  421.4 7.2 %gate_in_back.3.rest_0_.part = f32[256,1536]{1,0:T(8,128)} custom-call(s32[14]{0:T(128)} %concatenate.116.info, bf16[256,1536]{1,0:T(8,128)(2,1)} %get-tuple-element.181.dz, bf16[8,80,384]{2,1,0:T(8,128)(2,1)} %get-tuple-element.182.token, bf16[384,3072]{1,0:T(8,128)(2,1)} %get-tuple-element.138.rest_0_, bf16[384,3072]{1,0:T(8,128)(2,1)} %collective-permute-done.13.rest_1_, ...), custom_call_target="tpu_custom_call" | custom-call | flops 1207959552 | bytes 7000000 | tf_op jit(solution)/shard_map/gate_in_back/pallas_call | solution.py:937
  431.4 7.2 %all-to-all-start.7 = ((bf16[8,64,384]{2,1,0:T(8,128)(2,1)}), bf16[8,64,384]{2,1,0:T(8,128)(2,1)S(1)}, u32[]{:S(2)}, u32[]{:S(2)}) async-start(bf16[8,64,384]{2,1,0:T(8,128)(2,1)} %chunk_scan.7), calls=%async_computation.7 | async-start | bytes 786432 | tf_op jit(solution)/shard_map/all_to_all | solution.py:1258
  440.2 8.7 %inside_back.3 = (f32[256,1536]{1,0:T(8,128)}, f32[8,1536]{1,0:T(8,128)}, f32[32,256]{1,0:T(8,128)}, f32[256,128]{1,0:T(8,128)}, f32[256,256]{1,0:T(8,128)}) custom-call(bf16[256,1536]{1,0:T(8,128)(2,1)} %get-tuple-element.179.dy, f32[256,1536]{1,0:T(8,128)} %get-tuple-element.130.xa, f32[256,256]{1,0:T(8,128)} %get-tuple-element.131.bca, ...), custom_call_target="tpu_custom_call" | custom-call | flops 402653184 | bytes 4500000 | tf_op jit(solution)/shard_map/inside_back/pallas_call | solution.py:699
  449.7 12.2 %finish_back.3 = (bf16[256,1536]{1,0:T(8,128)(2,1)}, bf16[256,384]{1,0:T(8,128)(2,1)}, f32[16,1536]{1,0:T(8,128)}, f32[16,256]{1,0:T(8,128)}, bf16[16,1536]{1,0:...) custom-call(s32[14]{0:T(128)} %concatenate.116.info, ...), custom_call_target="tpu_custom_call" | custom-call | flops 503316480 | bytes 7500000 | tf_op jit(solution)/shard_map/finish_back/pallas_call | solution.py:852
  474.1 5.8 terms.2.rest_10_
  479.9 6.0 all-to-all-start.8
  487.3 8.9 %mixed_back.3 = (f32[256,1536]{1,0:T(8,128)}, f32[8,1536]{1,0:T(8,128)}) custom-call(s32[14]{0:T(128)} %concatenate.116.info, bf16[256,1920]{1,0:T(8,128)(2,1)} %patch.3.rest_1_.dxc, f32[256,1536]{1,0:T(8,128)} %gate_in_back.3.rest_0_.part, bf16[256,1536]{1,0:T(8,128)(2,1)} %get-tuple-element.262.refs_0_.h_ref, ...), custom_call_target="tpu_custom_call" | custom-call | flops 3019898880 | bytes 14000000 | tf_op jit(solution)/shard_map/mixed_back/pallas_call | solution.py:1008
  497.7 7.8 %terms.3 = (bf16[416,1792]{1,0:T(8,128)(2,1)}, bf16[416,1792]{1,0:T(8,128)(2,1)}, bf16[416,1792]{1,0:T(8,128)(2,1)}, bf16[416,1792]{1,0:T(8,128)(2,1)}) custom-call(s32[14]{0:T(128)} %concatenate.116.info, bf16[1536,256]{1,0:T(8,128)(2,1)} %bitcast.74, bf16[256,1920]{1,0:T(8,128)(2,1)} %patch.3.rest_1_.dxc, bf16[1536,256]{1,0:T(8,128)(2,1)} %get-tuple-element.199.rest_2_, ...), custom_call_target="tpu_custom_call" | custom-call | flops 1409286144 | bytes 8000000 | tf_op jit(solution)/shard_map/terms/pallas_call | solution.py:1160
  506.2 19.7 %reduce-scatter.11.cloned.1.call-done.rest_3_ = bf16[384,1536]{1,0:T(8,128)(2,1)} async-done(((bf16[1536,1536]{1,0:T(8,128)(2,1)}), bf16[384,1536]{1,0:T(8,128)(2,1)}) %reduce-scatter.11.cloned.1.call-update) | async-done | bytes 1179664 | tf_op jit(solution)/shard_map/reduce_scatter | solution.py:1473
  525.8 12.0 %collective-permute-done.29.rest_4_.rest_1_ = bf16[416,1792]{1,0:T(8,128)(2,1)S(1)} collective-permute-done((bf16[416,1792]{1,0:T(8,128)(2,1)}, bf16[416,1792]{1,0:T(8,128)(2,1)S(1)}, u32[]{:S(2)}, u32[]{:S(2)}) %collective-permute-start.29) | collective-permute-done | bytes 1490976 | tf_op jit(solution)/shard_map/ppermute | solution.py:1066
  544.0 5.4 all-to-all-start.9
  570.9 15.7 %collective-permute-done.33.rest_2_ = bf16[416,1792]{1,0:T(8,128)(2,1)S(1)} collective-permute-done((bf16[416,1792]{1,0:T(8,128)(2,1)}, bf16[416,1792]{1,0:T(8,128)(2,1)S(1)}, u32[]{:S(2)}, u32[]{:S(2)}) %collective-permute-start.33) | collective-permute-done | bytes 1490976 | tf_op jit(solution)/shard_map/ppermute | solution.py:1066
  586.6 30.1 %collective-permute-done.34.rest_3_ = bf16[416,1792]{1,0:T(8,128)(2,1)S(1)} collective-permute-done((bf16[416,1792]{1,0:T(8,128)(2,1)}, bf16[416,1792]{1,0:T(8,128)(2,1)S(1)}, u32[]{:S(2)}, u32[]{:S(2)}) %collective-permute-start.34) | collective-permute-done | bytes 1490976 | tf_op jit(solution)/shard_map/ppermute | solution.py:1066
  617.8 5.6 fold.6
  659.5 7.2 %collective-permute-done.38 = bf16[56,3456]{1,0:T(8,128)(2,1)S(1)} collective-permute-done((bf16[56,3456]{1,0:T(8,128)(2,1)}, bf16[56,3456]{1,0:T(8,128)(2,1)S(1)}, u32[]{:S(2)}, u32[]{:S(2)}) %collective-permute-start.38) | collective-permute-done | bytes 387104 | tf_op jit(solution)/shard_map/ppermute | solution.py:1066
  666.7 6.5 collective-permute-done.39
  687.7 6.7 collective-permute-done.47
  (373 shorter events, 251.1 us)
Async XLA Ops:
  7.2 110.9 %all-gather.9.cloned.1.call-start = ((), (), s32[]{:S(2)}) async-start(), calls=%async_computation.20 | async-start | bytes 2949120 | tf_op jit(solution)/shard_map/all_gather | solution.py:1545
  14.2 15.3 %collective-permute-start.2 = (bf16[400,1920]{1,0:T(8,128)(2,1)}, bf16[400,1920]{1,0:T(8,128)(2,1)}, u32[]{:S(2)}, u32[]{:S(2)}) collective-permute-start(bf16[400,1920]{1,0:T(8,128)(2,1)} %get-tuple-element.124), channel_id=1, source_target_pairs={{0,64},{64,0},{1,65},{65,1},{2,66},{66,2},{3,67},{67,3},{4,68},{68... | collective-permute-start | bytes 4608008 | tf_op jit(solution)/shard_map/ppermute | solution.py:1070
  24.6 36.5 %collective-permute-start.13 = (bf16[384,3072]{1,0:T(8,128)(2,1)}, bf16[384,3072]{1,0:T(8,128)(2,1)}, u32[]{:S(2)}, u32[]{:S(2)}) collective-permute-start(bf16[384,3072]{1,0:T(8,128)(2,1)} %get-tuple-element.139), channel_id=1, source_target_pairs={{0,64},{64,0},{1,65},{65,1},{2,66},{66,2},{3,67},{67,3},{4,68},{68... | collective-permute-start | bytes 7077896 | tf_op jit(solution)/shard_map/ppermute | solution.py:1070
  31.9 14.2 %collective-permute-start.5 = (bf16[112,1920]{1,0:T(8,128)(2,1)S(1)}, bf16[112,1920]{1,0:T(8,128)(2,1)S(1)}, u32[]{:S(2)}, u32[]{:S(2)}) collective-permute-start(bf16[112,1920]{1,0:T(8,128)(2,1)S(1)} %pad_maximum_fusion.5.rest_0_), channel_id=1, source_target_pairs={{0,16},{16,32},{32,48},{48,0},{1,17},{17,33},{33,49},{49,1},{2,18}... | collective-permute-start | bytes 1290248 | tf_op jit(solution)/shard_map/ppermute | solution.py:1066
  33.8 22.6 %collective-permute-start.4 = (bf16[112,1920]{1,0:T(8,128)(2,1)S(1)}, bf16[112,1920]{1,0:T(8,128)(2,1)S(1)}, u32[]{:S(2)}, u32[]{:S(2)}) collective-permute-start(bf16[112,1920]{1,0:T(8,128)(2,1)S(1)} %pad_maximum_fusion.5.rest_0_), channel_id=1, source_target_pairs={{0,32},{16,48},{32,0},{48,16},{1,33},{17,49},{33,1},{49,17},{2,34}... | collective-permute-start | bytes 1290248 | tf_op jit(solution)/shard_map/ppermute | solution.py:1066
  37.4 19.0 %collective-permute-start.3 = (bf16[112,1920]{1,0:T(8,128)(2,1)S(1)}, bf16[112,1920]{1,0:T(8,128)(2,1)S(1)}, u32[]{:S(2)}, u32[]{:S(2)}) collective-permute-start(bf16[112,1920]{1,0:T(8,128)(2,1)S(1)} %pad_maximum_fusion.5.rest_0_), channel_id=1, source_target_pairs={{0,48},{16,0},{32,16},{48,32},{1,49},{17,1},{33,17},{49,33},{2,50}... | collective-permute-start | bytes 1290248 | tf_op jit(solution)/shard_map/ppermute | solution.py:1066
  63.3 120.1 %all-gather.5.cloned.1.call-start = ((), (), s32[]{:S(2)}) async-start(), calls=%async_computation.14 | async-start | bytes 7680000 | tf_op jit(solution)/shard_map/all_gather | solution.py:1550
  85.5 181.9 %all-gather.7.cloned.1.call-start = ((), (), s32[]{:S(2)}) async-start(), calls=%async_computation.15 | async-start | bytes 11796480 | tf_op jit(solution)/shard_map/all_gather | solution.py:1551
  90.2 14.8 %collective-permute-start.8 = (bf16[144,1920]{1,0:T(8,128)(2,1)S(1)}, bf16[144,1920]{1,0:T(8,128)(2,1)S(1)}, u32[]{:S(2)}, u32[]{:S(2)}) collective-permute-start(bf16[144,1920]{1,0:T(8,128)(2,1)S(1)} %copy-done.16), channel_id=1, source_target_pairs={{0,1},{1,2},{2,3},{3,0},{4,5},{5,6},{6,7},{7,4},{8,9},{9,10},{10,1... | collective-permute-start | bytes 1658888 | tf_op jit(solution)/shard_map/ppermute | solution.py:1066
  92.0 21.8 %collective-permute-start.7 = (bf16[144,1920]{1,0:T(8,128)(2,1)S(1)}, bf16[144,1920]{1,0:T(8,128)(2,1)S(1)}, u32[]{:S(2)}, u32[]{:S(2)}) collective-permute-start(bf16[144,1920]{1,0:T(8,128)(2,1)S(1)} %copy-done.16), channel_id=1, source_target_pairs={{0,2},{1,3},{2,0},{3,1},{4,6},{5,7},{6,4},{7,5},{8,10},{9,11},{10,... | collective-permute-start | bytes 1658888 | tf_op jit(solution)/shard_map/ppermute | solution.py:1066
  92.8 21.0 %collective-permute-start.11 = (bf16[144,1920]{1,0:T(8,128)(2,1)}, bf16[144,1920]{1,0:T(8,128)(2,1)S(1)}, u32[]{:S(2)}, u32[]{:S(2)}) collective-permute-start(bf16[144,1920]{1,0:T(8,128)(2,1)} %pad_maximum_fusion.4.rest_6_), channel_id=1, source_target_pairs={{0,4},{1,5},{2,6},{3,7},{4,8},{5,9},{6,10},{7,11},{8,12},{9,13},{1... | collective-permute-start | bytes 1658888 | tf_op jit(solution)/shard_map/ppermute | solution.py:1066
  94.4 19.4 %collective-permute-start.10 = (bf16[144,1920]{1,0:T(8,128)(2,1)}, bf16[144,1920]{1,0:T(8,128)(2,1)S(1)}, u32[]{:S(2)}, u32[]{:S(2)}) collective-permute-start(bf16[144,1920]{1,0:T(8,128)(2,1)} %pad_maximum_fusion.4.rest_6_), channel_id=1, source_target_pairs={{0,8},{1,9},{2,10},{3,11},{4,12},{5,13},{6,14},{7,15},{8,0},{9,1},... | collective-permute-start | bytes 1658888 | tf_op jit(solution)/shard_map/ppermute | solution.py:1066
  120.6 27.3 %collective-permute-start.16 = (bf16[144,3072]{1,0:T(8,128)(2,1)S(1)}, bf16[144,3072]{1,0:T(8,128)(2,1)S(1)}, u32[]{:S(2)}, u32[]{:S(2)}) collective-permute-start(bf16[144,3072]{1,0:T(8,128)(2,1)S(1)} %pad_maximum_fusion.rest_2_), channel_id=1, source_target_pairs={{0,1},{1,2},{2,3},{3,0},{4,5},{5,6},{6,7},{7,4},{8,9},{9,10},{10,1... | collective-permute-start | bytes 2654216 | tf_op jit(solution)/shard_map/ppermute | solution.py:1066
  142.3 54.4 %collective-permute-start.15 = (bf16[144,3072]{1,0:T(8,128)(2,1)S(1)}, bf16[144,3072]{1,0:T(8,128)(2,1)S(1)}, u32[]{:S(2)}, u32[]{:S(2)}) collective-permute-start(bf16[144,3072]{1,0:T(8,128)(2,1)S(1)} %pad_maximum_fusion.rest_2_), channel_id=1, source_target_pairs={{0,2},{1,3},{2,0},{3,1},{4,6},{5,7},{6,4},{7,5},{8,10},{9,11},{10,... | collective-permute-start | bytes 2654216 | tf_op jit(solution)/shard_map/ppermute | solution.py:1066
  142.4 54.3 %collective-permute-start.14 = (bf16[144,3072]{1,0:T(8,128)(2,1)S(1)}, bf16[144,3072]{1,0:T(8,128)(2,1)}, u32[]{:S(2)}, u32[]{:S(2)}) collective-permute-start(bf16[144,3072]{1,0:T(8,128)(2,1)S(1)} %pad_maximum_fusion.rest_2_), channel_id=1, source_target_pairs={{0,3},{1,0},{2,1},{3,2},{4,7},{5,4},{6,5},{7,6},{8,11},{9,8},{10,9... | collective-permute-start | bytes 2654216 | tf_op jit(solution)/shard_map/ppermute | solution.py:1066
  144.8 52.0 %collective-permute-start.19 = (bf16[144,3072]{1,0:T(8,128)(2,1)S(1)}, bf16[144,3072]{1,0:T(8,128)(2,1)}, u32[]{:S(2)}, u32[]{:S(2)}) collective-permute-start(bf16[144,3072]{1,0:T(8,128)(2,1)S(1)} %pad_maximum_fusion.1.rest_6_), channel_id=1, source_target_pairs={{0,4},{1,5},{2,6},{3,7},{4,8},{5,9},{6,10},{7,11},{8,12},{9,13},{1... | collective-permute-start | bytes 2654216 | tf_op jit(solution)/shard_map/ppermute | solution.py:1066
  145.4 51.3 %collective-permute-start.18 = (bf16[144,3072]{1,0:T(8,128)(2,1)S(1)}, bf16[144,3072]{1,0:T(8,128)(2,1)}, u32[]{:S(2)}, u32[]{:S(2)}) collective-permute-start(bf16[144,3072]{1,0:T(8,128)(2,1)S(1)} %pad_maximum_fusion.1.rest_6_), channel_id=1, source_target_pairs={{0,8},{1,9},{2,10},{3,11},{4,12},{5,13},{6,14},{7,15},{8,0},{9,1},... | collective-permute-start | bytes 2654216 | tf_op jit(solution)/shard_map/ppermute | solution.py:1066
  147.9 48.9 %collective-permute-start.17 = (bf16[144,3072]{1,0:T(8,128)(2,1)S(1)}, bf16[144,3072]{1,0:T(8,128)(2,1)}, u32[]{:S(2)}, u32[]{:S(2)}) collective-permute-start(bf16[144,3072]{1,0:T(8,128)(2,1)S(1)} %pad_maximum_fusion.1.rest_6_), channel_id=1, source_target_pairs={{0,12},{1,13},{2,14},{3,15},{4,0},{5,1},{6,2},{7,3},{8,4},{9,5},{1... | collective-permute-start | bytes 2654216 | tf_op jit(solution)/shard_map/ppermute | solution.py:1066
  154.7 32.5 %all-to-all-start = ((bf16[8,80,384]{2,1,0:T(8,128)(2,1)}), bf16[8,80,384]{2,1,0:T(8,128)(2,1)}, u32[]{:S(2)}, u32[]{:S(2)}) async-start(bf16[8,80,384]{2,1,0:T(8,128)(2,1)} %get-tuple-element.134.msg_in), calls=%async_computation | async-start | bytes 983040 | tf_op jit(solution)/shard_map/all_to_all | solution.py:1258
  189.2 14.8 %all-to-all-start.1 = ((bf16[8,64,384]{2,1,0:T(8,128)(2,1)}), bf16[8,64,384]{2,1,0:T(8,128)(2,1)S(1)}, u32[]{:S(2)}, u32[]{:S(2)}) async-start(bf16[8,64,384]{2,1,0:T(8,128)(2,1)} %chunk_scan.4), calls=%async_computation.1 | async-start | bytes 786432 | tf_op jit(solution)/shard_map/all_to_all | solution.py:1258
  243.4 14.4 %all-to-all-start.2 = ((bf16[8,80,384]{2,1,0:T(8,128)(2,1)}), bf16[8,80,384]{2,1,0:T(8,128)(2,1)S(1)}, u32[]{:S(2)}, u32[]{:S(2)}) async-start(bf16[8,80,384]{2,1,0:T(8,128)(2,1)} %get-tuple-element.151.msg_in), calls=%async_computation.2 | async-start | bytes 983040 | tf_op jit(solution)/shard_map/all_to_all | solution.py:1258
  267.5 219.8 %reduce-scatter.7.cloned.1.call-start = ((), (), s32[]{:S(2)}) async-start(), calls=%async_computation.17 | async-start | bytes 5898240 | tf_op jit(solution)/shard_map/reduce_scatter | solution.py:1473
  302.7 184.6 %reduce-scatter.5.cloned.1.call-start = ((), (), s32[]{:S(2)}) async-start(), calls=%async_computation.16 | async-start | bytes 5898240 | tf_op jit(solution)/shard_map/reduce_scatter | solution.py:1473
  310.5 17.7 %all-to-all-start.4 = ((bf16[8,80,384]{2,1,0:T(8,128)(2,1)}), bf16[8,80,384]{2,1,0:T(8,128)(2,1)S(1)}, u32[]{:S(2)}, u32[]{:S(2)}) async-start(bf16[8,80,384]{2,1,0:T(8,128)(2,1)} %get-tuple-element.162.token), calls=%async_computation.4 | async-start | bytes 983040 | tf_op jit(solution)/shard_map/all_to_all | solution.py:1258
  320.3 43.3 %collective-permute-start.24 = (f32[128,1536]{1,0:T(8,128)}, f32[128,1536]{1,0:T(8,128)S(1)}, u32[]{:S(2)}, u32[]{:S(2)}) collective-permute-start(f32[128,1536]{1,0:T(8,128)} %get-tuple-element.257), channel_id=1, source_target_pairs={{64,65},{65,64},{66,67},{67,66},{68,69},{69,68},{70,71},{71,70},{7... | collective-permute-start | bytes 2359304 | tf_op jit(solution)/shard_map/ppermute | solution.py:1565
  331.0 15.9 %all-to-all-start.5 = ((bf16[8,64,384]{2,1,0:T(8,128)(2,1)}), bf16[8,64,384]{2,1,0:T(8,128)(2,1)S(1)}, u32[]{:S(2)}, u32[]{:S(2)}) async-start(bf16[8,64,384]{2,1,0:T(8,128)(2,1)} %chunk_scan.6), calls=%async_computation.5 | async-start | bytes 786432 | tf_op jit(solution)/shard_map/all_to_all | solution.py:1258
  338.2 149.1 %reduce-scatter.9.cloned.1.call-start = ((), (), s32[]{:S(2)}) async-start(), calls=%async_computation.18 | async-start | bytes 7372800 | tf_op jit(solution)/shard_map/reduce_scatter | solution.py:1473
  383.9 142.0 %reduce-scatter.11.cloned.1.call-start = ((), (), s32[]{:S(2)}) async-start(), calls=%async_computation.19 | async-start | bytes 5898240 | tf_op jit(solution)/shard_map/reduce_scatter | solution.py:1473
  411.6 17.0 %all-to-all-start.6 = ((bf16[8,80,384]{2,1,0:T(8,128)(2,1)}), bf16[8,80,384]{2,1,0:T(8,128)(2,1)S(1)}, u32[]{:S(2)}, u32[]{:S(2)}) async-start(bf16[8,80,384]{2,1,0:T(8,128)(2,1)} %get-tuple-element.182.token), calls=%async_computation.6 | async-start | bytes 983040 | tf_op jit(solution)/shard_map/all_to_all | solution.py:1258
  431.4 17.6 %all-to-all-start.7 = ((bf16[8,64,384]{2,1,0:T(8,128)(2,1)}), bf16[8,64,384]{2,1,0:T(8,128)(2,1)S(1)}, u32[]{:S(2)}, u32[]{:S(2)}) async-start(bf16[8,64,384]{2,1,0:T(8,128)(2,1)} %chunk_scan.7), calls=%async_computation.7 | async-start | bytes 786432 | tf_op jit(solution)/shard_map/all_to_all | solution.py:1258
  479.9 64.0 %all-to-all-start.8 = ((bf16[4,384,1664]{2,1,0:T(8,128)(2,1)}), bf16[4,384,1664]{2,1,0:T(8,128)(2,1)}, u32[]{:S(2)}, u32[]{:S(2)}) async-start(bf16[4,384,1664]{2,1,0:T(8,128)(2,1)} %terms.2.rest_10_), calls=%async_computation.11 | async-start | bytes 10223616 | tf_op jit(solution)/shard_map/all_to_all | solution.py:1254
  505.5 32.3 %collective-permute-start.29 = (bf16[416,1792]{1,0:T(8,128)(2,1)}, bf16[416,1792]{1,0:T(8,128)(2,1)S(1)}, u32[]{:S(2)}, u32[]{:S(2)}) collective-permute-start(bf16[416,1792]{1,0:T(8,128)(2,1)} %get-tuple-element.213), channel_id=1, source_target_pairs={{0,1},{1,2},{2,3},{3,0},{4,5},{5,6},{6,7},{7,4},{8,9},{9,10},{10,1... | collective-permute-start | bytes 4472840 | tf_op jit(solution)/shard_map/ppermute | solution.py:1066
  544.0 85.8 %all-to-all-start.9 = ((bf16[4,96,6528]{2,1,0:T(8,128)(2,1)}), bf16[4,96,6528]{2,1,0:T(8,128)(2,1)}, u32[]{:S(2)}, u32[]{:S(2)}) async-start(bf16[4,96,6528]{2,1,0:T(8,128)(2,1)} %fold.4.rest_1_), calls=%async_computation.13 | async-start | bytes 10027008 | tf_op jit(solution)/shard_map/all_to_all | solution.py:1254
  549.4 37.2 %collective-permute-start.33 = (bf16[416,1792]{1,0:T(8,128)(2,1)}, bf16[416,1792]{1,0:T(8,128)(2,1)S(1)}, u32[]{:S(2)}, u32[]{:S(2)}) collective-permute-start(bf16[416,1792]{1,0:T(8,128)(2,1)} %get-tuple-element.219), channel_id=1, source_target_pairs={{0,2},{1,3},{2,0},{3,1},{4,6},{5,7},{6,4},{7,5},{8,10},{9,11},{10,... | collective-permute-start | bytes 4472840 | tf_op jit(solution)/shard_map/ppermute | solution.py:1066
  550.5 66.2 %collective-permute-start.34 = (bf16[416,1792]{1,0:T(8,128)(2,1)}, bf16[416,1792]{1,0:T(8,128)(2,1)S(1)}, u32[]{:S(2)}, u32[]{:S(2)}) collective-permute-start(bf16[416,1792]{1,0:T(8,128)(2,1)} %get-tuple-element.220), channel_id=1, source_target_pairs={{0,3},{1,0},{2,1},{3,2},{4,7},{5,4},{6,5},{7,6},{8,11},{9,8},{10,9... | collective-permute-start | bytes 4472840 | tf_op jit(solution)/shard_map/ppermute | solution.py:1066
  561.0 82.7 %collective-permute-start.28 = (f32[128,1536]{1,0:T(8,128)}, f32[128,1536]{1,0:T(8,128)S(1)}, u32[]{:S(2)}, u32[]{:S(2)}) collective-permute-start(f32[128,1536]{1,0:T(8,128)} %get-tuple-element.260), channel_id=1, source_target_pairs={{0,1},{1,0},{2,3},{3,2},{4,5},{5,4},{6,7},{7,6},{8,9},{9,8},{10,11... | collective-permute-start | bytes 2359304 | tf_op jit(solution)/shard_map/ppermute | solution.py:1565
  568.5 57.8 %collective-permute-start.30 = (bf16[96,1664]{1,0:T(8,128)(2,1)}, bf16[96,1664]{1,0:T(8,128)(2,1)S(1)}, u32[]{:S(2)}, u32[]{:S(2)}) collective-permute-start(bf16[96,1664]{1,0:T(8,128)(2,1)} %get-tuple-element.215), channel_id=1, source_target_pairs={{0,1},{1,2},{2,3},{3,0},{4,5},{5,6},{6,7},{7,4},{8,9},{9,10},{10,1... | collective-permute-start | bytes 958472 | tf_op jit(solution)/shard_map/ppermute | solution.py:1066
  569.7 57.4 %collective-permute-start.31 = (bf16[96,1664]{1,0:T(8,128)(2,1)}, bf16[96,1664]{1,0:T(8,128)(2,1)}, u32[]{:S(2)}, u32[]{:S(2)}) collective-permute-start(bf16[96,1664]{1,0:T(8,128)(2,1)} %get-tuple-element.216), channel_id=1, source_target_pairs={{0,2},{1,3},{2,0},{3,1},{4,6},{5,7},{6,4},{7,5},{8,10},{9,11},{10,... | collective-permute-start | bytes 958472 | tf_op jit(solution)/shard_map/ppermute | solution.py:1066
  623.4 17.2 %collective-permute-start.35 = (bf16[128,1792]{1,0:T(8,128)(2,1)}, bf16[128,1792]{1,0:T(8,128)(2,1)}, u32[]{:S(2)}, u32[]{:S(2)}) collective-permute-start(bf16[128,1792]{1,0:T(8,128)(2,1)} %get-tuple-element.223), channel_id=1, source_target_pairs={{0,4},{1,5},{2,6},{3,7},{4,8},{5,9},{6,10},{7,11},{8,12},{9,13},{1... | collective-permute-start | bytes 1376264 | tf_op jit(solution)/shard_map/ppermute | solution.py:1066
  626.3 19.8 %collective-permute-start.36 = (bf16[128,1792]{1,0:T(8,128)(2,1)}, bf16[128,1792]{1,0:T(8,128)(2,1)}, u32[]{:S(2)}, u32[]{:S(2)}) collective-permute-start(bf16[128,1792]{1,0:T(8,128)(2,1)} %get-tuple-element.224), channel_id=1, source_target_pairs={{0,8},{1,9},{2,10},{3,11},{4,12},{5,13},{6,14},{7,15},{8,0},{9,1},... | collective-permute-start | bytes 1376264 | tf_op jit(solution)/shard_map/ppermute | solution.py:1066
  627.1 22.0 %collective-permute-start.37 = (bf16[128,1792]{1,0:T(8,128)(2,1)}, bf16[128,1792]{1,0:T(8,128)(2,1)}, u32[]{:S(2)}, u32[]{:S(2)}) collective-permute-start(bf16[128,1792]{1,0:T(8,128)(2,1)} %get-tuple-element.225), channel_id=1, source_target_pairs={{0,12},{1,13},{2,14},{3,15},{4,0},{5,1},{6,2},{7,3},{8,4},{9,5},{1... | collective-permute-start | bytes 1376264 | tf_op jit(solution)/shard_map/ppermute | solution.py:1066
  638.5 19.4 %collective-permute-start.42 = (bf16[24,6528]{1,0:T(8,128)(2,1)}, bf16[24,6528]{1,0:T(8,128)(2,1)S(1)}, u32[]{:S(2)}, u32[]{:S(2)}) collective-permute-start(bf16[24,6528]{1,0:T(8,128)(2,1)} %get-tuple-element.231), channel_id=1, source_target_pairs={{0,2},{1,3},{2,0},{3,1},{4,6},{5,7},{6,4},{7,5},{8,10},{9,11},{10,... | collective-permute-start | bytes 940040 | tf_op jit(solution)/shard_map/ppermute | solution.py:1066
  640.6 17.6 %collective-permute-start.43 = (bf16[24,6528]{1,0:T(8,128)(2,1)}, bf16[24,6528]{1,0:T(8,128)(2,1)}, u32[]{:S(2)}, u32[]{:S(2)}) collective-permute-start(bf16[24,6528]{1,0:T(8,128)(2,1)} %get-tuple-element.232), channel_id=1, source_target_pairs={{0,1},{1,2},{2,3},{3,0},{4,5},{5,6},{6,7},{7,4},{8,9},{9,10},{10,1... | collective-permute-start | bytes 940040 | tf_op jit(solution)/shard_map/ppermute | solution.py:1066
  643.7 14.5 %collective-permute-start.44 = (bf16[24,6528]{1,0:T(8,128)(2,1)}, bf16[24,6528]{1,0:T(8,128)(2,1)}, u32[]{:S(2)}, u32[]{:S(2)}) collective-permute-start(bf16[24,6528]{1,0:T(8,128)(2,1)} %get-tuple-element.233), channel_id=1, source_target_pairs={{0,3},{1,0},{2,1},{3,2},{4,7},{5,4},{6,5},{7,6},{8,11},{9,8},{10,9... | collective-permute-start | bytes 940040 | tf_op jit(solution)/shard_map/ppermute | solution.py:1066
  655.0 18.2 %collective-permute-start.39 = (bf16[56,3456]{1,0:T(8,128)(2,1)}, bf16[56,3456]{1,0:T(8,128)(2,1)S(1)}, u32[]{:S(2)}, u32[]{:S(2)}) collective-permute-start(bf16[56,3456]{1,0:T(8,128)(2,1)} %get-tuple-element.229), channel_id=1, source_target_pairs={{0,16},{16,32},{32,48},{48,0},{1,17},{17,33},{33,49},{49,1},{2,18}... | collective-permute-start | bytes 1161224 | tf_op jit(solution)/shard_map/ppermute | solution.py:1066
  657.9 16.7 %collective-permute-start.40 = (bf16[56,3456]{1,0:T(8,128)(2,1)}, bf16[56,3456]{1,0:T(8,128)(2,1)S(1)}, u32[]{:S(2)}, u32[]{:S(2)}) collective-permute-start(bf16[56,3456]{1,0:T(8,128)(2,1)} %get-tuple-element.230), channel_id=1, source_target_pairs={{0,48},{16,0},{32,16},{48,32},{1,49},{17,1},{33,17},{49,33},{2,50}... | collective-permute-start | bytes 1161224 | tf_op jit(solution)/shard_map/ppermute | solution.py:1066
  678.4 16.0 %collective-permute-start.47 = (f32[24,1536]{1,0:T(8,128)S(1)}, f32[24,1536]{1,0:T(8,128)S(1)}, u32[]{:S(2)}, u32[]{:S(2)}) collective-permute-start(f32[24,1536]{1,0:T(8,128)S(1)} %get-tuple-element.270), channel_id=1, source_target_pairs={{0,64},{1,0},{2,65},{3,1},{4,66},{5,2},{6,67},{7,3},{8,68},{9,4},{... | collective-permute-start | bytes 442376 | tf_op jit(solution)/shard_map/ppermute | solution.py:1604
  680.5 14.7 %collective-permute-start.45 = (f32[24,3456]{1,0:T(8,128)S(1)}, f32[24,3456]{1,0:T(8,128)S(1)}, u32[]{:S(2)}, u32[]{:S(2)}) collective-permute-start(f32[24,3456]{1,0:T(8,128)S(1)} %fusion.1), channel_id=1, source_target_pairs={{0,64},{64,0},{1,65},{65,1},{2,66},{66,2},{3,67},{67,3},{4,68},{68... | collective-permute-start | bytes 995336 | tf_op jit(solution)/shard_map/ppermute | solution.py:1070
  (74 other events, 638.0 us)
Sparse Core Ops, SparseCore 0:
  63.4 32.9 all-gather.8
  98.0 64.5 all-gather.4
  164.3 92.5 all-gather.6
  302.8 53.5 reduce-scatter.6
  358.7 50.8 reduce-scatter.4
  411.9 60.5 reduce-scatter.8
  474.9 50.8 reduce-scatter.10

commit v7 on v6

--- a/solution.py
+++ b/solution.py
@@ -1172,7 +1172,7 @@
 
 
 def fold_body(slot, counts, outer, inner, rest_rows, stacked, info, *rest):
-    refs, outs, total = rest[: sum(counts)], rest[sum(counts) + 1 : -1], rest[-1]
+    refs, outs, total = rest[: sum(counts)], rest[-2:-1] if stacked else rest[-5:-1], rest[-1]
     column = 0
     for count in counts:
         arrays, refs = refs[:count], refs[count:]
@@ -1198,6 +1198,7 @@
 def fold(info, axis, groups, outer, inner, token, stacked=False):
     slot = 10 + "zyx".index(axis)
     arrays = [a for group in groups for a in group]
+    tokens = token if isinstance(token, tuple) else (token,)
     rows, width = arrays[0].shape[-2], sum(group[0].shape[-1] for group in groups)
     more = rows - 4 * outer * inner
     outs, specs = four((outer * inner + more, width), stacked)
@@ -1205,13 +1206,13 @@
     return pl.pallas_call(
         functools.partial(fold_body, slot, counts, outer, inner, more, stacked),
         out_shape=outs,
-        in_specs=[SMEM] + [whole(a.shape) for a in arrays] + [ANYWHERE],
+        in_specs=[SMEM] + [whole(a.shape) for a in arrays] + [ANYWHERE] * len(tokens),
         out_specs=specs,
         scratch_shapes=[pltpu.VMEM((rows, width), F32)],
         compiler_params=params(),
         cost_estimate=pl.CostEstimate(flops=2_000_000, bytes_accessed=8_000_000, transcendentals=0),
         name="fold",
-    )(info, *arrays, token)
+    )(info, *arrays, *tokens)
 
 
 def last_fold_body(info, *rest):
@@ -1517,7 +1518,8 @@
         rows = jnp.concatenate([rows, higher_rows]).astype(BF16)
         cuts = [(normed_t, dxc, slice(middle, PACKED)), (grad_o, bg, slice(WIDTH // 2, WIDTH))]
         right = arrived(terms(info, "x", cuts, (rows,)), "x")
-        tall = fold(info, "y", [[v] for v in higher + sums], 1, 96, right[1], True)
+        near = (right[1], right[3])
+        tall = fold(info, "y", [[v] for v in higher + sums], 1, 96, near, True)
         left = fold(info, "x", [[traded(left, "y")]], 4, 24, tall)
         right = fold(info, "y", [right], 4, 24, dh_low)
         tall = fold(info, "x", [[traded(tall, "y")]], 1, 24, right[0])
@@ -1546,7 +1548,7 @@
     late = after(low_x[3:6] + low_x[7:10], place)["z"]
     got = [None] + [lax.dynamic_index_in_dim(got, (late + r) % 4, 0, False) for r in range(1, 4)]
     low_zo = pieces(mine_zo, came_zo, got, 0)
-    here = after([low_x[3], low_x[7]], {"section": section})["section"]
+    here = after([low_x[2], low_x[6]], {"section": section})["section"]
     high_x = [lax.all_gather(jnp.where(here == 1, mine_x, came_x), "dp", tiled=True)]
     high_zo = [lax.all_gather(jnp.where(here == 1, mine_zo, came_zo), "dp", tiled=True)]
     ready = low_zo[3:6] + low_zo[7:10]

time: 719 us -> 682 us (0.949)
  the two profiles are of different devices: /device:TPU:12 before, /device:TPU:11 now
where the time goes in v7:
time: 682 us; the launch traced here: 670 us
  Pallas kernels  261 us (38%)
  waiting for transfers between devices  175 us (26%)
  starting transfers between devices  141 us (21%)
  local copies, waits for them, and re-layouts  49 us (7%)
  other arithmetic  23 us (3%)
  between operations  21.7 us (3%)
    ppermute x30, waiting for transfers between devices, send(): return lax.ppermute(value, name, pairs)  92.3 us
    all_to_all x8, starting transfers between devices, exchange(): return lax.all_to_all(value, 'ctx', 0, 0, axis_index_groups=PARITY)  46.1 us
    ppermute x30, starting transfers between devices, send(): return lax.ppermute(value, name, pairs)  37.9 us
    pallas_call x2, Pallas kernels, finish_call(): pl.pallas_call(finish_body, grid=(GROUPS,), out_shape=(shape((ROWS, LOCAL...  24.6 us
    unnamed x116, local copies, waits for them, and re-layouts  21.6 us
    reduce_scatter x4, waiting for transfers between devices, first_stage(): return lax.psum_scatter(value, 'dp', tiled=True)  20.8 us
    pallas_call x4, Pallas kernels, fold(): pl.pallas_call(functools.partial(fold_body, slot, counts, outer, inner, m...  20.3 us
    pallas_call x2, Pallas kernels, mixed_back(): pl.pallas_call(functools.partial(mixed_back_body, weight, len(tokens)), g...  20.2 us
  transfers between devices with their start and end apart: 65, of which 31 were waited for; matrix products, arithmetic and copies ran while one was open for 7% of the time, Pallas kernels for 36%

profile of v7, /device:TPU:11, one launch (start us, length us, event | category | flops | bytes accessed | tf_op | source)
XLA Modules:
  0.0 670.0 jit_solution(17164579766166313263)
XLA Ops:
  37.7 7.9 %collective-permute-done.5.rest_3_.refs_2_ = bf16[112,1920]{1,0:T(8,128)(2,1)S(1)} collective-permute-done((bf16[112,1920]{1,0:T(8,128)(2,1)S(1)}, bf16[112,1920]{1,0:T(8,128)(2,1)S(1)}, u32[]{:S(2)}, u32[]{:S(2)}) %collective-permute-start.5) | collective-permute-done | bytes 430112 | tf_op jit(solution)/shard_map/ppermute | solution.py:1066
  45.6 10.1 %collective-permute-done.4.rest_2_.refs_1_ = bf16[112,1920]{1,0:T(8,128)(2,1)S(1)} collective-permute-done((bf16[112,1920]{1,0:T(8,128)(2,1)S(1)}, bf16[112,1920]{1,0:T(8,128)(2,1)S(1)}, u32[]{:S(2)}, u32[]{:S(2)}) %collective-permute-start.4) | collective-permute-done | bytes 430112 | tf_op jit(solution)/shard_map/ppermute | solution.py:1066
  79.4 5.1 collective-permute-done.8.rest_5_.refs_2_
  87.0 14.2 %collective-permute-done.6.rest_3_.refs_0_ = bf16[144,1920]{1,0:T(8,128)(2,1)S(1)} collective-permute-done((bf16[144,1920]{1,0:T(8,128)(2,1)S(1)}, bf16[144,1920]{1,0:T(8,128)(2,1)S(1)}, u32[]{:S(2)}, u32[]{:S(2)}) %collective-permute-start.6) | collective-permute-done | bytes 552992 | tf_op jit(solution)/shard_map/ppermute | solution.py:1066
  115.0 7.0 %in_proj.2 = (bf16[256,1536]{1,0:T(8,128)(2,1)}, bf16[256,1792]{1,0:T(8,128)(2,1)}, f32[256,128]{1,0:T(8,128)}) custom-call(s32[14]{0:T(128)} %concatenate.116.info, bf16[256,1536]{1,0:T(8,128)(2,1)} %get-tuple-element.262.refs_0_.h_ref, f32[1,1536]{1,0:T(1,128)} %get-tuple-element.125.gain_ref.gain, bf16[400,1920]{1,0:T(8,128)(2,1)} %get-tuple-element.123.rest_0_.token, ...), custom_call_target="tpu_custom_call" | custom-call | flops 1509949440 | bytes 8000000 | tf_op jit(solution)/shard_map/in_proj/pallas_call | solution.py:215
  122.9 5.2 collective-permute-start.12
  133.0 5.7 conv_state.2
  138.7 5.5 all-to-all-start
  144.2 5.8 inside.2.rest_0_.y_in
  150.0 12.6 %all-gather.5.cloned.1.call-done.rest_0_ = bf16[1600,1920]{1,0:T(8,128)(2,1)} async-done(((bf16[400,1920]{1,0:T(8,128)(2,1)}), bf16[1600,1920]{1,0:T(8,128)(2,1)}) %all-gather.5.cloned.1.call-update) | async-done | bytes 6144016 | tf_op jit(solution)/shard_map/all_gather | solution.py:1552
  165.0 12.1 %all-to-all-done.msg = bf16[8,80,384]{2,1,0:T(8,128)(2,1)} async-done(((bf16[8,80,384]{2,1,0:T(8,128)(2,1)}), bf16[8,80,384]{2,1,0:T(8,128)(2,1)}, u32[]{:S(2)}, u32[]{:S(2)}) %all-to-all-start) | async-done | bytes 491552 | tf_op jit(solution)/shard_map/all_to_all | solution.py:1259
  184.4 6.3 gate_proj.2.gate
  191.4 7.6 %out_proj.2 = (f32[256,1536]{1,0:T(8,128)}, f32[256,1664]{1,0:T(8,128)}) custom-call(s32[14]{0:T(128)} %concatenate.116.info, f32[256,1536]{1,0:T(8,128)} %inside.2.rest_0_.y_in, f32[256,256]{1,0:T(8,128)} %get-tuple-element.131.bca, f32[256,128]{1,0:T(8,128)} %get-tuple-element.132.cum, bf16[4,128,384]{2,1,0:T(8,128)(2,1)} %bitcast.71, ...), custom_call_target="tpu_custom_call" | custom-call | flops 1207959552 | bytes 13000000 | tf_op jit(solution)/shard_map/out_proj/pallas_call | solution.py:459
  210.6 7.0 %in_proj.3 = (bf16[256,1536]{1,0:T(8,128)(2,1)}, bf16[256,1792]{1,0:T(8,128)(2,1)}, f32[256,128]{1,0:T(8,128)}) custom-call(s32[14]{0:T(128)} %concatenate.116.info, bf16[256,1536]{1,0:T(8,128)(2,1)} %get-tuple-element.142.h_ref, f32[1,1536]{1,0:T(1,128)} %get-tuple-element.143.gain_ref.gain, bf16[1600,1920]{1,0:T(8,128)(2,1)} %all-gather.5.cloned.1.call-done.rest_0_), custom_call_target="tpu_custom_call" | custom-call | flops 1509949440 | bytes 8000000 | tf_op jit(solution)/shard_map/in_proj/pallas_call | solution.py:215
  226.6 5.7 conv_state.3
  232.4 5.2 all-to-all-start.2
  237.6 5.8 inside.3.rest_0_.y_in
  247.7 5.2 all-to-all-start.3
  256.8 6.3 gate_proj.3.gate
  263.9 7.5 %out_proj.3 = (f32[256,1536]{1,0:T(8,128)}, f32[256,1664]{1,0:T(8,128)}) custom-call(s32[14]{0:T(128)} %concatenate.116.info, f32[256,1536]{1,0:T(8,128)} %inside.3.rest_0_.y_in, f32[256,256]{1,0:T(8,128)} %get-tuple-element.148.bca, f32[256,128]{1,0:T(8,128)} %get-tuple-element.149.cum, bf16[4,128,384]{2,1,0:T(8,128)(2,1)} %bitcast.69, ...), custom_call_target="tpu_custom_call" | custom-call | flops 1207959552 | bytes 13000000 | tf_op jit(solution)/shard_map/out_proj/pallas_call | solution.py:459
  281.8 10.5 %gate_back.2 = (bf16[256,1536]{1,0:T(8,128)(2,1)}, bf16[256,1536]{1,0:T(8,128)(2,1)}, bf16[256,1536]{1,0:T(8,128)(2,1)}, bf16[1536,1536]{1,0:T(8,128)(2,1)}, f32[8,1536]{1,0:T(8,128)}) custom-call(s32[14]{0:T(128)} %concatenate.116.info, bf16[256,1536]{1,0:T(8,128)(2,1)} %get-tuple-element.261.cot, f32[256,1536]{1,0:T(8,128)} %get-tuple-element.155.y, ...), custom_call_target="tpu_custom_call" | custom-call | flops 2415919104 | bytes 17000000 | tf_op jit(solution)/shard_map/gate_back/pallas_call | solution.py:555
  292.4 7.7 %own_grad.2 = (f32[4,128,384]{2,1,0:T(8,128)}, bf16[8,80,384]{2,1,0:T(8,128)(2,1)}, bf16[1536,1536]{1,0:T(8,128)(2,1)}) custom-call(bf16[256,1536]{1,0:T(8,128)(2,1)} %get-tuple-element.159.dy, f32[256,256]{1,0:T(8,128)} %get-tuple-element.148.bca, f32[256,128]{1,0:T(8,128)} %get-tuple-element.149.cum, bf16[8,80,384]{2,1,0:T(8,128)(2,1)} %get-tuple-element.151.msg_in, ...), custom_call_target="tpu_custom_call" | custom-call | flops 1207959552 | bytes 8000000 | tf_op jit(solution)/shard_map/own_grad/pallas_call | solution.py:604
  300.1 5.7 all-to-all-start.4
  311.5 7.3 %gate_in_back.2.rest_0_.part = f32[256,1536]{1,0:T(8,128)} custom-call(s32[14]{0:T(128)} %concatenate.116.info, bf16[256,1536]{1,0:T(8,128)(2,1)} %get-tuple-element.161.dz, bf16[8,80,384]{2,1,0:T(8,128)(2,1)} %get-tuple-element.162.token, bf16[1536,3072]{1,0:T(8,128)(2,1)} %all-gather.7.cloned.1.call-done.rest_0_), custom_call_target="tpu_custom_call" | custom-call | flops 1207959552 | bytes 7000000 | tf_op jit(solution)/shard_map/gate_in_back/pallas_call | solution.py:937
  321.5 6.0 all-to-all-start.5
  327.5 8.7 %inside_back.2 = (f32[256,1536]{1,0:T(8,128)}, f32[8,1536]{1,0:T(8,128)}, f32[32,256]{1,0:T(8,128)}, f32[256,128]{1,0:T(8,128)}, f32[256,256]{1,0:T(8,128)}) custom-call(bf16[256,1536]{1,0:T(8,128)(2,1)} %get-tuple-element.159.dy, f32[256,1536]{1,0:T(8,128)} %get-tuple-element.147.xa, f32[256,256]{1,0:T(8,128)} %get-tuple-element.148.bca, ...), custom_call_target="tpu_custom_call" | custom-call | flops 402653184 | bytes 4500000 | tf_op jit(solution)/shard_map/inside_back/pallas_call | solution.py:699
  337.0 12.3 %finish_back.2 = (bf16[256,1536]{1,0:T(8,128)(2,1)}, bf16[256,384]{1,0:T(8,128)(2,1)}, f32[16,1536]{1,0:T(8,128)}, f32[16,256]{1,0:T(8,128)}, bf16[16,1536]{1,0:...) custom-call(s32[14]{0:T(128)} %concatenate.116.info, ...), custom_call_target="tpu_custom_call" | custom-call | flops 503316480 | bytes 7500000 | tf_op jit(solution)/shard_map/finish_back/pallas_call | solution.py:852
  359.4 11.1 %mixed_back.2 = (f32[256,1536]{1,0:T(8,128)}, f32[8,1536]{1,0:T(8,128)}, bf16[1536,1920]{1,0:T(8,128)(2,1)}) custom-call(s32[14]{0:T(128)} %concatenate.116.info, bf16[256,1920]{1,0:T(8,128)(2,1)} %patch.2.dxc, f32[256,1536]{1,0:T(8,128)} %gate_in_back.2.rest_0_.part, bf16[256,1536]{1,0:T(8,128)(2,1)} %get-tuple-element.142.h_ref, ...), custom_call_target="tpu_custom_call" | custom-call | flops 3019898880 | bytes 14000000 | tf_op jit(solution)/shard_map/mixed_back/pallas_call | solution.py:1008
  382.5 9.1 %gate_back.3 = (bf16[256,1536]{1,0:T(8,128)(2,1)}, bf16[256,1536]{1,0:T(8,128)(2,1)}, bf16[256,1536]{1,0:T(8,128)(2,1)}, bf16[1536,256]{1,0:T(8,128)(2,1)}, f32[8,1536]{1,0:T(8,128)}) custom-call(s32[14]{0:T(128)} %concatenate.116.info, bf16[256,1536]{1,0:T(8,128)(2,1)} %get-tuple-element.175.cot, f32[256,1536]{1,0:T(8,128)} %get-tuple-element.176.y, ...), custom_call_target="tpu_custom_call" | custom-call | flops 2415919104 | bytes 17000000 | tf_op jit(solution)/shard_map/gate_back/pallas_call | solution.py:555
  391.5 7.7 %own_grad.3 = (f32[4,128,384]{2,1,0:T(8,128)}, bf16[8,80,384]{2,1,0:T(8,128)(2,1)}, bf16[1536,1536]{1,0:T(8,128)(2,1)}) custom-call(bf16[256,1536]{1,0:T(8,128)(2,1)} %get-tuple-element.179.dy, f32[256,256]{1,0:T(8,128)} %get-tuple-element.131.bca, f32[256,128]{1,0:T(8,128)} %get-tuple-element.132.cum, bf16[8,80,384]{2,1,0:T(8,128)(2,1)} %get-tuple-element.134.msg_in, ...), custom_call_target="tpu_custom_call" | custom-call | flops 1207959552 | bytes 8000000 | tf_op jit(solution)/shard_map/own_grad/pallas_call | solution.py:604
  399.3 7.5 %all-to-all-start.6 = ((bf16[8,80,384]{2,1,0:T(8,128)(2,1)}), bf16[8,80,384]{2,1,0:T(8,128)(2,1)S(1)}, u32[]{:S(2)}, u32[]{:S(2)}) async-start(bf16[8,80,384]{2,1,0:T(8,128)(2,1)} %get-tuple-element.182.token), calls=%async_computation.6 | async-start | bytes 983040 | tf_op jit(solution)/shard_map/all_to_all | solution.py:1259
  409.2 7.4 %gate_in_back.3.rest_0_.part = f32[256,1536]{1,0:T(8,128)} custom-call(s32[14]{0:T(128)} %concatenate.116.info, bf16[256,1536]{1,0:T(8,128)(2,1)} %get-tuple-element.181.dz, bf16[8,80,384]{2,1,0:T(8,128)(2,1)} %get-tuple-element.182.token, bf16[384,3072]{1,0:T(8,128)(2,1)} %get-tuple-element.138.rest_0_, bf16[384,3072]{1,0:T(8,128)(2,1)} %collective-permute-done.13.rest_1_, ...), custom_call_target="tpu_custom_call" | custom-call | flops 1207959552 | bytes 7000000 | tf_op jit(solution)/shard_map/gate_in_back/pallas_call | solution.py:937
  419.4 6.5 all-to-all-start.7
  427.5 8.7 %inside_back.3 = (f32[256,1536]{1,0:T(8,128)}, f32[8,1536]{1,0:T(8,128)}, f32[32,256]{1,0:T(8,128)}, f32[256,128]{1,0:T(8,128)}, f32[256,256]{1,0:T(8,128)}) custom-call(bf16[256,1536]{1,0:T(8,128)(2,1)} %get-tuple-element.179.dy, f32[256,1536]{1,0:T(8,128)} %get-tuple-element.130.xa, f32[256,256]{1,0:T(8,128)} %get-tuple-element.131.bca, ...), custom_call_target="tpu_custom_call" | custom-call | flops 402653184 | bytes 4500000 | tf_op jit(solution)/shard_map/inside_back/pallas_call | solution.py:699
  436.9 12.3 %finish_back.3 = (bf16[256,1536]{1,0:T(8,128)(2,1)}, bf16[256,384]{1,0:T(8,128)(2,1)}, f32[16,1536]{1,0:T(8,128)}, f32[16,256]{1,0:T(8,128)}, bf16[16,1536]{1,0:...) custom-call(s32[14]{0:T(128)} %concatenate.116.info, ...), custom_call_target="tpu_custom_call" | custom-call | flops 503316480 | bytes 7500000 | tf_op jit(solution)/shard_map/finish_back/pallas_call | solution.py:852
  459.8 5.8 terms.2.rest_10_
  465.6 5.4 all-to-all-start.8
  472.5 9.1 %mixed_back.3 = (f32[256,1536]{1,0:T(8,128)}, f32[8,1536]{1,0:T(8,128)}) custom-call(s32[14]{0:T(128)} %concatenate.116.info, bf16[256,1920]{1,0:T(8,128)(2,1)} %patch.3.rest_1_.dxc, f32[256,1536]{1,0:T(8,128)} %gate_in_back.3.rest_0_.part, bf16[256,1536]{1,0:T(8,128)(2,1)} %get-tuple-element.262.refs_0_.h_ref, ...), custom_call_target="tpu_custom_call" | custom-call | flops 3019898880 | bytes 14000000 | tf_op jit(solution)/shard_map/mixed_back/pallas_call | solution.py:1008
  483.1 7.7 %terms.3 = (bf16[416,1792]{1,0:T(8,128)(2,1)}, bf16[416,1792]{1,0:T(8,128)(2,1)}, bf16[416,1792]{1,0:T(8,128)(2,1)}, bf16[416,1792]{1,0:T(8,128)(2,1)}) custom-call(s32[14]{0:T(128)} %concatenate.116.info, bf16[1536,256]{1,0:T(8,128)(2,1)} %bitcast.74, bf16[256,1920]{1,0:T(8,128)(2,1)} %patch.3.rest_1_.dxc, bf16[1536,256]{1,0:T(8,128)(2,1)} %get-tuple-element.199.rest_2_, ...), custom_call_target="tpu_custom_call" | custom-call | flops 1409286144 | bytes 8000000 | tf_op jit(solution)/shard_map/terms/pallas_call | solution.py:1160
  493.5 20.8 %reduce-scatter.11.cloned.1.call-done.rest_3_ = bf16[384,1536]{1,0:T(8,128)(2,1)} async-done(((bf16[1536,1536]{1,0:T(8,128)(2,1)}), bf16[384,1536]{1,0:T(8,128)(2,1)}) %reduce-scatter.11.cloned.1.call-update) | async-done | bytes 1179664 | tf_op jit(solution)/shard_map/reduce_scatter | solution.py:1474
  514.3 9.1 %collective-permute-done.29.rest_4_.rest_1_ = bf16[416,1792]{1,0:T(8,128)(2,1)S(1)} collective-permute-done((bf16[416,1792]{1,0:T(8,128)(2,1)}, bf16[416,1792]{1,0:T(8,128)(2,1)S(1)}, u32[]{:S(2)}, u32[]{:S(2)}) %collective-permute-start.29) | collective-permute-done | bytes 1490976 | tf_op jit(solution)/shard_map/ppermute | solution.py:1066
  530.7 5.5 all-to-all-start.9
  560.0 16.4 %collective-permute-done.34.rest_2_ = bf16[416,1792]{1,0:T(8,128)(2,1)S(1)} collective-permute-done((bf16[416,1792]{1,0:T(8,128)(2,1)}, bf16[416,1792]{1,0:T(8,128)(2,1)S(1)}, u32[]{:S(2)}, u32[]{:S(2)}) %collective-permute-start.34) | collective-permute-done | bytes 1490976 | tf_op jit(solution)/shard_map/ppermute | solution.py:1066
  577.4 5.6 fold.6
  599.1 5.1 collective-permute-done.35.rest_5_
  622.6 11.0 %collective-permute-done.39 = bf16[56,3456]{1,0:T(8,128)(2,1)S(1)} collective-permute-done((bf16[56,3456]{1,0:T(8,128)(2,1)}, bf16[56,3456]{1,0:T(8,128)(2,1)S(1)}, u32[]{:S(2)}, u32[]{:S(2)}) %collective-permute-start.39) | collective-permute-done | bytes 387104 | tf_op jit(solution)/shard_map/ppermute | solution.py:1066
  635.7 8.9 %collective-permute-start.46 = (f32[24,1536]{1,0:T(8,128)S(1)}, f32[24,1536]{1,0:T(8,128)S(1)}, u32[]{:S(2)}, u32[]{:S(2)}) collective-permute-start(f32[24,1536]{1,0:T(8,128)S(1)} %get-tuple-element.269), channel_id=1, source_target_pairs={{0,0},{1,64},{2,1},{3,65},{4,2},{5,66},{6,3},{7,67},{8,4},{9,68},{... | collective-permute-start | bytes 442376 | tf_op jit(solution)/shard_map/ppermute | solution.py:1606
  652.6 5.6 collective-permute-done.47
  (373 shorter events, 255.9 us)
Async XLA Ops:
  7.2 99.3 %all-gather.9.cloned.1.call-start = ((), (), s32[]{:S(2)}) async-start(), calls=%async_computation.20 | async-start | bytes 2949120 | tf_op jit(solution)/shard_map/all_gather | solution.py:1547
  13.3 16.3 %collective-permute-start.2 = (bf16[400,1920]{1,0:T(8,128)(2,1)}, bf16[400,1920]{1,0:T(8,128)(2,1)}, u32[]{:S(2)}, u32[]{:S(2)}) collective-permute-start(bf16[400,1920]{1,0:T(8,128)(2,1)} %get-tuple-element.124), channel_id=1, source_target_pairs={{0,64},{64,0},{1,65},{65,1},{2,66},{66,2},{3,67},{67,3},{4,68},{68... | collective-permute-start | bytes 4608008 | tf_op jit(solution)/shard_map/ppermute | solution.py:1070
  25.2 35.2 %collective-permute-start.13 = (bf16[384,3072]{1,0:T(8,128)(2,1)}, bf16[384,3072]{1,0:T(8,128)(2,1)}, u32[]{:S(2)}, u32[]{:S(2)}) collective-permute-start(bf16[384,3072]{1,0:T(8,128)(2,1)} %get-tuple-element.139), channel_id=1, source_target_pairs={{0,64},{64,0},{1,65},{65,1},{2,66},{66,2},{3,67},{67,3},{4,68},{68... | collective-permute-start | bytes 7077896 | tf_op jit(solution)/shard_map/ppermute | solution.py:1070
  31.9 13.7 %collective-permute-start.5 = (bf16[112,1920]{1,0:T(8,128)(2,1)S(1)}, bf16[112,1920]{1,0:T(8,128)(2,1)S(1)}, u32[]{:S(2)}, u32[]{:S(2)}) collective-permute-start(bf16[112,1920]{1,0:T(8,128)(2,1)S(1)} %pad_maximum_fusion.5.rest_0_), channel_id=1, source_target_pairs={{0,16},{16,32},{32,48},{48,0},{1,17},{17,33},{33,49},{49,1},{2,18}... | collective-permute-start | bytes 1290248 | tf_op jit(solution)/shard_map/ppermute | solution.py:1066
  33.6 22.0 %collective-permute-start.4 = (bf16[112,1920]{1,0:T(8,128)(2,1)S(1)}, bf16[112,1920]{1,0:T(8,128)(2,1)S(1)}, u32[]{:S(2)}, u32[]{:S(2)}) collective-permute-start(bf16[112,1920]{1,0:T(8,128)(2,1)S(1)} %pad_maximum_fusion.5.rest_0_), channel_id=1, source_target_pairs={{0,32},{16,48},{32,0},{48,16},{1,33},{17,49},{33,1},{49,17},{2,34}... | collective-permute-start | bytes 1290248 | tf_op jit(solution)/shard_map/ppermute | solution.py:1066
  36.9 18.7 %collective-permute-start.3 = (bf16[112,1920]{1,0:T(8,128)(2,1)S(1)}, bf16[112,1920]{1,0:T(8,128)(2,1)S(1)}, u32[]{:S(2)}, u32[]{:S(2)}) collective-permute-start(bf16[112,1920]{1,0:T(8,128)(2,1)S(1)} %pad_maximum_fusion.5.rest_0_), channel_id=1, source_target_pairs={{0,48},{16,0},{32,16},{48,32},{1,49},{17,1},{33,17},{49,33},{2,50}... | collective-permute-start | bytes 1290248 | tf_op jit(solution)/shard_map/ppermute | solution.py:1066
  62.6 100.1 %all-gather.5.cloned.1.call-start = ((), (), s32[]{:S(2)}) async-start(), calls=%async_computation.14 | async-start | bytes 7680000 | tf_op jit(solution)/shard_map/all_gather | solution.py:1552
  70.6 186.3 %all-gather.7.cloned.1.call-start = ((), (), s32[]{:S(2)}) async-start(), calls=%async_computation.15 | async-start | bytes 11796480 | tf_op jit(solution)/shard_map/all_gather | solution.py:1553
  75.5 25.7 %collective-permute-start.6 = (bf16[144,1920]{1,0:T(8,128)(2,1)S(1)}, bf16[144,1920]{1,0:T(8,128)(2,1)S(1)}, u32[]{:S(2)}, u32[]{:S(2)}) collective-permute-start(bf16[144,1920]{1,0:T(8,128)(2,1)S(1)} %copy-done.8), channel_id=1, source_target_pairs={{0,3},{1,0},{2,1},{3,2},{4,7},{5,4},{6,5},{7,6},{8,11},{9,8},{10,9... | collective-permute-start | bytes 1658888 | tf_op jit(solution)/shard_map/ppermute | solution.py:1066
  77.4 23.8 %collective-permute-start.11 = (bf16[144,1920]{1,0:T(8,128)(2,1)S(1)}, bf16[144,1920]{1,0:T(8,128)(2,1)}, u32[]{:S(2)}, u32[]{:S(2)}) collective-permute-start(bf16[144,1920]{1,0:T(8,128)(2,1)S(1)} %copy-done.7), channel_id=1, source_target_pairs={{0,4},{1,5},{2,6},{3,7},{4,8},{5,9},{6,10},{7,11},{8,12},{9,13},{1... | collective-permute-start | bytes 1658888 | tf_op jit(solution)/shard_map/ppermute | solution.py:1066
  78.6 22.5 %collective-permute-start.10 = (bf16[144,1920]{1,0:T(8,128)(2,1)S(1)}, bf16[144,1920]{1,0:T(8,128)(2,1)}, u32[]{:S(2)}, u32[]{:S(2)}) collective-permute-start(bf16[144,1920]{1,0:T(8,128)(2,1)S(1)} %copy-done.7), channel_id=1, source_target_pairs={{0,8},{1,9},{2,10},{3,11},{4,12},{5,13},{6,14},{7,15},{8,0},{9,1},... | collective-permute-start | bytes 1658888 | tf_op jit(solution)/shard_map/ppermute | solution.py:1066
  84.5 19.5 %collective-permute-start.9 = (bf16[144,1920]{1,0:T(8,128)(2,1)S(1)}, bf16[144,1920]{1,0:T(8,128)(2,1)}, u32[]{:S(2)}, u32[]{:S(2)}) collective-permute-start(bf16[144,1920]{1,0:T(8,128)(2,1)S(1)} %copy-done.7), channel_id=1, source_target_pairs={{0,12},{1,13},{2,14},{3,15},{4,0},{5,1},{6,2},{7,3},{8,4},{9,5},{1... | collective-permute-start | bytes 1658888 | tf_op jit(solution)/shard_map/ppermute | solution.py:1066
  109.1 23.4 %collective-permute-start.16 = (bf16[144,3072]{1,0:T(8,128)(2,1)S(1)}, bf16[144,3072]{1,0:T(8,128)(2,1)S(1)}, u32[]{:S(2)}, u32[]{:S(2)}) collective-permute-start(bf16[144,3072]{1,0:T(8,128)(2,1)S(1)} %pad_maximum_fusion.rest_2_), channel_id=1, source_target_pairs={{0,1},{1,2},{2,3},{3,0},{4,5},{5,6},{6,7},{7,4},{8,9},{9,10},{10,1... | collective-permute-start | bytes 2654216 | tf_op jit(solution)/shard_map/ppermute | solution.py:1066
  128.1 55.4 %collective-permute-start.15 = (bf16[144,3072]{1,0:T(8,128)(2,1)S(1)}, bf16[144,3072]{1,0:T(8,128)(2,1)S(1)}, u32[]{:S(2)}, u32[]{:S(2)}) collective-permute-start(bf16[144,3072]{1,0:T(8,128)(2,1)S(1)} %pad_maximum_fusion.rest_2_), channel_id=1, source_target_pairs={{0,2},{1,3},{2,0},{3,1},{4,6},{5,7},{6,4},{7,5},{8,10},{9,11},{10,... | collective-permute-start | bytes 2654216 | tf_op jit(solution)/shard_map/ppermute | solution.py:1066
  128.2 55.3 %collective-permute-start.14 = (bf16[144,3072]{1,0:T(8,128)(2,1)S(1)}, bf16[144,3072]{1,0:T(8,128)(2,1)}, u32[]{:S(2)}, u32[]{:S(2)}) collective-permute-start(bf16[144,3072]{1,0:T(8,128)(2,1)S(1)} %pad_maximum_fusion.rest_2_), channel_id=1, source_target_pairs={{0,3},{1,0},{2,1},{3,2},{4,7},{5,4},{6,5},{7,6},{8,11},{9,8},{10,9... | collective-permute-start | bytes 2654216 | tf_op jit(solution)/shard_map/ppermute | solution.py:1066
  128.4 55.1 %collective-permute-start.19 = (bf16[144,3072]{1,0:T(8,128)(2,1)S(1)}, bf16[144,3072]{1,0:T(8,128)(2,1)}, u32[]{:S(2)}, u32[]{:S(2)}) collective-permute-start(bf16[144,3072]{1,0:T(8,128)(2,1)S(1)} %pad_maximum_fusion.1.rest_6_), channel_id=1, source_target_pairs={{0,4},{1,5},{2,6},{3,7},{4,8},{5,9},{6,10},{7,11},{8,12},{9,13},{1... | collective-permute-start | bytes 2654216 | tf_op jit(solution)/shard_map/ppermute | solution.py:1066
  130.4 53.1 %collective-permute-start.18 = (bf16[144,3072]{1,0:T(8,128)(2,1)S(1)}, bf16[144,3072]{1,0:T(8,128)(2,1)}, u32[]{:S(2)}, u32[]{:S(2)}) collective-permute-start(bf16[144,3072]{1,0:T(8,128)(2,1)S(1)} %pad_maximum_fusion.1.rest_6_), channel_id=1, source_target_pairs={{0,8},{1,9},{2,10},{3,11},{4,12},{5,13},{6,14},{7,15},{8,0},{9,1},... | collective-permute-start | bytes 2654216 | tf_op jit(solution)/shard_map/ppermute | solution.py:1066
  132.6 50.9 %collective-permute-start.17 = (bf16[144,3072]{1,0:T(8,128)(2,1)S(1)}, bf16[144,3072]{1,0:T(8,128)(2,1)}, u32[]{:S(2)}, u32[]{:S(2)}) collective-permute-start(bf16[144,3072]{1,0:T(8,128)(2,1)S(1)} %pad_maximum_fusion.1.rest_6_), channel_id=1, source_target_pairs={{0,12},{1,13},{2,14},{3,15},{4,0},{5,1},{6,2},{7,3},{8,4},{9,5},{1... | collective-permute-start | bytes 2654216 | tf_op jit(solution)/shard_map/ppermute | solution.py:1066
  138.7 38.4 %all-to-all-start = ((bf16[8,80,384]{2,1,0:T(8,128)(2,1)}), bf16[8,80,384]{2,1,0:T(8,128)(2,1)}, u32[]{:S(2)}, u32[]{:S(2)}) async-start(bf16[8,80,384]{2,1,0:T(8,128)(2,1)} %get-tuple-element.134.msg_in), calls=%async_computation | async-start | bytes 983040 | tf_op jit(solution)/shard_map/all_to_all | solution.py:1259
  247.7 15.4 %all-to-all-start.3 = ((bf16[8,64,384]{2,1,0:T(8,128)(2,1)}), bf16[8,64,384]{2,1,0:T(8,128)(2,1)S(1)}, u32[]{:S(2)}, u32[]{:S(2)}) async-start(bf16[8,64,384]{2,1,0:T(8,128)(2,1)} %chunk_scan.5), calls=%async_computation.3 | async-start | bytes 786432 | tf_op jit(solution)/shard_map/all_to_all | solution.py:1259
  253.0 219.5 %reduce-scatter.7.cloned.1.call-start = ((), (), s32[]{:S(2)}) async-start(), calls=%async_computation.17 | async-start | bytes 5898240 | tf_op jit(solution)/shard_map/reduce_scatter | solution.py:1474
  292.3 180.1 %reduce-scatter.5.cloned.1.call-start = ((), (), s32[]{:S(2)}) async-start(), calls=%async_computation.16 | async-start | bytes 5898240 | tf_op jit(solution)/shard_map/reduce_scatter | solution.py:1474
  300.1 18.7 %all-to-all-start.4 = ((bf16[8,80,384]{2,1,0:T(8,128)(2,1)}), bf16[8,80,384]{2,1,0:T(8,128)(2,1)S(1)}, u32[]{:S(2)}, u32[]{:S(2)}) async-start(bf16[8,80,384]{2,1,0:T(8,128)(2,1)} %get-tuple-element.162.token), calls=%async_computation.4 | async-start | bytes 983040 | tf_op jit(solution)/shard_map/all_to_all | solution.py:1259
  308.4 46.3 %collective-permute-start.24 = (f32[128,1536]{1,0:T(8,128)S(1)}, f32[128,1536]{1,0:T(8,128)S(1)}, u32[]{:S(2)}, u32[]{:S(2)}) collective-permute-start(f32[128,1536]{1,0:T(8,128)S(1)} %get-tuple-element.257), channel_id=1, source_target_pairs={{64,65},{65,64},{66,67},{67,66},{68,69},{69,68},{70,71},{71,70},{7... | collective-permute-start | bytes 2359304 | tf_op jit(solution)/shard_map/ppermute | solution.py:1567
  321.5 14.7 %all-to-all-start.5 = ((bf16[8,64,384]{2,1,0:T(8,128)(2,1)}), bf16[8,64,384]{2,1,0:T(8,128)(2,1)S(1)}, u32[]{:S(2)}, u32[]{:S(2)}) async-start(bf16[8,64,384]{2,1,0:T(8,128)(2,1)} %chunk_scan.6), calls=%async_computation.5 | async-start | bytes 786432 | tf_op jit(solution)/shard_map/all_to_all | solution.py:1259
  327.5 145.0 %reduce-scatter.9.cloned.1.call-start = ((), (), s32[]{:S(2)}) async-start(), calls=%async_computation.18 | async-start | bytes 7372800 | tf_op jit(solution)/shard_map/reduce_scatter | solution.py:1474
  370.6 143.8 %reduce-scatter.11.cloned.1.call-start = ((), (), s32[]{:S(2)}) async-start(), calls=%async_computation.19 | async-start | bytes 5898240 | tf_op jit(solution)/shard_map/reduce_scatter | solution.py:1474
  399.3 17.3 %all-to-all-start.6 = ((bf16[8,80,384]{2,1,0:T(8,128)(2,1)}), bf16[8,80,384]{2,1,0:T(8,128)(2,1)S(1)}, u32[]{:S(2)}, u32[]{:S(2)}) async-start(bf16[8,80,384]{2,1,0:T(8,128)(2,1)} %get-tuple-element.182.token), calls=%async_computation.6 | async-start | bytes 983040 | tf_op jit(solution)/shard_map/all_to_all | solution.py:1259
  419.4 16.8 %all-to-all-start.7 = ((bf16[8,64,384]{2,1,0:T(8,128)(2,1)}), bf16[8,64,384]{2,1,0:T(8,128)(2,1)S(1)}, u32[]{:S(2)}, u32[]{:S(2)}) async-start(bf16[8,64,384]{2,1,0:T(8,128)(2,1)} %chunk_scan.7), calls=%async_computation.7 | async-start | bytes 786432 | tf_op jit(solution)/shard_map/all_to_all | solution.py:1259
  465.6 65.0 %all-to-all-start.8 = ((bf16[4,384,1664]{2,1,0:T(8,128)(2,1)}), bf16[4,384,1664]{2,1,0:T(8,128)(2,1)}, u32[]{:S(2)}, u32[]{:S(2)}) async-start(bf16[4,384,1664]{2,1,0:T(8,128)(2,1)} %terms.2.rest_10_), calls=%async_computation.11 | async-start | bytes 10223616 | tf_op jit(solution)/shard_map/all_to_all | solution.py:1255
  490.8 32.6 %collective-permute-start.29 = (bf16[416,1792]{1,0:T(8,128)(2,1)}, bf16[416,1792]{1,0:T(8,128)(2,1)S(1)}, u32[]{:S(2)}, u32[]{:S(2)}) collective-permute-start(bf16[416,1792]{1,0:T(8,128)(2,1)} %get-tuple-element.213), channel_id=1, source_target_pairs={{0,1},{1,2},{2,3},{3,0},{4,5},{5,6},{6,7},{7,4},{8,9},{9,10},{10,1... | collective-permute-start | bytes 4472840 | tf_op jit(solution)/shard_map/ppermute | solution.py:1066
  493.5 31.1 %collective-permute-start.30 = (bf16[416,1792]{1,0:T(8,128)(2,1)}, bf16[416,1792]{1,0:T(8,128)(2,1)S(1)}, u32[]{:S(2)}, u32[]{:S(2)}) collective-permute-start(bf16[416,1792]{1,0:T(8,128)(2,1)} %get-tuple-element.214), channel_id=1, source_target_pairs={{0,3},{1,0},{2,1},{3,2},{4,7},{5,4},{6,5},{7,6},{8,11},{9,8},{10,9... | collective-permute-start | bytes 4472840 | tf_op jit(solution)/shard_map/ppermute | solution.py:1066
  530.7 58.3 %all-to-all-start.9 = ((bf16[4,96,6528]{2,1,0:T(8,128)(2,1)}), bf16[4,96,6528]{2,1,0:T(8,128)(2,1)}, u32[]{:S(2)}, u32[]{:S(2)}) async-start(bf16[4,96,6528]{2,1,0:T(8,128)(2,1)} %fold.4.rest_1_), calls=%async_computation.13 | async-start | bytes 10027008 | tf_op jit(solution)/shard_map/all_to_all | solution.py:1255
  540.3 36.1 %collective-permute-start.34 = (bf16[416,1792]{1,0:T(8,128)(2,1)}, bf16[416,1792]{1,0:T(8,128)(2,1)S(1)}, u32[]{:S(2)}, u32[]{:S(2)}) collective-permute-start(bf16[416,1792]{1,0:T(8,128)(2,1)} %get-tuple-element.220), channel_id=1, source_target_pairs={{0,2},{1,3},{2,0},{3,1},{4,6},{5,7},{6,4},{7,5},{8,10},{9,11},{10,... | collective-permute-start | bytes 4472840 | tf_op jit(solution)/shard_map/ppermute | solution.py:1066
  551.6 53.7 %collective-permute-start.28 = (f32[128,1536]{1,0:T(8,128)}, f32[128,1536]{1,0:T(8,128)S(1)}, u32[]{:S(2)}, u32[]{:S(2)}) collective-permute-start(f32[128,1536]{1,0:T(8,128)} %get-tuple-element.260), channel_id=1, source_target_pairs={{0,1},{1,0},{2,3},{3,2},{4,5},{5,4},{6,7},{7,6},{8,9},{9,8},{10,11... | collective-permute-start | bytes 2359304 | tf_op jit(solution)/shard_map/ppermute | solution.py:1567
  557.1 28.2 %collective-permute-start.31 = (bf16[96,1664]{1,0:T(8,128)(2,1)}, bf16[96,1664]{1,0:T(8,128)(2,1)S(1)}, u32[]{:S(2)}, u32[]{:S(2)}) collective-permute-start(bf16[96,1664]{1,0:T(8,128)(2,1)} %get-tuple-element.216), channel_id=1, source_target_pairs={{0,1},{1,2},{2,3},{3,0},{4,5},{5,6},{6,7},{7,4},{8,9},{9,10},{10,1... | collective-permute-start | bytes 958472 | tf_op jit(solution)/shard_map/ppermute | solution.py:1066
  558.2 27.8 %collective-permute-start.32 = (bf16[96,1664]{1,0:T(8,128)(2,1)}, bf16[96,1664]{1,0:T(8,128)(2,1)}, u32[]{:S(2)}, u32[]{:S(2)}) collective-permute-start(bf16[96,1664]{1,0:T(8,128)(2,1)} %get-tuple-element.217), channel_id=1, source_target_pairs={{0,2},{1,3},{2,0},{3,1},{4,6},{5,7},{6,4},{7,5},{8,10},{9,11},{10,... | collective-permute-start | bytes 958472 | tf_op jit(solution)/shard_map/ppermute | solution.py:1066
  583.1 21.1 %collective-permute-start.35 = (bf16[128,1792]{1,0:T(8,128)(2,1)}, bf16[128,1792]{1,0:T(8,128)(2,1)}, u32[]{:S(2)}, u32[]{:S(2)}) collective-permute-start(bf16[128,1792]{1,0:T(8,128)(2,1)} %get-tuple-element.223), channel_id=1, source_target_pairs={{0,4},{1,5},{2,6},{3,7},{4,8},{5,9},{6,10},{7,11},{8,12},{9,13},{1... | collective-permute-start | bytes 1376264 | tf_op jit(solution)/shard_map/ppermute | solution.py:1066
  585.3 21.7 %collective-permute-start.36 = (bf16[128,1792]{1,0:T(8,128)(2,1)}, bf16[128,1792]{1,0:T(8,128)(2,1)}, u32[]{:S(2)}, u32[]{:S(2)}) collective-permute-start(bf16[128,1792]{1,0:T(8,128)(2,1)} %get-tuple-element.224), channel_id=1, source_target_pairs={{0,8},{1,9},{2,10},{3,11},{4,12},{5,13},{6,14},{7,15},{8,0},{9,1},... | collective-permute-start | bytes 1376264 | tf_op jit(solution)/shard_map/ppermute | solution.py:1066
  586.0 23.9 %collective-permute-start.37 = (bf16[128,1792]{1,0:T(8,128)(2,1)}, bf16[128,1792]{1,0:T(8,128)(2,1)}, u32[]{:S(2)}, u32[]{:S(2)}) collective-permute-start(bf16[128,1792]{1,0:T(8,128)(2,1)} %get-tuple-element.225), channel_id=1, source_target_pairs={{0,12},{1,13},{2,14},{3,15},{4,0},{5,1},{6,2},{7,3},{8,4},{9,5},{1... | collective-permute-start | bytes 1376264 | tf_op jit(solution)/shard_map/ppermute | solution.py:1066
  595.7 21.0 %collective-permute-start.42 = (bf16[24,6528]{1,0:T(8,128)(2,1)}, bf16[24,6528]{1,0:T(8,128)(2,1)S(1)}, u32[]{:S(2)}, u32[]{:S(2)}) collective-permute-start(bf16[24,6528]{1,0:T(8,128)(2,1)} %get-tuple-element.231), channel_id=1, source_target_pairs={{0,2},{1,3},{2,0},{3,1},{4,6},{5,7},{6,4},{7,5},{8,10},{9,11},{10,... | collective-permute-start | bytes 940040 | tf_op jit(solution)/shard_map/ppermute | solution.py:1066
  604.1 14.7 %collective-permute-start.43 = (bf16[24,6528]{1,0:T(8,128)(2,1)}, bf16[24,6528]{1,0:T(8,128)(2,1)}, u32[]{:S(2)}, u32[]{:S(2)}) collective-permute-start(bf16[24,6528]{1,0:T(8,128)(2,1)} %get-tuple-element.232), channel_id=1, source_target_pairs={{0,1},{1,2},{2,3},{3,0},{4,5},{5,6},{6,7},{7,4},{8,9},{9,10},{10,1... | collective-permute-start | bytes 940040 | tf_op jit(solution)/shard_map/ppermute | solution.py:1066
  605.3 13.6 %collective-permute-start.44 = (bf16[24,6528]{1,0:T(8,128)(2,1)}, bf16[24,6528]{1,0:T(8,128)(2,1)}, u32[]{:S(2)}, u32[]{:S(2)}) collective-permute-start(bf16[24,6528]{1,0:T(8,128)(2,1)} %get-tuple-element.233), channel_id=1, source_target_pairs={{0,3},{1,0},{2,1},{3,2},{4,7},{5,4},{6,5},{7,6},{8,11},{9,8},{10,9... | collective-permute-start | bytes 940040 | tf_op jit(solution)/shard_map/ppermute | solution.py:1066
  616.2 17.5 %collective-permute-start.39 = (bf16[56,3456]{1,0:T(8,128)(2,1)}, bf16[56,3456]{1,0:T(8,128)(2,1)S(1)}, u32[]{:S(2)}, u32[]{:S(2)}) collective-permute-start(bf16[56,3456]{1,0:T(8,128)(2,1)} %get-tuple-element.229), channel_id=1, source_target_pairs={{0,16},{16,32},{32,48},{48,0},{1,17},{17,33},{33,49},{49,1},{2,18}... | collective-permute-start | bytes 1161224 | tf_op jit(solution)/shard_map/ppermute | solution.py:1066
  616.8 16.9 %collective-permute-start.40 = (bf16[56,3456]{1,0:T(8,128)(2,1)}, bf16[56,3456]{1,0:T(8,128)(2,1)S(1)}, u32[]{:S(2)}, u32[]{:S(2)}) collective-permute-start(bf16[56,3456]{1,0:T(8,128)(2,1)} %get-tuple-element.230), channel_id=1, source_target_pairs={{0,48},{16,0},{32,16},{48,32},{1,49},{17,1},{33,17},{49,33},{2,50}... | collective-permute-start | bytes 1161224 | tf_op jit(solution)/shard_map/ppermute | solution.py:1066
  635.7 16.9 %collective-permute-start.46 = (f32[24,1536]{1,0:T(8,128)S(1)}, f32[24,1536]{1,0:T(8,128)S(1)}, u32[]{:S(2)}, u32[]{:S(2)}) collective-permute-start(f32[24,1536]{1,0:T(8,128)S(1)} %get-tuple-element.269), channel_id=1, source_target_pairs={{0,0},{1,64},{2,1},{3,65},{4,2},{5,66},{6,3},{7,67},{8,4},{9,68},{... | collective-permute-start | bytes 442376 | tf_op jit(solution)/shard_map/ppermute | solution.py:1606
  644.6 13.6 %collective-permute-start.47 = (f32[24,1536]{1,0:T(8,128)S(1)}, f32[24,1536]{1,0:T(8,128)S(1)}, u32[]{:S(2)}, u32[]{:S(2)}) collective-permute-start(f32[24,1536]{1,0:T(8,128)S(1)} %get-tuple-element.270), channel_id=1, source_target_pairs={{0,64},{1,0},{2,65},{3,1},{4,66},{5,2},{6,67},{7,3},{8,68},{9,4},{... | collective-permute-start | bytes 442376 | tf_op jit(solution)/shard_map/ppermute | solution.py:1606
  644.7 14.2 %collective-permute-start.45 = (f32[24,3456]{1,0:T(8,128)S(1)}, f32[24,3456]{1,0:T(8,128)S(1)}, u32[]{:S(2)}, u32[]{:S(2)}) collective-permute-start(f32[24,3456]{1,0:T(8,128)S(1)} %fusion.1), channel_id=1, source_target_pairs={{0,64},{64,0},{1,65},{65,1},{2,66},{66,2},{3,67},{67,3},{4,68},{68... | collective-permute-start | bytes 995336 | tf_op jit(solution)/shard_map/ppermute | solution.py:1070
  (74 other events, 614.7 us)
Sparse Core Ops, SparseCore 0:
  62.7 33.5 all-gather.8
  98.0 64.5 all-gather.4
  164.3 92.5 all-gather.6
  292.5 52.4 reduce-scatter.6
  347.2 50.8 reduce-scatter.4
  400.4 60.5 reduce-scatter.8
  463.4 50.8 reduce-scatter.10

commit v8 on v7

--- a/solution.py
+++ b/solution.py
@@ -195,7 +195,8 @@
             self.wait(refs, info, b, buffer, sems)
         step = 512 if self.width % 512 == 0 else 640
         for at in range(0, self.width, step):
-            total[:, at : at + step] = dot(left[...], buffer[:, at : at + step])
+            value = dot(left[...], buffer[:, at : at + step])
+            total[:, at : at + step] = value.astype(total.dtype)
 
 
 def in_proj_body(weight, tokens, info, h_ref, gain_ref, *rest):
@@ -451,14 +452,14 @@
         return 0
 
     lax.fori_loop(0, GROUPS, group, 0)
-    part_ref[:, WIDTH:] = sums[...]
+    part_ref[:, WIDTH:] = sums[...].astype(BF16)
     weight.product(w_refs, info, gained, buffer, sems, part_ref)
 
 
 def out_proj(info, y_in, bca, cum, hin, s0, gate, gain, weight):
     return pl.pallas_call(
         functools.partial(out_proj_body, weight),
-        out_shape=(shape((ROWS, LOCAL)), shape((ROWS, WIDTH + LANES))),
+        out_shape=(shape((ROWS, LOCAL)), shape((ROWS, WIDTH + LANES), BF16)),
         in_specs=[
             SMEM,
             whole((ROWS, LOCAL)),
@@ -482,9 +483,10 @@
 
 
 def join_body(info, h_ref, own, came, res_ref, branch_ref, scale_ref):
-    squares = jnp.sum(own[:, WIDTH:] + came[:, WIDTH:], axis=1, keepdims=True)
+    both = own[...].astype(F32) + came[...].astype(F32)
+    squares = jnp.sum(both[:, WIDTH:], axis=1, keepdims=True)
     scale = lax.rsqrt(squares / INNER + EPSILON)
-    branch = scale * (own[:, :WIDTH] + came[:, :WIDTH])
+    branch = scale * both[:, :WIDTH]
     branch_ref[...] = branch.astype(BF16)
     scale_ref[...] = jnp.broadcast_to(scale, (HALF // 2, LANES))
     first = pl.program_id(0) * (HALF // 2)
@@ -993,14 +995,14 @@
             weight.wait(w_refs, info, n, buffer, sems)
 
     d_norm = part[...] + dot_nt(dxc[...], buffer[block, :])
-    out_ref[...] = d_norm
+    out_ref[...] = d_norm.astype(BF16)
     total = jnp.sum(d_norm * h_ref[:, block].astype(F32) * scale_ref[:, :1], axis=0, keepdims=True)
     dgain_ref[...] = jnp.broadcast_to(total, (8, SHARD))
 
 
 def mixed_back(info, dxc, part, h, normed, weight, with_grad, tokens):
     wide, local = whole((ROWS, WIDTH)), columns(ROWS, SHARD)
-    outs = [shape((ROWS, WIDTH)), shape((8, WIDTH))]
+    outs = [shape((ROWS, WIDTH), BF16), shape((8, WIDTH))]
     specs = [local, columns(8, SHARD)]
     if with_grad:
         outs.append(shape((WIDTH, PACKED), BF16))
@@ -1025,7 +1027,7 @@
 def norm_back_body(own, came, h_ref, cot, gain, dh_ref, low_ref):
     h = h_ref[...].astype(F32)
     scale = lax.rsqrt(jnp.mean(h * h, axis=1, keepdims=True) + EPSILON)
-    d_norm = own[...] + came[...]
+    d_norm = own[...].astype(F32) + came[...].astype(F32)
     inner = jnp.mean(d_norm * gain[...] * h, axis=1, keepdims=True) * scale * scale * scale
     dh = cot[...].astype(F32) + scale * d_norm * gain[...] - h * inner
     dh_ref[...] = dh
@@ -1545,7 +1547,8 @@
     small_low = got
     low_x = pieces(mine_x, came_x, got, 0)
     got = lax.all_gather(fetched(mine_zo, came_zo, 0, section, after(got[1:], place)), "dp")
-    late = after(low_x[3:6] + low_x[7:10], place)["z"]
+    low_params = unpack(info, small_low)
+    late = after([*low_x[3:6], *low_x[7:10], low_params[0]], place)["z"]
     got = [None] + [lax.dynamic_index_in_dim(got, (late + r) % 4, 0, False) for r in range(1, 4)]
     low_zo = pieces(mine_zo, came_zo, got, 0)
     here = after([low_x[2], low_x[6]], {"section": section})["section"]
@@ -1556,7 +1559,7 @@
     weights_z = [Weight(v, n, LOCAL) for n, v in enumerate((low_zo, high_zo))]
     weights_o = [Weight(v, n, WIDTH, LOCAL) for n, v in enumerate((low_zo, high_zo))]
 
-    unpacked = [unpack(info, v) for v in (small_low, high_x)]
+    unpacked = [low_params, unpack(info, high_x)]
     cpars, gains_one, gains_two, hpars = zip(*unpacked, strict=True)
 
     def returned(rows, layer):

time: 682 us -> 678 us (level)
  the two profiles are of different devices: /device:TPU:11 before, /device:TPU:12 now
where the time goes in v8:
time: 678 us; the launch traced here: 666 us
  Pallas kernels  259 us (38%)
  waiting for transfers between devices  162 us (24%)
  starting transfers between devices  152 us (22%)
  local copies, waits for them, and re-layouts  46.1 us (7%)
  other arithmetic  24.8 us (4%)
  between operations  21.7 us (3%)
    ppermute x30, waiting for transfers between devices, send(): return lax.ppermute(value, name, pairs)  90.8 us
    all_to_all x8, starting transfers between devices, exchange(): return lax.all_to_all(value, 'ctx', 0, 0, axis_index_groups=PARITY)  72.9 us
    ppermute x30, starting transfers between devices, send(): return lax.ppermute(value, name, pairs)  40.1 us
    pallas_call x2, Pallas kernels, finish_call(): pl.pallas_call(finish_body, grid=(GROUPS,), out_shape=(shape((ROWS, LOCAL...  24.6 us
    ppermute x4, waiting for transfers between devices, halo_shift(): return lax.ppermute(value, 'ctx', pairs)  22.5 us
    unnamed x110, local copies, waits for them, and re-layouts  20.5 us
    pallas_call x4, Pallas kernels, fold(): pl.pallas_call(functools.partial(fold_body, slot, counts, outer, inner, m...  20.4 us
    pallas_call x2, Pallas kernels, mixed_back(): pl.pallas_call(functools.partial(mixed_back_body, weight, len(tokens)), g...  19.9 us
  transfers between devices with their start and end apart: 65, of which 31 were waited for; matrix products, arithmetic and copies ran while one was open for 7% of the time, Pallas kernels for 36%

profile of v8, /device:TPU:12, one launch (start us, length us, event | category | flops | bytes accessed | tf_op | source)
XLA Modules:
  0.0 665.5 jit_solution(3473118880546296797)
XLA Ops:
  38.3 7.6 %collective-permute-done.5.rest_3_.refs_2_ = bf16[112,1920]{1,0:T(8,128)(2,1)S(1)} collective-permute-done((bf16[112,1920]{1,0:T(8,128)(2,1)S(1)}, bf16[112,1920]{1,0:T(8,128)(2,1)S(1)}, u32[]{:S(2)}, u32[]{:S(2)}) %collective-permute-start.5) | collective-permute-done | bytes 430112 | tf_op jit(solution)/shard_map/ppermute | solution.py:1068
  45.9 10.4 %collective-permute-done.4.rest_2_.refs_1_ = bf16[112,1920]{1,0:T(8,128)(2,1)S(1)} collective-permute-done((bf16[112,1920]{1,0:T(8,128)(2,1)S(1)}, bf16[112,1920]{1,0:T(8,128)(2,1)S(1)}, u32[]{:S(2)}, u32[]{:S(2)}) %collective-permute-start.4) | collective-permute-done | bytes 430112 | tf_op jit(solution)/shard_map/ppermute | solution.py:1068
  81.5 9.8 %collective-permute-done.8.rest_5_.refs_2_ = bf16[144,1920]{1,0:T(8,128)(2,1)S(1)} collective-permute-done((bf16[144,1920]{1,0:T(8,128)(2,1)S(1)}, bf16[144,1920]{1,0:T(8,128)(2,1)S(1)}, u32[]{:S(2)}, u32[]{:S(2)}) %collective-permute-start.8) | collective-permute-done | bytes 552992 | tf_op jit(solution)/shard_map/ppermute | solution.py:1068
  110.4 7.0 %in_proj.2 = (bf16[256,1536]{1,0:T(8,128)(2,1)}, bf16[256,1792]{1,0:T(8,128)(2,1)}, f32[256,128]{1,0:T(8,128)}) custom-call(s32[14]{0:T(128)} %concatenate.116.info, bf16[256,1536]{1,0:T(8,128)(2,1)} %get-tuple-element.262.refs_0_.h_ref, f32[1,1536]{1,0:T(1,128)} %get-tuple-element.125.gain_ref.gain, bf16[400,1920]{1,0:T(8,128)(2,1)} %get-tuple-element.123.rest_0_.token, ...), custom_call_target="tpu_custom_call" | custom-call | flops 1509949440 | bytes 8000000 | tf_op jit(solution)/shard_map/in_proj/pallas_call | solution.py:216
  126.4 8.1 %collective-permute-done.12.halo.halo_bc = bf16[16,1792]{1,0:T(8,128)(2,1)S(1)} collective-permute-done((bf16[16,1792]{1,0:T(8,128)(2,1)S(1)}, bf16[16,1792]{1,0:T(8,128)(2,1)S(1)}, u32[]{:S(2)}, u32[]{:S(2)}) %collective-permute-start.12) | collective-permute-done | bytes 57376 | tf_op jit(solution)/shard_map/ppermute | solution.py:1266
  137.5 5.7 conv_state.2
  143.3 23.1 %all-to-all-start = ((bf16[8,80,384]{2,1,0:T(8,128)(2,1)}), bf16[8,80,384]{2,1,0:T(8,128)(2,1)}, u32[]{:S(2)}, u32[]{:S(2)}) async-start(bf16[8,80,384]{2,1,0:T(8,128)(2,1)} %get-tuple-element.134.msg_in), calls=%async_computation | async-start | bytes 983040 | tf_op jit(solution)/shard_map/all_to_all | solution.py:1261
  166.3 5.8 inside.2.rest_0_.y_in
  177.2 6.7 %all-to-all-start.1 = ((bf16[8,64,384]{2,1,0:T(8,128)(2,1)}), bf16[8,64,384]{2,1,0:T(8,128)(2,1)S(1)}, u32[]{:S(2)}, u32[]{:S(2)}) async-start(bf16[8,64,384]{2,1,0:T(8,128)(2,1)} %chunk_scan.4), calls=%async_computation.1 | async-start | bytes 786432 | tf_op jit(solution)/shard_map/all_to_all | solution.py:1261
  184.7 6.3 gate_proj.2.gate
  191.8 7.3 %out_proj.2 = (f32[256,1536]{1,0:T(8,128)}, bf16[256,1664]{1,0:T(8,128)(2,1)}) custom-call(s32[14]{0:T(128)} %concatenate.116.info, f32[256,1536]{1,0:T(8,128)} %inside.2.rest_0_.y_in, f32[256,256]{1,0:T(8,128)} %get-tuple-element.131.bca, f32[256,128]{1,0:T(8,128)} %get-tuple-element.132.cum, bf16[4,128,384]{2,1,0:T(8,128)(2,1)} %bitcast.71, ...), custom_call_target="tpu_custom_call" | custom-call | flops 1207959552 | bytes 13000000 | tf_op jit(solution)/shard_map/out_proj/pallas_call | solution.py:460
  206.7 7.1 %in_proj.3 = (bf16[256,1536]{1,0:T(8,128)(2,1)}, bf16[256,1792]{1,0:T(8,128)(2,1)}, f32[256,128]{1,0:T(8,128)}) custom-call(s32[14]{0:T(128)} %concatenate.116.info, bf16[256,1536]{1,0:T(8,128)(2,1)} %get-tuple-element.142.h_ref, f32[1,1536]{1,0:T(1,128)} %get-tuple-element.143.gain_ref.gain, bf16[1600,1920]{1,0:T(8,128)(2,1)} %all-gather.5.cloned.1.call-done.rest_0_), custom_call_target="tpu_custom_call" | custom-call | flops 1509949440 | bytes 8000000 | tf_op jit(solution)/shard_map/in_proj/pallas_call | solution.py:216
  222.8 5.8 conv_state.3
  228.6 7.2 %all-to-all-start.2 = ((bf16[8,80,384]{2,1,0:T(8,128)(2,1)}), bf16[8,80,384]{2,1,0:T(8,128)(2,1)S(1)}, u32[]{:S(2)}, u32[]{:S(2)}) async-start(bf16[8,80,384]{2,1,0:T(8,128)(2,1)} %get-tuple-element.151.msg_in), calls=%async_computation.2 | async-start | bytes 983040 | tf_op jit(solution)/shard_map/all_to_all | solution.py:1261
  235.8 5.8 inside.3.rest_0_.y_in
  245.6 6.9 %all-to-all-start.3 = ((bf16[8,64,384]{2,1,0:T(8,128)(2,1)}), bf16[8,64,384]{2,1,0:T(8,128)(2,1)S(1)}, u32[]{:S(2)}, u32[]{:S(2)}) async-start(bf16[8,64,384]{2,1,0:T(8,128)(2,1)} %chunk_scan.5), calls=%async_computation.3 | async-start | bytes 786432 | tf_op jit(solution)/shard_map/all_to_all | solution.py:1261
  256.8 6.3 gate_proj.3.gate
  263.9 7.3 %out_proj.3 = (f32[256,1536]{1,0:T(8,128)}, bf16[256,1664]{1,0:T(8,128)(2,1)}) custom-call(s32[14]{0:T(128)} %concatenate.116.info, f32[256,1536]{1,0:T(8,128)} %inside.3.rest_0_.y_in, f32[256,256]{1,0:T(8,128)} %get-tuple-element.148.bca, f32[256,128]{1,0:T(8,128)} %get-tuple-element.149.cum, bf16[4,128,384]{2,1,0:T(8,128)(2,1)} %bitcast.69, ...), custom_call_target="tpu_custom_call" | custom-call | flops 1207959552 | bytes 13000000 | tf_op jit(solution)/shard_map/out_proj/pallas_call | solution.py:460
  279.4 10.5 %gate_back.2 = (bf16[256,1536]{1,0:T(8,128)(2,1)}, bf16[256,1536]{1,0:T(8,128)(2,1)}, bf16[256,1536]{1,0:T(8,128)(2,1)}, bf16[1536,1536]{1,0:T(8,128)(2,1)}, f32[8,1536]{1,0:T(8,128)}) custom-call(s32[14]{0:T(128)} %concatenate.116.info, bf16[256,1536]{1,0:T(8,128)(2,1)} %get-tuple-element.261.cot, f32[256,1536]{1,0:T(8,128)} %get-tuple-element.155.y, ...), custom_call_target="tpu_custom_call" | custom-call | flops 2415919104 | bytes 17000000 | tf_op jit(solution)/shard_map/gate_back/pallas_call | solution.py:557
  290.0 7.7 %own_grad.2 = (f32[4,128,384]{2,1,0:T(8,128)}, bf16[8,80,384]{2,1,0:T(8,128)(2,1)}, bf16[1536,1536]{1,0:T(8,128)(2,1)}) custom-call(bf16[256,1536]{1,0:T(8,128)(2,1)} %get-tuple-element.159.dy, f32[256,256]{1,0:T(8,128)} %get-tuple-element.148.bca, f32[256,128]{1,0:T(8,128)} %get-tuple-element.149.cum, bf16[8,80,384]{2,1,0:T(8,128)(2,1)} %get-tuple-element.151.msg_in, ...), custom_call_target="tpu_custom_call" | custom-call | flops 1207959552 | bytes 8000000 | tf_op jit(solution)/shard_map/own_grad/pallas_call | solution.py:606
  297.7 7.2 %all-to-all-start.4 = ((bf16[8,80,384]{2,1,0:T(8,128)(2,1)}), bf16[8,80,384]{2,1,0:T(8,128)(2,1)S(1)}, u32[]{:S(2)}, u32[]{:S(2)}) async-start(bf16[8,80,384]{2,1,0:T(8,128)(2,1)} %get-tuple-element.162.token), calls=%async_computation.4 | async-start | bytes 983040 | tf_op jit(solution)/shard_map/all_to_all | solution.py:1261
  308.2 7.3 %gate_in_back.2.rest_0_.part = f32[256,1536]{1,0:T(8,128)} custom-call(s32[14]{0:T(128)} %concatenate.116.info, bf16[256,1536]{1,0:T(8,128)(2,1)} %get-tuple-element.161.dz, bf16[8,80,384]{2,1,0:T(8,128)(2,1)} %get-tuple-element.162.token, bf16[1536,3072]{1,0:T(8,128)(2,1)} %all-gather.7.cloned.1.call-done.rest_0_), custom_call_target="tpu_custom_call" | custom-call | flops 1207959552 | bytes 7000000 | tf_op jit(solution)/shard_map/gate_in_back/pallas_call | solution.py:939
  318.2 7.2 %all-to-all-start.5 = ((bf16[8,64,384]{2,1,0:T(8,128)(2,1)}), bf16[8,64,384]{2,1,0:T(8,128)(2,1)S(1)}, u32[]{:S(2)}, u32[]{:S(2)}) async-start(bf16[8,64,384]{2,1,0:T(8,128)(2,1)} %chunk_scan.6), calls=%async_computation.5 | async-start | bytes 786432 | tf_op jit(solution)/shard_map/all_to_all | solution.py:1261
  325.4 8.7 %inside_back.2 = (f32[256,1536]{1,0:T(8,128)}, f32[8,1536]{1,0:T(8,128)}, f32[32,256]{1,0:T(8,128)}, f32[256,128]{1,0:T(8,128)}, f32[256,256]{1,0:T(8,128)}) custom-call(bf16[256,1536]{1,0:T(8,128)(2,1)} %get-tuple-element.159.dy, f32[256,1536]{1,0:T(8,128)} %get-tuple-element.147.xa, f32[256,256]{1,0:T(8,128)} %get-tuple-element.148.bca, ...), custom_call_target="tpu_custom_call" | custom-call | flops 402653184 | bytes 4500000 | tf_op jit(solution)/shard_map/inside_back/pallas_call | solution.py:701
  334.8 12.3 %finish_back.2 = (bf16[256,1536]{1,0:T(8,128)(2,1)}, bf16[256,384]{1,0:T(8,128)(2,1)}, f32[16,1536]{1,0:T(8,128)}, f32[16,256]{1,0:T(8,128)}, bf16[16,1536]{1,0:...) custom-call(s32[14]{0:T(128)} %concatenate.116.info, ...), custom_call_target="tpu_custom_call" | custom-call | flops 503316480 | bytes 7500000 | tf_op jit(solution)/shard_map/finish_back/pallas_call | solution.py:854
  360.0 11.1 %mixed_back.2 = (bf16[256,1536]{1,0:T(8,128)(2,1)}, f32[8,1536]{1,0:T(8,128)}, bf16[1536,1920]{1,0:T(8,128)(2,1)}) custom-call(s32[14]{0:T(128)} %concatenate.116.info, bf16[256,1920]{1,0:T(8,128)(2,1)} %patch.2.dxc, f32[256,1536]{1,0:T(8,128)} %gate_in_back.2.rest_0_.part, bf16[256,1536]{1,0:T(8,128)(2,1)} %get-tuple-element.142.h_ref, ...), custom_call_target="tpu_custom_call" | custom-call | flops 3019898880 | bytes 14000000 | tf_op jit(solution)/shard_map/mixed_back/pallas_call | solution.py:1010
  380.1 9.1 %gate_back.3 = (bf16[256,1536]{1,0:T(8,128)(2,1)}, bf16[256,1536]{1,0:T(8,128)(2,1)}, bf16[256,1536]{1,0:T(8,128)(2,1)}, bf16[1536,256]{1,0:T(8,128)(2,1)}, f32[8,1536]{1,0:T(8,128)}) custom-call(s32[14]{0:T(128)} %concatenate.116.info, bf16[256,1536]{1,0:T(8,128)(2,1)} %get-tuple-element.175.cot, f32[256,1536]{1,0:T(8,128)} %get-tuple-element.176.y, ...), custom_call_target="tpu_custom_call" | custom-call | flops 2415919104 | bytes 17000000 | tf_op jit(solution)/shard_map/gate_back/pallas_call | solution.py:557
  389.2 7.7 %own_grad.3 = (f32[4,128,384]{2,1,0:T(8,128)}, bf16[8,80,384]{2,1,0:T(8,128)(2,1)}, bf16[1536,1536]{1,0:T(8,128)(2,1)}) custom-call(bf16[256,1536]{1,0:T(8,128)(2,1)} %get-tuple-element.179.dy, f32[256,256]{1,0:T(8,128)} %get-tuple-element.131.bca, f32[256,128]{1,0:T(8,128)} %get-tuple-element.132.cum, bf16[8,80,384]{2,1,0:T(8,128)(2,1)} %get-tuple-element.134.msg_in, ...), custom_call_target="tpu_custom_call" | custom-call | flops 1207959552 | bytes 8000000 | tf_op jit(solution)/shard_map/own_grad/pallas_call | solution.py:606
  396.9 7.3 %all-to-all-start.6 = ((bf16[8,80,384]{2,1,0:T(8,128)(2,1)}), bf16[8,80,384]{2,1,0:T(8,128)(2,1)S(1)}, u32[]{:S(2)}, u32[]{:S(2)}) async-start(bf16[8,80,384]{2,1,0:T(8,128)(2,1)} %get-tuple-element.182.token), calls=%async_computation.6 | async-start | bytes 983040 | tf_op jit(solution)/shard_map/all_to_all | solution.py:1261
  406.7 7.3 %gate_in_back.3.rest_0_.part = f32[256,1536]{1,0:T(8,128)} custom-call(s32[14]{0:T(128)} %concatenate.116.info, bf16[256,1536]{1,0:T(8,128)(2,1)} %get-tuple-element.181.dz, bf16[8,80,384]{2,1,0:T(8,128)(2,1)} %get-tuple-element.182.token, bf16[384,3072]{1,0:T(8,128)(2,1)} %get-tuple-element.138.rest_0_, bf16[384,3072]{1,0:T(8,128)(2,1)} %collective-permute-done.13.rest_1_, ...), custom_call_target="tpu_custom_call" | custom-call | flops 1207959552 | bytes 7000000 | tf_op jit(solution)/shard_map/gate_in_back/pallas_call | solution.py:939
  416.8 7.2 %all-to-all-start.7 = ((bf16[8,64,384]{2,1,0:T(8,128)(2,1)}), bf16[8,64,384]{2,1,0:T(8,128)(2,1)S(1)}, u32[]{:S(2)}, u32[]{:S(2)}) async-start(bf16[8,64,384]{2,1,0:T(8,128)(2,1)} %chunk_scan.7), calls=%async_computation.7 | async-start | bytes 786432 | tf_op jit(solution)/shard_map/all_to_all | solution.py:1261
  425.6 8.7 %inside_back.3 = (f32[256,1536]{1,0:T(8,128)}, f32[8,1536]{1,0:T(8,128)}, f32[32,256]{1,0:T(8,128)}, f32[256,128]{1,0:T(8,128)}, f32[256,256]{1,0:T(8,128)}) custom-call(bf16[256,1536]{1,0:T(8,128)(2,1)} %get-tuple-element.179.dy, f32[256,1536]{1,0:T(8,128)} %get-tuple-element.130.xa, f32[256,256]{1,0:T(8,128)} %get-tuple-element.131.bca, ...), custom_call_target="tpu_custom_call" | custom-call | flops 402653184 | bytes 4500000 | tf_op jit(solution)/shard_map/inside_back/pallas_call | solution.py:701
  435.0 12.2 %finish_back.3 = (bf16[256,1536]{1,0:T(8,128)(2,1)}, bf16[256,384]{1,0:T(8,128)(2,1)}, f32[16,1536]{1,0:T(8,128)}, f32[16,256]{1,0:T(8,128)}, bf16[16,1536]{1,0:...) custom-call(s32[14]{0:T(128)} %concatenate.116.info, ...), custom_call_target="tpu_custom_call" | custom-call | flops 503316480 | bytes 7500000 | tf_op jit(solution)/shard_map/finish_back/pallas_call | solution.py:854
  451.2 5.3 collective-permute-done.26.edge
  459.6 5.8 terms.2.rest_10_
  465.4 5.9 all-to-all-start.8
  472.7 8.8 %mixed_back.3 = (bf16[256,1536]{1,0:T(8,128)(2,1)}, f32[8,1536]{1,0:T(8,128)}) custom-call(s32[14]{0:T(128)} %concatenate.116.info, bf16[256,1920]{1,0:T(8,128)(2,1)} %patch.3.rest_1_.dxc, f32[256,1536]{1,0:T(8,128)} %gate_in_back.3.rest_0_.part, bf16[256,1536]{1,0:T(8,128)(2,1)} %get-tuple-element.262.refs_0_.h_ref, ...), custom_call_target="tpu_custom_call" | custom-call | flops 3019898880 | bytes 14000000 | tf_op jit(solution)/shard_map/mixed_back/pallas_call | solution.py:1010
  483.0 7.9 %terms.3 = (bf16[416,1792]{1,0:T(8,128)(2,1)}, bf16[416,1792]{1,0:T(8,128)(2,1)}, bf16[416,1792]{1,0:T(8,128)(2,1)}, bf16[416,1792]{1,0:T(8,128)(2,1)}) custom-call(s32[14]{0:T(128)} %concatenate.116.info, bf16[1536,256]{1,0:T(8,128)(2,1)} %bitcast.74, bf16[256,1920]{1,0:T(8,128)(2,1)} %patch.3.rest_1_.dxc, bf16[1536,256]{1,0:T(8,128)(2,1)} %get-tuple-element.199.rest_2_, ...), custom_call_target="tpu_custom_call" | custom-call | flops 1409286144 | bytes 8000000 | tf_op jit(solution)/shard_map/terms/pallas_call | solution.py:1162
  492.8 18.9 %reduce-scatter.11.cloned.1.call-done.rest_3_ = bf16[384,1536]{1,0:T(8,128)(2,1)} async-done(((bf16[1536,1536]{1,0:T(8,128)(2,1)}), bf16[384,1536]{1,0:T(8,128)(2,1)}) %reduce-scatter.11.cloned.1.call-update) | async-done | bytes 1179664 | tf_op jit(solution)/shard_map/reduce_scatter | solution.py:1476
  511.7 11.7 %collective-permute-done.29.rest_4_.rest_1_ = bf16[416,1792]{1,0:T(8,128)(2,1)S(1)} collective-permute-done((bf16[416,1792]{1,0:T(8,128)(2,1)}, bf16[416,1792]{1,0:T(8,128)(2,1)S(1)}, u32[]{:S(2)}, u32[]{:S(2)}) %collective-permute-start.29) | collective-permute-done | bytes 1490976 | tf_op jit(solution)/shard_map/ppermute | solution.py:1068
  530.6 5.4 all-to-all-start.9
  553.9 19.3 %collective-permute-done.34.rest_2_ = bf16[416,1792]{1,0:T(8,128)(2,1)S(1)} collective-permute-done((bf16[416,1792]{1,0:T(8,128)(2,1)}, bf16[416,1792]{1,0:T(8,128)(2,1)S(1)}, u32[]{:S(2)}, u32[]{:S(2)}) %collective-permute-start.34) | collective-permute-done | bytes 1490976 | tf_op jit(solution)/shard_map/ppermute | solution.py:1068
  574.3 5.7 fold.6
  603.6 6.0 collective-permute-done.37.rest_7_
  621.1 5.9 collective-permute-done.38
  627.0 7.3 %collective-permute-done.39 = bf16[56,3456]{1,0:T(8,128)(2,1)S(1)} collective-permute-done((bf16[56,3456]{1,0:T(8,128)(2,1)}, bf16[56,3456]{1,0:T(8,128)(2,1)S(1)}, u32[]{:S(2)}, u32[]{:S(2)}) %collective-permute-start.39) | collective-permute-done | bytes 387104 | tf_op jit(solution)/shard_map/ppermute | solution.py:1068
  637.0 6.2 collective-permute-start.47
  647.9 5.7 collective-permute-done.47
  (367 shorter events, 242.3 us)
Async XLA Ops:
  7.2 100.0 %all-gather.9.cloned.1.call-start = ((), (), s32[]{:S(2)}) async-start(), calls=%async_computation.20 | async-start | bytes 2949120 | tf_op jit(solution)/shard_map/all_gather | solution.py:1549
  14.2 15.1 %collective-permute-start.2 = (bf16[400,1920]{1,0:T(8,128)(2,1)}, bf16[400,1920]{1,0:T(8,128)(2,1)}, u32[]{:S(2)}, u32[]{:S(2)}) collective-permute-start(bf16[400,1920]{1,0:T(8,128)(2,1)} %get-tuple-element.124), channel_id=1, source_target_pairs={{0,64},{64,0},{1,65},{65,1},{2,66},{66,2},{3,67},{67,3},{4,68},{68... | collective-permute-start | bytes 4608008 | tf_op jit(solution)/shard_map/ppermute | solution.py:1072
  24.5 36.5 %collective-permute-start.13 = (bf16[384,3072]{1,0:T(8,128)(2,1)}, bf16[384,3072]{1,0:T(8,128)(2,1)}, u32[]{:S(2)}, u32[]{:S(2)}) collective-permute-start(bf16[384,3072]{1,0:T(8,128)(2,1)} %get-tuple-element.139), channel_id=1, source_target_pairs={{0,64},{64,0},{1,65},{65,1},{2,66},{66,2},{3,67},{67,3},{4,68},{68... | collective-permute-start | bytes 7077896 | tf_op jit(solution)/shard_map/ppermute | solution.py:1072
  33.7 22.6 %collective-permute-start.4 = (bf16[112,1920]{1,0:T(8,128)(2,1)S(1)}, bf16[112,1920]{1,0:T(8,128)(2,1)S(1)}, u32[]{:S(2)}, u32[]{:S(2)}) collective-permute-start(bf16[112,1920]{1,0:T(8,128)(2,1)S(1)} %pad_maximum_fusion.5.rest_0_), channel_id=1, source_target_pairs={{0,32},{16,48},{32,0},{48,16},{1,33},{17,49},{33,1},{49,17},{2,34}... | collective-permute-start | bytes 1290248 | tf_op jit(solution)/shard_map/ppermute | solution.py:1068
  37.3 19.0 %collective-permute-start.3 = (bf16[112,1920]{1,0:T(8,128)(2,1)S(1)}, bf16[112,1920]{1,0:T(8,128)(2,1)S(1)}, u32[]{:S(2)}, u32[]{:S(2)}) collective-permute-start(bf16[112,1920]{1,0:T(8,128)(2,1)S(1)} %pad_maximum_fusion.5.rest_0_), channel_id=1, source_target_pairs={{0,48},{16,0},{32,16},{48,32},{1,49},{17,1},{33,17},{49,33},{2,50}... | collective-permute-start | bytes 1290248 | tf_op jit(solution)/shard_map/ppermute | solution.py:1068
  63.2 109.0 %all-gather.5.cloned.1.call-start = ((), (), s32[]{:S(2)}) async-start(), calls=%async_computation.14 | async-start | bytes 7680000 | tf_op jit(solution)/shard_map/all_gather | solution.py:1555
  71.2 185.6 %all-gather.7.cloned.1.call-start = ((), (), s32[]{:S(2)}) async-start(), calls=%async_computation.15 | async-start | bytes 11796480 | tf_op jit(solution)/shard_map/all_gather | solution.py:1556
  75.8 15.5 %collective-permute-start.8 = (bf16[144,1920]{1,0:T(8,128)(2,1)S(1)}, bf16[144,1920]{1,0:T(8,128)(2,1)S(1)}, u32[]{:S(2)}, u32[]{:S(2)}) collective-permute-start(bf16[144,1920]{1,0:T(8,128)(2,1)S(1)} %copy-done.8), channel_id=1, source_target_pairs={{0,1},{1,2},{2,3},{3,0},{4,5},{5,6},{6,7},{7,4},{8,9},{9,10},{10,1... | collective-permute-start | bytes 1658888 | tf_op jit(solution)/shard_map/ppermute | solution.py:1068
  77.0 22.5 %collective-permute-start.7 = (bf16[144,1920]{1,0:T(8,128)(2,1)S(1)}, bf16[144,1920]{1,0:T(8,128)(2,1)S(1)}, u32[]{:S(2)}, u32[]{:S(2)}) collective-permute-start(bf16[144,1920]{1,0:T(8,128)(2,1)S(1)} %copy-done.8), channel_id=1, source_target_pairs={{0,2},{1,3},{2,0},{3,1},{4,6},{5,7},{6,4},{7,5},{8,10},{9,11},{10,... | collective-permute-start | bytes 1658888 | tf_op jit(solution)/shard_map/ppermute | solution.py:1068
  77.8 23.5 %collective-permute-start.6 = (bf16[144,1920]{1,0:T(8,128)(2,1)S(1)}, bf16[144,1920]{1,0:T(8,128)(2,1)S(1)}, u32[]{:S(2)}, u32[]{:S(2)}) collective-permute-start(bf16[144,1920]{1,0:T(8,128)(2,1)S(1)} %copy-done.8), channel_id=1, source_target_pairs={{0,3},{1,0},{2,1},{3,2},{4,7},{5,4},{6,5},{7,6},{8,11},{9,8},{10,9... | collective-permute-start | bytes 1658888 | tf_op jit(solution)/shard_map/ppermute | solution.py:1068
  78.9 22.4 %collective-permute-start.11 = (bf16[144,1920]{1,0:T(8,128)(2,1)S(1)}, bf16[144,1920]{1,0:T(8,128)(2,1)}, u32[]{:S(2)}, u32[]{:S(2)}) collective-permute-start(bf16[144,1920]{1,0:T(8,128)(2,1)S(1)} %copy-done.7), channel_id=1, source_target_pairs={{0,4},{1,5},{2,6},{3,7},{4,8},{5,9},{6,10},{7,11},{8,12},{9,13},{1... | collective-permute-start | bytes 1658888 | tf_op jit(solution)/shard_map/ppermute | solution.py:1068
  80.5 20.8 %collective-permute-start.10 = (bf16[144,1920]{1,0:T(8,128)(2,1)S(1)}, bf16[144,1920]{1,0:T(8,128)(2,1)}, u32[]{:S(2)}, u32[]{:S(2)}) collective-permute-start(bf16[144,1920]{1,0:T(8,128)(2,1)S(1)} %copy-done.7), channel_id=1, source_target_pairs={{0,8},{1,9},{2,10},{3,11},{4,12},{5,13},{6,14},{7,15},{8,0},{9,1},... | collective-permute-start | bytes 1658888 | tf_op jit(solution)/shard_map/ppermute | solution.py:1068
  109.1 26.5 %collective-permute-start.16 = (bf16[144,3072]{1,0:T(8,128)(2,1)S(1)}, bf16[144,3072]{1,0:T(8,128)(2,1)S(1)}, u32[]{:S(2)}, u32[]{:S(2)}) collective-permute-start(bf16[144,3072]{1,0:T(8,128)(2,1)S(1)} %pad_maximum_fusion.rest_2_), channel_id=1, source_target_pairs={{0,1},{1,2},{2,3},{3,0},{4,5},{5,6},{6,7},{7,4},{8,9},{9,10},{10,1... | collective-permute-start | bytes 2654216 | tf_op jit(solution)/shard_map/ppermute | solution.py:1068
  118.3 16.2 %collective-permute-start.12 = (bf16[16,1792]{1,0:T(8,128)(2,1)S(1)}, bf16[16,1792]{1,0:T(8,128)(2,1)S(1)}, u32[]{:S(2)}, u32[]{:S(2)}) collective-permute-start(bf16[16,1792]{1,0:T(8,128)(2,1)S(1)} %slice.182), channel_id=1, source_target_pairs={{0,2},{1,3},{2,4},{3,5},{4,6},{5,7},{6,8},{7,9},{8,10},{9,11},{10,... | collective-permute-start | bytes 172040 | tf_op jit(solution)/shard_map/ppermute | solution.py:1266
  122.6 61.2 %collective-permute-start.15 = (bf16[144,3072]{1,0:T(8,128)(2,1)S(1)}, bf16[144,3072]{1,0:T(8,128)(2,1)S(1)}, u32[]{:S(2)}, u32[]{:S(2)}) collective-permute-start(bf16[144,3072]{1,0:T(8,128)(2,1)S(1)} %pad_maximum_fusion.rest_2_), channel_id=1, source_target_pairs={{0,2},{1,3},{2,0},{3,1},{4,6},{5,7},{6,4},{7,5},{8,10},{9,11},{10,... | collective-permute-start | bytes 2654216 | tf_op jit(solution)/shard_map/ppermute | solution.py:1068
  123.8 60.0 %collective-permute-start.14 = (bf16[144,3072]{1,0:T(8,128)(2,1)S(1)}, bf16[144,3072]{1,0:T(8,128)(2,1)}, u32[]{:S(2)}, u32[]{:S(2)}) collective-permute-start(bf16[144,3072]{1,0:T(8,128)(2,1)S(1)} %pad_maximum_fusion.rest_2_), channel_id=1, source_target_pairs={{0,3},{1,0},{2,1},{3,2},{4,7},{5,4},{6,5},{7,6},{8,11},{9,8},{10,9... | collective-permute-start | bytes 2654216 | tf_op jit(solution)/shard_map/ppermute | solution.py:1068
  125.2 58.6 %collective-permute-start.19 = (bf16[144,3072]{1,0:T(8,128)(2,1)S(1)}, bf16[144,3072]{1,0:T(8,128)(2,1)}, u32[]{:S(2)}, u32[]{:S(2)}) collective-permute-start(bf16[144,3072]{1,0:T(8,128)(2,1)S(1)} %pad_maximum_fusion.1.rest_6_), channel_id=1, source_target_pairs={{0,4},{1,5},{2,6},{3,7},{4,8},{5,9},{6,10},{7,11},{8,12},{9,13},{1... | collective-permute-start | bytes 2654216 | tf_op jit(solution)/shard_map/ppermute | solution.py:1068
  134.5 49.3 %collective-permute-start.18 = (bf16[144,3072]{1,0:T(8,128)(2,1)S(1)}, bf16[144,3072]{1,0:T(8,128)(2,1)}, u32[]{:S(2)}, u32[]{:S(2)}) collective-permute-start(bf16[144,3072]{1,0:T(8,128)(2,1)S(1)} %pad_maximum_fusion.1.rest_6_), channel_id=1, source_target_pairs={{0,8},{1,9},{2,10},{3,11},{4,12},{5,13},{6,14},{7,15},{8,0},{9,1},... | collective-permute-start | bytes 2654216 | tf_op jit(solution)/shard_map/ppermute | solution.py:1068
  135.7 48.2 %collective-permute-start.17 = (bf16[144,3072]{1,0:T(8,128)(2,1)S(1)}, bf16[144,3072]{1,0:T(8,128)(2,1)}, u32[]{:S(2)}, u32[]{:S(2)}) collective-permute-start(bf16[144,3072]{1,0:T(8,128)(2,1)S(1)} %pad_maximum_fusion.1.rest_6_), channel_id=1, source_target_pairs={{0,12},{1,13},{2,14},{3,15},{4,0},{5,1},{6,2},{7,3},{8,4},{9,5},{1... | collective-permute-start | bytes 2654216 | tf_op jit(solution)/shard_map/ppermute | solution.py:1068
  143.3 31.9 %all-to-all-start = ((bf16[8,80,384]{2,1,0:T(8,128)(2,1)}), bf16[8,80,384]{2,1,0:T(8,128)(2,1)}, u32[]{:S(2)}, u32[]{:S(2)}) async-start(bf16[8,80,384]{2,1,0:T(8,128)(2,1)} %get-tuple-element.134.msg_in), calls=%async_computation | async-start | bytes 983040 | tf_op jit(solution)/shard_map/all_to_all | solution.py:1261
  245.6 17.5 %all-to-all-start.3 = ((bf16[8,64,384]{2,1,0:T(8,128)(2,1)}), bf16[8,64,384]{2,1,0:T(8,128)(2,1)S(1)}, u32[]{:S(2)}, u32[]{:S(2)}) async-start(bf16[8,64,384]{2,1,0:T(8,128)(2,1)} %chunk_scan.5), calls=%async_computation.3 | async-start | bytes 786432 | tf_op jit(solution)/shard_map/all_to_all | solution.py:1261
  252.6 220.1 %reduce-scatter.7.cloned.1.call-start = ((), (), s32[]{:S(2)}) async-start(), calls=%async_computation.17 | async-start | bytes 5898240 | tf_op jit(solution)/shard_map/reduce_scatter | solution.py:1476
  289.9 182.7 %reduce-scatter.5.cloned.1.call-start = ((), (), s32[]{:S(2)}) async-start(), calls=%async_computation.16 | async-start | bytes 5898240 | tf_op jit(solution)/shard_map/reduce_scatter | solution.py:1476
  297.7 17.8 %all-to-all-start.4 = ((bf16[8,80,384]{2,1,0:T(8,128)(2,1)}), bf16[8,80,384]{2,1,0:T(8,128)(2,1)S(1)}, u32[]{:S(2)}, u32[]{:S(2)}) async-start(bf16[8,80,384]{2,1,0:T(8,128)(2,1)} %get-tuple-element.162.token), calls=%async_computation.4 | async-start | bytes 983040 | tf_op jit(solution)/shard_map/all_to_all | solution.py:1261
  307.5 43.3 %collective-permute-start.24 = (f32[128,1536]{1,0:T(8,128)S(1)}, f32[128,1536]{1,0:T(8,128)S(1)}, u32[]{:S(2)}, u32[]{:S(2)}) collective-permute-start(f32[128,1536]{1,0:T(8,128)S(1)} %get-tuple-element.257), channel_id=1, source_target_pairs={{64,65},{65,64},{66,67},{67,66},{68,69},{69,68},{70,71},{71,70},{7... | collective-permute-start | bytes 2359304 | tf_op jit(solution)/shard_map/ppermute | solution.py:1570
  318.2 15.9 %all-to-all-start.5 = ((bf16[8,64,384]{2,1,0:T(8,128)(2,1)}), bf16[8,64,384]{2,1,0:T(8,128)(2,1)S(1)}, u32[]{:S(2)}, u32[]{:S(2)}) async-start(bf16[8,64,384]{2,1,0:T(8,128)(2,1)} %chunk_scan.6), calls=%async_computation.5 | async-start | bytes 786432 | tf_op jit(solution)/shard_map/all_to_all | solution.py:1261
  325.4 147.3 %reduce-scatter.9.cloned.1.call-start = ((), (), s32[]{:S(2)}) async-start(), calls=%async_computation.18 | async-start | bytes 7372800 | tf_op jit(solution)/shard_map/reduce_scatter | solution.py:1476
  371.2 140.5 %reduce-scatter.11.cloned.1.call-start = ((), (), s32[]{:S(2)}) async-start(), calls=%async_computation.19 | async-start | bytes 5898240 | tf_op jit(solution)/shard_map/reduce_scatter | solution.py:1476
  396.9 17.1 %all-to-all-start.6 = ((bf16[8,80,384]{2,1,0:T(8,128)(2,1)}), bf16[8,80,384]{2,1,0:T(8,128)(2,1)S(1)}, u32[]{:S(2)}, u32[]{:S(2)}) async-start(bf16[8,80,384]{2,1,0:T(8,128)(2,1)} %get-tuple-element.182.token), calls=%async_computation.6 | async-start | bytes 983040 | tf_op jit(solution)/shard_map/all_to_all | solution.py:1261
  416.8 17.5 %all-to-all-start.7 = ((bf16[8,64,384]{2,1,0:T(8,128)(2,1)}), bf16[8,64,384]{2,1,0:T(8,128)(2,1)S(1)}, u32[]{:S(2)}, u32[]{:S(2)}) async-start(bf16[8,64,384]{2,1,0:T(8,128)(2,1)} %chunk_scan.7), calls=%async_computation.7 | async-start | bytes 786432 | tf_op jit(solution)/shard_map/all_to_all | solution.py:1261
  465.4 65.2 %all-to-all-start.8 = ((bf16[4,384,1664]{2,1,0:T(8,128)(2,1)}), bf16[4,384,1664]{2,1,0:T(8,128)(2,1)}, u32[]{:S(2)}, u32[]{:S(2)}) async-start(bf16[4,384,1664]{2,1,0:T(8,128)(2,1)} %terms.2.rest_10_), calls=%async_computation.11 | async-start | bytes 10223616 | tf_op jit(solution)/shard_map/all_to_all | solution.py:1257
  490.8 32.6 %collective-permute-start.29 = (bf16[416,1792]{1,0:T(8,128)(2,1)}, bf16[416,1792]{1,0:T(8,128)(2,1)S(1)}, u32[]{:S(2)}, u32[]{:S(2)}) collective-permute-start(bf16[416,1792]{1,0:T(8,128)(2,1)} %get-tuple-element.213), channel_id=1, source_target_pairs={{0,1},{1,2},{2,3},{3,0},{4,5},{5,6},{6,7},{7,4},{8,9},{9,10},{10,1... | collective-permute-start | bytes 4472840 | tf_op jit(solution)/shard_map/ppermute | solution.py:1068
  491.8 32.3 %collective-permute-start.30 = (bf16[416,1792]{1,0:T(8,128)(2,1)}, bf16[416,1792]{1,0:T(8,128)(2,1)S(1)}, u32[]{:S(2)}, u32[]{:S(2)}) collective-permute-start(bf16[416,1792]{1,0:T(8,128)(2,1)} %get-tuple-element.214), channel_id=1, source_target_pairs={{0,3},{1,0},{2,1},{3,2},{4,7},{5,4},{6,5},{7,6},{8,11},{9,8},{10,9... | collective-permute-start | bytes 4472840 | tf_op jit(solution)/shard_map/ppermute | solution.py:1068
  530.6 62.4 %all-to-all-start.9 = ((bf16[4,96,6528]{2,1,0:T(8,128)(2,1)}), bf16[4,96,6528]{2,1,0:T(8,128)(2,1)}, u32[]{:S(2)}, u32[]{:S(2)}) async-start(bf16[4,96,6528]{2,1,0:T(8,128)(2,1)} %fold.4.rest_1_), calls=%async_computation.13 | async-start | bytes 10027008 | tf_op jit(solution)/shard_map/all_to_all | solution.py:1257
  536.0 37.2 %collective-permute-start.34 = (bf16[416,1792]{1,0:T(8,128)(2,1)}, bf16[416,1792]{1,0:T(8,128)(2,1)S(1)}, u32[]{:S(2)}, u32[]{:S(2)}) collective-permute-start(bf16[416,1792]{1,0:T(8,128)(2,1)} %get-tuple-element.220), channel_id=1, source_target_pairs={{0,2},{1,3},{2,0},{3,1},{4,6},{5,7},{6,4},{7,5},{8,10},{9,11},{10,... | collective-permute-start | bytes 4472840 | tf_op jit(solution)/shard_map/ppermute | solution.py:1068
  545.1 38.5 %collective-permute-start.28 = (f32[128,1536]{1,0:T(8,128)S(1)}, f32[128,1536]{1,0:T(8,128)S(1)}, u32[]{:S(2)}, u32[]{:S(2)}) collective-permute-start(f32[128,1536]{1,0:T(8,128)S(1)} %get-tuple-element.260), channel_id=1, source_target_pairs={{0,1},{1,0},{2,3},{3,2},{4,5},{5,4},{6,7},{7,6},{8,9},{9,8},{10,11... | collective-permute-start | bytes 2359304 | tf_op jit(solution)/shard_map/ppermute | solution.py:1570
  552.9 35.8 %collective-permute-start.31 = (bf16[96,1664]{1,0:T(8,128)(2,1)}, bf16[96,1664]{1,0:T(8,128)(2,1)S(1)}, u32[]{:S(2)}, u32[]{:S(2)}) collective-permute-start(bf16[96,1664]{1,0:T(8,128)(2,1)} %get-tuple-element.216), channel_id=1, source_target_pairs={{0,1},{1,2},{2,3},{3,0},{4,5},{5,6},{6,7},{7,4},{8,9},{9,10},{10,1... | collective-permute-start | bytes 958472 | tf_op jit(solution)/shard_map/ppermute | solution.py:1068
  580.0 21.5 %collective-permute-start.35 = (bf16[128,1792]{1,0:T(8,128)(2,1)}, bf16[128,1792]{1,0:T(8,128)(2,1)}, u32[]{:S(2)}, u32[]{:S(2)}) collective-permute-start(bf16[128,1792]{1,0:T(8,128)(2,1)} %get-tuple-element.223), channel_id=1, source_target_pairs={{0,4},{1,5},{2,6},{3,7},{4,8},{5,9},{6,10},{7,11},{8,12},{9,13},{1... | collective-permute-start | bytes 1376264 | tf_op jit(solution)/shard_map/ppermute | solution.py:1068
  581.5 16.5 %collective-permute-start.32 = (bf16[96,1664]{1,0:T(8,128)(2,1)}, bf16[96,1664]{1,0:T(8,128)(2,1)}, u32[]{:S(2)}, u32[]{:S(2)}) collective-permute-start(bf16[96,1664]{1,0:T(8,128)(2,1)} %get-tuple-element.217), channel_id=1, source_target_pairs={{0,2},{1,3},{2,0},{3,1},{4,6},{5,7},{6,4},{7,5},{8,10},{9,11},{10,... | collective-permute-start | bytes 958472 | tf_op jit(solution)/shard_map/ppermute | solution.py:1068
  582.8 16.6 %collective-permute-start.33 = (bf16[96,1664]{1,0:T(8,128)(2,1)}, bf16[96,1664]{1,0:T(8,128)(2,1)}, u32[]{:S(2)}, u32[]{:S(2)}) collective-permute-start(bf16[96,1664]{1,0:T(8,128)(2,1)} %get-tuple-element.218), channel_id=1, source_target_pairs={{0,3},{1,0},{2,1},{3,2},{4,7},{5,4},{6,5},{7,6},{8,11},{9,8},{10,9... | collective-permute-start | bytes 958472 | tf_op jit(solution)/shard_map/ppermute | solution.py:1068
  583.6 20.0 %collective-permute-start.36 = (bf16[128,1792]{1,0:T(8,128)(2,1)}, bf16[128,1792]{1,0:T(8,128)(2,1)}, u32[]{:S(2)}, u32[]{:S(2)}) collective-permute-start(bf16[128,1792]{1,0:T(8,128)(2,1)} %get-tuple-element.224), channel_id=1, source_target_pairs={{0,8},{1,9},{2,10},{3,11},{4,12},{5,13},{6,14},{7,15},{8,0},{9,1},... | collective-permute-start | bytes 1376264 | tf_op jit(solution)/shard_map/ppermute | solution.py:1068
  588.7 20.9 %collective-permute-start.37 = (bf16[128,1792]{1,0:T(8,128)(2,1)}, bf16[128,1792]{1,0:T(8,128)(2,1)}, u32[]{:S(2)}, u32[]{:S(2)}) collective-permute-start(bf16[128,1792]{1,0:T(8,128)(2,1)} %get-tuple-element.225), channel_id=1, source_target_pairs={{0,12},{1,13},{2,14},{3,15},{4,0},{5,1},{6,2},{7,3},{8,4},{9,5},{1... | collective-permute-start | bytes 1376264 | tf_op jit(solution)/shard_map/ppermute | solution.py:1068
  598.0 19.3 %collective-permute-start.42 = (bf16[24,6528]{1,0:T(8,128)(2,1)}, bf16[24,6528]{1,0:T(8,128)(2,1)S(1)}, u32[]{:S(2)}, u32[]{:S(2)}) collective-permute-start(bf16[24,6528]{1,0:T(8,128)(2,1)} %get-tuple-element.231), channel_id=1, source_target_pairs={{0,2},{1,3},{2,0},{3,1},{4,6},{5,7},{6,4},{7,5},{8,10},{9,11},{10,... | collective-permute-start | bytes 940040 | tf_op jit(solution)/shard_map/ppermute | solution.py:1068
  599.4 20.4 %collective-permute-start.43 = (bf16[24,6528]{1,0:T(8,128)(2,1)}, bf16[24,6528]{1,0:T(8,128)(2,1)}, u32[]{:S(2)}, u32[]{:S(2)}) collective-permute-start(bf16[24,6528]{1,0:T(8,128)(2,1)} %get-tuple-element.232), channel_id=1, source_target_pairs={{0,1},{1,2},{2,3},{3,0},{4,5},{5,6},{6,7},{7,4},{8,9},{9,10},{10,1... | collective-permute-start | bytes 940040 | tf_op jit(solution)/shard_map/ppermute | solution.py:1068
  601.5 18.3 %collective-permute-start.44 = (bf16[24,6528]{1,0:T(8,128)(2,1)}, bf16[24,6528]{1,0:T(8,128)(2,1)}, u32[]{:S(2)}, u32[]{:S(2)}) collective-permute-start(bf16[24,6528]{1,0:T(8,128)(2,1)} %get-tuple-element.233), channel_id=1, source_target_pairs={{0,3},{1,0},{2,1},{3,2},{4,7},{5,4},{6,5},{7,6},{8,11},{9,8},{10,9... | collective-permute-start | bytes 940040 | tf_op jit(solution)/shard_map/ppermute | solution.py:1068
  616.6 17.8 %collective-permute-start.39 = (bf16[56,3456]{1,0:T(8,128)(2,1)}, bf16[56,3456]{1,0:T(8,128)(2,1)S(1)}, u32[]{:S(2)}, u32[]{:S(2)}) collective-permute-start(bf16[56,3456]{1,0:T(8,128)(2,1)} %get-tuple-element.229), channel_id=1, source_target_pairs={{0,16},{16,32},{32,48},{48,0},{1,17},{17,33},{33,49},{49,1},{2,18}... | collective-permute-start | bytes 1161224 | tf_op jit(solution)/shard_map/ppermute | solution.py:1068
  617.2 17.4 %collective-permute-start.40 = (bf16[56,3456]{1,0:T(8,128)(2,1)}, bf16[56,3456]{1,0:T(8,128)(2,1)S(1)}, u32[]{:S(2)}, u32[]{:S(2)}) collective-permute-start(bf16[56,3456]{1,0:T(8,128)(2,1)} %get-tuple-element.230), channel_id=1, source_target_pairs={{0,48},{16,0},{32,16},{48,32},{1,49},{17,1},{33,17},{49,33},{2,50}... | collective-permute-start | bytes 1161224 | tf_op jit(solution)/shard_map/ppermute | solution.py:1068
  637.0 16.6 %collective-permute-start.47 = (f32[24,1536]{1,0:T(8,128)S(1)}, f32[24,1536]{1,0:T(8,128)S(1)}, u32[]{:S(2)}, u32[]{:S(2)}) collective-permute-start(f32[24,1536]{1,0:T(8,128)S(1)} %get-tuple-element.270), channel_id=1, source_target_pairs={{0,64},{1,0},{2,65},{3,1},{4,66},{5,2},{6,67},{7,3},{8,68},{9,4},{... | collective-permute-start | bytes 442376 | tf_op jit(solution)/shard_map/ppermute | solution.py:1609
  (71 other events, 542.6 us)
Sparse Core Ops, SparseCore 0:
  63.3 32.9 all-gather.8
  97.9 64.5 all-gather.4
  164.3 92.5 all-gather.6
  290.0 52.2 reduce-scatter.6
  344.6 50.8 reduce-scatter.4
  397.8 60.4 reduce-scatter.8
  460.8 50.8 reduce-scatter.10

commit v9 on v8

--- a/solution.py
+++ b/solution.py
@@ -1073,19 +1073,19 @@
 
 
 def nothing_body(*refs):
-    refs[-1][...] = jnp.zeros((8, LANES), jnp.int32)
+    refs[-1][0] = jnp.int32(0)
 
 
 def after(values, place):
     nothing = pl.pallas_call(
         nothing_body,
-        out_shape=shape((8, LANES), jnp.int32),
+        out_shape=shape((1,), jnp.int32),
         in_specs=[ANYWHERE] * len(values),
-        out_specs=whole((8, LANES)),
+        out_specs=SMEM,
         compiler_params=params(),
         cost_estimate=pl.CostEstimate(flops=0, bytes_accessed=4096, transcendentals=0),
         name="after",
-    )(*values)[0, 0]
+    )(*values)[0]
     return {axis: n + nothing for axis, n in place.items()}
 
 

time: 678 us -> 675 us (level)
  transfers between devices with their start and end apart: 65 -> 65, of which waited for: 31 -> 31; matrix products, arithmetic and copies ran while one was open for 7% -> 6% of each run, Pallas kernels for 36% -> 36%
where the time goes in v9:
time: 675 us; the launch traced here: 663 us
  Pallas kernels  259 us (38%)
  waiting for transfers between devices  164 us (24%)
  starting transfers between devices  152 us (23%)
  local copies, waits for them, and re-layouts  41.2 us (6%)
  other arithmetic  24.6 us (4%)
  between operations  21.7 us (3%)
    ppermute x30, waiting for transfers between devices, send(): return lax.ppermute(value, name, pairs)  91 us
    all_to_all x8, starting transfers between devices, exchange(): return lax.all_to_all(value, 'ctx', 0, 0, axis_index_groups=PARITY)  73 us
    ppermute x30, starting transfers between devices, send(): return lax.ppermute(value, name, pairs)  39.6 us
    pallas_call x2, Pallas kernels, finish_call(): pl.pallas_call(finish_body, grid=(GROUPS,), out_shape=(shape((ROWS, LOCAL...  24.6 us
    ppermute x4, waiting for transfers between devices, halo_shift(): return lax.ppermute(value, 'ctx', pairs)  22.3 us
    unnamed x110, local copies, waits for them, and re-layouts  20.6 us
    pallas_call x4, Pallas kernels, fold(): pl.pallas_call(functools.partial(fold_body, slot, counts, outer, inner, m...  20.4 us
    pallas_call x2, Pallas kernels, mixed_back(): pl.pallas_call(functools.partial(mixed_back_body, weight, len(tokens)), g...  19.9 us
  transfers between devices with their start and end apart: 65, of which 31 were waited for; matrix products, arithmetic and copies ran while one was open for 6% of the time, Pallas kernels for 36%

profile of v9, /device:TPU:12, one launch (start us, length us, event | category | flops | bytes accessed | tf_op | source)
XLA Modules:
  0.0 663.0 jit_solution(14756858182599687594)
XLA Ops:
  37.0 7.6 %collective-permute-done.5.rest_3_.refs_2_ = bf16[112,1920]{1,0:T(8,128)(2,1)S(1)} collective-permute-done((bf16[112,1920]{1,0:T(8,128)(2,1)S(1)}, bf16[112,1920]{1,0:T(8,128)(2,1)S(1)}, u32[]{:S(2)}, u32[]{:S(2)}) %collective-permute-start.5) | collective-permute-done | bytes 430112 | tf_op jit(solution)/shard_map/ppermute | solution.py:1068
  44.6 10.4 %collective-permute-done.4.rest_2_.refs_1_ = bf16[112,1920]{1,0:T(8,128)(2,1)S(1)} collective-permute-done((bf16[112,1920]{1,0:T(8,128)(2,1)S(1)}, bf16[112,1920]{1,0:T(8,128)(2,1)S(1)}, u32[]{:S(2)}, u32[]{:S(2)}) %collective-permute-start.4) | collective-permute-done | bytes 430112 | tf_op jit(solution)/shard_map/ppermute | solution.py:1068
  77.5 9.8 %collective-permute-done.8.rest_5_.refs_2_ = bf16[144,1920]{1,0:T(8,128)(2,1)S(1)} collective-permute-done((bf16[144,1920]{1,0:T(8,128)(2,1)S(1)}, bf16[144,1920]{1,0:T(8,128)(2,1)S(1)}, u32[]{:S(2)}, u32[]{:S(2)}) %collective-permute-start.8) | collective-permute-done | bytes 552992 | tf_op jit(solution)/shard_map/ppermute | solution.py:1068
  105.1 7.5 %in_proj.2 = (bf16[256,1536]{1,0:T(8,128)(2,1)}, bf16[256,1792]{1,0:T(8,128)(2,1)}, f32[256,128]{1,0:T(8,128)}) custom-call(s32[14]{0:T(128)} %concatenate.116.info, bf16[256,1536]{1,0:T(8,128)(2,1)} %get-tuple-element.262.refs_0_.h_ref, f32[1,1536]{1,0:T(1,128)} %get-tuple-element.125.gain_ref.gain, bf16[400,1920]{1,0:T(8,128)(2,1)} %get-tuple-element.123.rest_0_.token, ...), custom_call_target="tpu_custom_call" | custom-call | flops 1509949440 | bytes 8000000 | tf_op jit(solution)/shard_map/in_proj/pallas_call | solution.py:216
  121.5 8.0 %collective-permute-done.12.halo.halo_bc = bf16[16,1792]{1,0:T(8,128)(2,1)S(1)} collective-permute-done((bf16[16,1792]{1,0:T(8,128)(2,1)S(1)}, bf16[16,1792]{1,0:T(8,128)(2,1)S(1)}, u32[]{:S(2)}, u32[]{:S(2)}) %collective-permute-start.12) | collective-permute-done | bytes 57376 | tf_op jit(solution)/shard_map/ppermute | solution.py:1266
  132.3 5.8 conv_state.2
  138.1 23.0 %all-to-all-start = ((bf16[8,80,384]{2,1,0:T(8,128)(2,1)}), bf16[8,80,384]{2,1,0:T(8,128)(2,1)}, u32[]{:S(2)}, u32[]{:S(2)}) async-start(bf16[8,80,384]{2,1,0:T(8,128)(2,1)} %get-tuple-element.134.msg_in), calls=%async_computation | async-start | bytes 983040 | tf_op jit(solution)/shard_map/all_to_all | solution.py:1261
  161.1 5.8 inside.2.rest_0_.y_in
  171.7 6.8 %all-to-all-start.1 = ((bf16[8,64,384]{2,1,0:T(8,128)(2,1)}), bf16[8,64,384]{2,1,0:T(8,128)(2,1)S(1)}, u32[]{:S(2)}, u32[]{:S(2)}) async-start(bf16[8,64,384]{2,1,0:T(8,128)(2,1)} %chunk_scan.4), calls=%async_computation.1 | async-start | bytes 786432 | tf_op jit(solution)/shard_map/all_to_all | solution.py:1261
  179.4 6.3 gate_proj.2.gate
  186.4 7.3 %out_proj.2 = (f32[256,1536]{1,0:T(8,128)}, bf16[256,1664]{1,0:T(8,128)(2,1)}) custom-call(s32[14]{0:T(128)} %concatenate.116.info, f32[256,1536]{1,0:T(8,128)} %inside.2.rest_0_.y_in, f32[256,256]{1,0:T(8,128)} %get-tuple-element.131.bca, f32[256,128]{1,0:T(8,128)} %get-tuple-element.132.cum, bf16[4,128,384]{2,1,0:T(8,128)(2,1)} %bitcast.71, ...), custom_call_target="tpu_custom_call" | custom-call | flops 1207959552 | bytes 13000000 | tf_op jit(solution)/shard_map/out_proj/pallas_call | solution.py:460
  201.4 7.0 %in_proj.3 = (bf16[256,1536]{1,0:T(8,128)(2,1)}, bf16[256,1792]{1,0:T(8,128)(2,1)}, f32[256,128]{1,0:T(8,128)}) custom-call(s32[14]{0:T(128)} %concatenate.116.info, bf16[256,1536]{1,0:T(8,128)(2,1)} %get-tuple-element.142.h_ref, f32[1,1536]{1,0:T(1,128)} %get-tuple-element.143.gain_ref.gain, bf16[1600,1920]{1,0:T(8,128)(2,1)} %all-gather.5.cloned.1.call-done.rest_0_), custom_call_target="tpu_custom_call" | custom-call | flops 1509949440 | bytes 8000000 | tf_op jit(solution)/shard_map/in_proj/pallas_call | solution.py:216
  217.4 5.7 conv_state.3
  223.1 7.2 %all-to-all-start.2 = ((bf16[8,80,384]{2,1,0:T(8,128)(2,1)}), bf16[8,80,384]{2,1,0:T(8,128)(2,1)S(1)}, u32[]{:S(2)}, u32[]{:S(2)}) async-start(bf16[8,80,384]{2,1,0:T(8,128)(2,1)} %get-tuple-element.151.msg_in), calls=%async_computation.2 | async-start | bytes 983040 | tf_op jit(solution)/shard_map/all_to_all | solution.py:1261
  230.3 5.8 inside.3.rest_0_.y_in
  240.3 6.9 %all-to-all-start.3 = ((bf16[8,64,384]{2,1,0:T(8,128)(2,1)}), bf16[8,64,384]{2,1,0:T(8,128)(2,1)S(1)}, u32[]{:S(2)}, u32[]{:S(2)}) async-start(bf16[8,64,384]{2,1,0:T(8,128)(2,1)} %chunk_scan.5), calls=%async_computation.3 | async-start | bytes 786432 | tf_op jit(solution)/shard_map/all_to_all | solution.py:1261
  247.2 7.1 %all-gather.7.cloned.1.call-done.rest_0_ = bf16[1536,3072]{1,0:T(8,128)(2,1)} async-done(((bf16[384,3072]{1,0:T(8,128)(2,1)}), bf16[1536,3072]{1,0:T(8,128)(2,1)}) %all-gather.7.cloned.1.call-update) | async-done | bytes 9437200 | tf_op jit(solution)/shard_map/all_gather | solution.py:1556
  254.3 6.3 gate_proj.3.gate
  261.4 7.3 %out_proj.3 = (f32[256,1536]{1,0:T(8,128)}, bf16[256,1664]{1,0:T(8,128)(2,1)}) custom-call(s32[14]{0:T(128)} %concatenate.116.info, f32[256,1536]{1,0:T(8,128)} %inside.3.rest_0_.y_in, f32[256,256]{1,0:T(8,128)} %get-tuple-element.148.bca, f32[256,128]{1,0:T(8,128)} %get-tuple-element.149.cum, bf16[4,128,384]{2,1,0:T(8,128)(2,1)} %bitcast.69, ...), custom_call_target="tpu_custom_call" | custom-call | flops 1207959552 | bytes 13000000 | tf_op jit(solution)/shard_map/out_proj/pallas_call | solution.py:460
  276.9 10.5 %gate_back.2 = (bf16[256,1536]{1,0:T(8,128)(2,1)}, bf16[256,1536]{1,0:T(8,128)(2,1)}, bf16[256,1536]{1,0:T(8,128)(2,1)}, bf16[1536,1536]{1,0:T(8,128)(2,1)}, f32[8,1536]{1,0:T(8,128)}) custom-call(s32[14]{0:T(128)} %concatenate.116.info, bf16[256,1536]{1,0:T(8,128)(2,1)} %get-tuple-element.261.cot, f32[256,1536]{1,0:T(8,128)} %get-tuple-element.155.y, ...), custom_call_target="tpu_custom_call" | custom-call | flops 2415919104 | bytes 17000000 | tf_op jit(solution)/shard_map/gate_back/pallas_call | solution.py:557
  287.4 7.7 %own_grad.2 = (f32[4,128,384]{2,1,0:T(8,128)}, bf16[8,80,384]{2,1,0:T(8,128)(2,1)}, bf16[1536,1536]{1,0:T(8,128)(2,1)}) custom-call(bf16[256,1536]{1,0:T(8,128)(2,1)} %get-tuple-element.159.dy, f32[256,256]{1,0:T(8,128)} %get-tuple-element.148.bca, f32[256,128]{1,0:T(8,128)} %get-tuple-element.149.cum, bf16[8,80,384]{2,1,0:T(8,128)(2,1)} %get-tuple-element.151.msg_in, ...), custom_call_target="tpu_custom_call" | custom-call | flops 1207959552 | bytes 8000000 | tf_op jit(solution)/shard_map/own_grad/pallas_call | solution.py:606
  295.1 7.2 %all-to-all-start.4 = ((bf16[8,80,384]{2,1,0:T(8,128)(2,1)}), bf16[8,80,384]{2,1,0:T(8,128)(2,1)S(1)}, u32[]{:S(2)}, u32[]{:S(2)}) async-start(bf16[8,80,384]{2,1,0:T(8,128)(2,1)} %get-tuple-element.162.token), calls=%async_computation.4 | async-start | bytes 983040 | tf_op jit(solution)/shard_map/all_to_all | solution.py:1261
  305.7 7.3 %gate_in_back.2.rest_0_.part = f32[256,1536]{1,0:T(8,128)} custom-call(s32[14]{0:T(128)} %concatenate.116.info, bf16[256,1536]{1,0:T(8,128)(2,1)} %get-tuple-element.161.dz, bf16[8,80,384]{2,1,0:T(8,128)(2,1)} %get-tuple-element.162.token, bf16[1536,3072]{1,0:T(8,128)(2,1)} %all-gather.7.cloned.1.call-done.rest_0_), custom_call_target="tpu_custom_call" | custom-call | flops 1207959552 | bytes 7000000 | tf_op jit(solution)/shard_map/gate_in_back/pallas_call | solution.py:939
  315.7 7.2 %all-to-all-start.5 = ((bf16[8,64,384]{2,1,0:T(8,128)(2,1)}), bf16[8,64,384]{2,1,0:T(8,128)(2,1)S(1)}, u32[]{:S(2)}, u32[]{:S(2)}) async-start(bf16[8,64,384]{2,1,0:T(8,128)(2,1)} %chunk_scan.6), calls=%async_computation.5 | async-start | bytes 786432 | tf_op jit(solution)/shard_map/all_to_all | solution.py:1261
  322.9 8.7 %inside_back.2 = (f32[256,1536]{1,0:T(8,128)}, f32[8,1536]{1,0:T(8,128)}, f32[32,256]{1,0:T(8,128)}, f32[256,128]{1,0:T(8,128)}, f32[256,256]{1,0:T(8,128)}) custom-call(bf16[256,1536]{1,0:T(8,128)(2,1)} %get-tuple-element.159.dy, f32[256,1536]{1,0:T(8,128)} %get-tuple-element.147.xa, f32[256,256]{1,0:T(8,128)} %get-tuple-element.148.bca, ...), custom_call_target="tpu_custom_call" | custom-call | flops 402653184 | bytes 4500000 | tf_op jit(solution)/shard_map/inside_back/pallas_call | solution.py:701
  332.3 12.3 %finish_back.2 = (bf16[256,1536]{1,0:T(8,128)(2,1)}, bf16[256,384]{1,0:T(8,128)(2,1)}, f32[16,1536]{1,0:T(8,128)}, f32[16,256]{1,0:T(8,128)}, bf16[16,1536]{1,0:...) custom-call(s32[14]{0:T(128)} %concatenate.116.info, ...), custom_call_target="tpu_custom_call" | custom-call | flops 503316480 | bytes 7500000 | tf_op jit(solution)/shard_map/finish_back/pallas_call | solution.py:854
  357.5 11.1 %mixed_back.2 = (bf16[256,1536]{1,0:T(8,128)(2,1)}, f32[8,1536]{1,0:T(8,128)}, bf16[1536,1920]{1,0:T(8,128)(2,1)}) custom-call(s32[14]{0:T(128)} %concatenate.116.info, bf16[256,1920]{1,0:T(8,128)(2,1)} %patch.2.dxc, f32[256,1536]{1,0:T(8,128)} %gate_in_back.2.rest_0_.part, bf16[256,1536]{1,0:T(8,128)(2,1)} %get-tuple-element.142.h_ref, ...), custom_call_target="tpu_custom_call" | custom-call | flops 3019898880 | bytes 14000000 | tf_op jit(solution)/shard_map/mixed_back/pallas_call | solution.py:1010
  377.6 9.1 %gate_back.3 = (bf16[256,1536]{1,0:T(8,128)(2,1)}, bf16[256,1536]{1,0:T(8,128)(2,1)}, bf16[256,1536]{1,0:T(8,128)(2,1)}, bf16[1536,256]{1,0:T(8,128)(2,1)}, f32[8,1536]{1,0:T(8,128)}) custom-call(s32[14]{0:T(128)} %concatenate.116.info, bf16[256,1536]{1,0:T(8,128)(2,1)} %get-tuple-element.175.cot, f32[256,1536]{1,0:T(8,128)} %get-tuple-element.176.y, ...), custom_call_target="tpu_custom_call" | custom-call | flops 2415919104 | bytes 17000000 | tf_op jit(solution)/shard_map/gate_back/pallas_call | solution.py:557
  386.7 7.7 %own_grad.3 = (f32[4,128,384]{2,1,0:T(8,128)}, bf16[8,80,384]{2,1,0:T(8,128)(2,1)}, bf16[1536,1536]{1,0:T(8,128)(2,1)}) custom-call(bf16[256,1536]{1,0:T(8,128)(2,1)} %get-tuple-element.179.dy, f32[256,256]{1,0:T(8,128)} %get-tuple-element.131.bca, f32[256,128]{1,0:T(8,128)} %get-tuple-element.132.cum, bf16[8,80,384]{2,1,0:T(8,128)(2,1)} %get-tuple-element.134.msg_in, ...), custom_call_target="tpu_custom_call" | custom-call | flops 1207959552 | bytes 8000000 | tf_op jit(solution)/shard_map/own_grad/pallas_call | solution.py:606
  394.4 7.3 %all-to-all-start.6 = ((bf16[8,80,384]{2,1,0:T(8,128)(2,1)}), bf16[8,80,384]{2,1,0:T(8,128)(2,1)S(1)}, u32[]{:S(2)}, u32[]{:S(2)}) async-start(bf16[8,80,384]{2,1,0:T(8,128)(2,1)} %get-tuple-element.182.token), calls=%async_computation.6 | async-start | bytes 983040 | tf_op jit(solution)/shard_map/all_to_all | solution.py:1261
  404.2 7.3 %gate_in_back.3.rest_0_.part = f32[256,1536]{1,0:T(8,128)} custom-call(s32[14]{0:T(128)} %concatenate.116.info, bf16[256,1536]{1,0:T(8,128)(2,1)} %get-tuple-element.181.dz, bf16[8,80,384]{2,1,0:T(8,128)(2,1)} %get-tuple-element.182.token, bf16[384,3072]{1,0:T(8,128)(2,1)} %get-tuple-element.138.rest_0_, bf16[384,3072]{1,0:T(8,128)(2,1)} %collective-permute-done.13.rest_1_, ...), custom_call_target="tpu_custom_call" | custom-call | flops 1207959552 | bytes 7000000 | tf_op jit(solution)/shard_map/gate_in_back/pallas_call | solution.py:939
  414.3 7.2 %all-to-all-start.7 = ((bf16[8,64,384]{2,1,0:T(8,128)(2,1)}), bf16[8,64,384]{2,1,0:T(8,128)(2,1)S(1)}, u32[]{:S(2)}, u32[]{:S(2)}) async-start(bf16[8,64,384]{2,1,0:T(8,128)(2,1)} %chunk_scan.7), calls=%async_computation.7 | async-start | bytes 786432 | tf_op jit(solution)/shard_map/all_to_all | solution.py:1261
  423.1 8.7 %inside_back.3 = (f32[256,1536]{1,0:T(8,128)}, f32[8,1536]{1,0:T(8,128)}, f32[32,256]{1,0:T(8,128)}, f32[256,128]{1,0:T(8,128)}, f32[256,256]{1,0:T(8,128)}) custom-call(bf16[256,1536]{1,0:T(8,128)(2,1)} %get-tuple-element.179.dy, f32[256,1536]{1,0:T(8,128)} %get-tuple-element.130.xa, f32[256,256]{1,0:T(8,128)} %get-tuple-element.131.bca, ...), custom_call_target="tpu_custom_call" | custom-call | flops 402653184 | bytes 4500000 | tf_op jit(solution)/shard_map/inside_back/pallas_call | solution.py:701
  432.5 12.2 %finish_back.3 = (bf16[256,1536]{1,0:T(8,128)(2,1)}, bf16[256,384]{1,0:T(8,128)(2,1)}, f32[16,1536]{1,0:T(8,128)}, f32[16,256]{1,0:T(8,128)}, bf16[16,1536]{1,0:...) custom-call(s32[14]{0:T(128)} %concatenate.116.info, ...), custom_call_target="tpu_custom_call" | custom-call | flops 503316480 | bytes 7500000 | tf_op jit(solution)/shard_map/finish_back/pallas_call | solution.py:854
  457.1 5.8 terms.2.rest_10_
  462.9 5.9 all-to-all-start.8
  470.2 8.8 %mixed_back.3 = (bf16[256,1536]{1,0:T(8,128)(2,1)}, f32[8,1536]{1,0:T(8,128)}) custom-call(s32[14]{0:T(128)} %concatenate.116.info, bf16[256,1920]{1,0:T(8,128)(2,1)} %patch.3.rest_1_.dxc, f32[256,1536]{1,0:T(8,128)} %gate_in_back.3.rest_0_.part, bf16[256,1536]{1,0:T(8,128)(2,1)} %get-tuple-element.262.refs_0_.h_ref, ...), custom_call_target="tpu_custom_call" | custom-call | flops 3019898880 | bytes 14000000 | tf_op jit(solution)/shard_map/mixed_back/pallas_call | solution.py:1010
  480.4 7.9 %terms.3 = (bf16[416,1792]{1,0:T(8,128)(2,1)}, bf16[416,1792]{1,0:T(8,128)(2,1)}, bf16[416,1792]{1,0:T(8,128)(2,1)}, bf16[416,1792]{1,0:T(8,128)(2,1)}) custom-call(s32[14]{0:T(128)} %concatenate.116.info, bf16[1536,256]{1,0:T(8,128)(2,1)} %bitcast.74, bf16[256,1920]{1,0:T(8,128)(2,1)} %patch.3.rest_1_.dxc, bf16[1536,256]{1,0:T(8,128)(2,1)} %get-tuple-element.199.rest_2_, ...), custom_call_target="tpu_custom_call" | custom-call | flops 1409286144 | bytes 8000000 | tf_op jit(solution)/shard_map/terms/pallas_call | solution.py:1162
  490.3 18.8 %reduce-scatter.11.cloned.1.call-done.rest_3_ = bf16[384,1536]{1,0:T(8,128)(2,1)} async-done(((bf16[1536,1536]{1,0:T(8,128)(2,1)}), bf16[384,1536]{1,0:T(8,128)(2,1)}) %reduce-scatter.11.cloned.1.call-update) | async-done | bytes 1179664 | tf_op jit(solution)/shard_map/reduce_scatter | solution.py:1476
  509.2 11.7 %collective-permute-done.29.rest_4_.rest_1_ = bf16[416,1792]{1,0:T(8,128)(2,1)S(1)} collective-permute-done((bf16[416,1792]{1,0:T(8,128)(2,1)}, bf16[416,1792]{1,0:T(8,128)(2,1)S(1)}, u32[]{:S(2)}, u32[]{:S(2)}) %collective-permute-start.29) | collective-permute-done | bytes 1490976 | tf_op jit(solution)/shard_map/ppermute | solution.py:1068
  528.1 5.4 all-to-all-start.9
  551.3 19.3 %collective-permute-done.34.rest_2_ = bf16[416,1792]{1,0:T(8,128)(2,1)S(1)} collective-permute-done((bf16[416,1792]{1,0:T(8,128)(2,1)}, bf16[416,1792]{1,0:T(8,128)(2,1)S(1)}, u32[]{:S(2)}, u32[]{:S(2)}) %collective-permute-start.34) | collective-permute-done | bytes 1490976 | tf_op jit(solution)/shard_map/ppermute | solution.py:1068
  571.8 5.7 fold.6
  601.0 6.0 collective-permute-done.37.rest_7_
  618.5 6.0 collective-permute-done.38
  624.5 7.3 %collective-permute-done.39 = bf16[56,3456]{1,0:T(8,128)(2,1)S(1)} collective-permute-done((bf16[56,3456]{1,0:T(8,128)(2,1)}, bf16[56,3456]{1,0:T(8,128)(2,1)S(1)}, u32[]{:S(2)}, u32[]{:S(2)}) %collective-permute-start.39) | collective-permute-done | bytes 387104 | tf_op jit(solution)/shard_map/ppermute | solution.py:1068
  634.5 6.3 collective-permute-start.47
  645.4 5.7 collective-permute-done.47
  (363 shorter events, 237.6 us)
Async XLA Ops:
  7.2 94.9 %all-gather.9.cloned.1.call-start = ((), (), s32[]{:S(2)}) async-start(), calls=%async_computation.20 | async-start | bytes 2949120 | tf_op jit(solution)/shard_map/all_gather | solution.py:1549
  24.5 33.9 %collective-permute-start.13 = (bf16[384,3072]{1,0:T(8,128)(2,1)}, bf16[384,3072]{1,0:T(8,128)(2,1)}, u32[]{:S(2)}, u32[]{:S(2)}) collective-permute-start(bf16[384,3072]{1,0:T(8,128)(2,1)} %get-tuple-element.139), channel_id=1, source_target_pairs={{0,64},{64,0},{1,65},{65,1},{2,66},{66,2},{3,67},{67,3},{4,68},{68... | collective-permute-start | bytes 7077896 | tf_op jit(solution)/shard_map/ppermute | solution.py:1072
  32.4 22.6 %collective-permute-start.4 = (bf16[112,1920]{1,0:T(8,128)(2,1)S(1)}, bf16[112,1920]{1,0:T(8,128)(2,1)S(1)}, u32[]{:S(2)}, u32[]{:S(2)}) collective-permute-start(bf16[112,1920]{1,0:T(8,128)(2,1)S(1)} %pad_maximum_fusion.5.rest_0_), channel_id=1, source_target_pairs={{0,32},{16,48},{32,0},{48,16},{1,33},{17,49},{33,1},{49,17},{2,34}... | collective-permute-start | bytes 1290248 | tf_op jit(solution)/shard_map/ppermute | solution.py:1068
  36.0 19.0 %collective-permute-start.3 = (bf16[112,1920]{1,0:T(8,128)(2,1)S(1)}, bf16[112,1920]{1,0:T(8,128)(2,1)S(1)}, u32[]{:S(2)}, u32[]{:S(2)}) collective-permute-start(bf16[112,1920]{1,0:T(8,128)(2,1)S(1)} %pad_maximum_fusion.5.rest_0_), channel_id=1, source_target_pairs={{0,48},{16,0},{32,16},{48,32},{1,49},{17,1},{33,17},{49,33},{2,50}... | collective-permute-start | bytes 1290248 | tf_op jit(solution)/shard_map/ppermute | solution.py:1068
  60.7 106.3 %all-gather.5.cloned.1.call-start = ((), (), s32[]{:S(2)}) async-start(), calls=%async_computation.14 | async-start | bytes 7680000 | tf_op jit(solution)/shard_map/all_gather | solution.py:1555
  67.4 186.9 %all-gather.7.cloned.1.call-start = ((), (), s32[]{:S(2)}) async-start(), calls=%async_computation.15 | async-start | bytes 11796480 | tf_op jit(solution)/shard_map/all_gather | solution.py:1556
  71.9 15.5 %collective-permute-start.8 = (bf16[144,1920]{1,0:T(8,128)(2,1)S(1)}, bf16[144,1920]{1,0:T(8,128)(2,1)S(1)}, u32[]{:S(2)}, u32[]{:S(2)}) collective-permute-start(bf16[144,1920]{1,0:T(8,128)(2,1)S(1)} %copy-done.8), channel_id=1, source_target_pairs={{0,1},{1,2},{2,3},{3,0},{4,5},{5,6},{6,7},{7,4},{8,9},{9,10},{10,1... | collective-permute-start | bytes 1658888 | tf_op jit(solution)/shard_map/ppermute | solution.py:1068
  73.1 22.6 %collective-permute-start.7 = (bf16[144,1920]{1,0:T(8,128)(2,1)S(1)}, bf16[144,1920]{1,0:T(8,128)(2,1)S(1)}, u32[]{:S(2)}, u32[]{:S(2)}) collective-permute-start(bf16[144,1920]{1,0:T(8,128)(2,1)S(1)} %copy-done.8), channel_id=1, source_target_pairs={{0,2},{1,3},{2,0},{3,1},{4,6},{5,7},{6,4},{7,5},{8,10},{9,11},{10,... | collective-permute-start | bytes 1658888 | tf_op jit(solution)/shard_map/ppermute | solution.py:1068
  73.9 23.6 %collective-permute-start.6 = (bf16[144,1920]{1,0:T(8,128)(2,1)S(1)}, bf16[144,1920]{1,0:T(8,128)(2,1)S(1)}, u32[]{:S(2)}, u32[]{:S(2)}) collective-permute-start(bf16[144,1920]{1,0:T(8,128)(2,1)S(1)} %copy-done.8), channel_id=1, source_target_pairs={{0,3},{1,0},{2,1},{3,2},{4,7},{5,4},{6,5},{7,6},{8,11},{9,8},{10,9... | collective-permute-start | bytes 1658888 | tf_op jit(solution)/shard_map/ppermute | solution.py:1068
  75.0 22.5 %collective-permute-start.11 = (bf16[144,1920]{1,0:T(8,128)(2,1)S(1)}, bf16[144,1920]{1,0:T(8,128)(2,1)}, u32[]{:S(2)}, u32[]{:S(2)}) collective-permute-start(bf16[144,1920]{1,0:T(8,128)(2,1)S(1)} %copy-done.7), channel_id=1, source_target_pairs={{0,4},{1,5},{2,6},{3,7},{4,8},{5,9},{6,10},{7,11},{8,12},{9,13},{1... | collective-permute-start | bytes 1658888 | tf_op jit(solution)/shard_map/ppermute | solution.py:1068
  76.6 20.9 %collective-permute-start.10 = (bf16[144,1920]{1,0:T(8,128)(2,1)S(1)}, bf16[144,1920]{1,0:T(8,128)(2,1)}, u32[]{:S(2)}, u32[]{:S(2)}) collective-permute-start(bf16[144,1920]{1,0:T(8,128)(2,1)S(1)} %copy-done.7), channel_id=1, source_target_pairs={{0,8},{1,9},{2,10},{3,11},{4,12},{5,13},{6,14},{7,15},{8,0},{9,1},... | collective-permute-start | bytes 1658888 | tf_op jit(solution)/shard_map/ppermute | solution.py:1068
  103.8 26.5 %collective-permute-start.16 = (bf16[144,3072]{1,0:T(8,128)(2,1)S(1)}, bf16[144,3072]{1,0:T(8,128)(2,1)S(1)}, u32[]{:S(2)}, u32[]{:S(2)}) collective-permute-start(bf16[144,3072]{1,0:T(8,128)(2,1)S(1)} %pad_maximum_fusion.rest_2_), channel_id=1, source_target_pairs={{0,1},{1,2},{2,3},{3,0},{4,5},{5,6},{6,7},{7,4},{8,9},{9,10},{10,1... | collective-permute-start | bytes 2654216 | tf_op jit(solution)/shard_map/ppermute | solution.py:1068
  113.4 16.0 %collective-permute-start.12 = (bf16[16,1792]{1,0:T(8,128)(2,1)S(1)}, bf16[16,1792]{1,0:T(8,128)(2,1)S(1)}, u32[]{:S(2)}, u32[]{:S(2)}) collective-permute-start(bf16[16,1792]{1,0:T(8,128)(2,1)S(1)} %slice.169), channel_id=1, source_target_pairs={{0,2},{1,3},{2,4},{3,5},{4,6},{5,7},{6,8},{7,9},{8,10},{9,11},{10,... | collective-permute-start | bytes 172040 | tf_op jit(solution)/shard_map/ppermute | solution.py:1266
  117.9 60.6 %collective-permute-start.15 = (bf16[144,3072]{1,0:T(8,128)(2,1)S(1)}, bf16[144,3072]{1,0:T(8,128)(2,1)S(1)}, u32[]{:S(2)}, u32[]{:S(2)}) collective-permute-start(bf16[144,3072]{1,0:T(8,128)(2,1)S(1)} %pad_maximum_fusion.rest_2_), channel_id=1, source_target_pairs={{0,2},{1,3},{2,0},{3,1},{4,6},{5,7},{6,4},{7,5},{8,10},{9,11},{10,... | collective-permute-start | bytes 2654216 | tf_op jit(solution)/shard_map/ppermute | solution.py:1068
  119.0 59.5 %collective-permute-start.14 = (bf16[144,3072]{1,0:T(8,128)(2,1)S(1)}, bf16[144,3072]{1,0:T(8,128)(2,1)}, u32[]{:S(2)}, u32[]{:S(2)}) collective-permute-start(bf16[144,3072]{1,0:T(8,128)(2,1)S(1)} %pad_maximum_fusion.rest_2_), channel_id=1, source_target_pairs={{0,3},{1,0},{2,1},{3,2},{4,7},{5,4},{6,5},{7,6},{8,11},{9,8},{10,9... | collective-permute-start | bytes 2654216 | tf_op jit(solution)/shard_map/ppermute | solution.py:1068
  120.4 58.1 %collective-permute-start.19 = (bf16[144,3072]{1,0:T(8,128)(2,1)S(1)}, bf16[144,3072]{1,0:T(8,128)(2,1)}, u32[]{:S(2)}, u32[]{:S(2)}) collective-permute-start(bf16[144,3072]{1,0:T(8,128)(2,1)S(1)} %pad_maximum_fusion.1.rest_6_), channel_id=1, source_target_pairs={{0,4},{1,5},{2,6},{3,7},{4,8},{5,9},{6,10},{7,11},{8,12},{9,13},{1... | collective-permute-start | bytes 2654216 | tf_op jit(solution)/shard_map/ppermute | solution.py:1068
  129.5 49.0 %collective-permute-start.18 = (bf16[144,3072]{1,0:T(8,128)(2,1)S(1)}, bf16[144,3072]{1,0:T(8,128)(2,1)}, u32[]{:S(2)}, u32[]{:S(2)}) collective-permute-start(bf16[144,3072]{1,0:T(8,128)(2,1)S(1)} %pad_maximum_fusion.1.rest_6_), channel_id=1, source_target_pairs={{0,8},{1,9},{2,10},{3,11},{4,12},{5,13},{6,14},{7,15},{8,0},{9,1},... | collective-permute-start | bytes 2654216 | tf_op jit(solution)/shard_map/ppermute | solution.py:1068
  130.4 48.2 %collective-permute-start.17 = (bf16[144,3072]{1,0:T(8,128)(2,1)S(1)}, bf16[144,3072]{1,0:T(8,128)(2,1)}, u32[]{:S(2)}, u32[]{:S(2)}) collective-permute-start(bf16[144,3072]{1,0:T(8,128)(2,1)S(1)} %pad_maximum_fusion.1.rest_6_), channel_id=1, source_target_pairs={{0,12},{1,13},{2,14},{3,15},{4,0},{5,1},{6,2},{7,3},{8,4},{9,5},{1... | collective-permute-start | bytes 2654216 | tf_op jit(solution)/shard_map/ppermute | solution.py:1068
  138.1 31.7 %all-to-all-start = ((bf16[8,80,384]{2,1,0:T(8,128)(2,1)}), bf16[8,80,384]{2,1,0:T(8,128)(2,1)}, u32[]{:S(2)}, u32[]{:S(2)}) async-start(bf16[8,80,384]{2,1,0:T(8,128)(2,1)} %get-tuple-element.134.msg_in), calls=%async_computation | async-start | bytes 983040 | tf_op jit(solution)/shard_map/all_to_all | solution.py:1261
  223.1 14.5 %all-to-all-start.2 = ((bf16[8,80,384]{2,1,0:T(8,128)(2,1)}), bf16[8,80,384]{2,1,0:T(8,128)(2,1)S(1)}, u32[]{:S(2)}, u32[]{:S(2)}) async-start(bf16[8,80,384]{2,1,0:T(8,128)(2,1)} %get-tuple-element.151.msg_in), calls=%async_computation.2 | async-start | bytes 983040 | tf_op jit(solution)/shard_map/all_to_all | solution.py:1261
  240.3 20.3 %all-to-all-start.3 = ((bf16[8,64,384]{2,1,0:T(8,128)(2,1)}), bf16[8,64,384]{2,1,0:T(8,128)(2,1)S(1)}, u32[]{:S(2)}, u32[]{:S(2)}) async-start(bf16[8,64,384]{2,1,0:T(8,128)(2,1)} %chunk_scan.5), calls=%async_computation.3 | async-start | bytes 786432 | tf_op jit(solution)/shard_map/all_to_all | solution.py:1261
  247.2 222.9 %reduce-scatter.7.cloned.1.call-start = ((), (), s32[]{:S(2)}) async-start(), calls=%async_computation.17 | async-start | bytes 5898240 | tf_op jit(solution)/shard_map/reduce_scatter | solution.py:1476
  287.4 182.8 %reduce-scatter.5.cloned.1.call-start = ((), (), s32[]{:S(2)}) async-start(), calls=%async_computation.16 | async-start | bytes 5898240 | tf_op jit(solution)/shard_map/reduce_scatter | solution.py:1476
  295.1 17.8 %all-to-all-start.4 = ((bf16[8,80,384]{2,1,0:T(8,128)(2,1)}), bf16[8,80,384]{2,1,0:T(8,128)(2,1)S(1)}, u32[]{:S(2)}, u32[]{:S(2)}) async-start(bf16[8,80,384]{2,1,0:T(8,128)(2,1)} %get-tuple-element.162.token), calls=%async_computation.4 | async-start | bytes 983040 | tf_op jit(solution)/shard_map/all_to_all | solution.py:1261
  304.9 43.3 %collective-permute-start.24 = (f32[128,1536]{1,0:T(8,128)S(1)}, f32[128,1536]{1,0:T(8,128)S(1)}, u32[]{:S(2)}, u32[]{:S(2)}) collective-permute-start(f32[128,1536]{1,0:T(8,128)S(1)} %get-tuple-element.257), channel_id=1, source_target_pairs={{64,65},{65,64},{66,67},{67,66},{68,69},{69,68},{70,71},{71,70},{7... | collective-permute-start | bytes 2359304 | tf_op jit(solution)/shard_map/ppermute | solution.py:1570
  315.7 15.9 %all-to-all-start.5 = ((bf16[8,64,384]{2,1,0:T(8,128)(2,1)}), bf16[8,64,384]{2,1,0:T(8,128)(2,1)S(1)}, u32[]{:S(2)}, u32[]{:S(2)}) async-start(bf16[8,64,384]{2,1,0:T(8,128)(2,1)} %chunk_scan.6), calls=%async_computation.5 | async-start | bytes 786432 | tf_op jit(solution)/shard_map/all_to_all | solution.py:1261
  322.9 147.3 %reduce-scatter.9.cloned.1.call-start = ((), (), s32[]{:S(2)}) async-start(), calls=%async_computation.18 | async-start | bytes 7372800 | tf_op jit(solution)/shard_map/reduce_scatter | solution.py:1476
  368.7 140.5 %reduce-scatter.11.cloned.1.call-start = ((), (), s32[]{:S(2)}) async-start(), calls=%async_computation.19 | async-start | bytes 5898240 | tf_op jit(solution)/shard_map/reduce_scatter | solution.py:1476
  394.4 17.1 %all-to-all-start.6 = ((bf16[8,80,384]{2,1,0:T(8,128)(2,1)}), bf16[8,80,384]{2,1,0:T(8,128)(2,1)S(1)}, u32[]{:S(2)}, u32[]{:S(2)}) async-start(bf16[8,80,384]{2,1,0:T(8,128)(2,1)} %get-tuple-element.182.token), calls=%async_computation.6 | async-start | bytes 983040 | tf_op jit(solution)/shard_map/all_to_all | solution.py:1261
  414.3 17.5 %all-to-all-start.7 = ((bf16[8,64,384]{2,1,0:T(8,128)(2,1)}), bf16[8,64,384]{2,1,0:T(8,128)(2,1)S(1)}, u32[]{:S(2)}, u32[]{:S(2)}) async-start(bf16[8,64,384]{2,1,0:T(8,128)(2,1)} %chunk_scan.7), calls=%async_computation.7 | async-start | bytes 786432 | tf_op jit(solution)/shard_map/all_to_all | solution.py:1261
  462.9 65.2 %all-to-all-start.8 = ((bf16[4,384,1664]{2,1,0:T(8,128)(2,1)}), bf16[4,384,1664]{2,1,0:T(8,128)(2,1)}, u32[]{:S(2)}, u32[]{:S(2)}) async-start(bf16[4,384,1664]{2,1,0:T(8,128)(2,1)} %terms.2.rest_10_), calls=%async_computation.11 | async-start | bytes 10223616 | tf_op jit(solution)/shard_map/all_to_all | solution.py:1257
  488.3 32.6 %collective-permute-start.29 = (bf16[416,1792]{1,0:T(8,128)(2,1)}, bf16[416,1792]{1,0:T(8,128)(2,1)S(1)}, u32[]{:S(2)}, u32[]{:S(2)}) collective-permute-start(bf16[416,1792]{1,0:T(8,128)(2,1)} %get-tuple-element.213), channel_id=1, source_target_pairs={{0,1},{1,2},{2,3},{3,0},{4,5},{5,6},{6,7},{7,4},{8,9},{9,10},{10,1... | collective-permute-start | bytes 4472840 | tf_op jit(solution)/shard_map/ppermute | solution.py:1068
  489.3 32.3 %collective-permute-start.30 = (bf16[416,1792]{1,0:T(8,128)(2,1)}, bf16[416,1792]{1,0:T(8,128)(2,1)S(1)}, u32[]{:S(2)}, u32[]{:S(2)}) collective-permute-start(bf16[416,1792]{1,0:T(8,128)(2,1)} %get-tuple-element.214), channel_id=1, source_target_pairs={{0,3},{1,0},{2,1},{3,2},{4,7},{5,4},{6,5},{7,6},{8,11},{9,8},{10,9... | collective-permute-start | bytes 4472840 | tf_op jit(solution)/shard_map/ppermute | solution.py:1068
  528.1 62.4 %all-to-all-start.9 = ((bf16[4,96,6528]{2,1,0:T(8,128)(2,1)}), bf16[4,96,6528]{2,1,0:T(8,128)(2,1)}, u32[]{:S(2)}, u32[]{:S(2)}) async-start(bf16[4,96,6528]{2,1,0:T(8,128)(2,1)} %fold.4.rest_1_), calls=%async_computation.13 | async-start | bytes 10027008 | tf_op jit(solution)/shard_map/all_to_all | solution.py:1257
  533.5 37.2 %collective-permute-start.34 = (bf16[416,1792]{1,0:T(8,128)(2,1)}, bf16[416,1792]{1,0:T(8,128)(2,1)S(1)}, u32[]{:S(2)}, u32[]{:S(2)}) collective-permute-start(bf16[416,1792]{1,0:T(8,128)(2,1)} %get-tuple-element.220), channel_id=1, source_target_pairs={{0,2},{1,3},{2,0},{3,1},{4,6},{5,7},{6,4},{7,5},{8,10},{9,11},{10,... | collective-permute-start | bytes 4472840 | tf_op jit(solution)/shard_map/ppermute | solution.py:1068
  542.6 38.5 %collective-permute-start.28 = (f32[128,1536]{1,0:T(8,128)S(1)}, f32[128,1536]{1,0:T(8,128)S(1)}, u32[]{:S(2)}, u32[]{:S(2)}) collective-permute-start(f32[128,1536]{1,0:T(8,128)S(1)} %get-tuple-element.260), channel_id=1, source_target_pairs={{0,1},{1,0},{2,3},{3,2},{4,5},{5,4},{6,7},{7,6},{8,9},{9,8},{10,11... | collective-permute-start | bytes 2359304 | tf_op jit(solution)/shard_map/ppermute | solution.py:1570
  550.4 35.8 %collective-permute-start.31 = (bf16[96,1664]{1,0:T(8,128)(2,1)}, bf16[96,1664]{1,0:T(8,128)(2,1)S(1)}, u32[]{:S(2)}, u32[]{:S(2)}) collective-permute-start(bf16[96,1664]{1,0:T(8,128)(2,1)} %get-tuple-element.216), channel_id=1, source_target_pairs={{0,1},{1,2},{2,3},{3,0},{4,5},{5,6},{6,7},{7,4},{8,9},{9,10},{10,1... | collective-permute-start | bytes 958472 | tf_op jit(solution)/shard_map/ppermute | solution.py:1068
  577.5 21.5 %collective-permute-start.35 = (bf16[128,1792]{1,0:T(8,128)(2,1)}, bf16[128,1792]{1,0:T(8,128)(2,1)}, u32[]{:S(2)}, u32[]{:S(2)}) collective-permute-start(bf16[128,1792]{1,0:T(8,128)(2,1)} %get-tuple-element.223), channel_id=1, source_target_pairs={{0,4},{1,5},{2,6},{3,7},{4,8},{5,9},{6,10},{7,11},{8,12},{9,13},{1... | collective-permute-start | bytes 1376264 | tf_op jit(solution)/shard_map/ppermute | solution.py:1068
  578.9 16.5 %collective-permute-start.32 = (bf16[96,1664]{1,0:T(8,128)(2,1)}, bf16[96,1664]{1,0:T(8,128)(2,1)}, u32[]{:S(2)}, u32[]{:S(2)}) collective-permute-start(bf16[96,1664]{1,0:T(8,128)(2,1)} %get-tuple-element.217), channel_id=1, source_target_pairs={{0,2},{1,3},{2,0},{3,1},{4,6},{5,7},{6,4},{7,5},{8,10},{9,11},{10,... | collective-permute-start | bytes 958472 | tf_op jit(solution)/shard_map/ppermute | solution.py:1068
  580.2 16.6 %collective-permute-start.33 = (bf16[96,1664]{1,0:T(8,128)(2,1)}, bf16[96,1664]{1,0:T(8,128)(2,1)}, u32[]{:S(2)}, u32[]{:S(2)}) collective-permute-start(bf16[96,1664]{1,0:T(8,128)(2,1)} %get-tuple-element.218), channel_id=1, source_target_pairs={{0,3},{1,0},{2,1},{3,2},{4,7},{5,4},{6,5},{7,6},{8,11},{9,8},{10,9... | collective-permute-start | bytes 958472 | tf_op jit(solution)/shard_map/ppermute | solution.py:1068
  581.1 20.0 %collective-permute-start.36 = (bf16[128,1792]{1,0:T(8,128)(2,1)}, bf16[128,1792]{1,0:T(8,128)(2,1)}, u32[]{:S(2)}, u32[]{:S(2)}) collective-permute-start(bf16[128,1792]{1,0:T(8,128)(2,1)} %get-tuple-element.224), channel_id=1, source_target_pairs={{0,8},{1,9},{2,10},{3,11},{4,12},{5,13},{6,14},{7,15},{8,0},{9,1},... | collective-permute-start | bytes 1376264 | tf_op jit(solution)/shard_map/ppermute | solution.py:1068
  586.2 20.9 %collective-permute-start.37 = (bf16[128,1792]{1,0:T(8,128)(2,1)}, bf16[128,1792]{1,0:T(8,128)(2,1)}, u32[]{:S(2)}, u32[]{:S(2)}) collective-permute-start(bf16[128,1792]{1,0:T(8,128)(2,1)} %get-tuple-element.225), channel_id=1, source_target_pairs={{0,12},{1,13},{2,14},{3,15},{4,0},{5,1},{6,2},{7,3},{8,4},{9,5},{1... | collective-permute-start | bytes 1376264 | tf_op jit(solution)/shard_map/ppermute | solution.py:1068
  595.4 19.3 %collective-permute-start.42 = (bf16[24,6528]{1,0:T(8,128)(2,1)}, bf16[24,6528]{1,0:T(8,128)(2,1)S(1)}, u32[]{:S(2)}, u32[]{:S(2)}) collective-permute-start(bf16[24,6528]{1,0:T(8,128)(2,1)} %get-tuple-element.231), channel_id=1, source_target_pairs={{0,2},{1,3},{2,0},{3,1},{4,6},{5,7},{6,4},{7,5},{8,10},{9,11},{10,... | collective-permute-start | bytes 940040 | tf_op jit(solution)/shard_map/ppermute | solution.py:1068
  596.9 20.4 %collective-permute-start.43 = (bf16[24,6528]{1,0:T(8,128)(2,1)}, bf16[24,6528]{1,0:T(8,128)(2,1)}, u32[]{:S(2)}, u32[]{:S(2)}) collective-permute-start(bf16[24,6528]{1,0:T(8,128)(2,1)} %get-tuple-element.232), channel_id=1, source_target_pairs={{0,1},{1,2},{2,3},{3,0},{4,5},{5,6},{6,7},{7,4},{8,9},{9,10},{10,1... | collective-permute-start | bytes 940040 | tf_op jit(solution)/shard_map/ppermute | solution.py:1068
  599.0 18.2 %collective-permute-start.44 = (bf16[24,6528]{1,0:T(8,128)(2,1)}, bf16[24,6528]{1,0:T(8,128)(2,1)}, u32[]{:S(2)}, u32[]{:S(2)}) collective-permute-start(bf16[24,6528]{1,0:T(8,128)(2,1)} %get-tuple-element.233), channel_id=1, source_target_pairs={{0,3},{1,0},{2,1},{3,2},{4,7},{5,4},{6,5},{7,6},{8,11},{9,8},{10,9... | collective-permute-start | bytes 940040 | tf_op jit(solution)/shard_map/ppermute | solution.py:1068
  614.0 17.8 %collective-permute-start.39 = (bf16[56,3456]{1,0:T(8,128)(2,1)}, bf16[56,3456]{1,0:T(8,128)(2,1)S(1)}, u32[]{:S(2)}, u32[]{:S(2)}) collective-permute-start(bf16[56,3456]{1,0:T(8,128)(2,1)} %get-tuple-element.229), channel_id=1, source_target_pairs={{0,16},{16,32},{32,48},{48,0},{1,17},{17,33},{33,49},{49,1},{2,18}... | collective-permute-start | bytes 1161224 | tf_op jit(solution)/shard_map/ppermute | solution.py:1068
  614.7 17.4 %collective-permute-start.40 = (bf16[56,3456]{1,0:T(8,128)(2,1)}, bf16[56,3456]{1,0:T(8,128)(2,1)S(1)}, u32[]{:S(2)}, u32[]{:S(2)}) collective-permute-start(bf16[56,3456]{1,0:T(8,128)(2,1)} %get-tuple-element.230), channel_id=1, source_target_pairs={{0,48},{16,0},{32,16},{48,32},{1,49},{17,1},{33,17},{49,33},{2,50}... | collective-permute-start | bytes 1161224 | tf_op jit(solution)/shard_map/ppermute | solution.py:1068
  634.5 16.6 %collective-permute-start.47 = (f32[24,1536]{1,0:T(8,128)S(1)}, f32[24,1536]{1,0:T(8,128)S(1)}, u32[]{:S(2)}, u32[]{:S(2)}) collective-permute-start(f32[24,1536]{1,0:T(8,128)S(1)} %get-tuple-element.270), channel_id=1, source_target_pairs={{0,64},{1,0},{2,65},{3,1},{4,66},{5,2},{6,67},{7,3},{8,68},{9,4},{... | collective-permute-start | bytes 442376 | tf_op jit(solution)/shard_map/ppermute | solution.py:1609
  (71 other events, 537.2 us)
Sparse Core Ops, SparseCore 0:
  60.8 32.9 all-gather.8
  95.4 64.6 all-gather.4
  161.7 92.5 all-gather.6
  287.5 52.2 reduce-scatter.6
  342.1 50.8 reduce-scatter.4
  395.3 60.5 reduce-scatter.8
  458.2 50.8 reduce-scatter.10
